TPU v7x, 32 devices: a whole 2x2x4 slice. The times are simulated.
32 devices in a mesh: dp: 16 (over z, y, core), chan: 2 (over x).
Axes of the slice: x: 2, y: 2, z: 4, core: 2. Of those that a mesh axis runs over, the one named last changes fastest.
Arguments:
- patches: bfloat16 [16, 1600, 192], P('dp'), may hold values from -6 to 6
- labels: int32 [16, 1600], P('dp'), may hold values from 0 to 18
- offset_target: float32 [16, 2, 1600], P('dp'), may hold values from -8 to 8
- offset_valid: int32 [16, 1600], P('dp'), may hold values 0 or 1
- depth_target: float32 [16, 1600], P('dp'), may hold values from 0.2 to 2
- lidar_valid: int32 [16, 1600], P('dp'), may hold values from 0 to 1
- crop_mask: int32 [16, 1600], P('dp'), may hold values from 0 to 1, as said below
- stem_weight: float32 [192, 2, 1024], P(None, 'chan', 'dp'), may hold values from -0.4375 to 0.4375
- stem_first: float32 [192, 2, 1024], P(None, 'chan', 'dp'), may hold values from -2.3841858e-06 to 2.3841858e-06
- stem_second: float32 [192, 2, 1024], P(None, 'chan', 'dp'), may hold values from 2.4518851e-14 to 9.8075404e-14
- bottle_weight: float32 [2, 2048, 512], P(None, 'dp', 'chan'), may hold values from -0.125 to 0.125
- bottle_first: float32 [2, 2048, 512], P(None, 'dp', 'chan'), may hold values from -6.67572e-06 to 6.67572e-06
- bottle_second: float32 [2, 2048, 512], P(None, 'dp', 'chan'), may hold values from 1.9155352e-13 to 7.662141e-13
- middle_weight: float32 [9, 512, 512], P(None, 'dp', 'chan'), may hold values from -0.09375 to 0.09375
- middle_first: float32 [9, 512, 512], P(None, 'dp', 'chan'), may hold values from -5.722046e-06 to 5.722046e-06
- middle_second: float32 [9, 512, 512], P(None, 'dp', 'chan'), may hold values from 1.5324282e-13 to 6.1297126e-13
- pyramid_weight: float32 [29, 2048, 256], P(None, 'dp', 'chan'), may hold values from -0.078125 to 0.078125
- pyramid_first: float32 [29, 2048, 256], P(None, 'dp', 'chan'), may hold values from -3.0517578e-05 to 3.0517578e-05
- pyramid_second: float32 [29, 2048, 256], P(None, 'dp', 'chan'), may hold values from 2.451885e-12 to 3.923016e-11
- project_weight: float32 [5, 256, 256], P(None, 'chan', 'dp'), may hold values from -0.15625 to 0.15625
- project_first: float32 [5, 256, 256], P(None, 'chan', 'dp'), may hold values from -3.0517578e-05 to 3.0517578e-05
- project_second: float32 [5, 256, 256], P(None, 'chan', 'dp'), may hold values from 2.451885e-12 to 3.923016e-11
- head_weight: float32 [256, 22], P('dp'), may hold values from -0.375 to 0.375
- head_first: float32 [256, 22], P('dp'), may hold values from -3.0517578e-05 to 3.0517578e-05
- head_second: float32 [256, 22], P('dp'), may hold values from 2.451885e-12 to 3.923016e-11
- norm_gains: float32 [2, 2, 1280], P(None, 'chan'), may hold values from 0.5 to 1.5
- norm_first: float32 [2, 2, 1280], P(None, 'chan'), may hold values from -3.0517578e-05 to 3.0517578e-05
- norm_second: float32 [2, 2, 1280], P(None, 'chan'), may hold values from 2.451885e-12 to 3.923016e-11
- task_params: float32 [25], replicated, may hold values from -1 to 1
- task_first: float32 [25], replicated, may hold values from -3.0517578e-05 to 3.0517578e-05
- task_second: float32 [25], replicated, may hold values from 2.451885e-12 to 3.923016e-11
Outputs:
- total_loss: float32 [], replicated
- grad_norm: float32 [], replicated
- new_stem: float32 [192, 2, 1024], P(None, 'chan', 'dp')
- new_stem_first: float32 [192, 2, 1024], P(None, 'chan', 'dp')
- new_stem_second: float32 [192, 2, 1024], P(None, 'chan', 'dp')
- new_bottle: float32 [2, 2048, 512], P(None, 'dp', 'chan')
- new_bottle_first: float32 [2, 2048, 512], P(None, 'dp', 'chan')
- new_bottle_second: float32 [2, 2048, 512], P(None, 'dp', 'chan')
- new_middle: float32 [9, 512, 512], P(None, 'dp', 'chan')
- new_middle_first: float32 [9, 512, 512], P(None, 'dp', 'chan')
- new_middle_second: float32 [9, 512, 512], P(None, 'dp', 'chan')
- new_pyramid: float32 [29, 2048, 256], P(None, 'dp', 'chan')
- new_pyramid_first: float32 [29, 2048, 256], P(None, 'dp', 'chan')
- new_pyramid_second: float32 [29, 2048, 256], P(None, 'dp', 'chan')
- new_project: float32 [5, 256, 256], P(None, 'chan', 'dp')
- new_project_first: float32 [5, 256, 256], P(None, 'chan', 'dp')
- new_project_second: float32 [5, 256, 256], P(None, 'chan', 'dp')
- new_head: float32 [256, 22], P('dp')
- new_head_first: float32 [256, 22], P('dp')
- new_head_second: float32 [256, 22], P('dp')
- new_norm: float32 [2, 2, 1280], P(None, 'chan')
- new_norm_first: float32 [2, 2, 1280], P(None, 'chan')
- new_norm_second: float32 [2, 2, 1280], P(None, 'chan')
- new_task: float32 [25], replicated
- new_task_first: float32 [25], replicated
- new_task_second: float32 [25], replicated
Inputs may be any that keep to these rules, and one draw needn't show every extreme that they name: `crop_mask`: each image's mask is 1 on all positions or on exactly the positions of the first half of its 40 canvas rows.
All inputs are finite; a program needn't handle non-finite values. No bound on the sum of `offset_valid` on one device may be relied on, other than what follows from the above.
Results may differ from a plain program's by a relative error of at most 0.017.
Values may be sent and summed in bfloat16 or wider, within the bound.
A program may use at most 256 MiB of HBM per device.

v0:
```python
import jax
import jax.numpy as jnp
from jax import lax
from jax.sharding import PartitionSpec as P

D = 2048
MID = 512
BRANCH = 256
CLASSES = 19
PATCH = 192
FH = 40
FW = 40
STEP = 10
POSITIONS = 1600


pyramid_rates = (0, 12, 24, 36)
norm_eps = 1e-05
clip_level = 0.01
adam_eps = 1e-08
decay_rate = 0.01


def shift_map(field, row_step, col_step):
    canvas_rows, canvas_cols = (field.shape[1], field.shape[2])
    padded = jnp.pad(
        field,
        (
            (0, 0),
            (max(-row_step, 0), max(row_step, 0)),
            (max(-col_step, 0), max(col_step, 0)),
            (0, 0),
        ),
    )
    row_start = max(row_step, 0)
    col_start = max(col_step, 0)
    return padded[:, row_start : row_start + canvas_rows, col_start : col_start + canvas_cols, :]


def conv_taps(dilations):
    offsets = []
    owners = []
    for branch, dilation in enumerate(dilations):
        if dilation == 0:
            offsets.append((0, 0))
            owners.append(branch)
        else:
            for tap_index in range(9):
                offsets.append(((tap_index // 3 - 1) * dilation, (tap_index % 3 - 1) * dilation))
                owners.append(branch)
    return (offsets, owners)


def conv_forward(canvas, weight, offsets, owners):
    tap_parts = jnp.einsum("bhwc,tcd->bhwtd", canvas, weight, preferred_element_type=jnp.float32)
    totals = [
        jnp.zeros(tap_parts.shape[:3] + tap_parts.shape[4:], jnp.float32)
        for branch in range(owners[-1] + 1)
    ]
    for tap_index, offset in enumerate(offsets):
        totals[owners[tap_index]] = totals[owners[tap_index]] + shift_map(
            tap_parts[:, :, :, tap_index], offset[0], offset[1]
        )
    return totals


def conv_backward(canvas, weight, upstream, offsets, owners):
    shifted = jnp.stack(
        [
            shift_map(upstream[owners[tap_index]], -offset[0], -offset[1])
            for tap_index, offset in enumerate(offsets)
        ],
        axis=3,
    )
    back_grad = jnp.einsum("bhwtd,tcd->bhwc", shifted, weight, preferred_element_type=jnp.float32)
    weight_grad = jnp.einsum("bhwc,bhwtd->tcd", canvas, shifted, preferred_element_type=jnp.float32)
    return (back_grad, weight_grad)


def gelu_grad(values, upstream):
    return jax.vjp(jax.nn.gelu, values)[1](upstream)[0]


def chan_in(values):
    return lax.all_gather(values, "chan", axis=1, tiled=True)


def chan_sum(values):
    return lax.psum_scatter(
        values.astype(jnp.bfloat16), "chan", scatter_dimension=1, tiled=True
    ).astype(jnp.float32)


def rows_product(act_low, weight_low):
    return lax.psum_scatter(
        jnp.einsum("pc,dc->pd", act_low, weight_low, preferred_element_type=jnp.float32).astype(
            jnp.bfloat16
        ),
        "chan",
        scatter_dimension=1,
        tiled=True,
    ).astype(jnp.float32)


def norm_back(upstream, normed):
    return lax.psum((jnp.sum(upstream * normed, 0), jnp.sum(upstream, 0)), "dp")


def adam_step(weight, first, second, gradient, factor, rate, decay):
    gradient = gradient * factor
    first_new = 0.5 * first + 0.5 * gradient
    second_new = 0.5 * second + 0.5 * gradient * gradient
    direction = (
        first_new / (1.0 - 0.5**STEP) / (jnp.sqrt(second_new / (1.0 - 0.5**STEP)) + adam_eps)
    )
    return (weight - rate * (direction + decay * weight), first_new, second_new)


def on_device(
    patches,
    labels,
    offset_target,
    offset_valid,
    depth_target,
    lidar_valid,
    crop_mask,
    stem_weight,
    stem_first,
    stem_second,
    bottle_weight,
    bottle_first,
    bottle_second,
    middle_weight,
    middle_first,
    middle_second,
    pyramid_weight,
    pyramid_first,
    pyramid_second,
    project_weight,
    project_first,
    project_second,
    head_weight,
    head_first,
    head_second,
    norm_gains,
    norm_first,
    norm_second,
    task_params,
    task_first,
    task_second,
):
    chan_place = lax.axis_index("chan")
    images = patches.shape[0]
    row_count = images * FH * FW
    crop_field = crop_mask.astype(jnp.float32).reshape(row_count, 1)
    offset_field = crop_field[:, 0] * offset_valid.astype(jnp.float32).reshape(row_count)
    lidar_field = crop_field[:, 0] * lidar_valid.astype(jnp.float32).reshape(row_count)
    local_counts = jnp.stack([jnp.sum(crop_field), jnp.sum(offset_field), jnp.sum(lidar_field)])
    stem_low, bottle_low, middle_low, pyramid_low, project_low, head_low = (
        lax.all_gather(stem_weight.astype(jnp.bfloat16), "dp", axis=2, tiled=True),
        lax.all_gather(bottle_weight.astype(jnp.bfloat16), "dp", axis=1, tiled=True),
        lax.all_gather(middle_weight.astype(jnp.bfloat16), "dp", axis=1, tiled=True),
        lax.all_gather(pyramid_weight.astype(jnp.bfloat16), "dp", axis=1, tiled=True),
        lax.all_gather(project_weight.astype(jnp.bfloat16), "dp", axis=2, tiled=True),
        lax.all_gather(head_weight.astype(jnp.bfloat16), "dp", axis=0, tiled=True),
    )
    half_width = stem_low.shape[2]
    patch_rows = patches.reshape(row_count, PATCH)
    stream_own = crop_field * jnp.dot(
        patch_rows, stem_low.reshape(PATCH, half_width), preferred_element_type=jnp.float32
    )
    stream_low = chan_in(stream_own.astype(jnp.bfloat16))
    reduce_low = bottle_low[0]
    expand_low = bottle_low[1]
    mid_count = reduce_low.shape[1]
    first_pre = jnp.dot(stream_low, reduce_low, preferred_element_type=jnp.float32)
    sum_one, square_one, counts = lax.psum(
        (
            jnp.sum(crop_field * first_pre, 0),
            jnp.sum(crop_field * first_pre * first_pre, 0),
            local_counts,
        ),
        "dp",
    )
    crop_total = counts[0]
    mean_one = sum_one / crop_total
    scale_one = lax.rsqrt(square_one / crop_total - mean_one * mean_one + norm_eps)
    normed_one = (first_pre - mean_one) * scale_one
    gain_one = norm_gains[0, 0, :mid_count]
    shift_one = norm_gains[1, 0, :mid_count]
    act_input = gain_one * normed_one + shift_one
    hidden_low = chan_in((crop_field * jax.nn.gelu(act_input)).astype(jnp.bfloat16))
    canvas_one = hidden_low.reshape(images, FH, FW, MID)
    middle_offsets, middle_owners = conv_taps((4,))
    second_pre = conv_forward(canvas_one, middle_low, middle_offsets, middle_owners)[0].reshape(
        row_count, mid_count
    )
    second_low = second_pre.astype(jnp.bfloat16)
    expand_sum = rows_product(second_low, expand_low)
    sum_two, square_two = lax.psum(
        (jnp.sum(crop_field * expand_sum, 0), jnp.sum(crop_field * expand_sum * expand_sum, 0)),
        "dp",
    )
    mean_two = sum_two / crop_total
    scale_two = lax.rsqrt(square_two / crop_total - mean_two * mean_two + norm_eps)
    normed_two = (expand_sum - mean_two) * scale_two
    gain_two = norm_gains[0, 0, mid_count:]
    shift_two = norm_gains[1, 0, mid_count:]
    stream_out = stream_own + crop_field * (gain_two * normed_two + shift_two)
    output_low = chan_in(stream_out.astype(jnp.bfloat16))
    canvas_two = output_low.reshape(images, FH, FW, D)
    crop_image = crop_field.reshape(images, POSITIONS)
    image_count = jnp.sum(crop_image, 1, keepdims=True)
    pooled = (
        jnp.einsum(
            "bpd,bp->bd",
            output_low.reshape(images, POSITIONS, D),
            crop_image.astype(jnp.bfloat16),
            preferred_element_type=jnp.float32,
        )
        / image_count
    )
    pooled_low = pooled.astype(jnp.bfloat16)
    pyramid_offsets, pyramid_owners = conv_taps(pyramid_rates)
    branch_pre = conv_forward(canvas_two, pyramid_low[:28], pyramid_offsets, pyramid_owners)
    pool_pre = jnp.dot(pooled_low, pyramid_low[28], preferred_element_type=jnp.float32)
    branch_width = pool_pre.shape[1]
    branch_acts = [
        jax.nn.gelu(branch_in).reshape(images, POSITIONS, branch_width) for branch_in in branch_pre
    ]
    branch_acts.append(
        jnp.broadcast_to(jax.nn.gelu(pool_pre)[:, None, :], (images, POSITIONS, branch_width))
    )
    concat_low = jnp.stack(branch_acts, 2).reshape(row_count, 5, branch_width).astype(jnp.bfloat16)
    project_pre = lax.psum(
        jnp.einsum(
            "pkc,kcd->pd", concat_low, project_low, preferred_element_type=jnp.float32
        ).astype(jnp.bfloat16),
        "chan",
    ).astype(jnp.float32)
    feature_low = jax.nn.gelu(project_pre).astype(jnp.bfloat16)
    task_scale = task_params[:3]
    logits = jnp.dot(feature_low, head_low, preferred_element_type=jnp.float32) + task_params[3:]
    class_logits = logits[:, :CLASSES]
    class_top = jnp.max(class_logits, 1, keepdims=True)
    class_exp = jnp.exp(class_logits - class_top)
    class_total = jnp.sum(class_exp, 1, keepdims=True)
    onehot = (
        labels.reshape(row_count, 1) == lax.broadcasted_iota(jnp.int32, (1, CLASSES), 1)
    ).astype(jnp.float32)
    seg_terms = crop_field[:, 0] * (
        class_top[:, 0] + jnp.log(class_total[:, 0]) - jnp.sum(class_logits * onehot, 1)
    )
    offset_err = logits[:, CLASSES : CLASSES + 2] - jnp.swapaxes(offset_target, 1, 2).reshape(
        row_count, 2
    )
    offset_root = jnp.sqrt(offset_err * offset_err + 1.0)
    depth_pre = logits[:, CLASSES + 2]
    depth_err = jax.nn.softplus(depth_pre) - depth_target.reshape(row_count)
    depth_root = jnp.sqrt(depth_err * depth_err + 1.0)
    local_sums = jnp.stack(
        [
            jnp.sum(seg_terms),
            jnp.sum(offset_field * jnp.sum(offset_root - 1.0, 1)),
            jnp.sum(lidar_field * (depth_root - 1.0)),
        ]
    )
    task_weights = jnp.exp(-task_scale) / counts
    logit_grad = jnp.concatenate(
        [
            task_weights[0] * crop_field * (class_exp / class_total - onehot),
            task_weights[1] * offset_field[:, None] * offset_err / offset_root,
            (task_weights[2] * lidar_field * depth_err / depth_root * jax.nn.sigmoid(depth_pre))[
                :, None
            ],
        ],
        axis=1,
    )
    logit_low = logit_grad.astype(jnp.bfloat16)
    loss_sums, bias_grad = lax.psum((local_sums, jnp.sum(logit_low.astype(jnp.float32), 0)), "dp")
    task_means = loss_sums / counts
    total_loss = jnp.sum(jnp.exp(-task_scale) * task_means + task_scale)
    scale_grad = 1.0 - jnp.exp(-task_scale) * task_means
    head_grad = jnp.einsum("pc,pk->ck", feature_low, logit_low, preferred_element_type=jnp.float32)
    feature_grad = jnp.einsum("pk,ck->pc", logit_low, head_low, preferred_element_type=jnp.float32)
    project_grad_low = gelu_grad(project_pre, feature_grad).astype(jnp.bfloat16)
    project_grad = jnp.einsum(
        "pkc,pd->kcd", concat_low, project_grad_low, preferred_element_type=jnp.float32
    )
    concat_grad = jnp.einsum(
        "pd,kcd->pkc", project_grad_low, project_low, preferred_element_type=jnp.float32
    )
    concat_grad = concat_grad.reshape(images, POSITIONS, 5, branch_width)
    branch_grads = [
        gelu_grad(
            branch_pre[order], concat_grad[:, :, order, :].reshape(images, FH, FW, branch_width)
        ).astype(jnp.bfloat16)
        for order in range(4)
    ]
    pool_grad_low = gelu_grad(pool_pre, jnp.sum(concat_grad[:, :, 4, :], 1)).astype(jnp.bfloat16)
    canvas_grad, taps_grad = conv_backward(
        canvas_two, pyramid_low[:28], branch_grads, pyramid_offsets, pyramid_owners
    )
    pool_weight_grad = jnp.einsum(
        "bd,bk->dk", pooled_low, pool_grad_low, preferred_element_type=jnp.float32
    )
    pooled_grad = (
        jnp.einsum("bk,dk->bd", pool_grad_low, pyramid_low[28], preferred_element_type=jnp.float32)
        / image_count
    )
    pyramid_grad = jnp.concatenate([taps_grad, pool_weight_grad[None]], axis=0)
    stream_part = (
        canvas_grad.reshape(images, POSITIONS, D) + crop_image[:, :, None] * pooled_grad[:, None, :]
    )
    stream_grad = chan_sum(stream_part.reshape(row_count, D))
    upstream_two = crop_field * stream_grad
    gain_two_grad, shift_two_grad = norm_back(upstream_two, normed_two)
    expand_grad = (
        crop_field
        * gain_two
        * scale_two
        * (upstream_two - (shift_two_grad + normed_two * gain_two_grad) / crop_total)
    )
    expand_grad_low = chan_in(expand_grad.astype(jnp.bfloat16))
    expand_weight_grad = jnp.einsum(
        "pd,pc->dc", expand_grad_low, second_low, preferred_element_type=jnp.float32
    )
    second_grad_low = jnp.einsum(
        "pd,dc->pc", expand_grad_low, expand_low, preferred_element_type=jnp.float32
    ).astype(jnp.bfloat16)
    hidden_part, middle_grad = conv_backward(
        canvas_one,
        middle_low,
        [second_grad_low.reshape(images, FH, FW, mid_count)],
        middle_offsets,
        middle_owners,
    )
    hidden_grad = chan_sum(hidden_part.reshape(row_count, MID))
    upstream_one = gelu_grad(act_input, crop_field * hidden_grad)
    gain_one_grad, shift_one_grad = norm_back(upstream_one, normed_one)
    first_grad_low = (
        crop_field
        * gain_one
        * scale_one
        * (upstream_one - (shift_one_grad + normed_one * gain_one_grad) / crop_total)
    ).astype(jnp.bfloat16)
    reduce_weight_grad = jnp.einsum(
        "pd,pc->dc", stream_low, first_grad_low, preferred_element_type=jnp.float32
    )
    start_grad = rows_product(first_grad_low, reduce_low) + stream_grad
    start_grad_low = (crop_field * start_grad).astype(jnp.bfloat16)
    stem_grad = jnp.einsum(
        "pi,pd->id", patch_rows, start_grad_low, preferred_element_type=jnp.float32
    ).reshape(PATCH, 1, half_width)
    bottle_grad = jnp.stack([reduce_weight_grad, expand_weight_grad])
    stem_red, bottle_red, middle_red, pyramid_red, project_red, head_red = (
        lax.psum_scatter(stem_grad, "dp", scatter_dimension=2, tiled=True),
        lax.psum_scatter(bottle_grad, "dp", scatter_dimension=1, tiled=True),
        lax.psum_scatter(middle_grad, "dp", scatter_dimension=1, tiled=True),
        lax.psum_scatter(pyramid_grad, "dp", scatter_dimension=1, tiled=True),
        lax.psum_scatter(project_grad, "dp", scatter_dimension=2, tiled=True),
        lax.psum_scatter(head_grad, "dp", scatter_dimension=0, tiled=True),
    )
    norm_grad = jnp.stack(
        [
            jnp.concatenate([gain_one_grad, gain_two_grad]),
            jnp.concatenate([shift_one_grad, shift_two_grad]),
        ]
    )[:, None, :]
    task_grad = jnp.concatenate([scale_grad, bias_grad])
    dp_first = (lax.axis_index("dp") == 0).astype(jnp.float32)
    chan_first = (chan_place == 0).astype(jnp.float32)
    own_squares = (
        jnp.sum(stem_red * stem_red)
        + jnp.sum(bottle_red * bottle_red)
        + jnp.sum(middle_red * middle_red)
        + jnp.sum(pyramid_red * pyramid_red)
        + jnp.sum(project_red * project_red)
        + chan_first * jnp.sum(head_red * head_red)
        + dp_first * jnp.sum(norm_grad * norm_grad)
        + dp_first * chan_first * jnp.sum(task_grad * task_grad)
    )
    grad_norm = jnp.sqrt(lax.psum(own_squares, ("dp", "chan")))
    factor = clip_level / jnp.maximum(grad_norm, clip_level)
    new_stem = adam_step(
        stem_weight, stem_first, stem_second, stem_red, factor, PATCH ** (-0.5), decay_rate
    )
    new_bottle = adam_step(
        bottle_weight, bottle_first, bottle_second, bottle_red, factor, D ** (-0.5), decay_rate
    )
    new_middle = adam_step(
        middle_weight,
        middle_first,
        middle_second,
        middle_red,
        factor,
        (9 * MID) ** (-0.5),
        decay_rate,
    )
    new_pyramid = adam_step(
        pyramid_weight,
        pyramid_first,
        pyramid_second,
        pyramid_red,
        factor,
        (3 * D) ** (-0.5),
        decay_rate,
    )
    new_project = adam_step(
        project_weight,
        project_first,
        project_second,
        project_red,
        factor,
        (5 * BRANCH) ** (-0.5),
        decay_rate,
    )
    new_head = adam_step(
        head_weight, head_first, head_second, head_red, factor, BRANCH ** (-0.5), decay_rate
    )
    new_norm = adam_step(norm_gains, norm_first, norm_second, norm_grad, factor, 0.3, 0.0)
    new_task = adam_step(task_params, task_first, task_second, task_grad, factor, 0.3, 0.0)
    return (
        total_loss,
        grad_norm,
        new_stem[0],
        new_stem[1],
        new_stem[2],
        new_bottle[0],
        new_bottle[1],
        new_bottle[2],
        new_middle[0],
        new_middle[1],
        new_middle[2],
        new_pyramid[0],
        new_pyramid[1],
        new_pyramid[2],
        new_project[0],
        new_project[1],
        new_project[2],
        new_head[0],
        new_head[1],
        new_head[2],
        new_norm[0],
        new_norm[1],
        new_norm[2],
        new_task[0],
        new_task[1],
        new_task[2],
    )


def solution(mesh):
    return jax.shard_map(
        on_device,
        mesh=mesh,
        in_specs=(
            P("dp", None, None),
            P("dp", None),
            P("dp", None, None),
            P("dp", None),
            P("dp", None),
            P("dp", None),
            P("dp", None),
            P(None, "chan", "dp"),
            P(None, "chan", "dp"),
            P(None, "chan", "dp"),
            P(None, "dp", "chan"),
            P(None, "dp", "chan"),
            P(None, "dp", "chan"),
            P(None, "dp", "chan"),
            P(None, "dp", "chan"),
            P(None, "dp", "chan"),
            P(None, "dp", "chan"),
            P(None, "dp", "chan"),
            P(None, "dp", "chan"),
            P(None, "chan", "dp"),
            P(None, "chan", "dp"),
            P(None, "chan", "dp"),
            P("dp", None),
            P("dp", None),
            P("dp", None),
            P(None, "chan", None),
            P(None, "chan", None),
            P(None, "chan", None),
            P(),
            P(),
            P(),
        ),
        out_specs=(
            P(),
            P(),
            P(None, "chan", "dp"),
            P(None, "chan", "dp"),
            P(None, "chan", "dp"),
            P(None, "dp", "chan"),
            P(None, "dp", "chan"),
            P(None, "dp", "chan"),
            P(None, "dp", "chan"),
            P(None, "dp", "chan"),
            P(None, "dp", "chan"),
            P(None, "dp", "chan"),
            P(None, "dp", "chan"),
            P(None, "dp", "chan"),
            P(None, "chan", "dp"),
            P(None, "chan", "dp"),
            P(None, "chan", "dp"),
            P("dp", None),
            P("dp", None),
            P("dp", None),
            P(None, "chan", None),
            P(None, "chan", None),
            P(None, "chan", None),
            P(),
            P(),
            P(),
        ),
        check_vma=False,
    )
```

profile of v0, /device:TPU:0, one launch (start us, length us, event | category | flops | bytes accessed | tf_op | source)
XLA Modules:
  0.0 1846.1 jit_solution(5785996457019765867)
XLA Ops:
  11.2 24.8 %all_gather.30 = bf16[192,1,1024]{0,2,1:T(8,128)(2,1)S(1)} all-gather(bf16[192,1,64]{0,2,1:T(8,128)(2,1)S(1)} %convert_element_type.261), channel_id=1, replica_groups=mesh['dp'=16,'chan'=2] {'dp'}, dimensions={2}, use_global_device_ids=true | all-gather | bytes 417792 | tf_op jit(solution)/shard_map/all_gather | solution.py:160
  36.0 5.1 multiply_convert_fusion
  46.2 9.2 all-gather.10.cloned.1.call-done
  55.4 83.6 %all-gather.8.cloned.1.call-done = bf16[1600,2048]{1,0:T(8,128)(2,1)} async-done(((bf16[1600,1024]{1,0:T(8,128)(2,1)}), bf16[1600,2048]{1,0:T(8,128)(2,1)}) %all-gather.8.cloned.1.call-update) | async-done | bytes 6553616 | tf_op jit(solution)/shard_map/all_gather | solution.py:85
  139.0 5.0 fusion.55
  144.0 33.5 %all-reduce.68 = (f32[256]{0:T(256)S(1)}, f32[3]{0:T(128)S(1)}, f32[256]{0:T(256)S(1)}) all-reduce(f32[256]{0:T(256)S(1)} %get-tuple-element.109, f32[3]{0:T(128)S(1)} %pad_maximum_fusion.5, f32[256]{0:T(256)S(1)} %get-tuple-element.108), channel_id=1, replica_groups=mesh['dp'=16,'chan'=2] {'dp'}, use_global_device_ids=true, to_apply=%region_1.0 | all-reduce | flops 515 | bytes 4120 | tf_op jit(solution)/shard_map/psum | solution.py:177
  179.6 4.4 all-gather.14.cloned.1.call-done
  184.0 28.8 %all-gather.12.cloned.1.call-done = bf16[1600,512]{1,0:T(8,128)(2,1)} async-done(((bf16[1600,256]{1,0:T(8,128)(2,1)}), bf16[1600,512]{1,0:T(8,128)(2,1)}) %all-gather.12.cloned.1.call-update) | async-done | bytes 1638416 | tf_op jit(solution)/shard_map/all_gather | solution.py:85
  212.8 11.4 convolution_bitcast_fusion.1
  224.2 9.7 slice_bitcast_fusion
  233.9 5.8 fusion.54
  240.6 4.7 convolution_convert_fusion.1
  245.4 80.0 %reduce-scatter.10.cloned.1.call-done = bf16[1600,1024]{1,0:T(8,128)(2,1)} async-done(((bf16[1600,2048]{1,0:T(8,128)(2,1)}), bf16[1600,1024]{1,0:T(8,128)(2,1)}) %reduce-scatter.10.cloned.1.call-update) | async-done | bytes 3276816 | tf_op jit(solution)/shard_map/reduce_scatter | solution.py:95
  325.4 3.1 fusion.7
  328.4 33.7 %all-reduce.67 = (f32[1024]{0:T(1024)S(1)}, f32[1024]{0:T(1024)S(1)}) all-reduce(f32[1024]{0:T(1024)S(1)} %get-tuple-element.107, f32[1024]{0:T(1024)S(1)} %get-tuple-element.106), channel_id=1, replica_groups=mesh['dp'=16,'chan'=2] {'dp'}, use_global_device_ids=true, to_apply=%region_12.13 | all-reduce | flops 2048 | bytes 16384 | tf_op jit(solution)/shard_map/psum | solution.py:200
  362.2 6.1 fusion.29
  371.1 18.2 all_gather.37
  389.3 58.9 %all-gather.16.cloned.1.call-done = bf16[1600,2048]{1,0:T(8,128)(2,1)} async-done(((bf16[1600,1024]{1,0:T(8,128)(2,1)}), bf16[1600,2048]{1,0:T(8,128)(2,1)}) %all-gather.16.cloned.1.call-update) | async-done | bytes 6553616 | tf_op jit(solution)/shard_map/all_gather | solution.py:85
  448.2 3.8 fusion.225
  453.3 115.1 %all-gather.18.cloned.1.call-done = bf16[29,2048,128]{2,1,0:T(8,128)(2,1)} async-done(((bf16[29,128,128]{2,1,0:T(8,128)(2,1)}), bf16[29,2048,128]{2,1,0:T(8,128)(2,1)}) %all-gather.18.cloned.1.call-update) | async-done | bytes 15204368 | tf_op jit(solution)/shard_map/all_gather | solution.py:163
  568.3 29.9 %fusion.8 = f32[1,40,40,28,128]{4,2,3,1,0:T(8,128)S(1)} fusion(bf16[40,40,2048,1]{2,1,3,0:T(8,128)(2,1)} %bitcast.498, bf16[29,2048,128]{2,1,0:T(8,128)(2,1)} %all-gather.18.cloned.1.call-done), kind=kOutput, calls=%fused_computation.14 | convolution fusion | flops 23488102400 | bytes 44171264 | tf_op jit(solution)/shard_map/bhwc,tcd->bhwtd/dot_general | solution.py:55
  598.3 7.6 copy-done.1
  607.4 11.2 slice_bitcast_fusion.23
  620.2 3.6 multiply_convert_fusion.5
  625.1 3.2 multiply_convert_fusion.3
  633.6 19.0 %all_gather.38 = bf16[256,22]{1,0:T(8,128)(2,1)S(1)} all-gather(bf16[16,22]{1,0:T(8,128)(2,1)S(1)} %convert_element_type.281), channel_id=1, replica_groups=mesh['dp'=16,'chan'=2] {'dp'}, dimensions={0}, use_global_device_ids=true | all-gather | bytes 11968 | tf_op jit(solution)/shard_map/all_gather | solution.py:165
  653.8 13.0 all-reduce.72.cloned.1.call-done
  685.0 2.3 copy-done.74
  687.4 27.7 %fusion.2 = bf16[1600,2048]{1,0:T(8,128)(2,1)} fusion(bf16[1600,128,28]{1,0,2:T(8,128)(2,1)} %bitcast.521, bf16[29,2048,128]{2,1,0:T(8,128)(2,1)S(1)} %bitcast.516, f32[2048]{0:T(1024)S(1)} %broadcast_divide_fusion, f32[1600]{0:T(1024)S(1)} %get-tuple-element.115), kind=kOutput, calls=%fused_computation.5 | convolution fusion | flops 23497932800 | bytes 32718848 | tf_op jit(solution)/shard_map/bhwtd,tcd->bhwc/dot_general | solution.py:75
  715.1 80.0 %reduce-scatter.12.cloned.1.call-done = bf16[1600,1024]{1,0:T(8,128)(2,1)} async-done(((bf16[1600,2048]{1,0:T(8,128)(2,1)}), bf16[1600,1024]{1,0:T(8,128)(2,1)}) %reduce-scatter.12.cloned.1.call-update) | async-done | bytes 3276816 | tf_op jit(solution)/shard_map/reduce_scatter | solution.py:89
  795.1 3.9 fusion.13
  799.1 33.7 %all-reduce.66 = (f32[1024]{0:T(1024)S(1)}, f32[1024]{0:T(1024)S(1)}) all-reduce(f32[1024]{0:T(1024)S(1)} %get-tuple-element.105, f32[1024]{0:T(1024)S(1)} %get-tuple-element.104), channel_id=1, replica_groups=mesh['dp'=16,'chan'=2] {'dp'}, use_global_device_ids=true, to_apply=%region_28.29 | all-reduce | flops 2048 | bytes 16384 | tf_op jit(solution)/shard_map/psum | solution.py:106
  832.8 6.3 fusion.20
  839.2 79.7 %all-gather.20.cloned.1.call-done = bf16[1600,2048]{1,0:T(8,128)(2,1)} async-done(((bf16[1600,1024]{1,0:T(8,128)(2,1)}), bf16[1600,2048]{1,0:T(8,128)(2,1)}) %all-gather.20.cloned.1.call-update) | async-done | bytes 6553616 | tf_op jit(solution)/shard_map/all_gather | solution.py:85
  918.9 4.7 convolution_convert_fusion.2
  925.9 2.9 copy-done.43
  928.9 5.7 bitcast_convert_fusion
  938.1 23.4 %reduce-scatter.14.cloned.1.call-done = bf16[1600,256]{1,0:T(8,128)(2,1)} async-done(((bf16[1600,512]{1,0:T(8,128)(2,1)}), bf16[1600,256]{1,0:T(8,128)(2,1)}) %reduce-scatter.14.cloned.1.call-update) | async-done | bytes 819216 | tf_op jit(solution)/shard_map/reduce_scatter | solution.py:89
  961.5 3.9 fusion.243
  965.4 33.1 %all-reduce.65 = (f32[3]{0:T(128)S(1)}, f32[256]{0:T(256)S(1)}, f32[256]{0:T(256)S(1)}, f32[22]{0:T(128)S(1)}) all-reduce(f32[3]{0:T(128)S(1)} %pad_maximum_fusion.6, f32[256]{0:T(256)S(1)} %get-tuple-element.111, f32[256]{0:T(256)S(1)} %get-tuple-element.110, f32[22]{0:T(128)S(1)} %convert_reduce_fusion), channel_id=1, replica_groups=mesh['dp'=16,'chan'=2] {'dp'}, use_global_device_ids=true, to_apply=%region_21.22 | all-reduce | flops 537 | bytes 4296 | tf_op jit(solution)/shard_map/psum | solution.py:280
  1000.7 4.6 convolution_convert_fusion
  1007.7 3.8 fusion.42
  1011.5 10.1 fusion.39
  1021.6 8.9 copy.210
  1031.7 5.0 convolution_bitcast_fusion.3
  1036.7 5.4 convolution_bitcast_fusion.4
  1042.0 2.2 pad_maximum_fusion.1
  1045.1 34.7 %convolution_bitcast_fusion = f32[28,2048,128]{1,2,0:T(8,128)} fusion(bf16[40,40,2048,1]{2,1,0,3:T(8,128)(2,1)} %bitcast.499, bf16[1,40,40,28,128]{4,2,1,3,0:T(8,128)(2,1)} %copy-done.74), kind=kOutput, calls=%fused_computation.1 | convolution fusion | flops 23488102400 | bytes 47382528 | tf_op jit(solution)/shard_map/bhwc,bhwtd->tcd/dot_general | solution.py:76
  1081.7 4.3 fusion.72
  1088.0 21.3 %pad_maximum_fusion = f32[29,2048,128]{1,2,0:T(8,128)} fusion(f32[1,2048,128]{1,2,0:T(8,128)S(1)} %multiply_bitcast_fusion, f32[28,2048,128]{1,2,0:T(8,128)} %convolution_bitcast_fusion), kind=kLoop, calls=%fused_computation | loop fusion | flops 7602176 | bytes 60817408 | tf_op jit(solution)/shard_map/concatenate | solution.py:311
  1113.0 2.9 copy.213
  1115.9 2.2 copy.214
  1119.4 21.5 %reduce-scatter.26.cloned.1.call-done = f32[16,22]{1,0:T(8,128)} async-done(((f32[256,22]{1,0:T(8,128)}), f32[16,22]{1,0:T(8,128)}) %reduce-scatter.26.cloned.1.call-update) | async-done | bytes 1424 | tf_op jit(solution)/shard_map/reduce_scatter | solution.py:362
  1142.9 56.8 %reduce-scatter.24.cloned.1.call-done = f32[5,128,16]{1,2,0:T(8,128)} async-done(((f32[5,128,256]{1,2,0:T(8,128)}), f32[5,128,16]{1,2,0:T(8,128)}) %reduce-scatter.24.cloned.1.call-update) | async-done | bytes 40976 | tf_op jit(solution)/shard_map/reduce_scatter | solution.py:361
  1204.4 103.4 %reduce-scatter.20.cloned.1.call-done = f32[9,32,256]{2,0,1:T(8,128)} async-done(((f32[9,512,256]{2,0,1:T(8,128)}), f32[9,32,256]{2,0,1:T(8,128)}) %reduce-scatter.20.cloned.1.call-update) | async-done | bytes 294928 | tf_op jit(solution)/shard_map/reduce_scatter | solution.py:359
  1309.5 74.6 %reduce-scatter.18.cloned.1.call-done = f32[2,128,256]{2,1,0:T(8,128)} async-done(((f32[2,2048,256]{2,1,0:T(8,128)}), f32[2,128,256]{2,1,0:T(8,128)}) %reduce-scatter.18.cloned.1.call-update) | async-done | bytes 262160 | tf_op jit(solution)/shard_map/reduce_scatter | solution.py:358
  1385.7 94.2 %all-reduce.74.cloned.1.call-done = f32[192,1,1024]{0,1,2:T(1,128)} async-done(((f32[192,1,1024]{0,1,2:T(1,128)}), f32[192,1,1024]{0,1,2:T(1,128)}) %all-reduce.74.cloned.1.call-update) | async-done | bytes 786448
  1483.4 286.0 %reduce-scatter.22.cloned.1.call-done = f32[29,128,128]{1,2,0:T(8,128)} async-done(((f32[29,2048,128]{1,2,0:T(8,128)}), f32[29,128,128]{1,2,0:T(8,128)}) %reduce-scatter.22.cloned.1.call-update) | async-done | bytes 1900560 | tf_op jit(solution)/shard_map/reduce_scatter | solution.py:360
  1769.5 2.8 multiply_reduce_fusion.1
  1774.1 39.5 %psum.103 = f32[]{:T(128)} all-reduce(f32[]{:T(128)S(6)} %add.674), channel_id=1, replica_groups=mesh['dp'=16,'chan'=2] {'dp','chan'}, use_global_device_ids=true, to_apply=%region_51.52 | all-reduce | flops 1 | bytes 8 | tf_op jit(solution)/shard_map/psum | solution.py:383
  1814.4 6.3 multiply_subtract_fusion
  1820.7 2.8 copy.217
  1823.5 2.9 copy.218
  1833.1 2.3 multiply_subtract_fusion.2
  (338 shorter events, 84.1 us)
Async XLA Ops:
  7.2 28.8 %copy-start = (bf16[1,1600,192]{1,2,0:T(8,128)(2,1)S(1)}, bf16[1,1600,192]{1,2,0:T(8,128)(2,1)}, u32[]{:S(2)}) copy-start(bf16[1,1600,192]{1,2,0:T(8,128)(2,1)} %param.31) | copy-start | bytes 1843204
  7.2 48.2 %all-gather.10.cloned.1.call-start = ((), (), s32[]{:S(2)}) async-start(), calls=%async_computation.10 | async-start | bytes 2228224 | tf_op jit(solution)/shard_map/all_gather | solution.py:161
  9.0 130.0 %all-gather.8.cloned.1.call-start = ((), (), s32[]{:S(2)}) async-start(), calls=%async_computation.9 | async-start | bytes 9830400 | tf_op jit(solution)/shard_map/all_gather | solution.py:85
  41.2 5.0 copy-start.54
  41.2 142.8 %all-gather.14.cloned.1.call-start = ((), (), s32[]{:S(2)}) async-start(), calls=%async_computation.12 | async-start | bytes 2506752 | tf_op jit(solution)/shard_map/all_gather | solution.py:162
  42.8 170.0 %all-gather.12.cloned.1.call-start = ((), (), s32[]{:S(2)}) async-start(), calls=%async_computation.11 | async-start | bytes 2457600 | tf_op jit(solution)/shard_map/all_gather | solution.py:85
  46.2 131.5 %copy-start.68 = (f32[1,1,256]{2,1,0:T(1,128)}, f32[1,1,256]{2,1,0:T(1,128)S(1)}, u32[]{:S(2)}) copy-start(f32[1,1,256]{2,1,0:T(1,128)S(1)} %get-tuple-element.216) | copy-start | bytes 3076
  46.2 131.5 %copy-start.77 = (f32[1,1,256]{2,1,0:T(1,128)}, f32[1,1,256]{2,1,0:T(1,128)S(1)}, u32[]{:S(2)}) copy-start(f32[1,1,256]{2,1,0:T(1,128)S(1)} %get-tuple-element.217) | copy-start | bytes 3076
  144.0 80.2 %copy-start.2 = (f32[1600,256]{1,0:T(8,128)}, f32[1600,256]{1,0:T(8,128)S(1)}, u32[]{:S(2)}) copy-start(f32[1600,256]{1,0:T(8,128)S(1)} %get-tuple-element.229) | copy-start | bytes 4915204
  177.6 475.0 %copy-start.75 = (f32[3]{0:T(128)}, f32[3]{0:T(128)S(1)}, u32[]{:S(2)}) copy-start(f32[3]{0:T(128)S(1)} %get-tuple-element.125) | copy-start | bytes 40
  177.6 46.6 %copy-start.70 = (f32[256]{0:T(256)}, f32[256]{0:T(256)S(1)}, u32[]{:S(2)}) copy-start(f32[256]{0:T(256)S(1)} %get-tuple-element.164) | copy-start | bytes 3076
  177.6 46.6 %copy-start.72 = (f32[256]{0:T(256)}, f32[256]{0:T(256)S(1)}, u32[]{:S(2)}) copy-start(f32[256]{0:T(256)S(1)} %get-tuple-element.165) | copy-start | bytes 3076
  179.4 146.0 %reduce-scatter.10.cloned.1.call-start = ((), (), s32[]{:S(2)}) async-start(), calls=%async_computation.13 | async-start | bytes 9830400 | tf_op jit(solution)/shard_map/reduce_scatter | solution.py:95
  233.9 6.7 copy-start.26
  245.3 202.9 %all-gather.16.cloned.1.call-start = ((), (), s32[]{:S(2)}) async-start(), calls=%async_computation.14 | async-start | bytes 9830400 | tf_op jit(solution)/shard_map/all_gather | solution.py:85
  245.4 123.0 %copy-start.55 = (f32[1,1,1024]{2,1,0:T(1,128)}, f32[1,1,1024]{2,1,0:T(1,128)S(1)}, u32[]{:S(2)}) copy-start(f32[1,1,1024]{2,1,0:T(1,128)S(1)} %get-tuple-element.214) | copy-start | bytes 12292
  362.2 6.2 copy-start.45
  362.2 6.2 copy-start.47
  368.4 79.8 %copy-start.51 = (s32[1,1600]{1,0:T(1,128)S(1)}, s32[1,1600]{1,0:T(1,128)}, u32[]{:S(2)}) copy-start(s32[1,1600]{1,0:T(1,128)} %param.37) | copy-start | bytes 19204
  368.4 199.9 %all-gather.18.cloned.1.call-start = ((), (), s32[]{:S(2)}) async-start(), calls=%async_computation.15 | async-start | bytes 16154624 | tf_op jit(solution)/shard_map/all_gather | solution.py:163
  371.0 295.8 %all-reduce.72.cloned.1.call-start = ((), (), s32[]{:S(2)}) async-start(), calls=%async_computation.16 | async-start | bytes 1638400 | tf_op jit(solution)/shard_map/psum | solution.py:235
  598.3 7.6 copy-start.1
  618.5 5.4 copy-start.24
  618.6 5.4 copy-start.25
  620.2 4.6 copy-start.22
  620.2 4.9 copy-start.23
  633.4 161.7 %reduce-scatter.12.cloned.1.call-start = ((), (), s32[]{:S(2)}) async-start(), calls=%async_computation.17 | async-start | bytes 9830400 | tf_op jit(solution)/shard_map/reduce_scatter | solution.py:89
  652.6 17.7 copy-start.39
  666.8 5.8 copy-start.33
  668.6 6.2 copy-start.11
  676.8 6.4 slice-start
  715.0 80.1 %copy-start.46 = (f32[1024]{0:T(1024)S(1)}, f32[1024]{0:T(1024)}, u32[]{:S(2)}) copy-start(f32[1024]{0:T(1024)} %copy-done.45) | copy-start | bytes 12292
  715.0 80.1 %copy-start.48 = (f32[1024]{0:T(1024)S(1)}, f32[1024]{0:T(1024)}, u32[]{:S(2)}) copy-start(f32[1024]{0:T(1024)} %copy-done.47) | copy-start | bytes 12292
  715.1 117.7 %copy-start.56 = (f32[1,1,1024]{2,1,0:T(1,128)S(1)}, f32[1,1,1024]{2,1,0:T(1,128)}, u32[]{:S(2)}) copy-start(f32[1,1,1024]{2,1,0:T(1,128)} %copy-done.55) | copy-start | bytes 12292
  715.1 117.7 %copy-start.76 = (f32[3]{0:T(128)S(1)}, f32[3]{0:T(128)}, u32[]{:S(2)}) copy-start(f32[3]{0:T(128)} %copy-done.75) | copy-start | bytes 40
  715.1 203.8 %all-gather.20.cloned.1.call-start = ((), (), s32[]{:S(2)}) async-start(), calls=%async_computation.18 | async-start | bytes 9830400 | tf_op jit(solution)/shard_map/all_gather | solution.py:85
  839.1 79.8 %copy-start.27 = (bf16[2,2048,256]{2,1,0:T(8,128)(2,1)S(1)}, bf16[2,2048,256]{2,1,0:T(8,128)(2,1)}, u32[]{:S(2)}) copy-start(bf16[2,2048,256]{2,1,0:T(8,128)(2,1)} %all-gather.10.cloned.1.call-done) | copy-start | bytes 6291460
  839.1 122.4 %reduce-scatter.14.cloned.1.call-start = ((), (), s32[]{:S(2)}) async-start(), calls=%async_computation.19 | async-start | bytes 2457600 | tf_op jit(solution)/shard_map/reduce_scatter | solution.py:89
  928.8 5.8 copy-start.66
  928.8 5.9 copy-start.63
  928.8 5.9 copy-start.65
  928.8 6.6 copy-start.61
  928.8 32.7 %copy-start.69 = (f32[1,1,256]{2,1,0:T(1,128)S(1)}, f32[1,1,256]{2,1,0:T(1,128)}, u32[]{:S(2)}) copy-start(f32[1,1,256]{2,1,0:T(1,128)} %copy-done.68) | copy-start | bytes 3076
  928.8 32.7 %copy-start.71 = (f32[256]{0:T(256)S(1)}, f32[256]{0:T(256)}, u32[]{:S(2)}) copy-start(f32[256]{0:T(256)} %copy-done.70) | copy-start | bytes 3076
  928.8 32.7 %copy-start.73 = (f32[256]{0:T(256)S(1)}, f32[256]{0:T(256)}, u32[]{:S(2)}) copy-start(f32[256]{0:T(256)} %copy-done.72) | copy-start | bytes 3076
  928.8 32.7 %copy-start.78 = (f32[1,1,256]{2,1,0:T(1,128)S(1)}, f32[1,1,256]{2,1,0:T(1,128)}, u32[]{:S(2)}) copy-start(f32[1,1,256]{2,1,0:T(1,128)} %copy-done.77) | copy-start | bytes 3076
  934.5 27.0 %copy-start.3 = (f32[1600,256]{1,0:T(8,128)S(1)}, f32[1600,256]{1,0:T(8,128)}, u32[]{:S(2)}) copy-start(f32[1600,256]{1,0:T(8,128)} %copy-done.2) | copy-start | bytes 4915204
  934.6 147.2 %reduce-scatter.16.cloned.1.call-start = ((), (), s32[]{:S(2)}) async-start(), calls=%async_computation.20 | async-start | bytes 9830400 | tf_op jit(solution)/shard_map/reduce_scatter | solution.py:95
  998.5 204.5 %copy-start.86 = (f32[22]{0:T(128)}, f32[22]{0:T(128)S(1)}, u32[]{:S(2)}) copy-start(f32[22]{0:T(128)S(1)} %get-tuple-element.119) | copy-start | bytes 268
  1005.4 135.5 %reduce-scatter.26.cloned.1.call-start = ((), (), s32[]{:S(2)}) async-start(), calls=%async_computation.25 | async-start | bytes 139264 | tf_op jit(solution)/shard_map/reduce_scatter | solution.py:362
  1007.6 192.1 %reduce-scatter.24.cloned.1.call-start = ((), (), s32[]{:S(2)}) async-start(), calls=%async_computation.24 | async-start | bytes 696320 | tf_op jit(solution)/shard_map/reduce_scatter | solution.py:361
  1011.5 296.3 %reduce-scatter.20.cloned.1.call-start = ((), (), s32[]{:S(2)}) async-start(), calls=%async_computation.22 | async-start | bytes 8912896 | tf_op jit(solution)/shard_map/reduce_scatter | solution.py:359
  1030.5 353.6 %reduce-scatter.18.cloned.1.call-start = ((), (), s32[]{:S(2)}) async-start(), calls=%async_computation.21 | async-start | bytes 4456448 | tf_op jit(solution)/shard_map/reduce_scatter | solution.py:358
  1044.3 435.6 %all-reduce.74.cloned.1.call-start = ((), (), s32[]{:S(2)}) async-start(), calls=%async_computation.26 | async-start | bytes 2097152
  1087.9 681.5 %reduce-scatter.22.cloned.1.call-start = ((), (), s32[]{:S(2)}) async-start(), calls=%async_computation.23 | async-start | bytes 32309248 | tf_op jit(solution)/shard_map/reduce_scatter | solution.py:360
  1115.9 87.0 %copy-start.84 = (f32[25]{0:T(128)S(1)}, f32[25]{0:T(128)}, u32[]{:S(2)}) copy-start(f32[25]{0:T(128)} %param.59) | copy-start | bytes 304
  1203.0 617.7 %copy-start.85 = (f32[3]{0:T(128)}, f32[3]{0:T(128)S(1)}, u32[]{:S(2)}) copy-start(f32[3]{0:T(128)S(1)} %get-tuple-element.151) | copy-start | bytes 40
  1769.5 44.9 %copy-start.4 = (f32[29,128,128]{1,2,0:T(8,128)S(1)}, f32[29,128,128]{1,2,0:T(8,128)}, u32[]{:S(2)}) copy-start(f32[29,128,128]{1,2,0:T(8,128)} %reduce-scatter.22.cloned.1.call-done) | copy-start | bytes 5701636
  1826.4 5.0 copy-start.38
  1826.4 5.0 copy-start.49
  1826.4 8.9 copy-start.29
  1826.5 8.9 copy-start.32
  1828.6 6.7 copy-start.36
  1828.6 6.7 copy-start.37
  (48 other events, 127.1 us)
Sparse Core Ops, SparseCore 0:
  10.8 44.5 all-gather.9
  56.9 82.0 all-gather.7
  141.8 42.2 all-gather.13
  186.0 26.7 all-gather.11
  245.4 79.8 reduce-scatter.9
  368.5 79.6 all-gather.15
  451.2 117.0 all-gather.17
  633.5 33.1 all-reduce.71
  715.2 79.8 reduce-scatter.11
  839.2 79.6 all-gather.19
  934.7 26.7 reduce-scatter.13
  1005.5 76.1 reduce-scatter.15
  1085.8 55.0 reduce-scatter.25
  1144.3 55.3 reduce-scatter.23
  1204.1 103.5 reduce-scatter.19
  1312.0 72.0 reduce-scatter.17
  1387.4 92.4 all-reduce.73
  1483.9 285.4 reduce-scatter.21
where the time goes:
time: 1850 us
  waiting for transfers between devices  1210 us (65%)
  blocking collectives  236 us (13%)
  matrix products  174 us (9%)
  other arithmetic  117 us (6%)
  local copies, waits for them, and re-layouts  79.8 us (4%)
  between operations  23.6 us (1%)
    reduce_scatter x1, waiting for transfers between devices, on_device(): lax.psum_scatter(pyramid_grad, 'dp', scatter_dimension=1, tiled=True)  286 us
    all_gather x4, waiting for transfers between devices, chan_in(): return lax.all_gather(values, 'chan', axis=1, tiled=True)  251 us
    all_gather x1, waiting for transfers between devices, on_device(): lax.all_gather(pyramid_weight.astype(jnp.bfloat16), 'dp', axis=1, tiled=T...  115 us
    reduce_scatter x2, waiting for transfers between devices, chan_sum(): lax.psum_scatter(values.astype(jnp.bfloat16), 'chan', scatter_dimension=1...  103 us
    reduce_scatter x1, waiting for transfers between devices, on_device(): lax.psum_scatter(middle_grad, 'dp', scatter_dimension=1, tiled=True)  103 us
    unnamed x19, waiting for transfers between devices  94.5 us
    reduce_scatter x2, waiting for transfers between devices, rows_product(): lax.psum_scatter(jnp.einsum('pc,dc->pd', act_low, weight_low, preferred_e...  82 us
    reduce_scatter x1, waiting for transfers between devices, on_device(): lax.psum_scatter(bottle_grad, 'dp', scatter_dimension=1, tiled=True)  74.6 us
  transfers between devices with their start and end apart: 18, of which 18 were waited for; matrix products, arithmetic and copies ran while one was open for 8% of the time, Pallas kernels for 0%

commit v1 on v0

v1 whole, which is shorter than its diff:
```python
import functools

import jax
import jax.numpy as jnp
from jax import lax
from jax.experimental import pallas as pl
from jax.experimental.pallas import tpu as pltpu
from jax.sharding import PartitionSpec as P

D = 2048
MID = 512
BRANCH = 256
CLASSES = 19
PATCH = 192
FH = 40
FW = 40
STEP = 10
POSITIONS = 1600


pyramid_rates = (0, 12, 24, 36)
norm_eps = 1e-05
clip_level = 0.01
adam_eps = 1e-08
decay_rate = 0.01


MESH_ID = pl.DeviceIdType.MESH


def group_place(sizes, axes):
    place = jnp.int32(0)
    for axis in axes:
        place = place * sizes[axis] + lax.axis_index(axis)
    return place


def group_device(sizes, axes, index):
    coords = {}
    for axis in reversed(axes):
        coords[axis] = lax.rem(index, sizes[axis])
        index = lax.div(index, sizes[axis])
    return tuple(coords.get(axis, lax.axis_index(axis)) for axis in ("dp", "chan"))


def sum_kernel(sizes, axes, count, x_ref, o_ref, slots, send_sem, recv_sem):
    me = group_place(sizes, axes)
    barrier = pltpu.get_barrier_semaphore()

    def greet(step, carry):
        other = lax.rem(me + step, count)
        pl.semaphore_signal(
            barrier, inc=1, device_id=group_device(sizes, axes, other), device_id_type=MESH_ID
        )
        return carry

    lax.fori_loop(1, count, greet, 0)
    pl.semaphore_wait(barrier, count - 1)

    def copy_to(step):
        other = lax.rem(me + step, count)
        return pltpu.make_async_remote_copy(
            src_ref=x_ref,
            dst_ref=slots.at[me],
            send_sem=send_sem.at[step],
            recv_sem=recv_sem.at[me],
            device_id=group_device(sizes, axes, other),
            device_id_type=MESH_ID,
        )

    def copy_from(step):
        other = lax.rem(me + step, count)
        return pltpu.make_async_remote_copy(
            src_ref=x_ref,
            dst_ref=slots.at[other],
            send_sem=send_sem.at[step],
            recv_sem=recv_sem.at[other],
            device_id=group_device(sizes, axes, other),
            device_id_type=MESH_ID,
        )

    def start(step, carry):
        copy_to(step).start()
        return carry

    lax.fori_loop(1, count, start, 0)
    slots[me] = x_ref[...]

    def arrive(step, carry):
        copy_from(step).wait_recv()
        return carry

    lax.fori_loop(1, count, arrive, 0)
    o_ref[...] = lax.fori_loop(
        1, count, lambda index, total: total + slots[index], slots[0]
    )

    def leave(step, carry):
        copy_to(step).wait_send()
        return carry

    lax.fori_loop(1, count, leave, 0)


def small_sum(sizes, parts, axes, collective):
    flat = jnp.concatenate([part.reshape(-1) for part in parts])
    rows = -(-flat.shape[0] // 1024) * 8
    packed = jnp.pad(flat, (0, rows * 128 - flat.shape[0])).reshape(rows, 128)
    count = 1
    for axis in axes:
        count *= sizes[axis]
    summed = pl.pallas_call(
        functools.partial(sum_kernel, sizes, axes, count),
        out_shape=jax.ShapeDtypeStruct((rows, 128), jnp.float32),
        in_specs=[pl.BlockSpec(memory_space=pltpu.VMEM)],
        out_specs=pl.BlockSpec(memory_space=pltpu.VMEM),
        scratch_shapes=[
            pltpu.VMEM((count, rows, 128), jnp.float32),
            pltpu.SemaphoreType.DMA((count,)),
            pltpu.SemaphoreType.DMA((count,)),
        ],
        compiler_params=pltpu.CompilerParams(collective_id=collective, has_side_effects=True),
        name="small_sum",
    )(packed).reshape(-1)
    result = []
    start = 0
    for part in parts:
        size = part.size
        result.append(summed[start : start + size].reshape(part.shape))
        start += size
    return result


def swap_chan(values):
    return lax.ppermute(values, "chan", [(0, 1), (1, 0)])


def valid(step, length):
    return max(0, step), length + min(0, step)


def taps_of(rate):
    return [((tap // 3 - 1) * rate, (tap % 3 - 1) * rate) for tap in range(9)]


def shift_field(field, row_step, col_step):
    rows, cols = field.shape[:2]
    r0, r1 = valid(row_step, rows)
    c0, c1 = valid(col_step, cols)
    return jnp.pad(
        field[r0:r1, c0:c1],
        (
            (r0 - row_step, rows - (r1 - row_step)),
            (c0 - col_step, cols - (c1 - col_step)),
            (0, 0),
        ),
    )


def gelu_grad(values, upstream):
    return jax.vjp(jax.nn.gelu, values)[1](upstream)[0]


def dot(left, right, contract=(1, 0)):
    return lax.dot_general(
        left,
        right,
        (((contract[0],), (contract[1],)), ((), ())),
        preferred_element_type=jnp.float32,
    )


def adam_step(weight, first, second, gradient, factor, rate, decay):
    gradient = gradient * factor
    first_new = 0.5 * first + 0.5 * gradient
    second_new = 0.5 * second + 0.5 * gradient * gradient
    direction = (
        first_new / (1.0 - 0.5**STEP) / (jnp.sqrt(second_new / (1.0 - 0.5**STEP)) + adam_eps)
    )
    return (weight - rate * (direction + decay * weight), first_new, second_new)


def on_device(
    sizes,
    patches,
    labels,
    offset_target,
    offset_valid,
    depth_target,
    lidar_valid,
    crop_mask,
    stem_weight,
    stem_first,
    stem_second,
    bottle_weight,
    bottle_first,
    bottle_second,
    middle_weight,
    middle_first,
    middle_second,
    pyramid_weight,
    pyramid_first,
    pyramid_second,
    project_weight,
    project_first,
    project_second,
    head_weight,
    head_first,
    head_second,
    norm_gains,
    norm_first,
    norm_second,
    task_params,
    task_first,
    task_second,
):
    chan_place = lax.axis_index("chan")
    dp_size = sizes["dp"]
    low = jnp.bfloat16
    crop_field = crop_mask.astype(jnp.float32).reshape(POSITIONS, 1)
    offset_field = crop_field[:, 0] * offset_valid.astype(jnp.float32).reshape(POSITIONS)
    lidar_field = crop_field[:, 0] * lidar_valid.astype(jnp.float32).reshape(POSITIONS)
    local_counts = jnp.stack([jnp.sum(crop_field), jnp.sum(offset_field), jnp.sum(lidar_field)])
    half = D // 2
    mid_half = MID // 2

    row_share = bottle_weight.shape[1]
    mid_share = middle_weight.shape[1]
    stem_share = stem_weight.shape[2]
    project_share = project_weight.shape[2]
    head_share = head_weight.shape[0]
    small_parts = [stem_weight, project_weight, head_weight]
    small_flat = jnp.concatenate([part.astype(low).reshape(-1) for part in small_parts])
    small_rows = -(-small_flat.shape[0] // (16 * 256)) * 16
    small_flat = jnp.pad(small_flat, (0, small_rows * 256 - small_flat.shape[0]))
    packed = jnp.concatenate(
        [
            bottle_weight.astype(low).reshape(2 * row_share, 256),
            middle_weight.astype(low).reshape(9 * mid_share, 256),
            small_flat.reshape(small_rows, 256),
        ]
    )
    trunk = lax.all_gather(packed, ("dp", "chan")).reshape(dp_size, 2, packed.shape[0], 256)
    pyramid_low = lax.all_gather(pyramid_weight.astype(low), "dp", axis=1, tiled=True)
    reduce_low = trunk[:, :, :row_share].transpose(0, 2, 1, 3).reshape(D, MID)
    expand_low = trunk[:, :, row_share : 2 * row_share].transpose(0, 2, 1, 3).reshape(D, MID)
    start = 2 * row_share
    middle_low = (
        trunk[:, :, start : start + 9 * mid_share]
        .reshape(dp_size, 2, 9, mid_share, 256)
        .transpose(2, 0, 3, 1, 4)
        .reshape(9 * MID, MID)
    )
    small = trunk[:, :, start + 9 * mid_share :].reshape(dp_size, 2, small_rows * 256)
    size = PATCH * stem_share
    stem_low = (
        small[:, :, :size]
        .reshape(dp_size, 2, PATCH, stem_share)
        .transpose(2, 1, 0, 3)
        .reshape(PATCH, D)
    )
    own_small = lax.dynamic_index_in_dim(small, chan_place, 1, keepdims=False)
    project_low = (
        own_small[:, size : size + 5 * 128 * project_share]
        .reshape(dp_size, 5, 128, project_share)
        .transpose(1, 2, 0, 3)
        .reshape(5 * 128, BRANCH)
    )
    size += 5 * 128 * project_share
    head_low = own_small[:, size : size + head_share * 22].reshape(BRANCH, 22)

    gains_other = swap_chan(norm_gains)
    gains_all = jnp.where(
        chan_place == 0,
        jnp.concatenate([norm_gains, gains_other], 1),
        jnp.concatenate([gains_other, norm_gains], 1),
    )
    gain_one = gains_all[0, :, :mid_half].reshape(MID)
    shift_one = gains_all[1, :, :mid_half].reshape(MID)
    gain_two = gains_all[0, :, mid_half:].reshape(D)
    shift_two = gains_all[1, :, mid_half:].reshape(D)

    def own_half(values, axis):
        width = values.shape[axis] // 2
        return lax.dynamic_slice_in_dim(values, chan_place * width, width, axis)

    def other_half(values, axis):
        width = values.shape[axis] // 2
        return lax.dynamic_slice_in_dim(values, (1 - chan_place) * width, width, axis)

    patch_rows = patches.reshape(POSITIONS, PATCH)
    stream = crop_field * dot(patch_rows, stem_low)
    stream_low = stream.astype(low)
    first_pre = dot(stream_low, reduce_low)
    sum_one, square_one, counts = small_sum(
        sizes,
        [
            jnp.sum(crop_field * first_pre, 0),
            jnp.sum(crop_field * first_pre * first_pre, 0),
            local_counts,
        ],
        ("dp",),
        0,
    )
    crop_total = counts[0]
    mean_one = sum_one / crop_total
    scale_one = lax.rsqrt(square_one / crop_total - mean_one * mean_one + norm_eps)
    normed_one = (first_pre - mean_one) * scale_one
    act_input = gain_one * normed_one + shift_one
    hidden_low = (crop_field * jax.nn.gelu(act_input)).astype(low)
    hidden_canvas = hidden_low.reshape(FH, FW, MID)
    middle_taps = taps_of(4)
    hidden_stack = jnp.concatenate(
        [shift_field(hidden_canvas, step[0], step[1]) for step in middle_taps], 2
    ).reshape(POSITIONS, 9 * MID)
    second_low = dot(hidden_stack, middle_low).astype(low)
    expand_pre = dot(second_low, expand_low, (1, 1))
    sum_two, square_two = small_sum(
        sizes,
        [jnp.sum(crop_field * expand_pre, 0), jnp.sum(crop_field * expand_pre * expand_pre, 0)],
        ("dp",),
        1,
    )
    mean_two = sum_two / crop_total
    scale_two = lax.rsqrt(square_two / crop_total - mean_two * mean_two + norm_eps)
    stream_out = stream + crop_field * (gain_two * ((expand_pre - mean_two) * scale_two) + shift_two)
    output_low = stream_out.astype(low)
    canvas_two = output_low.reshape(FH, FW, D)
    image_count = jnp.sum(crop_field)
    pooled = jnp.sum(crop_field * output_low.astype(jnp.float32), 0, keepdims=True) / image_count
    pooled_low = pooled.astype(low)

    width = BRANCH // 2
    pyramid_taps = [(0, 0)] + taps_of(12) + taps_of(24) + taps_of(36)
    branch_of = [0] + [1] * 9 + [2] * 9 + [3] * 9
    branch_pre = [jnp.zeros((FH, FW, width), jnp.float32) for branch in range(4)]
    for tap, step in enumerate(pyramid_taps):
        r0, r1 = valid(step[0], FH)
        c0, c1 = valid(step[1], FW)
        part = dot(canvas_two[r0:r1].reshape(-1, D), pyramid_low[tap]).reshape(r1 - r0, FW, width)
        branch_pre[branch_of[tap]] = branch_pre[branch_of[tap]] + jnp.pad(
            part[:, c0:c1],
            (
                (r0 - step[0], FH - (r1 - step[0])),
                (c0 - step[1], FW - (c1 - step[1])),
                (0, 0),
            ),
        )
    branch_pre = [values.reshape(POSITIONS, width) for values in branch_pre]
    pool_pre = dot(pooled_low, pyramid_low[28])
    branch_acts = [jax.nn.gelu(values) for values in branch_pre]
    branch_acts.append(jnp.broadcast_to(jax.nn.gelu(pool_pre), (POSITIONS, width)))
    concat_low = jnp.concatenate(branch_acts, 1).astype(low)
    project_part = dot(concat_low, project_low).astype(low)
    project_pre = project_part.astype(jnp.float32) + swap_chan(project_part).astype(jnp.float32)
    feature_low = jax.nn.gelu(project_pre).astype(low)
    task_scale = task_params[:3]
    logits = dot(feature_low, head_low) + task_params[3:]
    class_logits = logits[:, :CLASSES]
    class_top = jnp.max(class_logits, 1, keepdims=True)
    class_exp = jnp.exp(class_logits - class_top)
    class_total = jnp.sum(class_exp, 1, keepdims=True)
    onehot = (
        labels.reshape(POSITIONS, 1) == lax.broadcasted_iota(jnp.int32, (1, CLASSES), 1)
    ).astype(jnp.float32)
    seg_terms = crop_field[:, 0] * (
        class_top[:, 0] + jnp.log(class_total[:, 0]) - jnp.sum(class_logits * onehot, 1)
    )
    offset_err = logits[:, CLASSES : CLASSES + 2] - jnp.swapaxes(offset_target, 1, 2).reshape(
        POSITIONS, 2
    )
    offset_root = jnp.sqrt(offset_err * offset_err + 1.0)
    depth_pre = logits[:, CLASSES + 2]
    depth_err = jax.nn.softplus(depth_pre) - depth_target.reshape(POSITIONS)
    depth_root = jnp.sqrt(depth_err * depth_err + 1.0)
    local_sums = jnp.stack(
        [
            jnp.sum(seg_terms),
            jnp.sum(offset_field * jnp.sum(offset_root - 1.0, 1)),
            jnp.sum(lidar_field * (depth_root - 1.0)),
        ]
    )
    task_weights = jnp.exp(-task_scale) / counts
    logit_grad = jnp.concatenate(
        [
            task_weights[0] * crop_field * (class_exp / class_total - onehot),
            task_weights[1] * offset_field[:, None] * offset_err / offset_root,
            (task_weights[2] * lidar_field * depth_err / depth_root * jax.nn.sigmoid(depth_pre))[
                :, None
            ],
        ],
        axis=1,
    )
    logit_low = logit_grad.astype(low)
    local_bias = jnp.sum(logit_low.astype(jnp.float32), 0)
    head_grad = dot(feature_low, logit_low, (0, 0))
    feature_grad = dot(logit_low, head_low, (1, 1))
    project_grad_low = gelu_grad(project_pre, feature_grad).astype(low)
    project_grad = dot(concat_low, project_grad_low, (0, 0))
    concat_grad = dot(project_grad_low, project_low, (1, 1))
    branch_grads = [
        gelu_grad(branch_pre[order], concat_grad[:, order * width : (order + 1) * width])
        .astype(low)
        .reshape(FH, FW, width)
        for order in range(4)
    ]
    pool_grad_low = gelu_grad(
        pool_pre, jnp.sum(concat_grad[:, 4 * width :], 0, keepdims=True)
    ).astype(low)
    grad_stack = jnp.concatenate(
        [
            shift_field(branch_grads[branch_of[tap]], -step[0], -step[1])
            for tap, step in enumerate(pyramid_taps)
        ],
        2,
    ).reshape(POSITIONS, 28 * width)

    pooled_grad = dot(pool_grad_low, pyramid_low[28], (1, 1)) / image_count
    weight_rows = pyramid_low[:28].transpose(1, 0, 2).reshape(D, 28 * width)
    other_part = dot(
        grad_stack, other_half(weight_rows, 0), (1, 1)
    ) + crop_field * other_half(pooled_grad, 1)
    other_sent = swap_chan(other_part.astype(low))
    taps_grad = dot(grad_stack, output_low, (0, 0)).astype(low)
    pool_weight_grad = dot(pool_grad_low, pooled_low, (0, 0)).astype(low)
    pyramid_grad = jnp.concatenate([taps_grad, pool_weight_grad], axis=0).reshape(29, width, D)
    pyramid_red = lax.psum_scatter(pyramid_grad, "dp", scatter_dimension=2, tiled=True)
    own_part = dot(grad_stack, own_half(weight_rows, 0), (1, 1)) + crop_field * own_half(
        pooled_grad, 1
    )
    stream_grad = own_part.astype(low).astype(jnp.float32) + other_sent.astype(jnp.float32)

    own_gain_two = own_half(gain_two, 0)
    own_scale_two = own_half(scale_two, 0)
    normed_two = (own_half(expand_pre, 1) - own_half(mean_two, 0)) * own_scale_two
    upstream_two = crop_field * stream_grad
    gain_two_grad, shift_two_grad, loss_sums, bias_grad = small_sum(
        sizes,
        [jnp.sum(upstream_two * normed_two, 0), jnp.sum(upstream_two, 0), local_sums, local_bias],
        ("dp",),
        2,
    )
    task_means = loss_sums / counts
    total_loss = jnp.sum(jnp.exp(-task_scale) * task_means + task_scale)
    scale_grad = 1.0 - jnp.exp(-task_scale) * task_means
    expand_grad_low = (
        crop_field
        * own_gain_two
        * own_scale_two
        * (upstream_two - (shift_two_grad + normed_two * gain_two_grad) / crop_total)
    ).astype(low)
    second_part = dot(expand_grad_low, own_half(expand_low, 0)).astype(low)
    second_other = swap_chan(second_part)
    expand_rows = dot(expand_grad_low, second_low, (0, 0)).astype(low)
    expand_sent = swap_chan(other_half(expand_rows, 1))
    second_grad_low = (
        second_part.astype(jnp.float32) + second_other.astype(jnp.float32)
    ).astype(low)
    second_canvas = second_grad_low.reshape(FH, FW, MID)
    second_stack = jnp.concatenate(
        [shift_field(second_canvas, -step[0], -step[1]) for step in middle_taps], 2
    ).reshape(POSITIONS, 9 * MID)
    middle_back = middle_low.reshape(9, MID, MID).transpose(0, 2, 1).reshape(9 * MID, MID)
    hidden_grad = dot(second_stack, middle_back)
    upstream_one = gelu_grad(act_input, crop_field * hidden_grad)
    gain_one_all, shift_one_all = small_sum(
        sizes,
        [jnp.sum(upstream_one * normed_one, 0), jnp.sum(upstream_one, 0)],
        ("dp",),
        3,
    )
    gain_one_grad = own_half(gain_one_all, 0)
    shift_one_grad = own_half(shift_one_all, 0)
    first_grad_low = (
        crop_field
        * gain_one
        * scale_one
        * (upstream_one - (shift_one_all + normed_one * gain_one_all) / crop_total)
    ).astype(low)
    middle_grad = dot(hidden_stack, own_half(second_grad_low, 1), (0, 0)).astype(low)
    reduce_grad = dot(stream_low, own_half(first_grad_low, 1), (0, 0)).astype(low)
    start_grad = dot(first_grad_low, own_half(reduce_low, 0), (1, 1)) + stream_grad
    start_grad_low = (crop_field * start_grad).astype(low)
    stem_grad = dot(patch_rows, start_grad_low, (0, 0)).astype(low)
    expand_own = own_half(expand_rows, 1)
    expand_grad = jnp.where(
        chan_place == 0,
        jnp.concatenate([expand_own, expand_sent], 0),
        jnp.concatenate([expand_sent, expand_own], 0),
    )

    small_grads = jnp.concatenate(
        [
            stem_grad.reshape(PATCH, dp_size, stem_share)
            .transpose(1, 0, 2)
            .reshape(dp_size, PATCH * stem_share),
            project_grad.astype(low)
            .reshape(5 * 128, dp_size, project_share)
            .transpose(1, 0, 2)
            .reshape(dp_size, 5 * 128 * project_share),
            head_grad.astype(low).reshape(dp_size, head_share * 22),
        ],
        1,
    )
    small_grads = jnp.pad(small_grads, ((0, 0), (0, small_rows * 256 - small_grads.shape[1])))
    packed_grads = jnp.concatenate(
        [
            reduce_grad.reshape(dp_size, row_share, 256),
            expand_grad.reshape(dp_size, row_share, 256),
            middle_grad.reshape(9, dp_size, mid_share, 256)
            .transpose(1, 0, 2, 3)
            .reshape(dp_size, 9 * mid_share, 256),
            small_grads.reshape(dp_size, small_rows, 256),
        ],
        1,
    )
    trunk_red = (
        lax.psum_scatter(packed_grads, "dp", scatter_dimension=0, tiled=True)
        .reshape(packed.shape)
        .astype(jnp.float32)
    )
    bottle_red = trunk_red[: 2 * row_share].reshape(bottle_weight.shape)
    middle_red = trunk_red[start : start + 9 * mid_share].reshape(middle_weight.shape)
    small_red = trunk_red[start + 9 * mid_share :].reshape(-1)
    stem_red = small_red[: stem_weight.size].reshape(stem_weight.shape)
    project_red = small_red[stem_weight.size : stem_weight.size + project_weight.size].reshape(
        project_weight.shape
    )
    size = stem_weight.size + project_weight.size
    head_red = small_red[size : size + head_weight.size].reshape(head_weight.shape)
    pyramid_red = pyramid_red.astype(jnp.float32).transpose(0, 2, 1)
    norm_grad = jnp.stack(
        [
            jnp.concatenate([gain_one_grad, gain_two_grad]),
            jnp.concatenate([shift_one_grad, shift_two_grad]),
        ]
    )[:, None, :]
    task_grad = jnp.concatenate([scale_grad, bias_grad])
    dp_first = (lax.axis_index("dp") == 0).astype(jnp.float32)
    chan_first = (chan_place == 0).astype(jnp.float32)
    own_squares = (
        jnp.sum(stem_red * stem_red)
        + jnp.sum(bottle_red * bottle_red)
        + jnp.sum(middle_red * middle_red)
        + jnp.sum(pyramid_red * pyramid_red)
        + jnp.sum(project_red * project_red)
        + chan_first * jnp.sum(head_red * head_red)
        + dp_first * jnp.sum(norm_grad * norm_grad)
        + dp_first * chan_first * jnp.sum(task_grad * task_grad)
    )
    grad_norm = jnp.sqrt(small_sum(sizes, [own_squares], ("dp", "chan"), 4)[0])
    factor = clip_level / jnp.maximum(grad_norm, clip_level)
    new_stem = adam_step(
        stem_weight, stem_first, stem_second, stem_red, factor, PATCH ** (-0.5), decay_rate
    )
    new_bottle = adam_step(
        bottle_weight, bottle_first, bottle_second, bottle_red, factor, D ** (-0.5), decay_rate
    )
    new_middle = adam_step(
        middle_weight,
        middle_first,
        middle_second,
        middle_red,
        factor,
        (9 * MID) ** (-0.5),
        decay_rate,
    )
    new_pyramid = adam_step(
        pyramid_weight,
        pyramid_first,
        pyramid_second,
        pyramid_red,
        factor,
        (3 * D) ** (-0.5),
        decay_rate,
    )
    new_project = adam_step(
        project_weight,
        project_first,
        project_second,
        project_red,
        factor,
        (5 * BRANCH) ** (-0.5),
        decay_rate,
    )
    new_head = adam_step(
        head_weight, head_first, head_second, head_red, factor, BRANCH ** (-0.5), decay_rate
    )
    new_norm = adam_step(norm_gains, norm_first, norm_second, norm_grad, factor, 0.3, 0.0)
    new_task = adam_step(task_params, task_first, task_second, task_grad, factor, 0.3, 0.0)
    return (
        total_loss,
        grad_norm,
        new_stem[0],
        new_stem[1],
        new_stem[2],
        new_bottle[0],
        new_bottle[1],
        new_bottle[2],
        new_middle[0],
        new_middle[1],
        new_middle[2],
        new_pyramid[0],
        new_pyramid[1],
        new_pyramid[2],
        new_project[0],
        new_project[1],
        new_project[2],
        new_head[0],
        new_head[1],
        new_head[2],
        new_norm[0],
        new_norm[1],
        new_norm[2],
        new_task[0],
        new_task[1],
        new_task[2],
    )


def solution(mesh):
    return jax.shard_map(
        functools.partial(on_device, dict(mesh.shape)),
        mesh=mesh,
        in_specs=(
            P("dp", None, None),
            P("dp", None),
            P("dp", None, None),
            P("dp", None),
            P("dp", None),
            P("dp", None),
            P("dp", None),
            P(None, "chan", "dp"),
            P(None, "chan", "dp"),
            P(None, "chan", "dp"),
            P(None, "dp", "chan"),
            P(None, "dp", "chan"),
            P(None, "dp", "chan"),
            P(None, "dp", "chan"),
            P(None, "dp", "chan"),
            P(None, "dp", "chan"),
            P(None, "dp", "chan"),
            P(None, "dp", "chan"),
            P(None, "dp", "chan"),
            P(None, "chan", "dp"),
            P(None, "chan", "dp"),
            P(None, "chan", "dp"),
            P("dp", None),
            P("dp", None),
            P("dp", None),
            P(None, "chan", None),
            P(None, "chan", None),
            P(None, "chan", None),
            P(),
            P(),
            P(),
        ),
        out_specs=(
            P(),
            P(),
            P(None, "chan", "dp"),
            P(None, "chan", "dp"),
            P(None, "chan", "dp"),
            P(None, "dp", "chan"),
            P(None, "dp", "chan"),
            P(None, "dp", "chan"),
            P(None, "dp", "chan"),
            P(None, "dp", "chan"),
            P(None, "dp", "chan"),
            P(None, "dp", "chan"),
            P(None, "dp", "chan"),
            P(None, "dp", "chan"),
            P(None, "chan", "dp"),
            P(None, "chan", "dp"),
            P(None, "chan", "dp"),
            P("dp", None),
            P("dp", None),
            P("dp", None),
            P(None, "chan", None),
            P(None, "chan", None),
            P(None, "chan", None),
            P(),
            P(),
            P(),
        ),
        check_vma=False,
    )
```

time: 1850 us -> 957 us (0.52)
  waiting for transfers between devices: 1210 us -> 316 us
  blocking collectives: 236 us -> 0 us
  local copies, waits for them, and re-layouts: 79.8 us -> 243 us
  Pallas kernels: 0 us -> 49.1 us
    reduce_scatter x9 -> x2, waiting for transfers between devices: 728 us -> 155 us  [the longest x1 149 us: on_device(): lax.psum_scatter(pyramid_grad, 'dp', scatter_dimension=2, tiled=True)]
    all_gather x7 -> x2, waiting for transfers between devices: 380 us -> 82.1 us  [the longest x1 82.1 us: on_device(): lax.all_gather(packed, ('dp', 'chan'))]
    psum x5 -> x0, blocking collectives: 174 us -> none  [the longest x1 39.5 us: on_device(): grad_norm = jnp.sqrt(lax.psum(own_squares, ('dp', 'chan')))]
    unnamed x19 -> x4, waiting for transfers between devices: 94.5 us -> 0.07 us
    ppermute x0 -> x5, waiting for transfers between devices: none -> 77.9 us  [swap_chan(): return lax.ppermute(values, 'chan', [(0, 1), (1, 0)])]
    transpose x1 -> x10, local copies, waits for them, and re-layouts: 8.86 us -> 76.1 us  [the longest x2 26.2 us: on_device(): weight_rows = pyramid_low[:28].transpose(1, 0, 2).reshape(D, 28 * width)]
    all_gather x3 -> x0, blocking collectives: 62 us -> none  [the longest x1 24.8 us: on_device(): lax.all_gather(stem_weight.astype(jnp.bfloat16), 'dp', axis=2, tiled=True)]
    pallas_call x0 -> x5, Pallas kernels: none -> 49.1 us  [small_sum(): pl.pallas_call(functools.partial(sum_kernel, sizes, axes, count), out_sha...]
  transfers between devices with their start and end apart: 18 -> 9, of which waited for: 18 -> 5; matrix products, arithmetic and copies ran while one was open for 8% -> 32% of each run, Pallas kernels for 0% -> 2%
where the time goes in v1:
time: 957 us; the launch traced here: 943 us
  waiting for transfers between devices  316 us (33%)
  local copies, waits for them, and re-layouts  243 us (25%)
  matrix products  190 us (20%)
  other arithmetic  114 us (12%)
  Pallas kernels  49.1 us (5%)
  between operations  23.6 us (2%)
    dot_general x46, matrix products, dot(): lax.dot_general(left, right, (((contract[0],), (contract[1],)), ((), ()))...  184 us
    reduce_scatter x1, waiting for transfers between devices, on_device(): lax.psum_scatter(pyramid_grad, 'dp', scatter_dimension=2, tiled=True)  149 us
    all_gather x1, waiting for transfers between devices, on_device(): lax.all_gather(packed, ('dp', 'chan'))  82.1 us
    ppermute x5, waiting for transfers between devices, swap_chan(): return lax.ppermute(values, 'chan', [(0, 1), (1, 0)])  77.9 us
    unnamed x308, local copies, waits for them, and re-layouts  53.5 us
    pallas_call x5, Pallas kernels, small_sum(): pl.pallas_call(functools.partial(sum_kernel, sizes, axes, count), out_sha...  49.1 us
    transpose x2, local copies, waits for them, and re-layouts, on_device(): weight_rows = pyramid_low[:28].transpose(1, 0, 2).reshape(D, 28 * width)  26.2 us
    transpose x1, local copies, waits for them, and re-layouts, on_device(): middle_low = trunk[:, :, start:start + 9 * mid_share].reshape(dp_size, 2,...  26.2 us
  transfers between devices with their start and end apart: 9, of which 5 were waited for; matrix products, arithmetic and copies ran while one was open for 32% of the time, Pallas kernels for 2%

profile of v1, /device:TPU:0, one launch (start us, length us, event | category | flops | bytes accessed | tf_op | source)
XLA Modules:
  0.0 943.3 jit_solution(10679273361453057921)
XLA Ops:
  14.5 3.0 collective-permute-start
  20.8 82.1 %all-gather.6.cloned.1.call-done = bf16[20480,256]{1,0:T(8,128)(2,1)} async-done(((bf16[640,256]{1,0:T(8,128)(2,1)}), bf16[20480,256]{1,0:T(8,128)(2,1)}) %all-gather.6.cloned.1.call-update) | async-done | bytes 10485776 | tf_op jit(solution)/shard_map/all_gather | solution.py:243
  102.9 2.7 slice.649
  105.6 4.9 slice.665
  110.5 3.8 reshape.690
  122.1 4.8 slice_bitcast_fusion.1
  126.9 3.5 copy.127
  130.3 3.9 fusion.128
  134.3 5.6 fusion.24
  142.6 8.2 small_sum.5
  154.8 3.5 multiply_convert_fusion.3
  172.9 26.2 %copy.128 = bf16[9,16,32,2,256]{4,3,2,1,0:T(2,128)(2,1)} copy(bf16[9,16,32,2,256]{4,2,0,3,1:T(8,128)(2,1)} %bitcast.489) | data formatting | bytes 9437184 | tf_op jit(solution)/shard_map/transpose | solution.py:251
  199.1 5.3 copy.156
  204.4 3.5 copy.129
  207.9 2.3 constant_dynamic-update-slice_fusion.8
  217.2 8.3 convolution_convert_fusion.3
  225.5 6.8 multiply_reduce_fusion
  232.9 11.2 %small_sum.6 = f32[32,128]{1,0:T(8,128)} custom-call(f32[32,128]{1,0:T(8,128)} %pad_maximum_fusion.4.x_ref), custom_call_target="tpu_custom_call" | custom-call | tf_op jit(solution)/shard_map/small_sum/pallas_call | solution.py:112
  246.9 13.8 %multiply_reduce_fusion.1 = (f32[2048]{0:T(1024)S(1)}, bf16[1600,2048]{1,0:T(8,128)(2,1)}) fusion(f32[1600]{0:T(1024)S(1)} %get-tuple-element.115, f32[2048]{0:T(1024)S(1)} %bitcast.614, f32[2048]{0:T(1024)S(1)} %fusion.174, f32[1600,2048]{1,0:T(8,128)} %get-tuple-element.226, f32[2048]{0:T(1024)S(1)} %divide_bitcast_fusion, f32[2048]{0:T(1024)S(1)} %bitcast.606, ...), kind=kLoop, calls=%fused_computation.9 | loop fusion | flops 36042752 | bytes 32815360 | tf_op jit(solution)/shard_map/reduce_sum | solution.py:330
  262.0 2.8 reshape.706
  264.9 2.5 copy.131
  270.7 2.6 fusion.213
  273.3 4.8 fusion.214
  278.2 4.4 fusion.215
  282.6 4.0 fusion.138
  286.6 4.1 fusion.16
  290.7 3.5 fusion.18
  301.5 3.0 fusion.143
  316.5 2.3 fusion.133
  324.4 5.8 slice_bitcast_fusion
  330.3 20.3 %copy.132 = bf16[2048,28,128]{0,2,1:T(8,128)(2,1)} copy(bf16[2048,28,128]{2,0,1:T(8,128)(2,1)} %slice_bitcast_fusion) | data formatting | bytes 29360128 | tf_op jit(solution)/shard_map/transpose | solution.py:419
  356.3 2.9 fusion.44
  391.7 16.2 %add_convert_fusion = bf16[1600,1024]{1,0:T(8,128)(2,1)} fusion(bf16[1600,3584]{1,0:T(8,128)(2,1)} %constant_dynamic-update-slice_fusion.12, bf16[2048,3584]{0,1:T(8,128)(2,1)S(1)} %bitcast.499, s32[]{:T(128)S(6)} %select_n.60, f32[1024]{0:T(1024)S(1)} %get-tuple-element.217, f32[1600]{0:T(1024)S(1)} %copy-done.40), kind=kOutput, calls=%fused_computation.19 | convolution fusion | flops 11748966400 | bytes 22097924 | tf_op jit(solution)/shard_map/dot_general | solution.py:165
  416.4 64.9 %collective-permute-done.2 = bf16[1600,1024]{1,0:T(8,128)(2,1)} collective-permute-done((bf16[1600,1024]{1,0:T(8,128)(2,1)}, bf16[1600,1024]{1,0:T(8,128)(2,1)}, u32[]{:S(2)}, u32[]{:S(2)}) %collective-permute-start.2) | collective-permute-done | bytes 3276832 | tf_op jit(solution)/shard_map/ppermute | solution.py:135
  481.3 21.3 %fusion.11 = (f32[1024]{0:T(1024)S(1)}, f32[1024]{0:T(1024)S(1)}, bf16[1600,1024]{1,0:T(8,128)(2,1)}) fusion(bf16[1600,1024]{1,0:T(8,128)(2,1)} %collective-permute-done.2, f32[1600]{0:T(1024)S(1)} %copy-done.41, f32[1024]{0:T(1024)S(1)} %dynamic_slice.53, f32[1024]{0:T(1024)S(1)} %dynamic_slice.52, f32[1600,2048]{1,0:T(8,128)} %get-tuple-element.226, ...), kind=kOutput, calls=%fused_computation.28 | convolution fusion | flops 11763709952 | bytes 31943936 | tf_op jit(solution)/shard_map/dot_general | solution.py:165
  505.3 10.7 %small_sum.7 = f32[24,128]{1,0:T(8,128)} custom-call(f32[24,128]{1,0:T(8,128)} %pad_bitcast_fusion.x_ref), custom_call_target="tpu_custom_call" | custom-call | tf_op jit(solution)/shard_map/small_sum/pallas_call | solution.py:112
  516.7 7.5 multiply_convert_fusion.1
  524.2 3.1 convolution_convert_fusion.2
  528.7 8.7 reshape_reshape.3
  539.3 6.7 copy.134
  546.0 4.6 convolution_convert_fusion.6
  552.8 3.2 convolution_convert_fusion.8
  556.1 2.1 copy.138
  558.2 5.7 reshape.726
  563.8 13.0 %collective-permute-done.4 = bf16[1024,256]{1,0:T(8,128)(2,1)} collective-permute-done((bf16[1024,256]{1,0:T(8,128)(2,1)}, bf16[1024,256]{1,0:T(8,128)(2,1)}, u32[]{:S(2)}, u32[]{:S(2)}) %collective-permute-start.4) | collective-permute-done | bytes 524320 | tf_op jit(solution)/shard_map/ppermute | solution.py:135
  576.9 2.8 maximum_select_fusion
  579.6 2.4 add_convert_fusion.2
  584.3 11.2 %convolution_convert_fusion.1 = bf16[4608,256]{1,0:T(8,128)(2,1)} fusion(bf16[1600,4608]{1,0:T(8,128)(2,1)} %copy-done.52, bf16[1600,512]{1,0:T(8,128)(2,1)S(1)} %add_convert_fusion.2, s32[]{:T(128)S(6)} %select_n.62), kind=kOutput, calls=%fused_computation.21 | convolution fusion | flops 3776053248 | bytes 17924100 | tf_op jit(solution)/shard_map/dot_general | solution.py:165
  602.2 12.7 %multiply_reduce_fusion.4 = (f32[512]{0:T(512)S(1)}, f32[512]{0:T(512)S(1)}, f32[1600,512]{1,0:T(8,128)}) fusion(f32[1600,512]{1,0:T(8,128)S(1)} %copy-done.3, f32[512]{0:T(512)S(1)} %copy-done.77, f32[512]{0:T(512)S(1)} %copy-done.75, f32[512]{0:T(512)S(1)} %bitcast.621, f32[512]{0:T(512)S(1)} %bitcast.612, ...), kind=kOutput, calls=%fused_computation.50 | convolution fusion | flops 7571864576 | bytes 26036480 | tf_op jit(solution)/shard_map/dot_general | solution.py:165
  615.5 9.2 small_sum.8
  625.4 4.4 multiply_convert_fusion.2
  629.9 8.9 convolution_convert_fusion.5
  639.0 7.5 fusion.69
  652.4 5.7 pad_maximum_fusion.1
  658.9 31.6 %convolution_convert_fusion = bf16[3584,2048]{1,0:T(8,128)(2,1)S(1)} fusion(bf16[1600,3584]{1,0:T(8,128)(2,1)} %constant_dynamic-update-slice_fusion.12, bf16[1600,2048]{1,0:T(8,128)(2,1)} %get-tuple-element.145), kind=kOutput, calls=%fused_computation.3 | convolution fusion | flops 23495442432 | bytes 32702464 | tf_op jit(solution)/shard_map/dot_general | solution.py:165
  690.5 12.3 %pad_maximum_fusion = bf16[3712,2048]{1,0:T(8,128)(2,1)} fusion(bf16[128,2048]{1,0:T(8,128)(2,1)S(1)} %multiply_convert_fusion.5, bf16[3584,2048]{1,0:T(8,128)(2,1)S(1)} %convolution_convert_fusion), kind=kLoop, calls=%fused_computation.2 | loop fusion | flops 30408704 | bytes 30408704 | tf_op jit(solution)/shard_map/concatenate | solution.py:426
  702.9 20.6 %copy.140 = bf16[29,128,2048]{1,2,0:T(8,128)(2,1)} copy(bf16[29,128,2048]{2,1,0:T(8,128)(2,1)} %bitcast.485) | data formatting | bytes 30408704 | tf_op jit(solution)/shard_map/reshape | solution.py:426
  731.4 6.3 reduce-scatter.3.cloned.1.call-done
  744.6 149.1 %reduce-scatter.5.cloned.1.call-done = bf16[29,128,128]{1,2,0:T(8,128)(2,1)} async-done(((bf16[29,128,2048]{1,2,0:T(8,128)(2,1)}), bf16[29,128,128]{1,2,0:T(8,128)(2,1)}) %reduce-scatter.5.cloned.1.call-update) | async-done | bytes 950288 | tf_op jit(solution)/shard_map/reduce_scatter | solution.py:427
  893.7 2.3 fusion.35
  897.9 9.8 %small_sum.9 = f32[8,128]{1,0:T(8,128)} custom-call(f32[8,128]{1,0:T(8,128)} %pad_bitcast_fusion.2.x_ref), custom_call_target="tpu_custom_call" | custom-call | tf_op jit(solution)/shard_map/small_sum/pallas_call | solution.py:112
  925.9 2.2 multiply_subtract_fusion.1
  928.1 2.0 multiply_subtract_fusion.2
  930.2 5.0 multiply_subtract_fusion
  (525 shorter events, 179.5 us)
Async XLA Ops:
  7.2 123.1 %copy-start = (bf16[1,1600,192]{1,2,0:T(8,128)(2,1)S(1)}, bf16[1,1600,192]{1,2,0:T(8,128)(2,1)}, u32[]{:S(2)}) copy-start(bf16[1,1600,192]{1,2,0:T(8,128)(2,1)} %param.31) | copy-start | bytes 1843204
  7.2 7.3 copy-start.67
  7.2 10.3 %copy-start.84 = (s32[1,1600]{1,0:T(1,128)S(1)}, s32[1,1600]{1,0:T(1,128)}, u32[]{:S(2)}) copy-start(s32[1,1600]{1,0:T(1,128)} %param.37) | copy-start | bytes 19204
  7.3 10.9 %copy-start.86 = (s32[1,1600]{1,0:T(1,128)S(1)}, s32[1,1600]{1,0:T(1,128)}, u32[]{:S(2)}) copy-start(s32[1,1600]{1,0:T(1,128)} %param.36) | copy-start | bytes 19204
  7.3 10.9 %copy-start.95 = (s32[1,1600]{1,0:T(1,128)S(1)}, s32[1,1600]{1,0:T(1,128)}, u32[]{:S(2)}) copy-start(s32[1,1600]{1,0:T(1,128)} %param.34) | copy-start | bytes 19204
  7.3 12.2 %copy-start.98 = (f32[25]{0:T(128)S(1)}, f32[25]{0:T(128)}, u32[]{:S(2)}) copy-start(f32[25]{0:T(128)} %param.59) | copy-start | bytes 304
  7.3 12.7 %copy-start.96 = (s32[1,1600]{1,0:T(1,128)S(1)}, s32[1,1600]{1,0:T(1,128)}, u32[]{:S(2)}) copy-start(s32[1,1600]{1,0:T(1,128)} %param.32) | copy-start | bytes 19204
  7.3 95.6 %all-gather.6.cloned.1.call-start = ((), (), s32[]{:S(2)}) async-start(), calls=%async_computation.5 | async-start | bytes 10813440 | tf_op jit(solution)/shard_map/all_gather | solution.py:243
  13.2 269.3 %all-gather.4.cloned.1.call-start = ((), (), s32[]{:S(2)}) async-start(), calls=%async_computation.2 | async-start | bytes 16154624 | tf_op jit(solution)/shard_map/all_gather | solution.py:244
  14.5 723.3 %reduce-scatter.3.cloned.1.call-start = ((), (), s32[]{:S(2)}) async-start(), calls=%async_computation.3 | async-start | bytes 5570560 | tf_op jit(solution)/shard_map/reduce_scatter | solution.py:518
  14.5 6.1 collective-permute-start
  18.2 228.8 %copy-start.39 = (f32[1600]{0:T(1024)}, f32[1600]{0:T(1024)S(1)}, u32[]{:S(2)}) copy-start(f32[1600]{0:T(1024)S(1)} %get-tuple-element.115) | copy-start | bytes 19204
  19.4 250.0 %copy-start.54 = (f32[1600]{0:T(1024)}, f32[1600]{0:T(1024)S(1)}, u32[]{:S(2)}) copy-start(f32[1600]{0:T(1024)S(1)} %get-tuple-element.219) | copy-start | bytes 19204
  20.7 191.4 %copy-start.72 = (f32[1,2,2,128]{3,1,2,0:T(2,128)}, f32[1,2,2,128]{3,1,2,0:T(2,128)S(1)}, u32[]{:S(2)}) copy-start(f32[1,2,2,128]{3,1,2,0:T(2,128)S(1)} %copy.154) | copy-start | bytes 6148
  20.7 191.4 %copy-start.89 = (f32[1,2,2,128]{3,1,2,0:T(2,128)}, f32[1,2,2,128]{3,1,2,0:T(2,128)S(1)}, u32[]{:S(2)}) copy-start(f32[1,2,2,128]{3,1,2,0:T(2,128)S(1)} %copy.155) | copy-start | bytes 6148
  20.8 226.2 %copy-start.65 = (f32[1,8,2,128]{3,1,2,0:T(8,128)}, f32[1,8,2,128]{3,1,2,0:T(8,128)S(1)}, u32[]{:S(2)}) copy-start(f32[1,8,2,128]{3,1,2,0:T(8,128)S(1)} %copy.185) | copy-start | bytes 24580
  153.3 58.8 %copy-start.74 = (f32[512]{0:T(512)}, f32[512]{0:T(512)S(1)}, u32[]{:S(2)}) copy-start(f32[512]{0:T(512)S(1)} %divide_bitcast_fusion.1) | copy-start | bytes 6148
  154.8 57.4 %copy-start.76 = (f32[512]{0:T(512)}, f32[512]{0:T(512)S(1)}, u32[]{:S(2)}) copy-start(f32[512]{0:T(512)S(1)} %fusion.186) | copy-start | bytes 6148
  207.9 17.6 %copy-start.7 = (bf16[16,128,2,256]{1,0,3,2:T(8,128)(2,1)}, bf16[16,128,2,256]{1,0,3,2:T(8,128)(2,1)S(1)}, u32[]{:S(2)}) copy-start(bf16[16,128,2,256]{1,0,3,2:T(8,128)(2,1)S(1)} %copy.129) | copy-start | bytes 6291460
  217.1 8.4 copy-start.52
  225.5 6.8 copy-start.108
  245.5 15.2 %copy-start.66 = (f32[2048]{0:T(1024)}, f32[2048]{0:T(1024)S(1)}, u32[]{:S(2)}) copy-start(f32[2048]{0:T(1024)S(1)} %divide_bitcast_fusion) | copy-start | bytes 24580
  246.9 13.8 %copy-start.64 = (f32[2048]{0:T(1024)}, f32[2048]{0:T(1024)S(1)}, u32[]{:S(2)}) copy-start(f32[2048]{0:T(1024)S(1)} %fusion.174) | copy-start | bytes 24580
  270.7 7.5 slice-start
  282.6 8.1 copy-start.4
  282.6 11.6 %slice-start.4 = ((s8[4587520]{0:T(1024)(128)(4,1)}), s8[4194304]{0:T(1024)(128)(4,1)S(1)}, s32[]{:S(2)}) async-start(s8[4587520]{0:T(1024)(128)(4,1)} %bitcast.491), calls=%async_computation.10 | async-start | bytes 8388608
  286.5 7.6 slice-start.5
  323.8 26.8 %copy-start.45 = (bf16[1600,256]{1,0:T(8,128)(2,1)}, bf16[1600,256]{1,0:T(8,128)(2,1)S(1)}, u32[]{:S(2)}) copy-start(bf16[1600,256]{1,0:T(8,128)(2,1)S(1)} %convolution_convert_fusion.4) | copy-start | bytes 2457604
  323.8 26.8 %collective-permute-start.1 = (bf16[1600,256]{1,0:T(8,128)(2,1)S(1)}, bf16[1600,256]{1,0:T(8,128)(2,1)}, u32[]{:S(2)}, u32[]{:S(2)}) collective-permute-start(bf16[1600,256]{1,0:T(8,128)(2,1)S(1)} %convolution_convert_fusion.4), channel_id=1, source_target_pairs={{0,1},{1,0},{2,3},{3,2},{4,5},{5,4},{6,7},{7,6},{8,9},{9,8},{10,11... | collective-permute-start | bytes 2457608 | tf_op jit(solution)/shard_map/ppermute | solution.py:135
  330.2 22.3 %copy-start.51 = (bf16[256,22]{1,0:T(8,128)(2,1)S(1)}, bf16[256,22]{1,0:T(8,128)(2,1)}, u32[]{:S(2)}) copy-start(bf16[256,22]{1,0:T(8,128)(2,1)} %reshape.708) | copy-start | bytes 33796
  330.2 22.3 %copy-start.103 = (f32[22]{0:T(128)S(1)}, f32[22]{0:T(128)}, u32[]{:S(2)}) copy-start(f32[22]{0:T(128)} %slice.560) | copy-start | bytes 268
  362.7 23.1 %copy-start.101 = (f32[128]{0:T(128)}, f32[128]{0:T(128)S(1)}, u32[]{:S(2)}) copy-start(f32[128]{0:T(128)S(1)} %get-tuple-element.158) | copy-start | bytes 1540
  367.9 23.8 %slice-start.6 = ((s8[14680064]{0:T(1024)(128)(4,1)}), s8[4194304]{0:T(1024)(128)(4,1)S(1)}, s32[]{:S(2)}) async-start(s8[14680064]{0:T(1024)(128)(4,1)} %bitcast.497), calls=%async_computation.12 | async-start | bytes 8388608
  370.9 20.7 %slice-start.7 = ((s8[14680064]{0:T(1024)(128)(4,1)}), s8[4194304]{0:T(1024)(128)(4,1)S(1)}, s32[]{:S(2)}) async-start(s8[14680064]{0:T(1024)(128)(4,1)} %bitcast.497), calls=%async_computation.13 | async-start | bytes 8388608
  377.7 14.0 %slice-start.8 = ((s8[14680064]{0:T(1024)(128)(4,1)}), s8[4194304]{0:T(1024)(128)(4,1)S(1)}, s32[]{:S(2)}) async-start(s8[14680064]{0:T(1024)(128)(4,1)} %bitcast.497), calls=%async_computation.14 | async-start | bytes 8388608
  383.1 8.6 slice-start.9
  391.7 22.0 %copy-start.8 = (bf16[16,128,2,256]{1,0,3,2:T(8,128)(2,1)S(1)}, bf16[16,128,2,256]{1,0,3,2:T(8,128)(2,1)}, u32[]{:S(2)}) copy-start(bf16[16,128,2,256]{1,0,3,2:T(8,128)(2,1)} %copy-done.7) | copy-start | bytes 6291460
  407.9 73.4 %collective-permute-start.2 = (bf16[1600,1024]{1,0:T(8,128)(2,1)}, bf16[1600,1024]{1,0:T(8,128)(2,1)}, u32[]{:S(2)}, u32[]{:S(2)}) collective-permute-start(bf16[1600,1024]{1,0:T(8,128)(2,1)} %add_convert_fusion), channel_id=1, source_target_pairs={{0,1},{1,0},{2,3},{3,2},{4,5},{5,4},{6,7},{7,6},{8,9},{9,8},{10,11... | collective-permute-start | bytes 9830408 | tf_op jit(solution)/shard_map/ppermute | solution.py:135
  410.8 70.4 %copy-start.41 = (f32[1600]{0:T(1024)S(1)}, f32[1600]{0:T(1024)}, u32[]{:S(2)}) copy-start(f32[1600]{0:T(1024)} %copy-done.39) | copy-start | bytes 19204
  410.9 70.4 %copy-start.97 = (f32[1024]{0:T(1024)S(1)}, f32[1024]{0:T(1024)}, u32[]{:S(2)}) copy-start(f32[1024]{0:T(1024)} %get-tuple-element.216) | copy-start | bytes 12292
  412.9 89.7 %copy-start.92 = (f32[1024]{0:T(1024)}, f32[1024]{0:T(1024)S(1)}, u32[]{:S(2)}) copy-start(f32[1024]{0:T(1024)S(1)} %dynamic_slice.52) | copy-start | bytes 12292
  413.6 89.0 %copy-start.93 = (f32[1024]{0:T(1024)}, f32[1024]{0:T(1024)S(1)}, u32[]{:S(2)}) copy-start(f32[1024]{0:T(1024)S(1)} %dynamic_slice.53) | copy-start | bytes 12292
  481.3 35.4 %copy-start.42 = (f32[1600]{0:T(1024)S(1)}, f32[1600]{0:T(1024)}, u32[]{:S(2)}) copy-start(f32[1600]{0:T(1024)} %copy-done.39) | copy-start | bytes 19204
  481.3 35.4 %copy-start.91 = (f32[1024]{0:T(1024)S(1)}, f32[1024]{0:T(1024)}, u32[]{:S(2)}) copy-start(f32[1024]{0:T(1024)} %dynamic_slice.54) | copy-start | bytes 12292
  516.7 7.5 copy-start.68
  516.7 7.5 copy-start.70
  516.7 7.5 copy-start.31
  527.4 52.3 %collective-permute-start.3 = (bf16[1600,512]{1,0:T(8,128)(2,1)}, bf16[1600,512]{1,0:T(8,128)(2,1)}, u32[]{:S(2)}, u32[]{:S(2)}) collective-permute-start(bf16[1600,512]{1,0:T(8,128)(2,1)} %convolution_convert_fusion.2), channel_id=1, source_target_pairs={{0,1},{1,0},{2,3},{3,2},{4,5},{5,4},{6,7},{7,6},{8,9},{9,8},{10,11... | collective-permute-start | bytes 4915208 | tf_op jit(solution)/shard_map/ppermute | solution.py:135
  528.7 8.7 copy-start.6
  546.0 6.4 copy-start.60
  546.0 6.4 copy-start.63
  546.0 6.9 copy-start.28
  551.6 25.2 %collective-permute-start.4 = (bf16[1024,256]{1,0:T(8,128)(2,1)}, bf16[1024,256]{1,0:T(8,128)(2,1)}, u32[]{:S(2)}, u32[]{:S(2)}) collective-permute-start(bf16[1024,256]{1,0:T(8,128)(2,1)} %get-tuple-element.179), channel_id=1, source_target_pairs={{0,1},{1,0},{2,3},{3,2},{4,5},{5,4},{6,7},{7,6},{8,9},{9,8},{10,11... | collective-permute-start | bytes 1572872 | tf_op jit(solution)/shard_map/ppermute | solution.py:135
  629.9 8.9 copy-start.24
  629.9 8.9 copy-start.30
  658.1 235.6 %reduce-scatter.5.cloned.1.call-start = ((), (), s32[]{:S(2)}) async-start(), calls=%async_computation.4 | async-start | bytes 16154624 | tf_op jit(solution)/shard_map/reduce_scatter | solution.py:427
  723.5 6.6 copy-start.71
  723.5 6.6 copy-start.69
  724.3 201.6 %copy-start.36 = (f32[9,32,256]{2,1,0:T(8,128)S(1)}, f32[9,32,256]{2,1,0:T(8,128)}, u32[]{:S(2)}) copy-start(f32[9,32,256]{2,1,0:T(8,128)} %param.44) | copy-start | bytes 884740
  910.3 19.9 %copy-start.10 = (f32[29,128,128]{2,1,0:T(8,128)S(1)}, f32[29,128,128]{2,1,0:T(8,128)}, u32[]{:S(2)}) copy-start(f32[29,128,128]{2,1,0:T(8,128)} %param.47) | copy-start | bytes 5701636
  911.7 16.4 %copy-start.37 = (f32[1,256,256]{2,1,0:T(8,128)S(1)}, f32[1,256,256]{2,1,0:T(8,128)}, u32[]{:S(2)}) copy-start(f32[1,256,256]{2,1,0:T(8,128)} %slice_multiply_fusion.1) | copy-start | bytes 786436
  912.9 15.3 %copy-start.38 = (f32[2,128,256]{2,1,0:T(8,128)S(1)}, f32[2,128,256]{2,1,0:T(8,128)}, u32[]{:S(2)}) copy-start(f32[2,128,256]{2,1,0:T(8,128)} %param.41) | copy-start | bytes 786436
  920.2 10.0 %copy-start.32 = (f32[29,128,128]{2,1,0:T(8,128)S(1)}, f32[29,128,128]{2,1,0:T(8,128)}, u32[]{:S(2)}) copy-start(f32[29,128,128]{2,1,0:T(8,128)} %param.48) | copy-start | bytes 5701636
  920.2 10.0 %copy-start.33 = (f32[29,128,128]{2,1,0:T(8,128)S(1)}, f32[29,128,128]{2,1,0:T(8,128)}, u32[]{:S(2)}) copy-start(f32[29,128,128]{2,1,0:T(8,128)} %param.49) | copy-start | bytes 5701636
  (68 other events, 211.0 us)
Sparse Core Ops, SparseCore 0:
  13.4 89.4 all-gather.5
  105.1 115.5 all-gather.3
  658.2 79.4 reduce-scatter.2
  741.7 151.9 reduce-scatter.4

commit v2 on v1

--- a/solution.py
+++ b/solution.py
@@ -168,6 +168,317 @@
         (((contract[0],), (contract[1],)), ((), ())),
         preferred_element_type=jnp.float32,
     )
+
+
+PAD = 128
+PYRAMID_ROWS = (-36, -24, -12, 0, 12, 24, 36)
+
+
+def taps_by_row():
+    fields = [(0, 0)] + [(rate, col * rate) for rate in (12, 24, 36) for col in (-1, 0, 1)]
+    groups = []
+    for row_step in PYRAMID_ROWS:
+        group = []
+        for place, (rate, col_step) in enumerate(fields):
+            if rate == 0:
+                if row_step == 0:
+                    group.append((0, place))
+            elif row_step == 0 or abs(row_step) == rate:
+                turn = (1 if row_step > 0 else -1 if row_step < 0 else 0) + 1
+                tap = 1 + 9 * (rate // 12 - 1) + 3 * turn + (col_step // rate + 1)
+                group.append((tap, place))
+        groups.append(group)
+    return fields, groups
+
+
+FIELDS, ROW_GROUPS = taps_by_row()
+TAP_ORDER = [tap for group in ROW_GROUPS for tap, place in group]
+PLACE_ORDER = [place for group in ROW_GROUPS for tap, place in group]
+
+
+def roll_cols(values, columns, step):
+    if step == 0:
+        return values
+    moved = pltpu.roll(values, (-step) % values.shape[0], 0)
+    target = columns[:, :1] + float(step)
+    return jnp.where((target >= 0.0) & (target < float(FW)), moved, 0.0)
+
+
+def vmem(count):
+    return [pl.BlockSpec(memory_space=pltpu.VMEM)] * count
+
+
+def middle_kernel(back, x_ref, w_ref, col_ref, o_ref, canvas):
+    edge = 4 * FW
+    mid = x_ref.shape[1]
+    values = x_ref[...].astype(jnp.float32)
+    sign = -1 if back else 1
+    for turn in range(3):
+        canvas[turn, :edge] = jnp.zeros((edge, mid), canvas.dtype)
+        canvas[turn, POSITIONS + edge :] = jnp.zeros((edge, mid), canvas.dtype)
+        canvas[turn, edge : POSITIONS + edge] = roll_cols(
+            values, col_ref, sign * 4 * (turn - 1)
+        ).astype(canvas.dtype)
+    block = 400
+
+    def step(index, carry):
+        total = None
+        for row in range(3):
+            first = pl.multiple_of(index * block + edge * (1 + sign * (row - 1)), 16)
+            for turn in range(3):
+                part = dot(
+                    canvas[turn, pl.ds(first, block)],
+                    w_ref[3 * row + turn],
+                    (1, 1) if back else (1, 0),
+                )
+                total = part if total is None else total + part
+        o_ref[pl.ds(pl.multiple_of(index * block, 16), block)] = total.astype(o_ref.dtype)
+        return carry
+
+    lax.fori_loop(0, POSITIONS // block, step, 0)
+
+
+def middle_conv(field, weights, columns, back, dtype):
+    return pl.pallas_call(
+        functools.partial(middle_kernel, back),
+        out_shape=jax.ShapeDtypeStruct((POSITIONS, MID), dtype),
+        in_specs=vmem(3),
+        out_specs=vmem(1)[0],
+        scratch_shapes=[pltpu.VMEM((3, POSITIONS + 8 * FW, MID), jnp.bfloat16)],
+        compiler_params=pltpu.CompilerParams(vmem_limit_bytes=40 << 20),
+        cost_estimate=pl.CostEstimate(
+            flops=2 * POSITIONS * 9 * MID * MID, bytes_accessed=16 << 20, transcendentals=0
+        ),
+        name="middle_back" if back else "middle_fwd",
+    )(field, weights, columns)
+
+
+def middle_weight_kernel(xt_ref, g_ref, col_ref, o_ref, fields):
+    width = g_ref.shape[1]
+    values = g_ref[...].astype(jnp.float32)
+    for turn in range(3):
+        fields[turn, :PAD] = jnp.zeros((PAD, width), fields.dtype)
+        fields[turn, PAD + POSITIONS :] = jnp.zeros((PAD, width), fields.dtype)
+        fields[turn, PAD : PAD + POSITIONS] = roll_cols(values, col_ref, -4 * (turn - 1)).astype(
+            fields.dtype
+        )
+    for row in range(3):
+        row_step = 4 * (row - 1)
+        r0, r1 = valid(row_step, FH)
+        first = r0 * FW // 128 * 128
+        last = min(POSITIONS, -(-r1 * FW // 128) * 128)
+        base = PAD + first - row_step * FW
+        for turn in range(3):
+            o_ref[3 * row + turn] = dot(
+                xt_ref[:, first:last], fields[turn, base : base + last - first]
+            ).astype(o_ref.dtype)
+
+
+def middle_weights(field_t, grads, columns):
+    depth, width = field_t.shape[0], grads.shape[1]
+    return pl.pallas_call(
+        middle_weight_kernel,
+        out_shape=jax.ShapeDtypeStruct((9, depth, width), jnp.bfloat16),
+        in_specs=vmem(3),
+        out_specs=vmem(1)[0],
+        scratch_shapes=[pltpu.VMEM((3, POSITIONS + 2 * PAD, width), jnp.bfloat16)],
+        compiler_params=pltpu.CompilerParams(vmem_limit_bytes=40 << 20),
+        cost_estimate=pl.CostEstimate(
+            flops=2 * POSITIONS * 9 * depth * width, bytes_accessed=6 << 20, transcendentals=0
+        ),
+        name="middle_weights",
+    )(field_t, grads, columns)
+
+
+def pyramid_kernel(x_ref, w_hbm, col_ref, o_ref, weights, fields, sems):
+    width = o_ref.shape[2]
+    copies = []
+    order = [3, 2, 4, 1, 5, 0, 6]
+    starts = []
+    place = 0
+    for group in ROW_GROUPS:
+        starts.append(place)
+        place += len(group)
+    for turn in order:
+        group_copies = []
+        for offset, (tap, _) in enumerate(ROW_GROUPS[turn]):
+            slot = starts[turn] + offset
+            copy = pltpu.make_async_copy(
+                w_hbm.at[tap], weights.at[:, pl.ds(slot * width, width)], sems.at[slot]
+            )
+            copy.start()
+            group_copies.append(copy)
+        copies.append(group_copies)
+    for turn, group_copies in zip(order, copies):
+        for copy in group_copies:
+            copy.wait()
+        row_step = PYRAMID_ROWS[turn]
+        group = ROW_GROUPS[turn]
+        r0, r1 = valid(row_step, FH)
+        count = (r1 - r0) * FW
+        block = {1600: 800, 1120: 560, 640: 640, 160: 160}[count]
+        cols = pl.ds(starts[turn] * width, len(group) * width)
+
+        def step(index, carry):
+            source = pl.multiple_of(index * block + r0 * FW, 16)
+            target = pl.multiple_of(index * block + (r0 - row_step) * FW, 16)
+            part = dot(x_ref[pl.ds(source, block)], weights[:, cols])
+            for offset, (tap, field) in enumerate(group):
+                piece = part[:, offset * width : (offset + 1) * width]
+                rows = pl.ds(target, block)
+                if row_step == 0:
+                    fields[field, rows] = piece
+                else:
+                    fields[field, rows] += piece
+            return carry
+
+        lax.fori_loop(0, count // block, step, 0)
+    o_ref[0] = fields[0]
+    for branch in range(3):
+        total = fields[2 + 3 * branch]
+        for turn in (0, 2):
+            place = 1 + 3 * branch + turn
+            total = total + roll_cols(fields[place], col_ref, FIELDS[place][1])
+        o_ref[1 + branch] = total
+
+
+def pyramid_forward(field, weights, columns):
+    depth, width = weights.shape[1:]
+    return pl.pallas_call(
+        pyramid_kernel,
+        out_shape=jax.ShapeDtypeStruct((4, POSITIONS, width), jnp.float32),
+        in_specs=[
+            pl.BlockSpec(memory_space=pltpu.VMEM),
+            pl.BlockSpec(memory_space=pl.ANY),
+            pl.BlockSpec(memory_space=pltpu.VMEM),
+        ],
+        out_specs=vmem(1)[0],
+        scratch_shapes=[
+            pltpu.VMEM((depth, 28 * width), jnp.bfloat16),
+            pltpu.VMEM((10, POSITIONS, width), jnp.float32),
+            pltpu.SemaphoreType.DMA((28,)),
+        ],
+        compiler_params=pltpu.CompilerParams(vmem_limit_bytes=56 << 20),
+        cost_estimate=pl.CostEstimate(
+            flops=2 * POSITIONS * 17 * depth * width, bytes_accessed=25 << 20, transcendentals=0
+        ),
+        name="pyramid_fwd",
+    )(field, weights, columns)
+
+
+def fill_fields(g_ref, col_ref, fields):
+    width = g_ref.shape[2]
+    for place, (rate, col_step) in enumerate(FIELDS):
+        fields[place, :PAD] = jnp.zeros((PAD, width), fields.dtype)
+        fields[place, PAD + POSITIONS :] = jnp.zeros((PAD, width), fields.dtype)
+        values = g_ref[rate // 12]
+        fields[place, PAD : PAD + POSITIONS] = roll_cols(
+            values.astype(jnp.float32), col_ref, -col_step
+        ).astype(fields.dtype)
+
+
+def weight_kernel(xt_ref, g_ref, col_ref, pool_ref, pool_grad_ref, o_ref, fields):
+    width = g_ref.shape[2]
+    depth = xt_ref.shape[0]
+    fill_fields(g_ref, col_ref, fields)
+    block = 512
+    for row_step, group in zip(PYRAMID_ROWS, ROW_GROUPS):
+        r0, r1 = valid(row_step, FH)
+        first = r0 * FW // 128 * 128
+        last = min(POSITIONS, -(-r1 * FW // 128) * 128)
+        base = PAD + first - row_step * FW
+        sets = [group[at : at + 2] for at in range(0, 10, 2)] if row_step == 0 else [group]
+        for chosen in sets:
+            right = jnp.concatenate(
+                [fields[place, base : base + last - first] for tap, place in chosen], 1
+            )
+
+            def step(index, carry):
+                rows = pl.ds(pl.multiple_of(index * block, 16), block)
+                part = dot(xt_ref[rows, first:last], right)
+                for offset, (tap, place) in enumerate(chosen):
+                    o_ref[tap, rows] = part[:, offset * width : (offset + 1) * width].astype(
+                        o_ref.dtype
+                    )
+                return carry
+
+            lax.fori_loop(0, depth // block, step, 0)
+    o_ref[28] = (pool_ref[...] * pool_grad_ref[...]).astype(o_ref.dtype)
+
+
+def pyramid_weights(field_t, grads, columns, pooled, pool_grad):
+    depth = field_t.shape[0]
+    width = grads.shape[2]
+    return pl.pallas_call(
+        weight_kernel,
+        out_shape=jax.ShapeDtypeStruct((29, depth, width), jnp.bfloat16),
+        in_specs=vmem(5),
+        out_specs=vmem(1)[0],
+        scratch_shapes=[pltpu.VMEM((10, POSITIONS + 2 * PAD, width), jnp.bfloat16)],
+        compiler_params=pltpu.CompilerParams(vmem_limit_bytes=56 << 20),
+        cost_estimate=pl.CostEstimate(
+            flops=2 * POSITIONS * 18 * depth * width, bytes_accessed=25 << 20, transcendentals=0
+        ),
+        name="pyramid_weights",
+    )(field_t, grads, columns, pooled, pool_grad)
+
+
+def field_kernel(half_ref, w_hbm, g_ref, col_ref, o_ref, weights, fields, stack, sems):
+    width = g_ref.shape[2]
+    depth = o_ref.shape[1]
+    half = pl.ds(pl.multiple_of(half_ref[0] * depth, 16), depth)
+    copies = []
+    for slot, tap in enumerate(TAP_ORDER):
+        copy = pltpu.make_async_copy(
+            w_hbm.at[tap, half], weights.at[:, pl.ds(slot * width, width)], sems.at[slot]
+        )
+        copy.start()
+        copies.append(copy)
+    fill_fields(g_ref, col_ref, fields)
+    for copy in copies:
+        copy.wait()
+    step_of = [step for step, group in zip(PYRAMID_ROWS, ROW_GROUPS) for entry in group]
+    for r0, r1 in ((0, 4), (4, 12), (12, 16), (16, 24), (24, 28), (28, 36), (36, 40)):
+        slots = [
+            slot for slot, step in enumerate(step_of) if r0 - step >= 0 and r1 - step <= FH
+        ]
+        count = (r1 - r0) * FW
+        for at, slot in enumerate(slots):
+            base = PAD + (r0 - step_of[slot]) * FW
+            stack[:count, at * width : (at + 1) * width] = fields[
+                PLACE_ORDER[slot], base : base + count
+            ]
+        o_ref[r0 * FW : r1 * FW] = dot(
+            stack[:count, : len(slots) * width],
+            weights[:, slots[0] * width : (slots[-1] + 1) * width],
+            (1, 1),
+        ).astype(o_ref.dtype)
+
+
+def pyramid_field(half, weights, grads, columns):
+    depth, width = weights.shape[1] // 2, weights.shape[2]
+    return pl.pallas_call(
+        field_kernel,
+        out_shape=jax.ShapeDtypeStruct((POSITIONS, depth), jnp.bfloat16),
+        in_specs=[
+            pl.BlockSpec(memory_space=pltpu.SMEM),
+            pl.BlockSpec(memory_space=pl.ANY),
+            pl.BlockSpec(memory_space=pltpu.VMEM),
+            pl.BlockSpec(memory_space=pltpu.VMEM),
+        ],
+        out_specs=vmem(1)[0],
+        scratch_shapes=[
+            pltpu.VMEM((depth, 28 * width), jnp.bfloat16),
+            pltpu.VMEM((10, POSITIONS + 2 * PAD, width), jnp.bfloat16),
+            pltpu.VMEM((8 * FW, 19 * width), jnp.bfloat16),
+            pltpu.SemaphoreType.DMA((28,)),
+        ],
+        compiler_params=pltpu.CompilerParams(vmem_limit_bytes=56 << 20),
+        cost_estimate=pl.CostEstimate(
+            flops=2 * POSITIONS * 17 * depth * width, bytes_accessed=15 << 20, transcendentals=0
+        ),
+        name="pyramid_field",
+    )(half, weights, grads, columns)
 
 
 def adam_step(weight, first, second, gradient, factor, rate, decay):
@@ -249,7 +560,7 @@
         trunk[:, :, start : start + 9 * mid_share]
         .reshape(dp_size, 2, 9, mid_share, 256)
         .transpose(2, 0, 3, 1, 4)
-        .reshape(9 * MID, MID)
+        .reshape(9, MID, MID)
     )
     small = trunk[:, :, start + 9 * mid_share :].reshape(dp_size, 2, small_rows * 256)
     size = PATCH * stem_share
@@ -308,12 +619,11 @@
     normed_one = (first_pre - mean_one) * scale_one
     act_input = gain_one * normed_one + shift_one
     hidden_low = (crop_field * jax.nn.gelu(act_input)).astype(low)
-    hidden_canvas = hidden_low.reshape(FH, FW, MID)
-    middle_taps = taps_of(4)
-    hidden_stack = jnp.concatenate(
-        [shift_field(hidden_canvas, step[0], step[1]) for step in middle_taps], 2
-    ).reshape(POSITIONS, 9 * MID)
-    second_low = dot(hidden_stack, middle_low).astype(low)
+    columns = jnp.broadcast_to(
+        lax.rem(lax.broadcasted_iota(jnp.int32, (POSITIONS, 1), 0), FW).astype(jnp.float32),
+        (POSITIONS, 128),
+    )
+    second_low = middle_conv(hidden_low, middle_low, columns, False, low)
     expand_pre = dot(second_low, expand_low, (1, 1))
     sum_two, square_two = small_sum(
         sizes,
@@ -325,30 +635,14 @@
     scale_two = lax.rsqrt(square_two / crop_total - mean_two * mean_two + norm_eps)
     stream_out = stream + crop_field * (gain_two * ((expand_pre - mean_two) * scale_two) + shift_two)
     output_low = stream_out.astype(low)
-    canvas_two = output_low.reshape(FH, FW, D)
     image_count = jnp.sum(crop_field)
     pooled = jnp.sum(crop_field * output_low.astype(jnp.float32), 0, keepdims=True) / image_count
     pooled_low = pooled.astype(low)
 
     width = BRANCH // 2
-    pyramid_taps = [(0, 0)] + taps_of(12) + taps_of(24) + taps_of(36)
-    branch_of = [0] + [1] * 9 + [2] * 9 + [3] * 9
-    branch_pre = [jnp.zeros((FH, FW, width), jnp.float32) for branch in range(4)]
-    for tap, step in enumerate(pyramid_taps):
-        r0, r1 = valid(step[0], FH)
-        c0, c1 = valid(step[1], FW)
-        part = dot(canvas_two[r0:r1].reshape(-1, D), pyramid_low[tap]).reshape(r1 - r0, FW, width)
-        branch_pre[branch_of[tap]] = branch_pre[branch_of[tap]] + jnp.pad(
-            part[:, c0:c1],
-            (
-                (r0 - step[0], FH - (r1 - step[0])),
-                (c0 - step[1], FW - (c1 - step[1])),
-                (0, 0),
-            ),
-        )
-    branch_pre = [values.reshape(POSITIONS, width) for values in branch_pre]
+    branch_pre = pyramid_forward(output_low, pyramid_low, columns)
     pool_pre = dot(pooled_low, pyramid_low[28])
-    branch_acts = [jax.nn.gelu(values) for values in branch_pre]
+    branch_acts = [jax.nn.gelu(branch_pre[order]) for order in range(4)]
     branch_acts.append(jnp.broadcast_to(jax.nn.gelu(pool_pre), (POSITIONS, width)))
     concat_low = jnp.concatenate(branch_acts, 1).astype(low)
     project_part = dot(concat_low, project_low).astype(low)
@@ -398,37 +692,34 @@
     project_grad_low = gelu_grad(project_pre, feature_grad).astype(low)
     project_grad = dot(concat_low, project_grad_low, (0, 0))
     concat_grad = dot(project_grad_low, project_low, (1, 1))
-    branch_grads = [
-        gelu_grad(branch_pre[order], concat_grad[:, order * width : (order + 1) * width])
-        .astype(low)
-        .reshape(FH, FW, width)
-        for order in range(4)
-    ]
+    branch_grads = jnp.stack(
+        [
+            gelu_grad(branch_pre[order], concat_grad[:, order * width : (order + 1) * width])
+            for order in range(4)
+        ]
+    ).astype(low)
     pool_grad_low = gelu_grad(
         pool_pre, jnp.sum(concat_grad[:, 4 * width :], 0, keepdims=True)
     ).astype(low)
-    grad_stack = jnp.concatenate(
-        [
-            shift_field(branch_grads[branch_of[tap]], -step[0], -step[1])
-            for tap, step in enumerate(pyramid_taps)
-        ],
-        2,
-    ).reshape(POSITIONS, 28 * width)
-
-    pooled_grad = dot(pool_grad_low, pyramid_low[28], (1, 1)) / image_count
-    weight_rows = pyramid_low[:28].transpose(1, 0, 2).reshape(D, 28 * width)
-    other_part = dot(
-        grad_stack, other_half(weight_rows, 0), (1, 1)
-    ) + crop_field * other_half(pooled_grad, 1)
-    other_sent = swap_chan(other_part.astype(low))
-    taps_grad = dot(grad_stack, output_low, (0, 0)).astype(low)
-    pool_weight_grad = dot(pool_grad_low, pooled_low, (0, 0)).astype(low)
-    pyramid_grad = jnp.concatenate([taps_grad, pool_weight_grad], axis=0).reshape(29, width, D)
-    pyramid_red = lax.psum_scatter(pyramid_grad, "dp", scatter_dimension=2, tiled=True)
-    own_part = dot(grad_stack, own_half(weight_rows, 0), (1, 1)) + crop_field * own_half(
-        pooled_grad, 1
-    )
-    stream_grad = own_part.astype(low).astype(jnp.float32) + other_sent.astype(jnp.float32)
+    own_place = chan_place.reshape(1)
+    other_part = pyramid_field(1 - own_place, pyramid_low, branch_grads, columns)
+    other_sent = swap_chan(other_part)
+    later_grads, other_part = lax.optimization_barrier((branch_grads, other_part))
+    pyramid_grad = pyramid_weights(
+        output_low.T,
+        later_grads,
+        columns,
+        pooled_low.astype(jnp.float32).reshape(D, 1),
+        pool_grad_low.astype(jnp.float32),
+    )
+    pyramid_red = lax.psum_scatter(pyramid_grad, "dp", scatter_dimension=1, tiled=True)
+    later_grads, pyramid_grad = lax.optimization_barrier((later_grads, pyramid_grad))
+    own_part = pyramid_field(own_place, pyramid_low, later_grads, columns)
+    pool_part = dot(pool_grad_low, pyramid_low[28], (1, 1)) / image_count
+    pool_sum = own_half(pool_part, 1) + swap_chan(other_half(pool_part, 1))
+    stream_grad = (
+        own_part.astype(jnp.float32) + other_sent.astype(jnp.float32) + crop_field * pool_sum
+    )
 
     own_gain_two = own_half(gain_two, 0)
     own_scale_two = own_half(scale_two, 0)
@@ -456,12 +747,7 @@
     second_grad_low = (
         second_part.astype(jnp.float32) + second_other.astype(jnp.float32)
     ).astype(low)
-    second_canvas = second_grad_low.reshape(FH, FW, MID)
-    second_stack = jnp.concatenate(
-        [shift_field(second_canvas, -step[0], -step[1]) for step in middle_taps], 2
-    ).reshape(POSITIONS, 9 * MID)
-    middle_back = middle_low.reshape(9, MID, MID).transpose(0, 2, 1).reshape(9 * MID, MID)
-    hidden_grad = dot(second_stack, middle_back)
+    hidden_grad = middle_conv(second_grad_low, middle_low, columns, True, jnp.float32)
     upstream_one = gelu_grad(act_input, crop_field * hidden_grad)
     gain_one_all, shift_one_all = small_sum(
         sizes,
@@ -477,7 +763,7 @@
         * scale_one
         * (upstream_one - (shift_one_all + normed_one * gain_one_all) / crop_total)
     ).astype(low)
-    middle_grad = dot(hidden_stack, own_half(second_grad_low, 1), (0, 0)).astype(low)
+    middle_grad = middle_weights(hidden_low.T, own_half(second_grad_low, 1), columns)
     reduce_grad = dot(stream_low, own_half(first_grad_low, 1), (0, 0)).astype(low)
     start_grad = dot(first_grad_low, own_half(reduce_low, 0), (1, 1)) + stream_grad
     start_grad_low = (crop_field * start_grad).astype(low)
@@ -528,7 +814,7 @@
     )
     size = stem_weight.size + project_weight.size
     head_red = small_red[size : size + head_weight.size].reshape(head_weight.shape)
-    pyramid_red = pyramid_red.astype(jnp.float32).transpose(0, 2, 1)
+    pyramid_red = pyramid_red.astype(jnp.float32)
     norm_grad = jnp.stack(
         [
             jnp.concatenate([gain_one_grad, gain_two_grad]),

time: 957 us -> 903 us (0.944)
  matrix products: 190 us -> 48.4 us
  Pallas kernels: 49.1 us -> 176 us
  local copies, waits for them, and re-layouts: 243 us -> 145 us
  waiting for transfers between devices: 316 us -> 350 us
  other arithmetic: 114 us -> 144 us
    dot_general x46 -> x15, matrix products: 184 us -> 48.4 us  [dot(): lax.dot_general(left, right, (((contract[0],), (contract[1],)), ((), ()))...]
    pallas_call x0 -> x7, Pallas kernels: none -> 124 us  [the longest x1 38.1 us: pyramid_weights(): pl.pallas_call(weight_kernel, out_shape=jax.ShapeDtypeStruct((29, depth,...]
    reduce_scatter x1, waiting for transfers between devices: 6.34 us -> 70.2 us  [on_device(): lax.psum_scatter(packed_grads, 'dp', scatter_dimension=0, tiled=True)]
    transpose x3 -> x0, local copies, waits for them, and re-layouts: 32.9 us -> none  [the longest x2 26.2 us: on_device(): weight_rows = pyramid_low[:28].transpose(1, 0, 2).reshape(D, 28 * width)]
    ppermute x5 -> x6, waiting for transfers between devices: 77.9 us -> 45.9 us  [swap_chan(): return lax.ppermute(values, 'chan', [(0, 1), (1, 0)])]
    unnamed x308 -> x104, local copies, waits for them, and re-layouts: 53.5 us -> 23.3 us
    convert_element_type x1 -> x4, other arithmetic: 0.12 us -> 18.5 us  [the longest x1 17.4 us: on_device(): output_low = stream_out.astype(low)]
    reduce_sum x1 -> x3, other arithmetic: 1.71 us -> 19.9 us  [the longest x1 7.19 us: on_device(): jnp.sum(crop_field * expand_pre, 0)]
  transfers between devices with their start and end apart: 9 -> 10, of which waited for: 5 -> 6; matrix products, arithmetic and copies ran while one was open for 32% -> 22% of each run, Pallas kernels for 2% -> 10%
where the time goes in v2:
time: 903 us; the launch traced here: 893 us
  waiting for transfers between devices  350 us (39%)
  Pallas kernels  176 us (19%)
  local copies, waits for them, and re-layouts  145 us (16%)
  other arithmetic  144 us (16%)
  matrix products  48.4 us (5%)
  between operations  22.4 us (2%)
    reduce_scatter x1, waiting for transfers between devices, on_device(): lax.psum_scatter(pyramid_grad, 'dp', scatter_dimension=1, tiled=True)  149 us
    all_gather x1, waiting for transfers between devices, on_device(): lax.all_gather(packed, ('dp', 'chan'))  83.7 us
    reduce_scatter x1, waiting for transfers between devices, on_device(): lax.psum_scatter(packed_grads, 'dp', scatter_dimension=0, tiled=True)  70.2 us
    pallas_call x5, Pallas kernels, small_sum(): pl.pallas_call(functools.partial(sum_kernel, sizes, axes, count), out_sha...  52.3 us
    dot_general x15, matrix products, dot(): lax.dot_general(left, right, (((contract[0],), (contract[1],)), ((), ()))...  48.4 us
    ppermute x6, waiting for transfers between devices, swap_chan(): return lax.ppermute(values, 'chan', [(0, 1), (1, 0)])  45.9 us
    pallas_call x1, Pallas kernels, pyramid_weights(): pl.pallas_call(weight_kernel, out_shape=jax.ShapeDtypeStruct((29, depth,...  38.1 us
    pallas_call x2, Pallas kernels, pyramid_field(): pl.pallas_call(field_kernel, out_shape=jax.ShapeDtypeStruct((POSITIONS, d...  35.7 us
  transfers between devices with their start and end apart: 10, of which 6 were waited for; matrix products, arithmetic and copies ran while one was open for 22% of the time, Pallas kernels for 10%

profile of v2, /device:TPU:0, one launch (start us, length us, event | category | flops | bytes accessed | tf_op | source)
XLA Modules:
  0.0 893.3 jit_solution(17308506598464808858)
XLA Ops:
  14.4 3.0 collective-permute-start
  19.2 83.7 %all-gather.6.cloned.1.call-done = bf16[20480,256]{1,0:T(8,128)(2,1)} async-done(((bf16[640,256]{1,0:T(8,128)(2,1)}), bf16[20480,256]{1,0:T(8,128)(2,1)}) %all-gather.6.cloned.1.call-update) | async-done | bytes 10485776 | tf_op jit(solution)/shard_map/all_gather | solution.py:554
  102.9 2.7 slice.216
  105.6 5.0 slice.223
  110.6 3.8 reshape.533
  122.6 2.8 reshape.545
  125.5 2.6 copy.126
  128.1 14.0 %copy.118 = bf16[9,16,32,2,256]{4,3,2,1,0:T(2,128)(2,1)} copy(bf16[9,16,32,2,256]{4,2,0,3,1:T(8,128)(2,1)} %bitcast.289) | data formatting | bytes 9437184 | tf_op jit(solution)/shard_map/transpose | solution.py:562
  142.1 8.6 reshape.543.w_ref
  150.7 4.6 slice_bitcast_fusion
  155.3 3.1 copy.120
  158.3 3.7 copy.114
  162.0 4.0 fusion.69
  166.1 5.9 fusion.3
  172.0 2.0 concatenate.83
  174.6 8.9 small_sum.5
  187.5 5.0 multiply_convert_fusion.3
  192.5 2.8 copy.119.x_ref
  195.5 2.5 copy-done.1
  198.1 9.3 %middle_fwd.1 = bf16[1600,512]{1,0:T(8,128)(2,1)S(1)} custom-call(bf16[1600,512]{1,0:T(8,128)(2,1)S(1)} %copy.119.x_ref, bf16[9,512,512]{2,1,0:T(8,128)(2,1)S(1)} %copy-done.1, f32[1600,128]{1,0:T(8,128)S(1)} %broadcast_in_dim.16.col_ref), custom_call_target="tpu_custom_call" | custom-call | flops 7549747200 | bytes 16777216 | tf_op jit(solution)/shard_map/middle_fwd/pallas_call | solution.py:242
  208.6 6.8 fusion.127
  215.3 14.1 %copy.123 = f32[1600,2048]{0,1:T(8,128)} copy(f32[1600,2048]{1,0:T(8,128)} %fusion.127) | data formatting | bytes 26214400 | tf_op jit(solution)/shard_map/dot_general | solution.py:165
  229.4 7.2 multiply_reduce_fusion
  237.2 13.1 %small_sum.6 = f32[32,128]{1,0:T(8,128)} custom-call(f32[32,128]{1,0:T(8,128)} %pad_maximum_fusion.4.x_ref), custom_call_target="tpu_custom_call" | custom-call | tf_op jit(solution)/shard_map/small_sum/pallas_call | solution.py:112
  253.0 13.2 %multiply_reduce_fusion.1 = (f32[2048]{0:T(1024)S(1)}, bf16[1600,2048]{0,1:T(8,128)(2,1)}) fusion(f32[1600]{0:T(1024)S(1)} %get-tuple-element.93, f32[2048]{0:T(1024)S(1)} %bitcast.323, f32[2048]{0:T(1024)S(1)} %fusion.106, f32[1600,2048]{0,1:T(8,128)} %copy.123, f32[2048]{0:T(1024)S(1)} %divide_bitcast_fusion, f32[2048]{0:T(1024)S(1)} %bitcast.320, ...), kind=kLoop, calls=%fused_computation.8 | loop fusion | flops 36042752 | bytes 32815360 | tf_op jit(solution)/shard_map/reduce_sum | solution.py:639
  266.9 10.3 %copy.124.x_ref = bf16[1600,2048]{1,0:T(8,128)(2,1)} copy(bf16[1600,2048]{0,1:T(8,128)(2,1)} %get-tuple-element.124) | data formatting | bytes 13107200 | tf_op jit(solution)/shard_map/convert_element_type | solution.py:637
  277.2 27.3 %pyramid_fwd.1 = f32[4,1600,128]{2,1,0:T(8,128)} custom-call(bf16[1600,2048]{1,0:T(8,128)(2,1)} %copy.124.x_ref, bf16[29,2048,128]{2,1,0:T(8,128)(2,1)} %all-gather.4.cloned.1.call-done.w_hbm, f32[1600,128]{1,0:T(8,128)} %copy-done.4), custom_call_target="tpu_custom_call" | custom-call | flops 14260633600 | bytes 26214400 | tf_op jit(solution)/shard_map/pyramid_fwd/pallas_call | solution.py:347
  317.2 17.6 %collective-permute-done.1 = bf16[1600,256]{1,0:T(8,128)(2,1)} collective-permute-done((bf16[1600,256]{1,0:T(8,128)(2,1)S(1)}, bf16[1600,256]{1,0:T(8,128)(2,1)}, u32[]{:S(2)}, u32[]{:S(2)}) %collective-permute-start.1) | collective-permute-done | bytes 819232 | tf_op jit(solution)/shard_map/ppermute | solution.py:135
  339.2 2.6 fusion.28
  344.6 2.5 fusion.79
  348.4 17.9 %pyramid_field.2 = bf16[1600,1024]{1,0:T(8,128)(2,1)} custom-call(s32[1]{0:T(128)S(6)} %sub.149.half_ref, bf16[29,2048,128]{2,1,0:T(8,128)(2,1)} %all-gather.4.cloned.1.call-done.w_hbm, bf16[4,1600,128]{2,1,0:T(8,128)(2,1)} %pad_maximum_fusion.1.g_ref, f32[1600,128]{1,0:T(8,128)} %copy-done.4), custom_call_target="tpu_custom_call" | custom-call | flops 7130316800 | bytes 15728640 | tf_op jit(solution)/shard_map/pyramid_field/pallas_call | solution.py:460
  366.7 17.4 %fusion.1.xt_ref = bf16[2048,1600]{1,0:T(8,128)(2,1)} fusion(f32[2048,1600]{1,0:T(8,128)} %copy-done.8, f32[1600,2048]{0,1:T(8,128)} %copy.123, f32[2048]{0:T(1024)S(1)} %bitcast.324, f32[2048]{0:T(1024)S(1)} %fusion.106, f32[2048]{0:T(1024)S(1)} %divide_bitcast_fusion, f32[2048]{0:T(1024)S(1)} %bitcast.322, f32[1600]{0:T(1024)S(1)} %get-tuple-element.93), kind=kLoop, calls=%fused_computation.4 | loop fusion | flops 26214400 | bytes 32807168 | tf_op jit(solution)/shard_map/convert_element_type | solution.py:637
  391.5 38.1 %pyramid_weights.1 = bf16[29,2048,128]{2,1,0:T(8,128)(2,1)} custom-call(bf16[2048,1600]{1,0:T(8,128)(2,1)} %fusion.1.xt_ref, bf16[4,1600,128]{2,1,0:T(8,128)(2,1)} %pad_maximum_fusion.1.g_ref, f32[1600,128]{1,0:T(8,128)} %copy-done.4, f32[2048,1]{1,0:T(8,128)} %copy.127.pool_ref, f32[1,128]{1,0:T(1,128)} %bitcast_convert_fusion.3.pool_grad_ref), custom_call_target="tpu_custom_call" | custom-call | flops 15099494400 | bytes 26214400 | tf_op jit(solution)/shard_map/pyramid_weights/pallas_call | solution.py:412
  430.3 17.8 %pyramid_field.3 = bf16[1600,1024]{1,0:T(8,128)(2,1)} custom-call(s32[1]{0:T(128)} %bitcast.half_ref, bf16[29,2048,128]{2,1,0:T(8,128)(2,1)} %all-gather.4.cloned.1.call-done.w_hbm, bf16[4,1600,128]{2,1,0:T(8,128)(2,1)} %pad_maximum_fusion.1.g_ref, f32[1600,128]{1,0:T(8,128)} %copy-done.4), custom_call_target="tpu_custom_call" | custom-call | flops 7130316800 | bytes 15728640 | tf_op jit(solution)/shard_map/pyramid_field/pallas_call | solution.py:460
  448.3 6.1 multiply_reduce_fusion.3
  454.4 2.0 concatenate.91
  457.1 10.7 %small_sum.7 = f32[24,128]{1,0:T(8,128)} custom-call(f32[24,128]{1,0:T(8,128)} %pad_bitcast_fusion.x_ref), custom_call_target="tpu_custom_call" | custom-call | tf_op jit(solution)/shard_map/small_sum/pallas_call | solution.py:112
  468.5 7.9 multiply_convert_fusion.1
  476.4 3.1 convolution_convert_fusion
  479.9 2.7 fusion.18.xt_ref
  484.4 2.1 convolution_convert_fusion.3
  489.8 2.7 convolution_convert_fusion.5
  492.5 2.0 copy.132
  494.4 6.6 reshape.559
  501.1 27.9 %collective-permute-done.5 = bf16[1024,256]{1,0:T(8,128)(2,1)} collective-permute-done((bf16[1024,256]{1,0:T(8,128)(2,1)}, bf16[1024,256]{1,0:T(8,128)(2,1)}, u32[]{:S(2)}, u32[]{:S(2)}) %collective-permute-start.5) | collective-permute-done | bytes 524320 | tf_op jit(solution)/shard_map/ppermute | solution.py:135
  529.0 2.5 maximum_select_fusion
  531.5 2.4 add_convert_fusion.x_ref
  533.9 2.3 copy-done.2
  536.2 9.4 %middle_back.1 = f32[1600,512]{1,0:T(8,128)S(1)} custom-call(bf16[1600,512]{1,0:T(8,128)(2,1)S(1)} %add_convert_fusion.x_ref, bf16[9,512,512]{2,1,0:T(8,128)(2,1)S(1)} %copy-done.2, f32[1600,128]{1,0:T(8,128)S(1)} %copy-done.5), custom_call_target="tpu_custom_call" | custom-call | flops 7549747200 | bytes 16777216 | tf_op jit(solution)/shard_map/middle_back/pallas_call | solution.py:242
  545.7 4.2 middle_weights.1
  550.2 4.6 copy.128
  554.8 6.6 multiply_reduce_fusion.5
  562.0 9.2 %small_sum.8 = f32[8,128]{1,0:T(8,128)} custom-call(f32[8,128]{1,0:T(8,128)} %pad_maximum_fusion.7.x_ref), custom_call_target="tpu_custom_call" | custom-call | tf_op jit(solution)/shard_map/small_sum/pallas_call | solution.py:112
  572.0 6.9 multiply_convert_fusion.2
  578.8 8.6 convolution_convert_fusion.1
  587.4 8.0 fusion.32
  601.2 5.7 pad_maximum_fusion
  615.4 70.2 %reduce-scatter.3.cloned.1.call-done = bf16[1,640,256]{2,1,0:T(8,128)(2,1)} async-done(((bf16[16,640,256]{2,1,0:T(8,128)(2,1)}), bf16[1,640,256]{2,1,0:T(8,128)(2,1)}) %reduce-scatter.3.cloned.1.call-update) | async-done | bytes 327696 | tf_op jit(solution)/shard_map/reduce_scatter | solution.py:804
  692.5 149.3 %reduce-scatter.5.cloned.1.call-done = bf16[29,128,128]{2,1,0:T(8,128)(2,1)} async-done(((bf16[29,2048,128]{2,1,0:T(8,128)(2,1)}), bf16[29,128,128]{2,1,0:T(8,128)(2,1)}) %reduce-scatter.5.cloned.1.call-update) | async-done | bytes 950288 | tf_op jit(solution)/shard_map/reduce_scatter | solution.py:715
  841.8 2.3 fusion.20
  846.0 10.4 %small_sum.9 = f32[8,128]{1,0:T(8,128)} custom-call(f32[8,128]{1,0:T(8,128)} %pad_bitcast_fusion.2.x_ref), custom_call_target="tpu_custom_call" | custom-call | tf_op jit(solution)/shard_map/small_sum/pallas_call | solution.py:112
  876.9 2.2 multiply_subtract_fusion.2
  879.1 2.3 multiply_subtract_fusion.1
  881.4 3.8 multiply_subtract_fusion
  (237 shorter events, 102.5 us)
Async XLA Ops:
  7.2 154.8 %copy-start = (bf16[1,1600,192]{1,2,0:T(8,128)(2,1)S(1)}, bf16[1,1600,192]{1,2,0:T(8,128)(2,1)}, u32[]{:S(2)}) copy-start(bf16[1,1600,192]{1,2,0:T(8,128)(2,1)} %param.31) | copy-start | bytes 1843204
  7.2 6.0 copy-start.16
  7.2 7.2 copy-start.32
  7.2 10.2 %copy-start.37 = (s32[1,1600]{1,0:T(1,128)S(1)}, s32[1,1600]{1,0:T(1,128)}, u32[]{:S(2)}) copy-start(s32[1,1600]{1,0:T(1,128)} %param.34) | copy-start | bytes 19204
  7.3 10.2 %copy-start.34 = (s32[1,1600]{1,0:T(1,128)S(1)}, s32[1,1600]{1,0:T(1,128)}, u32[]{:S(2)}) copy-start(s32[1,1600]{1,0:T(1,128)} %param.36) | copy-start | bytes 19204
  7.3 10.3 %copy-start.33 = (s32[1,1600]{1,0:T(1,128)S(1)}, s32[1,1600]{1,0:T(1,128)}, u32[]{:S(2)}) copy-start(s32[1,1600]{1,0:T(1,128)} %param.37) | copy-start | bytes 19204
  7.3 95.6 %all-gather.6.cloned.1.call-start = ((), (), s32[]{:S(2)}) async-start(), calls=%async_computation.5 | async-start | bytes 10813440 | tf_op jit(solution)/shard_map/all_gather | solution.py:554
  13.2 264.0 %all-gather.4.cloned.1.call-start = ((), (), s32[]{:S(2)}) async-start(), calls=%async_computation.2 | async-start | bytes 16154624 | tf_op jit(solution)/shard_map/all_gather | solution.py:555
  14.4 671.2 %reduce-scatter.3.cloned.1.call-start = ((), (), s32[]{:S(2)}) async-start(), calls=%async_computation.3 | async-start | bytes 5570560 | tf_op jit(solution)/shard_map/reduce_scatter | solution.py:804
  14.4 4.7 collective-permute-start
  117.7 0.9 copy-start.26
  162.0 4.1 copy-start.11
  166.1 5.9 copy-start.8
  195.5 2.5 copy-start.1
  198.1 9.3 %copy-start.4 = (f32[1600,128]{1,0:T(8,128)}, f32[1600,128]{1,0:T(8,128)S(1)}, u32[]{:S(2)}) copy-start(f32[1600,128]{1,0:T(8,128)S(1)} %broadcast_in_dim.16.col_ref) | copy-start | bytes 2457604
  198.1 10.5 %copy-start.13 = (bf16[16,128,2,256]{1,0,3,2:T(8,128)(2,1)S(1)}, bf16[16,128,2,256]{1,0,3,2:T(8,128)(2,1)}, u32[]{:S(2)}) copy-start(bf16[16,128,2,256]{1,0,3,2:T(8,128)(2,1)} %copy.120) | copy-start | bytes 6291460
  207.4 1.2 copy-start.6
  304.5 8.6 copy-start.27
  311.6 2.7 copy-start.39
  311.6 2.8 copy-start.38
  311.6 2.8 copy-start.35
  311.8 1.3 copy-start.29
  314.0 25.2 %copy-start.36 = (f32[1,2,1600]{2,1,0:T(2,128)S(1)}, f32[1,2,1600]{2,1,0:T(2,128)}, u32[]{:S(2)}) copy-start(f32[1,2,1600]{2,1,0:T(2,128)} %param.33) | copy-start | bytes 38404
  314.0 20.8 %collective-permute-start.1 = (bf16[1600,256]{1,0:T(8,128)(2,1)S(1)}, bf16[1600,256]{1,0:T(8,128)(2,1)}, u32[]{:S(2)}, u32[]{:S(2)}) collective-permute-start(bf16[1600,256]{1,0:T(8,128)(2,1)S(1)} %convolution_convert_fusion.2), channel_id=1, source_target_pairs={{0,1},{1,0},{2,3},{3,2},{4,5},{5,4},{6,7},{7,6},{8,9},{9,8},{10,11... | collective-permute-start | bytes 2457608 | tf_op jit(solution)/shard_map/ppermute | solution.py:135
  341.8 0.9 copy-start.21
  342.7 1.9 copy-start.10
  366.4 17.7 %copy-start.14 = (bf16[16,128,2,256]{1,0,3,2:T(8,128)(2,1)S(1)}, bf16[16,128,2,256]{1,0,3,2:T(8,128)(2,1)}, u32[]{:S(2)}) copy-start(bf16[16,128,2,256]{1,0,3,2:T(8,128)(2,1)} %copy.120) | copy-start | bytes 6291460
  366.4 81.9 %collective-permute-start.2 = (bf16[1600,1024]{1,0:T(8,128)(2,1)}, bf16[1600,1024]{1,0:T(8,128)(2,1)}, u32[]{:S(2)}, u32[]{:S(2)}) collective-permute-start(bf16[1600,1024]{1,0:T(8,128)(2,1)} %pyramid_field.2), channel_id=1, source_target_pairs={{0,1},{1,0},{2,3},{3,2},{4,5},{5,4},{6,7},{7,6},{8,9},{9,8},{10,11... | collective-permute-start | bytes 9830408 | tf_op jit(solution)/shard_map/ppermute | solution.py:135
  389.3 59.0 %collective-permute-start.3 = (f32[1,1024]{1,0:T(1,128)S(1)}, f32[1,1024]{1,0:T(1,128)S(1)}, u32[]{:S(2)}, u32[]{:S(2)}) collective-permute-start(f32[1,1024]{1,0:T(1,128)S(1)} %bitcast.347), channel_id=1, source_target_pairs={{0,1},{1,0},{2,3},{3,2},{4,5},{5,4},{6,7},{7,6},{8,9},{9,8},{10,11... | collective-permute-start | bytes 12296 | tf_op jit(solution)/shard_map/ppermute | solution.py:135
  468.5 7.9 copy-start.22
  476.4 3.5 copy-start.9
  479.5 3.0 copy-start.12
  479.5 4.9 copy-start.7
  479.5 52.0 %collective-permute-start.4 = (bf16[1600,512]{1,0:T(8,128)(2,1)}, bf16[1600,512]{1,0:T(8,128)(2,1)}, u32[]{:S(2)}, u32[]{:S(2)}) collective-permute-start(bf16[1600,512]{1,0:T(8,128)(2,1)} %convolution_convert_fusion), channel_id=1, source_target_pairs={{0,1},{1,0},{2,3},{3,2},{4,5},{5,4},{6,7},{7,6},{8,9},{9,8},{10,11... | collective-permute-start | bytes 4915208 | tf_op jit(solution)/shard_map/ppermute | solution.py:135
  487.6 41.4 %collective-permute-start.5 = (bf16[1024,256]{1,0:T(8,128)(2,1)}, bf16[1024,256]{1,0:T(8,128)(2,1)}, u32[]{:S(2)}, u32[]{:S(2)}) collective-permute-start(bf16[1024,256]{1,0:T(8,128)(2,1)} %get-tuple-element.137), channel_id=1, source_target_pairs={{0,1},{1,0},{2,3},{3,2},{4,5},{5,4},{6,7},{7,6},{8,9},{9,8},{10,11... | collective-permute-start | bytes 1572872 | tf_op jit(solution)/shard_map/ppermute | solution.py:135
  492.5 36.6 %copy-start.23 = (bf16[1024,256]{1,0:T(8,128)(2,1)S(1)}, bf16[1024,256]{1,0:T(8,128)(2,1)}, u32[]{:S(2)}) copy-start(bf16[1024,256]{1,0:T(8,128)(2,1)} %get-tuple-element.136) | copy-start | bytes 1572868
  529.0 4.9 copy-start.5
  533.9 2.3 copy-start.2
  545.7 4.3 copy-start.3
  578.8 8.6 copy-start.19
  599.6 1.4 copy-start.15
  599.6 1.6 copy-start.18
  607.0 0.8 copy-start.28
  607.0 1.6 copy-start.30
  607.0 2.3 copy-start.31
  607.0 234.8 %reduce-scatter.5.cloned.1.call-start = ((), (), s32[]{:S(2)}) async-start(), calls=%async_computation.4 | async-start | bytes 16154624 | tf_op jit(solution)/shard_map/reduce_scatter | solution.py:715
  610.8 0.7 copy-start.41
  611.5 0.5 copy-start.40
  859.7 21.7 %copy-start.17 = (f32[29,128,128]{2,1,0:T(8,128)S(1)}, f32[29,128,128]{2,1,0:T(8,128)}, u32[]{:S(2)}) copy-start(f32[29,128,128]{2,1,0:T(8,128)} %param.47) | copy-start | bytes 5701636
  860.4 21.0 %copy-start.20 = (bf16[29,128,128]{2,1,0:T(8,128)(2,1)S(1)}, bf16[29,128,128]{2,1,0:T(8,128)(2,1)}, u32[]{:S(2)}) copy-start(bf16[29,128,128]{2,1,0:T(8,128)(2,1)} %reduce-scatter.5.cloned.1.call-done) | copy-start | bytes 2850820
  871.1 10.2 %copy-start.24 = (f32[29,128,128]{2,1,0:T(8,128)S(1)}, f32[29,128,128]{2,1,0:T(8,128)}, u32[]{:S(2)}) copy-start(f32[29,128,128]{2,1,0:T(8,128)} %param.48) | copy-start | bytes 5701636
  871.2 10.2 %copy-start.25 = (f32[29,128,128]{2,1,0:T(8,128)S(1)}, f32[29,128,128]{2,1,0:T(8,128)}, u32[]{:S(2)}) copy-start(f32[29,128,128]{2,1,0:T(8,128)} %param.49) | copy-start | bytes 5701636
Sparse Core Ops, SparseCore 0:
  13.3 89.5 all-gather.5
  105.7 117.0 all-gather.3
  607.1 78.4 reduce-scatter.2
  689.6 152.1 reduce-scatter.4

commit v3 on v2

--- a/solution.py
+++ b/solution.py
@@ -102,26 +102,32 @@
     lax.fori_loop(1, count, leave, 0)
 
 
+def all_sum(sizes, values, axes, collective):
+    count = 1
+    for axis in axes:
+        count *= sizes[axis]
+    return pl.pallas_call(
+        functools.partial(sum_kernel, sizes, axes, count),
+        out_shape=jax.ShapeDtypeStruct(values.shape, jnp.float32),
+        in_specs=[pl.BlockSpec(memory_space=pltpu.VMEM)],
+        out_specs=pl.BlockSpec(memory_space=pltpu.VMEM),
+        scratch_shapes=[
+            pltpu.VMEM((count,) + values.shape, jnp.float32),
+            pltpu.SemaphoreType.DMA((count,)),
+            pltpu.SemaphoreType.DMA((count,)),
+        ],
+        compiler_params=pltpu.CompilerParams(
+            collective_id=collective, has_side_effects=True, vmem_limit_bytes=32 << 20
+        ),
+        name="small_sum",
+    )(values)
+
+
 def small_sum(sizes, parts, axes, collective):
     flat = jnp.concatenate([part.reshape(-1) for part in parts])
     rows = -(-flat.shape[0] // 1024) * 8
     packed = jnp.pad(flat, (0, rows * 128 - flat.shape[0])).reshape(rows, 128)
-    count = 1
-    for axis in axes:
-        count *= sizes[axis]
-    summed = pl.pallas_call(
-        functools.partial(sum_kernel, sizes, axes, count),
-        out_shape=jax.ShapeDtypeStruct((rows, 128), jnp.float32),
-        in_specs=[pl.BlockSpec(memory_space=pltpu.VMEM)],
-        out_specs=pl.BlockSpec(memory_space=pltpu.VMEM),
-        scratch_shapes=[
-            pltpu.VMEM((count, rows, 128), jnp.float32),
-            pltpu.SemaphoreType.DMA((count,)),
-            pltpu.SemaphoreType.DMA((count,)),
-        ],
-        compiler_params=pltpu.CompilerParams(collective_id=collective, has_side_effects=True),
-        name="small_sum",
-    )(packed).reshape(-1)
+    summed = all_sum(sizes, packed, axes, collective).reshape(-1)
     result = []
     start = 0
     for part in parts:
@@ -168,6 +174,234 @@
         (((contract[0],), (contract[1],)), ((), ())),
         preferred_element_type=jnp.float32,
     )
+
+
+def place_of():
+    dp = lax.axis_index("dp")
+    return lax.div(dp, 4), lax.rem(lax.div(dp, 2), 2), lax.rem(dp, 2), lax.axis_index("chan")
+
+
+def device_at(z, y, core, x):
+    return ((z * 2 + y) * 2 + core, x)
+
+
+def flip(value, turn):
+    return lax.rem(value + turn, 2)
+
+
+def z_flip(z, turn):
+    return flip(lax.div(z, 2), turn // 2) * 2 + flip(lax.rem(z, 2), turn % 2)
+
+
+def greet_neighbours(layers):
+    z, y, core, x = place_of()
+    barrier = pltpu.get_barrier_semaphore()
+    for target in (
+        device_at(z, y, 1 - core, x),
+        device_at(z, 1 - y, core, x),
+        device_at(z, y, core, 1 - x),
+    ):
+        pl.semaphore_signal(barrier, inc=1, device_id=target, device_id_type=MESH_ID)
+
+    @pl.when(z > 0)
+    def _():
+        pl.semaphore_signal(
+            barrier, inc=1, device_id=device_at(z - 1, y, core, x), device_id_type=MESH_ID
+        )
+
+    @pl.when(z < layers - 1)
+    def _():
+        pl.semaphore_signal(
+            barrier, inc=1, device_id=device_at(z + 1, y, core, x), device_id_type=MESH_ID
+        )
+
+    peers = 3 + jnp.where(z > 0, 1, 0) + jnp.where(z < layers - 1, 1, 0)
+    pl.semaphore_wait(barrier, peers)
+
+
+def gather_kernel(
+    layers,
+    bottle,
+    middle,
+    small,
+    bottle_all,
+    middle_all,
+    small_all,
+    send_sems,
+    recv_sems,
+    local_sems,
+):
+    z, y, core, x = place_of()
+    rows = bottle.shape[1]
+    mid_rows = middle.shape[1]
+    own_refs = (bottle, middle, small)
+
+    def region(kind, block):
+        zz, yy, kk, xx = block
+        index = (zz * 2 + yy) * 2 + kk
+        cols = pl.ds(pl.multiple_of(xx * 256, 256), 256)
+        if kind == 0:
+            return bottle_all.at[:, pl.ds(pl.multiple_of(index * rows, 16), rows), cols]
+        if kind == 1:
+            return middle_all.at[:, pl.ds(pl.multiple_of(index * mid_rows, 16), mid_rows), cols]
+        return small_all.at[index, xx]
+
+    def semaphore(kind, block):
+        zz, yy, kk, xx = block
+        return recv_sems.at[kind, ((zz * 2 + yy) * 2 + kk) * 2 + xx]
+
+    own = (z, y, core, x)
+    pending = []
+
+    def send(kind, block, target, when=None):
+        copy = pltpu.make_async_remote_copy(
+            src_ref=own_refs[kind] if block is own else region(kind, block),
+            dst_ref=region(kind, block),
+            send_sem=send_sems.at[len(pending)],
+            recv_sem=semaphore(kind, block),
+            device_id=target,
+            device_id_type=MESH_ID,
+        )
+        if when is None:
+            copy.start()
+        else:
+            pl.when(when)(copy.start)
+        pending.append((when, copy))
+
+    def arrive(kind, block):
+        pltpu.make_async_remote_copy(
+            src_ref=region(kind, block),
+            dst_ref=region(kind, block),
+            send_sem=send_sems.at[0],
+            recv_sem=semaphore(kind, block),
+            device_id=device_at(z, y, 1 - core, x),
+            device_id_type=MESH_ID,
+        ).wait_recv()
+
+    locals_ = [
+        pltpu.make_async_copy(own_refs[kind], region(kind, own), local_sems.at[kind])
+        for kind in range(3)
+    ]
+    for copy in locals_:
+        copy.start()
+    greet_neighbours(layers)
+    sibling = device_at(z, y, 1 - core, x)
+    other_x = device_at(z, y, core, 1 - x)
+    other_y = device_at(z, 1 - y, core, x)
+
+    def along_z(kind, block):
+        if block[0] is z:
+            send(kind, block, device_at(z + 1, y, core, x), z < layers - 1)
+            send(kind, block, device_at(z - 1, y, core, x), z > 0)
+        else:
+            below = block[0] < z
+            ahead = z + jnp.where(below, 1, -1)
+            send(
+                kind,
+                block,
+                device_at(ahead, y, core, x),
+                jnp.logical_and(ahead >= 0, ahead < layers),
+            )
+
+    for kind in (0, 1):
+        along_z(kind, own)
+    send(2, own, other_x)
+    send(2, own, other_y)
+    send(1, own, other_x)
+    send(0, own, other_y)
+    along_z(2, own)
+    send(0, own, other_x)
+    send(1, own, other_y)
+    for kind in range(3):
+        send(kind, own, sibling)
+
+    block = (z, y, core, 1 - x)
+    arrive(2, block)
+    send(2, block, other_y)
+    along_z(2, block)
+    send(2, block, sibling)
+    for xx in (x, 1 - x):
+        block = (z, 1 - y, core, xx)
+        arrive(2, block)
+        along_z(2, block)
+        send(2, block, sibling)
+
+    for turn in range(layers):
+        zz = z if turn == 0 else z_flip(z, turn)
+        if turn:
+            for kind, near, far in ((0, other_y, other_x), (1, other_x, other_y)):
+                block = (zz, y, core, x)
+                arrive(kind, block)
+                along_z(kind, block)
+                send(kind, block, near)
+                send(kind, block, far)
+                send(kind, block, sibling)
+        block = (zz, 1 - y, core, x)
+        arrive(0, block)
+        send(0, block, other_x)
+        send(0, block, sibling)
+        block = (zz, y, core, 1 - x)
+        arrive(1, block)
+        send(1, block, other_y)
+        send(1, block, sibling)
+        if turn:
+            for yy, xx in ((y, x), (y, 1 - x), (1 - y, x), (1 - y, 1 - x)):
+                block = (zz, yy, core, xx)
+                arrive(2, block)
+                along_z(2, block)
+                send(2, block, sibling)
+    for turn in range(layers):
+        zz = z if turn == 0 else z_flip(z, turn)
+        for yy in (y, 1 - y):
+            block = (zz, yy, core, 1 - x)
+            arrive(0, block)
+            send(0, block, sibling)
+        for xx in (x, 1 - x):
+            block = (zz, 1 - y, core, xx)
+            arrive(1, block)
+            send(1, block, sibling)
+    for kind in range(3):
+        for turn in range(layers):
+            zz = z if turn == 0 else z_flip(z, turn)
+            for yy in (y, 1 - y):
+                for xx in (x, 1 - x):
+                    arrive(kind, (zz, yy, 1 - core, xx))
+    for copy in locals_:
+        copy.wait()
+    for when, copy in pending:
+        if when is None:
+            copy.wait_send()
+        else:
+            pl.when(when)(copy.wait_send)
+
+
+def gather_trunk(sizes, bottle, middle, small):
+    count = sizes["dp"]
+    if count != 16 or middle.shape[1] % 16:
+        packed = [
+            lax.all_gather(
+                lax.all_gather(part, "dp", axis=1, tiled=True), "chan", axis=2, tiled=True
+            )
+            for part in (bottle, middle)
+        ]
+        return packed + [lax.all_gather(small, ("dp", "chan")).reshape((count, 2) + small.shape)]
+    return pl.pallas_call(
+        functools.partial(gather_kernel, count // 4),
+        out_shape=[
+            jax.ShapeDtypeStruct((2, D, MID), jnp.bfloat16),
+            jax.ShapeDtypeStruct((9, MID, MID), jnp.bfloat16),
+            jax.ShapeDtypeStruct((count, 2) + small.shape, jnp.bfloat16),
+        ],
+        in_specs=[pl.BlockSpec(memory_space=pl.ANY)] * 3,
+        out_specs=[pl.BlockSpec(memory_space=pl.ANY)] * 3,
+        scratch_shapes=[
+            pltpu.SemaphoreType.DMA((160,)),
+            pltpu.SemaphoreType.DMA((3, 2 * count)),
+            pltpu.SemaphoreType.DMA((3,)),
+        ],
+        compiler_params=pltpu.CompilerParams(collective_id=5, has_side_effects=True),
+        name="gather_trunk",
+    )(bottle, middle, small)
 
 
 PAD = 128
@@ -288,82 +522,6 @@
         ),
         name="middle_weights",
     )(field_t, grads, columns)
-
-
-def pyramid_kernel(x_ref, w_hbm, col_ref, o_ref, weights, fields, sems):
-    width = o_ref.shape[2]
-    copies = []
-    order = [3, 2, 4, 1, 5, 0, 6]
-    starts = []
-    place = 0
-    for group in ROW_GROUPS:
-        starts.append(place)
-        place += len(group)
-    for turn in order:
-        group_copies = []
-        for offset, (tap, _) in enumerate(ROW_GROUPS[turn]):
-            slot = starts[turn] + offset
-            copy = pltpu.make_async_copy(
-                w_hbm.at[tap], weights.at[:, pl.ds(slot * width, width)], sems.at[slot]
-            )
-            copy.start()
-            group_copies.append(copy)
-        copies.append(group_copies)
-    for turn, group_copies in zip(order, copies):
-        for copy in group_copies:
-            copy.wait()
-        row_step = PYRAMID_ROWS[turn]
-        group = ROW_GROUPS[turn]
-        r0, r1 = valid(row_step, FH)
-        count = (r1 - r0) * FW
-        block = {1600: 800, 1120: 560, 640: 640, 160: 160}[count]
-        cols = pl.ds(starts[turn] * width, len(group) * width)
-
-        def step(index, carry):
-            source = pl.multiple_of(index * block + r0 * FW, 16)
-            target = pl.multiple_of(index * block + (r0 - row_step) * FW, 16)
-            part = dot(x_ref[pl.ds(source, block)], weights[:, cols])
-            for offset, (tap, field) in enumerate(group):
-                piece = part[:, offset * width : (offset + 1) * width]
-                rows = pl.ds(target, block)
-                if row_step == 0:
-                    fields[field, rows] = piece
-                else:
-                    fields[field, rows] += piece
-            return carry
-
-        lax.fori_loop(0, count // block, step, 0)
-    o_ref[0] = fields[0]
-    for branch in range(3):
-        total = fields[2 + 3 * branch]
-        for turn in (0, 2):
-            place = 1 + 3 * branch + turn
-            total = total + roll_cols(fields[place], col_ref, FIELDS[place][1])
-        o_ref[1 + branch] = total
-
-
-def pyramid_forward(field, weights, columns):
-    depth, width = weights.shape[1:]
-    return pl.pallas_call(
-        pyramid_kernel,
-        out_shape=jax.ShapeDtypeStruct((4, POSITIONS, width), jnp.float32),
-        in_specs=[
-            pl.BlockSpec(memory_space=pltpu.VMEM),
-            pl.BlockSpec(memory_space=pl.ANY),
-            pl.BlockSpec(memory_space=pltpu.VMEM),
-        ],
-        out_specs=vmem(1)[0],
-        scratch_shapes=[
-            pltpu.VMEM((depth, 28 * width), jnp.bfloat16),
-            pltpu.VMEM((10, POSITIONS, width), jnp.float32),
-            pltpu.SemaphoreType.DMA((28,)),
-        ],
-        compiler_params=pltpu.CompilerParams(vmem_limit_bytes=56 << 20),
-        cost_estimate=pl.CostEstimate(
-            flops=2 * POSITIONS * 17 * depth * width, bytes_accessed=25 << 20, transcendentals=0
-        ),
-        name="pyramid_fwd",
-    )(field, weights, columns)
 
 
 def fill_fields(g_ref, col_ref, fields):
@@ -479,6 +637,399 @@
         ),
         name="pyramid_field",
     )(half, weights, grads, columns)
+
+
+BLOCK = 320
+
+
+def block_rows(index):
+    return pl.ds(pl.multiple_of(index * BLOCK, 16), BLOCK)
+
+
+def gelu_slope(values, upstream):
+    return jax.vjp(jax.nn.gelu, values)[1](upstream)[0]
+
+
+def stem_kernel(p_ref, stem_ref, reduce_ref, crop_ref, count_ref, x_ref, a_ref, stat_ref):
+    def step(index, carry):
+        rows = block_rows(index)
+        low = (crop_ref[rows] * dot(p_ref[rows], stem_ref[...])).astype(x_ref.dtype)
+        x_ref[rows] = low
+        value = dot(low, reduce_ref[0])
+        a_ref[rows] = value
+        return (
+            carry[0] + jnp.sum(value, 0, keepdims=True),
+            carry[1] + jnp.sum(value * value, 0, keepdims=True),
+        )
+
+    zero = jnp.zeros((1, MID), jnp.float32)
+    total, square = lax.fori_loop(0, POSITIONS // BLOCK, step, (zero, zero))
+    stat_ref[...] = jnp.concatenate(
+        [total, square, count_ref[...], jnp.zeros((5, MID), jnp.float32)], 0
+    )
+
+
+def stem_reduce(patches, stem, bottle, crop, counts):
+    return pl.pallas_call(
+        stem_kernel,
+        grid=(1,),
+        out_shape=[
+            jax.ShapeDtypeStruct((POSITIONS, D), jnp.bfloat16),
+            jax.ShapeDtypeStruct((POSITIONS, MID), jnp.float32),
+            jax.ShapeDtypeStruct((8, MID), jnp.float32),
+        ],
+        in_specs=[
+            pl.BlockSpec((POSITIONS, PATCH), lambda i: (0, 0)),
+            pl.BlockSpec((PATCH, D), lambda i: (0, 0)),
+            pl.BlockSpec((1, D, MID), lambda i: (0, 0, 0)),
+            pl.BlockSpec((POSITIONS, 1), lambda i: (0, 0)),
+            pl.BlockSpec((1, MID), lambda i: (0, 0)),
+        ],
+        out_specs=[
+            pl.BlockSpec((POSITIONS, D), lambda i: (0, 0)),
+            pl.BlockSpec((POSITIONS, MID), lambda i: (0, 0)),
+            pl.BlockSpec((8, MID), lambda i: (0, 0)),
+        ],
+        compiler_params=pltpu.CompilerParams(vmem_limit_bytes=50 << 20),
+        cost_estimate=pl.CostEstimate(flops=5 * 10**9, bytes_accessed=14 << 20, transcendentals=0),
+        name="stem_reduce",
+    )(patches, stem, bottle, crop, counts)
+
+
+def norm_rows(stat, count):
+    mean = stat[0:1] / count
+    return mean, lax.rsqrt(stat[1:2] / count - mean * mean + norm_eps)
+
+
+def norm_middle_kernel(
+    a_ref, stat_ref, gain_ref, crop_ref, w_ref, col_ref, h_ref, ht_ref, o_ref, canvas
+):
+    edge = 4 * FW
+    mean, scale = norm_rows(stat_ref[...], stat_ref[2:3, 0:1])
+    gain = gain_ref[0:1] * scale
+    shift = gain_ref[1:2] - mean * gain
+    low = (crop_ref[...] * jax.nn.gelu(a_ref[...] * gain + shift)).astype(h_ref.dtype)
+    h_ref[...] = low
+    ht_ref[...] = low.T
+    values = low.astype(jnp.float32)
+    for turn in range(3):
+        canvas[turn, :edge] = jnp.zeros((edge, MID), canvas.dtype)
+        canvas[turn, POSITIONS + edge :] = jnp.zeros((edge, MID), canvas.dtype)
+        canvas[turn, edge : POSITIONS + edge] = roll_cols(values, col_ref, 4 * (turn - 1)).astype(
+            canvas.dtype
+        )
+    block = 400
+
+    def step(index, carry):
+        total = None
+        for row in range(3):
+            first = pl.multiple_of(index * block + edge * row, 16)
+            for turn in range(3):
+                part = dot(canvas[turn, pl.ds(first, block)], w_ref[3 * row + turn])
+                total = part if total is None else total + part
+        o_ref[pl.ds(pl.multiple_of(index * block, 16), block)] = total.astype(o_ref.dtype)
+        return carry
+
+    lax.fori_loop(0, POSITIONS // block, step, 0)
+
+
+def norm_middle(first_pre, stat, gains, crop, weights, columns):
+    return pl.pallas_call(
+        norm_middle_kernel,
+        out_shape=[
+            jax.ShapeDtypeStruct((POSITIONS, MID), jnp.bfloat16),
+            jax.ShapeDtypeStruct((MID, POSITIONS), jnp.bfloat16),
+            jax.ShapeDtypeStruct((POSITIONS, MID), jnp.bfloat16),
+        ],
+        in_specs=vmem(6),
+        out_specs=vmem(3),
+        scratch_shapes=[pltpu.VMEM((3, POSITIONS + 8 * FW, MID), jnp.bfloat16)],
+        compiler_params=pltpu.CompilerParams(vmem_limit_bytes=50 << 20),
+        cost_estimate=pl.CostEstimate(flops=8 * 10**9, bytes_accessed=14 << 20, transcendentals=0),
+        name="norm_middle",
+    )(first_pre, stat, gains, crop, weights, columns)
+
+
+def expand_kernel(a_ref, w_ref, crop_ref, y_ref, stat_ref):
+    def step(index, carry):
+        rows = block_rows(index)
+        value = dot(a_ref[rows], w_ref[0], (1, 1))
+        y_ref[rows] = value.astype(y_ref.dtype)
+        kept = crop_ref[rows] * value
+        return (
+            carry[0] + jnp.sum(kept, 0, keepdims=True),
+            carry[1] + jnp.sum(kept * value, 0, keepdims=True),
+        )
+
+    zero = jnp.zeros((1, D), jnp.float32)
+    sums = lax.fori_loop(0, POSITIONS // BLOCK, step, (zero, zero))
+    for turn, values in enumerate(sums):
+        for part in range(4):
+            stat_ref[4 * turn + part : 4 * turn + part + 1] = values[
+                :, part * MID : (part + 1) * MID
+            ]
+
+
+def expand_forward(second, bottle, crop):
+    return pl.pallas_call(
+        expand_kernel,
+        grid=(1,),
+        out_shape=[
+            jax.ShapeDtypeStruct((POSITIONS, D), jnp.bfloat16),
+            jax.ShapeDtypeStruct((8, MID), jnp.float32),
+        ],
+        in_specs=[
+            pl.BlockSpec((POSITIONS, MID), lambda i: (0, 0)),
+            pl.BlockSpec((1, D, MID), lambda i: (1, 0, 0)),
+            pl.BlockSpec((POSITIONS, 1), lambda i: (0, 0)),
+        ],
+        out_specs=[
+            pl.BlockSpec((POSITIONS, D), lambda i: (0, 0)),
+            pl.BlockSpec((8, MID), lambda i: (0, 0)),
+        ],
+        compiler_params=pltpu.CompilerParams(vmem_limit_bytes=50 << 20),
+        cost_estimate=pl.CostEstimate(flops=4 * 10**9, bytes_accessed=12 << 20, transcendentals=0),
+        name="expand_forward",
+    )(second, bottle, crop)
+
+
+def pyramid_kernel(
+    p_ref,
+    stem_ref,
+    y_ref,
+    stat_ref,
+    count_ref,
+    gain_ref,
+    crop_ref,
+    w_hbm,
+    project_ref,
+    col_ref,
+    x_ref,
+    xt_ref,
+    pool_ref,
+    o_ref,
+    pool_pre_ref,
+    cat_ref,
+    part_ref,
+    weights,
+    pool_weights,
+    fields,
+    sems,
+):
+    width = o_ref.shape[2]
+    copies = []
+    order = [3, 2, 4, 1, 5, 0, 6]
+    starts = []
+    place = 0
+    for group in ROW_GROUPS:
+        starts.append(place)
+        place += len(group)
+    for turn in order:
+        group_copies = []
+        for offset, (tap, _) in enumerate(ROW_GROUPS[turn]):
+            slot = starts[turn] + offset
+            copy = pltpu.make_async_copy(
+                w_hbm.at[tap], weights.at[:, pl.ds(slot * width, width)], sems.at[slot]
+            )
+            copy.start()
+            group_copies.append(copy)
+        copies.append(group_copies)
+    pool_copy = pltpu.make_async_copy(w_hbm.at[28], pool_weights, sems.at[28])
+    pool_copy.start()
+
+    count = count_ref[2:3, 0:1]
+    stat = stat_ref[...]
+    total = jnp.concatenate([stat[part : part + 1] for part in range(4)], 1)
+    square = jnp.concatenate([stat[part : part + 1] for part in range(4, 8)], 1)
+    mean = total / count
+    gain = gain_ref[0:1] * lax.rsqrt(square / count - mean * mean + norm_eps)
+    shift = gain_ref[1:2] - mean * gain
+
+    def residual(index, carry):
+        rows = block_rows(index)
+        value = dot(p_ref[rows], stem_ref[...]) + (y_ref[rows].astype(jnp.float32) * gain + shift)
+        low = (crop_ref[rows] * value).astype(x_ref.dtype)
+        x_ref[rows] = low
+        return carry + jnp.sum(low.astype(jnp.float32), 0, keepdims=True)
+
+    pooled = lax.fori_loop(0, POSITIONS // BLOCK, residual, jnp.zeros((1, D), jnp.float32))
+    pooled = (pooled / jnp.sum(crop_ref[...], keepdims=True)).astype(jnp.bfloat16)
+    pool_ref[...] = pooled.astype(jnp.float32)
+    for at in range(0, D, 256):
+        xt_ref[at : at + 256] = x_ref[:, at : at + 256].T
+
+    for turn, group_copies in zip(order, copies):
+        for copy in group_copies:
+            copy.wait()
+        row_step = PYRAMID_ROWS[turn]
+        group = ROW_GROUPS[turn]
+        r0, r1 = valid(row_step, FH)
+        length = (r1 - r0) * FW
+        block = {1600: 800, 1120: 560, 640: 640, 160: 160}[length]
+        cols = pl.ds(starts[turn] * width, len(group) * width)
+
+        def step(index, carry):
+            source = pl.multiple_of(index * block + r0 * FW, 16)
+            target = pl.multiple_of(index * block + (r0 - row_step) * FW, 16)
+            part = dot(x_ref[pl.ds(source, block)], weights[:, cols])
+            for offset, (tap, field) in enumerate(group):
+                piece = part[:, offset * width : (offset + 1) * width]
+                rows = pl.ds(target, block)
+                if row_step == 0:
+                    fields[field, rows] = piece
+                else:
+                    fields[field, rows] += piece
+            return carry
+
+        lax.fori_loop(0, length // block, step, 0)
+    pool_copy.wait()
+    pool_pre = dot(jnp.broadcast_to(pooled, (16, D)), pool_weights[...])[0:1]
+    pool_pre_ref[...] = pool_pre
+    for branch in range(4):
+        values = fields[0] if branch == 0 else fields[3 * branch - 1]
+        if branch:
+            for turn in (0, 2):
+                place = 3 * branch - 2 + turn
+                values = values + roll_cols(fields[place], col_ref, FIELDS[place][1])
+        o_ref[branch] = values
+        cat_ref[:, branch * width : (branch + 1) * width] = jax.nn.gelu(values).astype(
+            cat_ref.dtype
+        )
+    cat_ref[:, 4 * width :] = jnp.broadcast_to(
+        jax.nn.gelu(pool_pre).astype(cat_ref.dtype), (POSITIONS, width)
+    )
+
+    def project(index, carry):
+        rows = block_rows(index)
+        part_ref[rows] = dot(cat_ref[rows], project_ref[...]).astype(part_ref.dtype)
+        return carry
+
+    lax.fori_loop(0, POSITIONS // BLOCK, project, 0)
+
+
+def pyramid_forward(patches, stem, expanded, stat, counts, gains, crop, weights, project, columns):
+    depth, width = weights.shape[1:]
+    low = jnp.bfloat16
+    return pl.pallas_call(
+        pyramid_kernel,
+        out_shape=[
+            jax.ShapeDtypeStruct((POSITIONS, depth), low),
+            jax.ShapeDtypeStruct((depth, POSITIONS), low),
+            jax.ShapeDtypeStruct((1, depth), jnp.float32),
+            jax.ShapeDtypeStruct((4, POSITIONS, width), jnp.float32),
+            jax.ShapeDtypeStruct((1, width), jnp.float32),
+            jax.ShapeDtypeStruct((POSITIONS, 5 * width), low),
+            jax.ShapeDtypeStruct((POSITIONS, BRANCH), low),
+        ],
+        in_specs=vmem(7) + [pl.BlockSpec(memory_space=pl.ANY)] + vmem(2),
+        out_specs=vmem(7),
+        scratch_shapes=[
+            pltpu.VMEM((depth, 28 * width), low),
+            pltpu.VMEM((depth, width), low),
+            pltpu.VMEM((10, POSITIONS, width), jnp.float32),
+            pltpu.SemaphoreType.DMA((29,)),
+        ],
+        compiler_params=pltpu.CompilerParams(vmem_limit_bytes=60 << 20),
+        cost_estimate=pl.CostEstimate(
+            flops=2 * POSITIONS * 19 * depth * width, bytes_accessed=40 << 20, transcendentals=0
+        ),
+        name="pyramid_fwd",
+    )(patches, stem, expanded, stat, counts, gains, crop, weights, project, columns)
+
+
+def head_kernel(
+    own_ref,
+    other_ref,
+    head_ref,
+    row_ref,
+    label_ref,
+    target_ref,
+    mask_ref,
+    project_ref,
+    z_ref,
+    pool_pre_ref,
+    feature_ref,
+    logit_ref,
+    mixed_ref,
+    grad_ref,
+    pool_ref,
+    stat_ref,
+):
+    width = grad_ref.shape[2]
+    bias, scale = row_ref[0:1], row_ref[1:2]
+    class_lane, depth_lane = row_ref[2:3], row_ref[4:5]
+
+    def step(index, carry):
+        rows = block_rows(index)
+        mixed = own_ref[rows].astype(jnp.float32) + other_ref[rows].astype(jnp.float32)
+        feature = jax.nn.gelu(mixed).astype(feature_ref.dtype)
+        feature_ref[rows] = feature
+        logits = dot(feature, head_ref[...]) + bias
+        is_class = class_lane > 0.0
+        top = jnp.max(jnp.where(is_class, logits, -jnp.inf), 1, keepdims=True)
+        powers = jnp.where(is_class, jnp.exp(jnp.where(is_class, logits - top, 0.0)), 0.0)
+        total = jnp.sum(powers, 1, keepdims=True)
+        onehot = label_ref[rows]
+        mask = mask_ref[rows]
+        seg = mask[:, 0:1] * (
+            top + jnp.log(total) - jnp.sum(logits * onehot, 1, keepdims=True)
+        )
+        is_depth = depth_lane > 0.0
+        inverse = jnp.exp(-jnp.abs(logits))
+        soft = jnp.maximum(logits, 0.0) + jnp.log(1.0 + inverse)
+        slope = jnp.where(logits >= 0.0, 1.0, inverse) / (1.0 + inverse)
+        error = jnp.where(is_depth, soft, logits) - target_ref[rows]
+        root = jnp.sqrt(error * error + 1.0)
+        other = error / root * jnp.where(is_depth, slope, 1.0)
+        grad = scale * mask * jnp.where(is_class, powers / total - onehot, other)
+        low = grad.astype(logit_ref.dtype)
+        logit_ref[rows] = low
+        up = gelu_slope(mixed, dot(low, head_ref[...], (1, 1))).astype(mixed_ref.dtype)
+        mixed_ref[rows] = up
+        cat = dot(up, project_ref[...], (1, 1))
+        for branch in range(4):
+            grad_ref[branch, rows] = gelu_slope(
+                z_ref[branch, rows], cat[:, branch * width : (branch + 1) * width]
+            ).astype(grad_ref.dtype)
+        return (
+            carry[0] + jnp.sum(low.astype(jnp.float32), 0, keepdims=True),
+            carry[1] + jnp.sum(mask * (root - 1.0), 0, keepdims=True),
+            carry[2] + jnp.sum(seg, 0, keepdims=True),
+            carry[3] + jnp.sum(cat[:, 4 * width :], 0, keepdims=True),
+        )
+
+    zero = jnp.zeros((1, 128), jnp.float32)
+    bias_sum, error_sum, seg_sum, pool_sum = lax.fori_loop(
+        0,
+        POSITIONS // BLOCK,
+        step,
+        (zero, zero, jnp.zeros((1, 1), jnp.float32), jnp.zeros((1, width), jnp.float32)),
+    )
+    pool_ref[...] = gelu_slope(pool_pre_ref[...], pool_sum).astype(jnp.bfloat16).astype(jnp.float32)
+    stat_ref[...] = jnp.concatenate(
+        [bias_sum, error_sum, jnp.broadcast_to(seg_sum, (1, 128)), jnp.zeros((5, 128))], 0
+    )
+
+
+def head_step(own, other, head, rows, label, target, mask, project, branches, pool_pre):
+    width = branches.shape[2]
+    low = jnp.bfloat16
+    return pl.pallas_call(
+        head_kernel,
+        out_shape=[
+            jax.ShapeDtypeStruct((POSITIONS, BRANCH), low),
+            jax.ShapeDtypeStruct((POSITIONS, 128), low),
+            jax.ShapeDtypeStruct((POSITIONS, BRANCH), low),
+            jax.ShapeDtypeStruct((4, POSITIONS, width), low),
+            jax.ShapeDtypeStruct((1, width), jnp.float32),
+            jax.ShapeDtypeStruct((8, 128), jnp.float32),
+        ],
+        in_specs=vmem(10),
+        out_specs=vmem(6),
+        compiler_params=pltpu.CompilerParams(vmem_limit_bytes=50 << 20),
+        cost_estimate=pl.CostEstimate(flops=2 * 10**9, bytes_accessed=16 << 20, transcendentals=0),
+        name="head_step",
+    )(own, other, head, rows, label, target, mask, project, branches, pool_pre)
 
 
 def adam_step(weight, first, second, gradient, factor, rate, decay):
@@ -544,25 +1095,12 @@
     small_flat = jnp.concatenate([part.astype(low).reshape(-1) for part in small_parts])
     small_rows = -(-small_flat.shape[0] // (16 * 256)) * 16
     small_flat = jnp.pad(small_flat, (0, small_rows * 256 - small_flat.shape[0]))
-    packed = jnp.concatenate(
-        [
-            bottle_weight.astype(low).reshape(2 * row_share, 256),
-            middle_weight.astype(low).reshape(9 * mid_share, 256),
-            small_flat.reshape(small_rows, 256),
-        ]
-    )
-    trunk = lax.all_gather(packed, ("dp", "chan")).reshape(dp_size, 2, packed.shape[0], 256)
+    small_flat = small_flat.reshape(small_rows, 256)
     pyramid_low = lax.all_gather(pyramid_weight.astype(low), "dp", axis=1, tiled=True)
-    reduce_low = trunk[:, :, :row_share].transpose(0, 2, 1, 3).reshape(D, MID)
-    expand_low = trunk[:, :, row_share : 2 * row_share].transpose(0, 2, 1, 3).reshape(D, MID)
-    start = 2 * row_share
-    middle_low = (
-        trunk[:, :, start : start + 9 * mid_share]
-        .reshape(dp_size, 2, 9, mid_share, 256)
-        .transpose(2, 0, 3, 1, 4)
-        .reshape(9, MID, MID)
-    )
-    small = trunk[:, :, start + 9 * mid_share :].reshape(dp_size, 2, small_rows * 256)
+    bottle_low, middle_low, small = gather_trunk(
+        sizes, bottle_weight.astype(low), middle_weight.astype(low), small_flat
+    )
+    small = small.reshape(dp_size, 2, small_rows * 256)
     size = PATCH * stem_share
     stem_low = (
         small[:, :, :size]
@@ -599,118 +1137,108 @@
         width = values.shape[axis] // 2
         return lax.dynamic_slice_in_dim(values, (1 - chan_place) * width, width, axis)
 
-    patch_rows = patches.reshape(POSITIONS, PATCH)
-    stream = crop_field * dot(patch_rows, stem_low)
-    stream_low = stream.astype(low)
-    first_pre = dot(stream_low, reduce_low)
-    sum_one, square_one, counts = small_sum(
-        sizes,
-        [
-            jnp.sum(crop_field * first_pre, 0),
-            jnp.sum(crop_field * first_pre * first_pre, 0),
-            local_counts,
-        ],
-        ("dp",),
-        0,
-    )
-    crop_total = counts[0]
-    mean_one = sum_one / crop_total
-    scale_one = lax.rsqrt(square_one / crop_total - mean_one * mean_one + norm_eps)
-    normed_one = (first_pre - mean_one) * scale_one
-    act_input = gain_one * normed_one + shift_one
-    hidden_low = (crop_field * jax.nn.gelu(act_input)).astype(low)
     columns = jnp.broadcast_to(
         lax.rem(lax.broadcasted_iota(jnp.int32, (POSITIONS, 1), 0), FW).astype(jnp.float32),
         (POSITIONS, 128),
     )
-    second_low = middle_conv(hidden_low, middle_low, columns, False, low)
-    expand_pre = dot(second_low, expand_low, (1, 1))
-    sum_two, square_two = small_sum(
-        sizes,
-        [jnp.sum(crop_field * expand_pre, 0), jnp.sum(crop_field * expand_pre * expand_pre, 0)],
-        ("dp",),
-        1,
-    )
-    mean_two = sum_two / crop_total
-    scale_two = lax.rsqrt(square_two / crop_total - mean_two * mean_two + norm_eps)
-    stream_out = stream + crop_field * (gain_two * ((expand_pre - mean_two) * scale_two) + shift_two)
-    output_low = stream_out.astype(low)
+    lane = lax.broadcasted_iota(jnp.int32, (1, 128), 1)
+    class_lane = (lane < CLASSES).astype(jnp.float32)
+    offset_lane = ((lane >= CLASSES) & (lane < CLASSES + 2)).astype(jnp.float32)
+    depth_lane = (lane == CLASSES + 2).astype(jnp.float32)
+    onehot = (labels.reshape(POSITIONS, 1) == lane).astype(jnp.float32)
+    mask = (
+        class_lane * crop_field
+        + offset_lane * offset_field[:, None]
+        + depth_lane * lidar_field[:, None]
+    )
+    target = jnp.pad(
+        jnp.concatenate([offset_target[0], depth_target], 0).T,
+        ((0, 0), (CLASSES, 128 - CLASSES - 3)),
+    )
+    head_wide = jnp.pad(head_low, ((0, 0), (0, 128 - 22)))
+    task_scale = task_params[:3]
+
+    patch_rows = patches.reshape(POSITIONS, PATCH)
+    stream_low, first_pre, stat_one = stem_reduce(
+        patch_rows,
+        stem_low,
+        bottle_low,
+        crop_field,
+        jnp.pad(local_counts, (0, MID - 3)).reshape(1, MID),
+    )
+    stat_one = all_sum(sizes, stat_one, ("dp",), 0)
+    hidden_low, hidden_t, second_low = norm_middle(
+        first_pre, stat_one, jnp.stack([gain_one, shift_one]), crop_field, middle_low, columns
+    )
+    expand_pre, stat_two = expand_forward(second_low, bottle_low, crop_field)
+    stat_two = all_sum(sizes, stat_two, ("dp",), 1)
+    output_low, output_t, pooled, branch_pre, pool_pre, concat_low, project_part = pyramid_forward(
+        patch_rows,
+        stem_low,
+        expand_pre,
+        stat_two,
+        stat_one,
+        jnp.stack([gain_two, shift_two]),
+        crop_field,
+        pyramid_low,
+        project_low,
+        columns,
+    )
+    counts = stat_one[2, :3]
+    crop_total = counts[0]
+    mean_one = stat_one[0] / crop_total
+    scale_one = lax.rsqrt(stat_one[1] / crop_total - mean_one * mean_one + norm_eps)
+    mean_two = stat_two[:4].reshape(D) / crop_total
+    scale_two = lax.rsqrt(stat_two[4:].reshape(D) / crop_total - mean_two * mean_two + norm_eps)
     image_count = jnp.sum(crop_field)
-    pooled = jnp.sum(crop_field * output_low.astype(jnp.float32), 0, keepdims=True) / image_count
-    pooled_low = pooled.astype(low)
-
-    width = BRANCH // 2
-    branch_pre = pyramid_forward(output_low, pyramid_low, columns)
-    pool_pre = dot(pooled_low, pyramid_low[28])
-    branch_acts = [jax.nn.gelu(branch_pre[order]) for order in range(4)]
-    branch_acts.append(jnp.broadcast_to(jax.nn.gelu(pool_pre), (POSITIONS, width)))
-    concat_low = jnp.concatenate(branch_acts, 1).astype(low)
-    project_part = dot(concat_low, project_low).astype(low)
-    project_pre = project_part.astype(jnp.float32) + swap_chan(project_part).astype(jnp.float32)
-    feature_low = jax.nn.gelu(project_pre).astype(low)
-    task_scale = task_params[:3]
-    logits = dot(feature_low, head_low) + task_params[3:]
-    class_logits = logits[:, :CLASSES]
-    class_top = jnp.max(class_logits, 1, keepdims=True)
-    class_exp = jnp.exp(class_logits - class_top)
-    class_total = jnp.sum(class_exp, 1, keepdims=True)
-    onehot = (
-        labels.reshape(POSITIONS, 1) == lax.broadcasted_iota(jnp.int32, (1, CLASSES), 1)
-    ).astype(jnp.float32)
-    seg_terms = crop_field[:, 0] * (
-        class_top[:, 0] + jnp.log(class_total[:, 0]) - jnp.sum(class_logits * onehot, 1)
-    )
-    offset_err = logits[:, CLASSES : CLASSES + 2] - jnp.swapaxes(offset_target, 1, 2).reshape(
-        POSITIONS, 2
-    )
-    offset_root = jnp.sqrt(offset_err * offset_err + 1.0)
-    depth_pre = logits[:, CLASSES + 2]
-    depth_err = jax.nn.softplus(depth_pre) - depth_target.reshape(POSITIONS)
-    depth_root = jnp.sqrt(depth_err * depth_err + 1.0)
+    task_weights = jnp.exp(-task_scale) / counts
+    lane_rows = jnp.concatenate(
+        [
+            jnp.pad(task_params[3:], (0, 128 - 22)).reshape(1, 128),
+            task_weights[0] * class_lane
+            + task_weights[1] * offset_lane
+            + task_weights[2] * depth_lane,
+            class_lane,
+            offset_lane,
+            depth_lane,
+            jnp.zeros((3, 128), jnp.float32),
+        ],
+        0,
+    )
+    feature_low, logit_low, project_grad_low, branch_grads, pool_grad, head_stat = head_step(
+        project_part,
+        swap_chan(project_part),
+        head_wide,
+        lane_rows,
+        onehot,
+        target,
+        mask,
+        project_low,
+        branch_pre,
+        pool_pre,
+    )
+    local_bias = head_stat[0, :22]
     local_sums = jnp.stack(
         [
-            jnp.sum(seg_terms),
-            jnp.sum(offset_field * jnp.sum(offset_root - 1.0, 1)),
-            jnp.sum(lidar_field * (depth_root - 1.0)),
+            head_stat[2, 0],
+            head_stat[1, CLASSES] + head_stat[1, CLASSES + 1],
+            head_stat[1, CLASSES + 2],
         ]
     )
-    task_weights = jnp.exp(-task_scale) / counts
-    logit_grad = jnp.concatenate(
-        [
-            task_weights[0] * crop_field * (class_exp / class_total - onehot),
-            task_weights[1] * offset_field[:, None] * offset_err / offset_root,
-            (task_weights[2] * lidar_field * depth_err / depth_root * jax.nn.sigmoid(depth_pre))[
-                :, None
-            ],
-        ],
-        axis=1,
-    )
-    logit_low = logit_grad.astype(low)
-    local_bias = jnp.sum(logit_low.astype(jnp.float32), 0)
-    head_grad = dot(feature_low, logit_low, (0, 0))
-    feature_grad = dot(logit_low, head_low, (1, 1))
-    project_grad_low = gelu_grad(project_pre, feature_grad).astype(low)
+    head_grad = dot(feature_low, logit_low, (0, 0))[:, :22]
     project_grad = dot(concat_low, project_grad_low, (0, 0))
-    concat_grad = dot(project_grad_low, project_low, (1, 1))
-    branch_grads = jnp.stack(
-        [
-            gelu_grad(branch_pre[order], concat_grad[:, order * width : (order + 1) * width])
-            for order in range(4)
-        ]
-    ).astype(low)
-    pool_grad_low = gelu_grad(
-        pool_pre, jnp.sum(concat_grad[:, 4 * width :], 0, keepdims=True)
-    ).astype(low)
+    pool_grad_low = pool_grad.astype(low)
+
     own_place = chan_place.reshape(1)
     other_part = pyramid_field(1 - own_place, pyramid_low, branch_grads, columns)
     other_sent = swap_chan(other_part)
     later_grads, other_part = lax.optimization_barrier((branch_grads, other_part))
     pyramid_grad = pyramid_weights(
-        output_low.T,
+        output_t,
         later_grads,
         columns,
-        pooled_low.astype(jnp.float32).reshape(D, 1),
-        pool_grad_low.astype(jnp.float32),
+        pooled.reshape(D, 1),
+        pool_grad,
     )
     pyramid_red = lax.psum_scatter(pyramid_grad, "dp", scatter_dimension=1, tiled=True)
     later_grads, pyramid_grad = lax.optimization_barrier((later_grads, pyramid_grad))
@@ -723,7 +1251,7 @@
 
     own_gain_two = own_half(gain_two, 0)
     own_scale_two = own_half(scale_two, 0)
-    normed_two = (own_half(expand_pre, 1) - own_half(mean_two, 0)) * own_scale_two
+    normed_two = (own_half(expand_pre, 1).astype(jnp.float32) - own_half(mean_two, 0)) * own_scale_two
     upstream_two = crop_field * stream_grad
     gain_two_grad, shift_two_grad, loss_sums, bias_grad = small_sum(
         sizes,
@@ -740,7 +1268,7 @@
         * own_scale_two
         * (upstream_two - (shift_two_grad + normed_two * gain_two_grad) / crop_total)
     ).astype(low)
-    second_part = dot(expand_grad_low, own_half(expand_low, 0)).astype(low)
+    second_part = dot(expand_grad_low, own_half(bottle_low[1], 0)).astype(low)
     second_other = swap_chan(second_part)
     expand_rows = dot(expand_grad_low, second_low, (0, 0)).astype(low)
     expand_sent = swap_chan(other_half(expand_rows, 1))
@@ -748,6 +1276,8 @@
         second_part.astype(jnp.float32) + second_other.astype(jnp.float32)
     ).astype(low)
     hidden_grad = middle_conv(second_grad_low, middle_low, columns, True, jnp.float32)
+    normed_one = (first_pre - mean_one) * scale_one
+    act_input = gain_one * normed_one + shift_one
     upstream_one = gelu_grad(act_input, crop_field * hidden_grad)
     gain_one_all, shift_one_all = small_sum(
         sizes,
@@ -763,9 +1293,9 @@
         * scale_one
         * (upstream_one - (shift_one_all + normed_one * gain_one_all) / crop_total)
     ).astype(low)
-    middle_grad = middle_weights(hidden_low.T, own_half(second_grad_low, 1), columns)
+    middle_grad = middle_weights(hidden_t, own_half(second_grad_low, 1), columns)
     reduce_grad = dot(stream_low, own_half(first_grad_low, 1), (0, 0)).astype(low)
-    start_grad = dot(first_grad_low, own_half(reduce_low, 0), (1, 1)) + stream_grad
+    start_grad = dot(first_grad_low, own_half(bottle_low[0], 0), (1, 1)) + stream_grad
     start_grad_low = (crop_field * start_grad).astype(low)
     stem_grad = dot(patch_rows, start_grad_low, (0, 0)).astype(low)
     expand_own = own_half(expand_rows, 1)
@@ -800,11 +1330,13 @@
         ],
         1,
     )
+    packed_grads, pyramid_red = lax.optimization_barrier((packed_grads, pyramid_red))
     trunk_red = (
         lax.psum_scatter(packed_grads, "dp", scatter_dimension=0, tiled=True)
-        .reshape(packed.shape)
+        .reshape(packed_grads.shape[1:])
         .astype(jnp.float32)
     )
+    start = 2 * row_share
     bottle_red = trunk_red[: 2 * row_share].reshape(bottle_weight.shape)
     middle_red = trunk_red[start : start + 9 * mid_share].reshape(middle_weight.shape)
     small_red = trunk_red[start + 9 * mid_share :].reshape(-1)

time: 903 us -> 706 us (0.78)
  waiting for transfers between devices: 350 us -> 160 us
  Pallas kernels: 176 us -> 341 us
  local copies, waits for them, and re-layouts: 145 us -> 67.5 us
  other arithmetic: 144 us -> 73.8 us
  matrix products: 48.4 us -> 21.4 us
    pallas_call x6 -> x11, Pallas kernels: 79.6 us -> 253 us  [the longest x1 118 us: gather_trunk(): pl.pallas_call(functools.partial(gather_kernel, count // 4), out_shape=[j...]
    reduce_scatter x1, waiting for transfers between devices: 149 us -> 0.01 us  [on_device(): lax.psum_scatter(pyramid_grad, 'dp', scatter_dimension=1, tiled=True)]
    all_gather x1 -> x0, waiting for transfers between devices: 83.7 us -> none  [on_device(): lax.all_gather(packed, ('dp', 'chan'))]
    ppermute x6, waiting for transfers between devices: 45.9 us -> 89.4 us  [swap_chan(): return lax.ppermute(values, 'chan', [(0, 1), (1, 0)])]
    dot_general x15 -> x7, matrix products: 48.4 us -> 21.4 us  [dot(): lax.dot_general(left, right, (((contract[0],), (contract[1],)), ((), ()))...]
    convert_element_type x9 -> x7, other arithmetic: 30 us -> 4.58 us  [the longest x1 1.17 us: on_device(): onehot = (labels.reshape(POSITIONS, 1) == lane).astype(jnp.float32)]
    transpose x4 -> x0, local copies, waits for them, and re-layouts: 25.3 us -> none  [the longest x1 14 us: on_device(): middle_low = trunk[:, :, start:start + 9 * mid_share].reshape(dp_size, 2,...]
    reduce_sum x8 -> x1, other arithmetic: 23.1 us -> 1.21 us  [on_device(): jnp.sum(offset_field)]
  transfers between devices with their start and end apart: 10 -> 9, of which waited for: 6 -> 4; matrix products, arithmetic and copies ran while one was open for 22% -> 19% of each run, Pallas kernels for 10% -> 33%
where the time goes in v3:
time: 706 us; the launch traced here: 696 us
  Pallas kernels  341 us (48%)
  waiting for transfers between devices  160 us (23%)
  other arithmetic  73.8 us (10%)
  local copies, waits for them, and re-layouts  67.5 us (10%)
  between operations  23.8 us (3%)
  matrix products  21.4 us (3%)
  starting transfers between devices  7.71 us (1%)
    pallas_call x1, Pallas kernels, gather_trunk(): pl.pallas_call(functools.partial(gather_kernel, count // 4), out_shape=[j...  118 us
    ppermute x6, waiting for transfers between devices, swap_chan(): return lax.ppermute(values, 'chan', [(0, 1), (1, 0)])  89.4 us
    reduce_scatter x1, waiting for transfers between devices, on_device(): lax.psum_scatter(packed_grads, 'dp', scatter_dimension=0, tiled=True)  71 us
    pallas_call x5, Pallas kernels, all_sum(): pl.pallas_call(functools.partial(sum_kernel, sizes, axes, count), out_sha...  49.6 us
    pallas_call x1, Pallas kernels, pyramid_forward(): pl.pallas_call(pyramid_kernel, out_shape=[jax.ShapeDtypeStruct((POSITIONS...  40 us
    pallas_call x1, Pallas kernels, pyramid_weights(): pl.pallas_call(weight_kernel, out_shape=jax.ShapeDtypeStruct((29, depth,...  38 us
    pallas_call x2, Pallas kernels, pyramid_field(): pl.pallas_call(field_kernel, out_shape=jax.ShapeDtypeStruct((POSITIONS, d...  37.2 us
    dot_general x7, matrix products, dot(): lax.dot_general(left, right, (((contract[0],), (contract[1],)), ((), ()))...  21.4 us
  transfers between devices with their start and end apart: 9, of which 4 were waited for; matrix products, arithmetic and copies ran while one was open for 19% of the time, Pallas kernels for 33%

profile of v3, /device:TPU:0, one launch (start us, length us, event | category | flops | bytes accessed | tf_op | source)
XLA Modules:
  0.0 696.2 jit_solution(419959680873675273)
XLA Ops:
  7.4 2.7 convert_element_type.169
  10.1 3.0 collective-permute-start
  16.6 118.3 %gather_trunk.1 = (bf16[2,2048,512]{2,1,0:T(8,128)(2,1)}, bf16[9,512,512]{2,1,0:T(8,128)(2,1)}, bf16[16,2,96,256]{3,2,1,0:T(8,128)(2,1)}) custom-call(bf16[2,128,256]{2,1,0:T(8,128)(2,1)} %convert_element_type.170.bottle, bf16[9,32,256]{2,1,0:T(8,128)(2,1)} %convert_element_type.171.middle, bf16[96,256]{1,0:T(8,128)(2,1)} %reshape.460.small), custom_call_target="tpu_custom_call" | custom-call | tf_op jit(solution)/shard_map/gather_trunk/pallas_call | solution.py:388
  134.9 3.7 reshape.461
  139.3 1.3 copy.170
  140.6 3.4 reshape.462
  144.0 2.6 copy.143
  146.6 1.4 copy.150.stem_ref
  148.9 1.2 fusion.58
  150.1 2.0 select_maximum_fusion
  152.1 10.6 %stem_reduce.1 = (bf16[1600,2048]{1,0:T(8,128)(2,1)}, f32[1600,512]{1,0:T(8,128)}, f32[8,512]{1,0:T(8,128)S(1)}) custom-call(bf16[1600,192]{1,0:T(8,128)(2,1)S(1)} %bitcast.146, bf16[192,2048]{1,0:T(8,128)(2,1)S(1)} %copy.150.stem_ref, bf16[2,2048,512]{2,1,0:T(8,128)(2,1)} %get-tuple-element.53.reduce_ref.w_ref, f32[1600,1]{1,0:T(8,128)S(1)} %copy.145.crop_ref, ...), custom_call_target="tpu_custom_call" | custom-call | flops 5000000000 | bytes 14680064 | tf_op jit(solution)/shard_map/stem_reduce/pallas_call | solution.py:673
  162.7 7.8 %small_sum.5.stat_ref.count_ref = f32[8,512]{1,0:T(8,128)S(1)} custom-call(f32[8,512]{1,0:T(8,128)S(1)} %get-tuple-element.55.x_ref), custom_call_target="tpu_custom_call" | custom-call | tf_op jit(solution)/shard_map/small_sum/pallas_call | solution.py:109
  174.3 3.2 constant_dynamic-slice_fusion.3
  177.6 2.5 fusion.42
  181.7 1.2 copy.153
  183.0 2.9 reshape.468
  185.9 2.3 copy.149
  190.2 2.3 pad.36.target_ref
  194.6 15.6 %norm_middle.1 = (bf16[1600,512]{1,0:T(8,128)(2,1)}, bf16[512,1600]{1,0:T(8,128)(2,1)}, bf16[1600,512]{1,0:T(8,128)(2,1)}) custom-call(f32[1600,512]{1,0:T(8,128)} %get-tuple-element.54.a_ref, f32[8,512]{1,0:T(8,128)S(1)} %small_sum.5.stat_ref.count_ref, f32[2,512]{1,0:T(2,128)S(1)} %pad_maximum_fusion.5.gain_ref, f32[1600,1]{1,0:T(8,128)S(1)} %copy.145.crop_ref, ...), custom_call_target="tpu_custom_call" | custom-call | flops 8000000000 | bytes 14680064 | tf_op jit(solution)/shard_map/norm_middle/pallas_call | solution.py:737
  210.2 1.4 copy-done.13
  211.6 8.8 %expand_forward.1 = (bf16[1600,2048]{1,0:T(8,128)(2,1)}, f32[8,512]{1,0:T(8,128)S(1)}) custom-call(bf16[1600,512]{1,0:T(8,128)(2,1)S(1)} %copy-done.13, bf16[2,2048,512]{2,1,0:T(8,128)(2,1)} %get-tuple-element.53.reduce_ref.w_ref, f32[1600,1]{1,0:T(8,128)S(1)} %copy.145.crop_ref), custom_call_target="tpu_custom_call" | custom-call | flops 4000000000 | bytes 12582912 | tf_op jit(solution)/shard_map/expand_forward/pallas_call | solution.py:774
  220.4 10.2 %small_sum.6.stat_ref = f32[8,512]{1,0:T(8,128)S(1)} custom-call(f32[8,512]{1,0:T(8,128)S(1)} %get-tuple-element.59.x_ref), custom_call_target="tpu_custom_call" | custom-call | tf_op jit(solution)/shard_map/small_sum/pallas_call | solution.py:109
  232.0 40.0 %pyramid_fwd.1 = (bf16[1600,2048]{1,0:T(8,128)(2,1)}, bf16[2048,1600]{1,0:T(8,128)(2,1)}, f32[1,2048]{1,0:T(1,128)}, f32[4,1600,128]{2,1,0:T(8,128)}, f32[1,128]...) custom-call(bf16[1600,192]{1,0:T(8,128)(2,1)} %bitcast.147, bf16[192,2048]{1,0:T(8,128)(2,1)} %copy-done.6, ...), custom_call_target="tpu_custom_call" | custom-call | flops 15938355200 | bytes 41943040 | tf_op jit(solution)/shard_map/pyramid_fwd/pallas_call | solution.py:913
  272.4 1.2 fusion.19.label_ref
  273.6 1.8 multiply_add_fusion.2.mask_ref
  275.4 2.0 copy.155.pool_ref
  277.5 15.8 %collective-permute-done.1.other_ref = bf16[1600,256]{1,0:T(8,128)(2,1)S(1)} collective-permute-done((bf16[1600,256]{1,0:T(8,128)(2,1)}, bf16[1600,256]{1,0:T(8,128)(2,1)S(1)}, u32[]{:S(2)}, u32[]{:S(2)}) %collective-permute-start.1) | collective-permute-done | bytes 819232 | tf_op jit(solution)/shard_map/ppermute | solution.py:141
  295.0 9.6 %head_step.1 = (bf16[1600,256]{1,0:T(8,128)(2,1)S(1)}, bf16[1600,128]{1,0:T(8,128)(2,1)S(1)}, bf16[1600,256]{1,0:T(8,128)(2,1)S(1)}, bf16[4,1600,128]{2,1,0:T(8,...) custom-call(bf16[1600,256]{1,0:T(8,128)(2,1)S(1)} %copy-done.1, ...), custom_call_target="tpu_custom_call" | custom-call | flops 2000000000 | bytes 16777216 | tf_op jit(solution)/shard_map/head_step/pallas_call | solution.py:1017
  304.6 17.8 %pyramid_field.2 = bf16[1600,1024]{1,0:T(8,128)(2,1)} custom-call(s32[1]{0:T(128)S(6)} %sub.68.half_ref, bf16[29,2048,128]{2,1,0:T(8,128)(2,1)} %all-gather.2.cloned.1.call-done.w_hbm, bf16[4,1600,128]{2,1,0:T(8,128)(2,1)} %get-tuple-element.68.g_ref, f32[1600,128]{1,0:T(8,128)} %copy-done.2), custom_call_target="tpu_custom_call" | custom-call | flops 7130316800 | bytes 15728640 | tf_op jit(solution)/shard_map/pyramid_field/pallas_call | solution.py:618
  322.4 38.0 %pyramid_weights.1 = bf16[29,2048,128]{2,1,0:T(8,128)(2,1)} custom-call(bf16[2048,1600]{1,0:T(8,128)(2,1)} %get-tuple-element.65.xt_ref, bf16[4,1600,128]{2,1,0:T(8,128)(2,1)} %get-tuple-element.68.g_ref, f32[1600,128]{1,0:T(8,128)} %copy-done.2, f32[2048,1]{1,0:T(8,128)} %copy.155.pool_ref, f32[1,128]{1,0:T(1,128)} %copy-done.10), custom_call_target="tpu_custom_call" | custom-call | flops 15099494400 | bytes 26214400 | tf_op jit(solution)/shard_map/pyramid_weights/pallas_call | solution.py:570
  361.0 1.2 slice.151
  362.2 4.6 fusion.60
  367.5 1.3 fusion.23
  369.5 1.7 collective-permute-start.3
  371.2 19.4 %pyramid_field.3 = bf16[1600,1024]{1,0:T(8,128)(2,1)} custom-call(s32[1]{0:T(128)} %bitcast.half_ref, bf16[29,2048,128]{2,1,0:T(8,128)(2,1)} %all-gather.2.cloned.1.call-done.w_hbm, bf16[4,1600,128]{2,1,0:T(8,128)(2,1)} %get-tuple-element.68.g_ref, f32[1600,128]{1,0:T(8,128)} %copy-done.2), custom_call_target="tpu_custom_call" | custom-call | flops 7130316800 | bytes 15728640 | tf_op jit(solution)/shard_map/pyramid_field/pallas_call | solution.py:618
  392.6 41.2 %collective-permute-done.3 = f32[1,1024]{1,0:T(1,128)S(1)} collective-permute-done((f32[1,1024]{1,0:T(1,128)S(1)}, f32[1,1024]{1,0:T(1,128)S(1)}, u32[]{:S(2)}, u32[]{:S(2)}) %collective-permute-start.3) | collective-permute-done | bytes 4128 | tf_op jit(solution)/shard_map/ppermute | solution.py:141
  433.8 5.8 multiply_reduce_fusion.1
  439.6 1.4 concatenate.70
  441.0 11.7 %small_sum.7 = f32[24,128]{1,0:T(8,128)S(1)} custom-call(f32[24,128]{1,0:T(8,128)S(1)} %pad_bitcast_fusion.x_ref), custom_call_target="tpu_custom_call" | custom-call | tf_op jit(solution)/shard_map/small_sum/pallas_call | solution.py:109
  452.7 7.4 %multiply_convert_fusion.1 = bf16[1600,1024]{1,0:T(8,128)(2,1)S(1)} fusion(f32[]{:T(128)} %bitcast.26, f32[1024]{0:T(1024)S(1)} %get-tuple-element.211, f32[1024]{0:T(1024)S(1)} %get-tuple-element.210, f32[1024]{0:T(1024)S(1)} %dynamic_slice.56, f32[1024]{0:T(1024)S(1)} %get-tuple-element.191, f32[1024]{0:T(1024)S(1)} %get-tuple-element.192, ...), kind=kLoop, calls=%fused_computation.1 | loop fusion | flops 27852800 | bytes 13138184 | tf_op jit(solution)/shard_map/convert_element_type | solution.py:1270
  460.2 3.0 convolution_convert_fusion
  463.5 1.4 add_rsqrt_fusion
  465.0 2.1 convolution_convert_fusion.2
  468.0 1.7 collective-permute-start.5
  470.3 2.5 convolution_convert_fusion.4
  472.8 2.0 copy.159
  474.8 6.0 reshape.482
  480.8 32.4 %collective-permute-done.5 = bf16[1024,256]{1,0:T(8,128)(2,1)S(1)} collective-permute-done((bf16[1024,256]{1,0:T(8,128)(2,1)}, bf16[1024,256]{1,0:T(8,128)(2,1)S(1)}, u32[]{:S(2)}, u32[]{:S(2)}) %collective-permute-start.5) | collective-permute-done | bytes 524320 | tf_op jit(solution)/shard_map/ppermute | solution.py:141
  513.5 2.5 add_convert_fusion.x_ref
  516.2 4.2 middle_weights.1
  520.4 1.6 copy.156
  522.0 9.4 %middle_back.1 = f32[1600,512]{1,0:T(8,128)S(1)} custom-call(bf16[1600,512]{1,0:T(8,128)(2,1)S(1)} %add_convert_fusion.x_ref, bf16[9,512,512]{2,1,0:T(8,128)(2,1)S(1)} %bitcast.153, f32[1600,128]{1,0:T(8,128)S(1)} %copy-done.3), custom_call_target="tpu_custom_call" | custom-call | flops 7549747200 | bytes 16777216 | tf_op jit(solution)/shard_map/middle_back/pallas_call | solution.py:476
  531.5 3.8 multiply_reduce_fusion.2
  535.2 10.7 %small_sum.8 = f32[8,128]{1,0:T(8,128)S(1)} custom-call(f32[8,128]{1,0:T(8,128)S(1)} %pad_maximum_fusion.6.x_ref), custom_call_target="tpu_custom_call" | custom-call | tf_op jit(solution)/shard_map/small_sum/pallas_call | solution.py:109
  545.9 3.3 multiply_convert_fusion.2
  549.2 6.8 fusion.11
  557.5 5.3 convolution_convert_fusion.1
  562.9 5.8 pad_maximum_fusion
  577.0 71.0 %reduce-scatter.5.cloned.1.call-done = bf16[1,640,256]{2,1,0:T(8,128)(2,1)} async-done(((bf16[16,640,256]{2,1,0:T(8,128)(2,1)}), bf16[1,640,256]{2,1,0:T(8,128)(2,1)}) %reduce-scatter.5.cloned.1.call-update) | async-done | bytes 327696 | tf_op jit(solution)/shard_map/reduce_scatter | solution.py:1335
  656.8 9.2 %small_sum.9 = f32[8,128]{1,0:T(8,128)S(1)} custom-call(f32[8,128]{1,0:T(8,128)S(1)} %pad_bitcast_fusion.1.x_ref), custom_call_target="tpu_custom_call" | custom-call | tf_op jit(solution)/shard_map/small_sum/pallas_call | solution.py:109
  667.3 1.3 slice_multiply_fusion.4
  675.7 1.4 multiply_subtract_fusion.7
  677.1 1.4 multiply_subtract_fusion.5
  678.7 6.0 multiply_subtract_fusion
  (264 shorter events, 46.9 us)
Async XLA Ops:
  7.2 2.9 copy-start.44
  7.2 5.9 copy-start.58
  7.2 6.0 copy-start.48
  7.2 6.1 copy-start.36
  7.3 6.1 copy-start.34
  7.3 6.3 copy-start.26
  7.3 8.0 %copy-start.22 = (f32[9,32,256]{2,1,0:T(8,128)S(1)}, f32[9,32,256]{2,1,0:T(8,128)}, u32[]{:S(2)}) copy-start(f32[9,32,256]{2,1,0:T(8,128)} %param.44) | copy-start | bytes 884740
  7.3 8.7 %copy-start.50 = (s32[1,1600]{1,0:T(1,128)S(1)}, s32[1,1600]{1,0:T(1,128)}, u32[]{:S(2)}) copy-start(s32[1,1600]{1,0:T(1,128)} %param.37) | copy-start | bytes 19204
  7.3 9.0 %copy-start.28 = (bf16[1,1600,192]{1,2,0:T(8,128)(2,1)S(1)}, bf16[1,1600,192]{1,2,0:T(8,128)(2,1)}, u32[]{:S(2)}) copy-start(bf16[1,1600,192]{1,2,0:T(8,128)(2,1)} %param.31) | copy-start | bytes 1843204
  7.3 224.6 %all-gather.2.cloned.1.call-start = ((), (), s32[]{:S(2)}) async-start(), calls=%async_computation.2 | async-start | bytes 16154624 | tf_op jit(solution)/shard_map/all_gather | solution.py:1099
  10.1 558.6 %reduce-scatter.3.cloned.1.call-start = ((), (), s32[]{:S(2)}) async-start(), calls=%async_computation.3 | async-start | bytes 16154624 | tf_op jit(solution)/shard_map/reduce_scatter | solution.py:1243
  10.1 183.2 %collective-permute-start = (f32[2,1,1280]{2,1,0:T(1,128)S(1)}, f32[2,1,1280]{2,1,0:T(1,128)}, u32[]{:S(2)}, u32[]{:S(2)}) collective-permute-start(f32[2,1,1280]{2,1,0:T(1,128)S(1)} %copy-done.44), channel_id=1, source_target_pairs={{0,1},{1,0},{2,3},{3,2},{4,5},{5,4},{6,7},{7,6},{8,9},{9,8},{10,11... | collective-permute-start | bytes 30728 | tf_op jit(solution)/shard_map/ppermute | solution.py:141
  16.3 193.9 %copy-start.4 = (f32[1600,1]{1,0:T(8,128)}, f32[1600,1]{1,0:T(8,128)S(1)}, u32[]{:S(2)}) copy-start(f32[1600,1]{1,0:T(8,128)S(1)} %copy.145.crop_ref) | copy-start | bytes 19204
  16.6 135.5 %copy-start.5 = (bf16[1,1600,192]{2,1,0:T(8,128)(2,1)}, bf16[1,1600,192]{2,1,0:T(8,128)(2,1)S(1)}, u32[]{:S(2)}) copy-start(bf16[1,1600,192]{2,1,0:T(8,128)(2,1)S(1)} %copy.139) | copy-start | bytes 1843204
  138.7 7.9 %copy-start.17 = (bf16[16,2,24576]{2,1,0:T(2,128)(2,1)}, bf16[16,2,24576]{2,1,0:T(2,128)(2,1)S(1)}, u32[]{:S(2)}) copy-start(bf16[16,2,24576]{2,1,0:T(2,128)(2,1)S(1)} %reshape.461) | copy-start | bytes 4718596
  140.6 8.2 %copy-start.56 = (s32[1,1600]{1,0:T(1,128)S(1)}, s32[1,1600]{1,0:T(1,128)}, u32[]{:S(2)}) copy-start(s32[1,1600]{1,0:T(1,128)} %param.36) | copy-start | bytes 19204
  140.6 8.2 %copy-start.57 = (s32[1,1600]{1,0:T(1,128)S(1)}, s32[1,1600]{1,0:T(1,128)}, u32[]{:S(2)}) copy-start(s32[1,1600]{1,0:T(1,128)} %param.34) | copy-start | bytes 19204
  148.1 14.6 %copy-start.6 = (bf16[192,2048]{1,0:T(8,128)(2,1)}, bf16[192,2048]{1,0:T(8,128)(2,1)S(1)}, u32[]{:S(2)}) copy-start(bf16[192,2048]{1,0:T(8,128)(2,1)S(1)} %copy.150.stem_ref) | copy-start | bytes 2359300
  152.1 22.2 %copy-start.51 = (f32[1,2,1600]{2,1,0:T(2,128)S(1)}, f32[1,2,1600]{2,1,0:T(2,128)}, u32[]{:S(2)}) copy-start(f32[1,2,1600]{2,1,0:T(2,128)} %param.33) | copy-start | bytes 38404
  152.1 22.2 %copy-start.54 = (f32[1,1600]{1,0:T(1,128)S(1)}, f32[1,1600]{1,0:T(1,128)}, u32[]{:S(2)}) copy-start(f32[1,1600]{1,0:T(1,128)} %param.35) | copy-start | bytes 19204
  162.7 19.0 %copy-start.55 = (s32[1,1600]{1,0:T(1,128)S(1)}, s32[1,1600]{1,0:T(1,128)}, u32[]{:S(2)}) copy-start(s32[1,1600]{1,0:T(1,128)} %param.32) | copy-start | bytes 19204
  170.5 24.0 %copy-start.9 = (f32[8,512]{1,0:T(8,128)}, f32[8,512]{1,0:T(8,128)S(1)}, u32[]{:S(2)}) copy-start(f32[8,512]{1,0:T(8,128)S(1)} %small_sum.5.stat_ref.count_ref) | copy-start | bytes 49156
  188.2 6.1 copy-start.45
  194.5 15.7 %copy-start.2 = (f32[1600,128]{1,0:T(8,128)}, f32[1600,128]{1,0:T(8,128)S(1)}, u32[]{:S(2)}) copy-start(f32[1600,128]{1,0:T(8,128)S(1)} %broadcast_in_dim.16.col_ref) | copy-start | bytes 2457604
  231.9 41.6 %copy-start.46 = (f32[1600]{0:T(1024)S(1)}, f32[1600]{0:T(1024)}, u32[]{:S(2)}) copy-start(f32[1600]{0:T(1024)} %get-tuple-element.194) | copy-start | bytes 19204
  231.9 41.6 %copy-start.47 = (f32[1600]{0:T(1024)S(1)}, f32[1600]{0:T(1024)}, u32[]{:S(2)}) copy-start(f32[1600]{0:T(1024)} %get-tuple-element.215) | copy-start | bytes 19204
  231.9 41.6 %copy-start.61 = (f32[128]{0:T(128)S(1)}, f32[128]{0:T(128)}, u32[]{:S(2)}) copy-start(f32[128]{0:T(128)} %compare_convert_fusion.1) | copy-start | bytes 1540
  231.9 41.6 %copy-start.62 = (f32[128]{0:T(128)S(1)}, f32[128]{0:T(128)}, u32[]{:S(2)}) copy-start(f32[128]{0:T(128)} %get-tuple-element.229) | copy-start | bytes 1540
  231.9 41.6 %copy-start.63 = (f32[128]{0:T(128)S(1)}, f32[128]{0:T(128)}, u32[]{:S(2)}) copy-start(f32[128]{0:T(128)} %get-tuple-element.230) | copy-start | bytes 1540
  232.0 61.3 %copy-start = (bf16[640,256]{1,0:T(8,128)(2,1)S(1)}, bf16[640,256]{1,0:T(8,128)(2,1)}, u32[]{:S(2)}) copy-start(bf16[640,256]{1,0:T(8,128)(2,1)} %copy.152.project_ref) | copy-start | bytes 983044
  272.0 21.3 %collective-permute-start.1 = (bf16[1600,256]{1,0:T(8,128)(2,1)}, bf16[1600,256]{1,0:T(8,128)(2,1)S(1)}, u32[]{:S(2)}, u32[]{:S(2)}) collective-permute-start(bf16[1600,256]{1,0:T(8,128)(2,1)} %get-tuple-element.60.own_ref), channel_id=1, source_target_pairs={{0,1},{1,0},{2,3},{3,2},{4,5},{5,4},{6,7},{7,6},{8,9},{9,8},{10,11... | collective-permute-start | bytes 2457608 | tf_op jit(solution)/shard_map/ppermute | solution.py:141
  304.6 17.8 %copy-start.10 = (f32[1,128]{1,0:T(1,128)}, f32[1,128]{1,0:T(1,128)S(1)}, u32[]{:S(2)}) copy-start(f32[1,128]{1,0:T(1,128)S(1)} %get-tuple-element.67.pool_grad_ref) | copy-start | bytes 1540
  360.5 287.5 %reduce-scatter.5.cloned.1.call-start = ((), (), s32[]{:S(2)}) async-start(), calls=%async_computation.4 | async-start | bytes 5570560 | tf_op jit(solution)/shard_map/reduce_scatter | solution.py:1335
  360.5 73.2 %collective-permute-start.2 = (bf16[1600,1024]{1,0:T(8,128)(2,1)}, bf16[1600,1024]{1,0:T(8,128)(2,1)}, u32[]{:S(2)}, u32[]{:S(2)}) collective-permute-start(bf16[1600,1024]{1,0:T(8,128)(2,1)} %pyramid_field.2), channel_id=1, source_target_pairs={{0,1},{1,0},{2,3},{3,2},{4,5},{5,4},{6,7},{7,6},{8,9},{9,8},{10,11... | collective-permute-start | bytes 9830408 | tf_op jit(solution)/shard_map/ppermute | solution.py:141
  362.2 4.6 copy-start.8
  362.2 5.3 copy-start.11
  369.5 64.3 %collective-permute-start.3 = (f32[1,1024]{1,0:T(1,128)S(1)}, f32[1,1024]{1,0:T(1,128)S(1)}, u32[]{:S(2)}, u32[]{:S(2)}) collective-permute-start(f32[1,1024]{1,0:T(1,128)S(1)} %bitcast.197), channel_id=1, source_target_pairs={{0,1},{1,0},{2,3},{3,2},{4,5},{5,4},{6,7},{7,6},{8,9},{9,8},{10,11... | collective-permute-start | bytes 12296 | tf_op jit(solution)/shard_map/ppermute | solution.py:141
  452.7 7.5 %copy-start.21 = (bf16[1,2048,512]{2,1,0:T(8,128)(2,1)S(1)}, bf16[1,2048,512]{2,1,0:T(8,128)(2,1)}, u32[]{:S(2)}) copy-start(bf16[1,2048,512]{2,1,0:T(8,128)(2,1)} %get-tuple-element.198) | copy-start | bytes 6291460
  460.2 4.8 copy-start.14
  463.2 50.3 %collective-permute-start.4 = (bf16[1600,512]{1,0:T(8,128)(2,1)}, bf16[1600,512]{1,0:T(8,128)(2,1)}, u32[]{:S(2)}, u32[]{:S(2)}) collective-permute-start(bf16[1600,512]{1,0:T(8,128)(2,1)} %convolution_convert_fusion), channel_id=1, source_target_pairs={{0,1},{1,0},{2,3},{3,2},{4,5},{5,4},{6,7},{7,6},{8,9},{9,8},{10,11... | collective-permute-start | bytes 4915208 | tf_op jit(solution)/shard_map/ppermute | solution.py:141
  468.0 45.2 %collective-permute-start.5 = (bf16[1024,256]{1,0:T(8,128)(2,1)}, bf16[1024,256]{1,0:T(8,128)(2,1)S(1)}, u32[]{:S(2)}, u32[]{:S(2)}) collective-permute-start(bf16[1024,256]{1,0:T(8,128)(2,1)} %get-tuple-element.200), channel_id=1, source_target_pairs={{0,1},{1,0},{2,3},{3,2},{4,5},{5,4},{6,7},{7,6},{8,9},{9,8},{10,11... | collective-permute-start | bytes 1572872 | tf_op jit(solution)/shard_map/ppermute | solution.py:141
  513.5 8.5 %slice-start = ((s8[4718592]{0:T(1024)(128)(4,1)}), s8[4194304]{0:T(1024)(128)(4,1)S(1)}, s32[]{:S(2)}) async-start(s8[4718592]{0:T(1024)(128)(4,1)} %bitcast.152), calls=%async_computation.5 | async-start | bytes 8388608
  516.2 5.8 slice-start.1
  522.0 9.4 %copy-start.16 = (f32[1600,512]{1,0:T(8,128)S(1)}, f32[1600,512]{1,0:T(8,128)}, u32[]{:S(2)}) copy-start(f32[1600,512]{1,0:T(8,128)} %get-tuple-element.54.a_ref) | copy-start | bytes 9830404
  545.9 3.3 copy-start.29
  557.5 5.3 copy-start.18
  568.7 7.2 %copy-start.20 = (bf16[29,128,128]{2,1,0:T(8,128)(2,1)S(1)}, bf16[29,128,128]{2,1,0:T(8,128)(2,1)}, u32[]{:S(2)}) copy-start(bf16[29,128,128]{2,1,0:T(8,128)(2,1)} %reduce-scatter.3.cloned.1.call-done) | copy-start | bytes 2850820
  571.8 96.8 %copy-start.60 = (f32[22]{0:T(128)}, f32[22]{0:T(128)S(1)}, u32[]{:S(2)}) copy-start(f32[22]{0:T(128)S(1)} %slice.192) | copy-start | bytes 268
  572.5 96.1 %copy-start.59 = (f32[3]{0:T(128)}, f32[3]{0:T(128)S(1)}, u32[]{:S(2)}) copy-start(f32[3]{0:T(128)S(1)} %get-tuple-element.186) | copy-start | bytes 40
  573.8 104.7 %copy-start.19 = (f32[29,128,128]{2,1,0:T(8,128)S(1)}, f32[29,128,128]{2,1,0:T(8,128)}, u32[]{:S(2)}) copy-start(f32[29,128,128]{2,1,0:T(8,128)} %param.47) | copy-start | bytes 5701636
  678.5 6.1 copy-start.49
  678.5 6.1 copy-start.52
  678.5 6.1 copy-start.53
  678.5 6.7 copy-start.37
  678.5 6.7 copy-start.42
  678.6 6.7 copy-start.43
  678.6 7.4 %copy-start.25 = (f32[1,256,256]{2,1,0:T(8,128)S(1)}, f32[1,256,256]{2,1,0:T(8,128)}, u32[]{:S(2)}) copy-start(f32[1,256,256]{2,1,0:T(8,128)} %slice_multiply_fusion.1) | copy-start | bytes 786436
  678.6 7.4 %copy-start.27 = (f32[2,128,256]{2,1,0:T(8,128)S(1)}, f32[2,128,256]{2,1,0:T(8,128)}, u32[]{:S(2)}) copy-start(f32[2,128,256]{2,1,0:T(8,128)} %param.41) | copy-start | bytes 786436
  678.6 7.4 %copy-start.32 = (f32[2,128,256]{2,1,0:T(8,128)S(1)}, f32[2,128,256]{2,1,0:T(8,128)}, u32[]{:S(2)}) copy-start(f32[2,128,256]{2,1,0:T(8,128)} %param.42) | copy-start | bytes 786436
  678.6 7.3 %copy-start.33 = (f32[2,128,256]{2,1,0:T(8,128)S(1)}, f32[2,128,256]{2,1,0:T(8,128)}, u32[]{:S(2)}) copy-start(f32[2,128,256]{2,1,0:T(8,128)} %param.43) | copy-start | bytes 786436
  678.6 8.3 %copy-start.23 = (f32[9,32,256]{2,1,0:T(8,128)S(1)}, f32[9,32,256]{2,1,0:T(8,128)}, u32[]{:S(2)}) copy-start(f32[9,32,256]{2,1,0:T(8,128)} %param.44) | copy-start | bytes 884740
  678.6 8.3 %copy-start.24 = (f32[1,288,256]{2,1,0:T(8,128)S(1)}, f32[1,288,256]{2,1,0:T(8,128)}, u32[]{:S(2)}) copy-start(f32[1,288,256]{2,1,0:T(8,128)} %slice_multiply_fusion) | copy-start | bytes 884740
  678.6 8.3 %copy-start.30 = (f32[9,32,256]{2,1,0:T(8,128)S(1)}, f32[9,32,256]{2,1,0:T(8,128)}, u32[]{:S(2)}) copy-start(f32[9,32,256]{2,1,0:T(8,128)} %param.45) | copy-start | bytes 884740
  678.7 8.3 %copy-start.31 = (f32[9,32,256]{2,1,0:T(8,128)S(1)}, f32[9,32,256]{2,1,0:T(8,128)}, u32[]{:S(2)}) copy-start(f32[9,32,256]{2,1,0:T(8,128)} %param.46) | copy-start | bytes 884740
  (11 other events, 16.9 us)
Sparse Core Ops, SparseCore 0:
  10.3 147.3 all-gather.1
  360.6 160.1 reduce-scatter.2
  568.8 79.1 reduce-scatter.4

commit v4 on v3

--- a/solution.py
+++ b/solution.py
@@ -234,6 +234,7 @@
     z, y, core, x = place_of()
     rows = bottle.shape[1]
     mid_rows = middle.shape[1]
+    small_rows = small.shape[0]
     own_refs = (bottle, middle, small)
 
     def region(kind, block):
@@ -244,7 +245,8 @@
             return bottle_all.at[:, pl.ds(pl.multiple_of(index * rows, 16), rows), cols]
         if kind == 1:
             return middle_all.at[:, pl.ds(pl.multiple_of(index * mid_rows, 16), mid_rows), cols]
-        return small_all.at[index, xx]
+        first = xx * (small_all.shape[0] // 2) + index * small_rows
+        return small_all.at[pl.ds(pl.multiple_of(first, 16), small_rows)]
 
     def semaphore(kind, block):
         zz, yy, kk, xx = block
@@ -384,13 +386,13 @@
             )
             for part in (bottle, middle)
         ]
-        return packed + [lax.all_gather(small, ("dp", "chan")).reshape((count, 2) + small.shape)]
+        return packed + [lax.all_gather(small, ("chan", "dp")).reshape(D, small.shape[1])]
     return pl.pallas_call(
         functools.partial(gather_kernel, count // 4),
         out_shape=[
             jax.ShapeDtypeStruct((2, D, MID), jnp.bfloat16),
             jax.ShapeDtypeStruct((9, MID, MID), jnp.bfloat16),
-            jax.ShapeDtypeStruct((count, 2) + small.shape, jnp.bfloat16),
+            jax.ShapeDtypeStruct((D, small.shape[1]), jnp.bfloat16),
         ],
         in_specs=[pl.BlockSpec(memory_space=pl.ANY)] * 3,
         out_specs=[pl.BlockSpec(memory_space=pl.ANY)] * 3,
@@ -581,62 +583,80 @@
     )(field_t, grads, columns, pooled, pool_grad)
 
 
-def field_kernel(half_ref, w_hbm, g_ref, col_ref, o_ref, weights, fields, stack, sems):
+def field_kernel(
+    place_ref, w_hbm, near_hbm, far_hbm, g_ref, other_ref, col_ref, o_ref, weights, fields, stack, sems
+):
     width = g_ref.shape[2]
+    both = 2 * width
     depth = o_ref.shape[1]
-    half = pl.ds(pl.multiple_of(half_ref[0] * depth, 16), depth)
-    copies = []
+    half = pl.ds(pl.multiple_of(place_ref[0] * depth, 16), depth)
+    core = place_ref[1]
+    part = near_hbm.shape[0]
+    own = []
+    other = []
     for slot, tap in enumerate(TAP_ORDER):
         copy = pltpu.make_async_copy(
-            w_hbm.at[tap, half], weights.at[:, pl.ds(slot * width, width)], sems.at[slot]
+            w_hbm.at[tap, half], weights.at[:, pl.ds(slot * both, width)], sems.at[0, slot]
         )
         copy.start()
-        copies.append(copy)
-    fill_fields(g_ref, col_ref, fields)
-    for copy in copies:
-        copy.wait()
+        own.append(copy)
+        target = weights.at[:, pl.ds(slot * both + width, width)]
+        near = pltpu.make_async_copy(near_hbm.at[tap % part], target, sems.at[1, slot])
+        far = pltpu.make_async_copy(far_hbm.at[tap % part], target, sems.at[1, slot])
+        is_near = core == tap // part
+        pl.when(is_near)(near.start)
+        pl.when(jnp.logical_not(is_near))(far.start)
+        other.append(near)
+    for place, (rate, col_step) in enumerate(FIELDS):
+        fields[place, :PAD] = jnp.zeros((PAD, both), fields.dtype)
+        fields[place, PAD + POSITIONS :] = jnp.zeros((PAD, both), fields.dtype)
+        for side, ref in enumerate((g_ref, other_ref)):
+            fields[place, PAD : PAD + POSITIONS, side * width : (side + 1) * width] = roll_cols(
+                ref[rate // 12].astype(jnp.float32), col_ref, -col_step
+            ).astype(fields.dtype)
     step_of = [step for step, group in zip(PYRAMID_ROWS, ROW_GROUPS) for entry in group]
-    for r0, r1 in ((0, 4), (4, 12), (12, 16), (16, 24), (24, 28), (28, 36), (36, 40)):
+    waited = set()
+    for r0, r1 in ((16, 24), (12, 16), (24, 28), (4, 12), (28, 36), (0, 4), (36, 40)):
         slots = [
             slot for slot, step in enumerate(step_of) if r0 - step >= 0 and r1 - step <= FH
         ]
         count = (r1 - r0) * FW
         for at, slot in enumerate(slots):
+            if slot not in waited:
+                waited.add(slot)
+                own[slot].wait()
+                other[slot].wait()
             base = PAD + (r0 - step_of[slot]) * FW
-            stack[:count, at * width : (at + 1) * width] = fields[
+            stack[:count, at * both : (at + 1) * both] = fields[
                 PLACE_ORDER[slot], base : base + count
             ]
         o_ref[r0 * FW : r1 * FW] = dot(
-            stack[:count, : len(slots) * width],
-            weights[:, slots[0] * width : (slots[-1] + 1) * width],
+            stack[:count, : len(slots) * both],
+            weights[:, slots[0] * both : (slots[-1] + 1) * both],
             (1, 1),
         ).astype(o_ref.dtype)
 
 
-def pyramid_field(half, weights, grads, columns):
+def pyramid_field(place, weights, near, far, grads, other, columns):
     depth, width = weights.shape[1] // 2, weights.shape[2]
+    hbm = pl.BlockSpec(memory_space=pl.ANY)
     return pl.pallas_call(
         field_kernel,
-        out_shape=jax.ShapeDtypeStruct((POSITIONS, depth), jnp.bfloat16),
-        in_specs=[
-            pl.BlockSpec(memory_space=pltpu.SMEM),
-            pl.BlockSpec(memory_space=pl.ANY),
-            pl.BlockSpec(memory_space=pltpu.VMEM),
-            pl.BlockSpec(memory_space=pltpu.VMEM),
-        ],
+        out_shape=jax.ShapeDtypeStruct((POSITIONS, depth), jnp.float32),
+        in_specs=[pl.BlockSpec(memory_space=pltpu.SMEM), hbm, hbm, hbm] + vmem(3),
         out_specs=vmem(1)[0],
         scratch_shapes=[
-            pltpu.VMEM((depth, 28 * width), jnp.bfloat16),
-            pltpu.VMEM((10, POSITIONS + 2 * PAD, width), jnp.bfloat16),
-            pltpu.VMEM((8 * FW, 19 * width), jnp.bfloat16),
-            pltpu.SemaphoreType.DMA((28,)),
+            pltpu.VMEM((depth, 28 * 2 * width), jnp.bfloat16),
+            pltpu.VMEM((10, POSITIONS + 2 * PAD, 2 * width), jnp.bfloat16),
+            pltpu.VMEM((8 * FW, 19 * 2 * width), jnp.bfloat16),
+            pltpu.SemaphoreType.DMA((2, 28)),
         ],
         compiler_params=pltpu.CompilerParams(vmem_limit_bytes=56 << 20),
         cost_estimate=pl.CostEstimate(
-            flops=2 * POSITIONS * 17 * depth * width, bytes_accessed=15 << 20, transcendentals=0
+            flops=2 * POSITIONS * 34 * depth * width, bytes_accessed=25 << 20, transcendentals=0
         ),
         name="pyramid_field",
-    )(half, weights, grads, columns)
+    )(place, weights, near, far, grads, other, columns)
 
 
 BLOCK = 320
@@ -653,7 +673,7 @@
 def stem_kernel(p_ref, stem_ref, reduce_ref, crop_ref, count_ref, x_ref, a_ref, stat_ref):
     def step(index, carry):
         rows = block_rows(index)
-        low = (crop_ref[rows] * dot(p_ref[rows], stem_ref[...])).astype(x_ref.dtype)
+        low = (crop_ref[rows] * dot(p_ref[rows], stem_ref[:, :PATCH], (1, 1))).astype(x_ref.dtype)
         x_ref[rows] = low
         value = dot(low, reduce_ref[0])
         a_ref[rows] = value
@@ -680,7 +700,7 @@
         ],
         in_specs=[
             pl.BlockSpec((POSITIONS, PATCH), lambda i: (0, 0)),
-            pl.BlockSpec((PATCH, D), lambda i: (0, 0)),
+            pl.BlockSpec(stem.shape, lambda i: (0, 0)),
             pl.BlockSpec((1, D, MID), lambda i: (0, 0, 0)),
             pl.BlockSpec((POSITIONS, 1), lambda i: (0, 0)),
             pl.BlockSpec((1, MID), lambda i: (0, 0)),
@@ -847,7 +867,7 @@
 
     def residual(index, carry):
         rows = block_rows(index)
-        value = dot(p_ref[rows], stem_ref[...]) + (y_ref[rows].astype(jnp.float32) * gain + shift)
+        value = dot(p_ref[rows], stem_ref[:, :PATCH], (1, 1)) + (y_ref[rows].astype(jnp.float32) * gain + shift)
         low = (crop_ref[rows] * value).astype(x_ref.dtype)
         x_ref[rows] = low
         return carry + jnp.sum(low.astype(jnp.float32), 0, keepdims=True)
@@ -1091,32 +1111,41 @@
     stem_share = stem_weight.shape[2]
     project_share = project_weight.shape[2]
     head_share = head_weight.shape[0]
-    small_parts = [stem_weight, project_weight, head_weight]
-    small_flat = jnp.concatenate([part.astype(low).reshape(-1) for part in small_parts])
-    small_rows = -(-small_flat.shape[0] // (16 * 256)) * 16
-    small_flat = jnp.pad(small_flat, (0, small_rows * 256 - small_flat.shape[0]))
-    small_flat = small_flat.reshape(small_rows, 256)
-    pyramid_low = lax.all_gather(pyramid_weight.astype(low), "dp", axis=1, tiled=True)
-    bottle_low, middle_low, small = gather_trunk(
-        sizes, bottle_weight.astype(low), middle_weight.astype(low), small_flat
-    )
-    small = small.reshape(dp_size, 2, small_rows * 256)
-    size = PATCH * stem_share
-    stem_low = (
-        small[:, :, :size]
-        .reshape(dp_size, 2, PATCH, stem_share)
-        .transpose(2, 1, 0, 3)
-        .reshape(PATCH, D)
-    )
-    own_small = lax.dynamic_index_in_dim(small, chan_place, 1, keepdims=False)
+    small_flat = jnp.concatenate(
+        [project_weight.astype(low).reshape(-1), head_weight.astype(low).reshape(-1)]
+    )
+    small_room = stem_share * PATCH
+    small_flat = jnp.pad(small_flat, (0, small_room - small_flat.shape[0]))
+    stem_shard = jnp.concatenate(
+        [stem_weight.astype(low).reshape(PATCH, stem_share).T, small_flat.reshape(stem_share, PATCH)],
+        1,
+    )
+    bottle_low, middle_low, stem_low = gather_trunk(
+        sizes, bottle_weight.astype(low), middle_weight.astype(low), stem_shard
+    )
+    pyramid_shard, bottle_low = lax.optimization_barrier((pyramid_weight.astype(low), bottle_low))
+    pyramid_low = lax.all_gather(pyramid_shard, "dp", axis=1, tiled=True)
+    own_small = lax.dynamic_slice_in_dim(stem_low, chan_place * half, half, 0)[:, PATCH:].reshape(
+        dp_size, small_room
+    )
+    size = 5 * 128 * project_share
     project_low = (
-        own_small[:, size : size + 5 * 128 * project_share]
+        own_small[:, :size]
         .reshape(dp_size, 5, 128, project_share)
         .transpose(1, 2, 0, 3)
         .reshape(5 * 128, BRANCH)
     )
-    size += 5 * 128 * project_share
     head_low = own_small[:, size : size + head_share * 22].reshape(BRANCH, 22)
+
+    core = lax.rem(lax.axis_index("dp"), 2)
+    near_rows = swap_chan(
+        lax.dynamic_slice(
+            pyramid_low, (14 * core, (1 - chan_place) * half, 0), (14, half, BRANCH // 2)
+        )
+    )
+    far_rows = lax.ppermute(
+        near_rows, "dp", [(place, place + 1 - 2 * (place % 2)) for place in range(dp_size)]
+    )
 
     gains_other = swap_chan(norm_gains)
     gains_all = jnp.where(
@@ -1229,25 +1258,24 @@
     project_grad = dot(concat_low, project_grad_low, (0, 0))
     pool_grad_low = pool_grad.astype(low)
 
-    own_place = chan_place.reshape(1)
-    other_part = pyramid_field(1 - own_place, pyramid_low, branch_grads, columns)
-    other_sent = swap_chan(other_part)
-    later_grads, other_part = lax.optimization_barrier((branch_grads, other_part))
+    other_grads = swap_chan(branch_grads)
     pyramid_grad = pyramid_weights(
-        output_t,
+        output_t, branch_grads, columns, pooled.reshape(D, 1), pool_grad
+    )
+    pyramid_red = lax.psum_scatter(pyramid_grad, "dp", scatter_dimension=1, tiled=True)
+    later_grads, pyramid_grad = lax.optimization_barrier((branch_grads, pyramid_grad))
+    field_grad = pyramid_field(
+        jnp.stack([chan_place, core]),
+        pyramid_low,
+        near_rows,
+        far_rows,
         later_grads,
+        other_grads,
         columns,
-        pooled.reshape(D, 1),
-        pool_grad,
-    )
-    pyramid_red = lax.psum_scatter(pyramid_grad, "dp", scatter_dimension=1, tiled=True)
-    later_grads, pyramid_grad = lax.optimization_barrier((later_grads, pyramid_grad))
-    own_part = pyramid_field(own_place, pyramid_low, later_grads, columns)
+    )
     pool_part = dot(pool_grad_low, pyramid_low[28], (1, 1)) / image_count
     pool_sum = own_half(pool_part, 1) + swap_chan(other_half(pool_part, 1))
-    stream_grad = (
-        own_part.astype(jnp.float32) + other_sent.astype(jnp.float32) + crop_field * pool_sum
-    )
+    stream_grad = field_grad + crop_field * pool_sum
 
     own_gain_two = own_half(gain_two, 0)
     own_scale_two = own_half(scale_two, 0)
@@ -1297,7 +1325,7 @@
     reduce_grad = dot(stream_low, own_half(first_grad_low, 1), (0, 0)).astype(low)
     start_grad = dot(first_grad_low, own_half(bottle_low[0], 0), (1, 1)) + stream_grad
     start_grad_low = (crop_field * start_grad).astype(low)
-    stem_grad = dot(patch_rows, start_grad_low, (0, 0)).astype(low)
+    stem_grad = dot(start_grad_low, patch_rows, (0, 0)).astype(low)
     expand_own = own_half(expand_rows, 1)
     expand_grad = jnp.where(
         chan_place == 0,
@@ -1307,21 +1335,18 @@
 
     small_grads = jnp.concatenate(
         [
-            stem_grad.reshape(PATCH, dp_size, stem_share)
-            .transpose(1, 0, 2)
-            .reshape(dp_size, PATCH * stem_share),
             project_grad.astype(low)
             .reshape(5 * 128, dp_size, project_share)
             .transpose(1, 0, 2)
-            .reshape(dp_size, 5 * 128 * project_share),
+            .reshape(dp_size, size),
             head_grad.astype(low).reshape(dp_size, head_share * 22),
         ],
         1,
     )
+    small_rows = -(-small_grads.shape[1] // 4096) * 16
     small_grads = jnp.pad(small_grads, ((0, 0), (0, small_rows * 256 - small_grads.shape[1])))
-    packed_grads = jnp.concatenate(
+    early_grads = jnp.concatenate(
         [
-            reduce_grad.reshape(dp_size, row_share, 256),
             expand_grad.reshape(dp_size, row_share, 256),
             middle_grad.reshape(9, dp_size, mid_share, 256)
             .transpose(1, 0, 2, 3)
@@ -1330,22 +1355,25 @@
         ],
         1,
     )
-    packed_grads, pyramid_red = lax.optimization_barrier((packed_grads, pyramid_red))
-    trunk_red = (
-        lax.psum_scatter(packed_grads, "dp", scatter_dimension=0, tiled=True)
-        .reshape(packed_grads.shape[1:])
-        .astype(jnp.float32)
-    )
-    start = 2 * row_share
-    bottle_red = trunk_red[: 2 * row_share].reshape(bottle_weight.shape)
-    middle_red = trunk_red[start : start + 9 * mid_share].reshape(middle_weight.shape)
-    small_red = trunk_red[start + 9 * mid_share :].reshape(-1)
-    stem_red = small_red[: stem_weight.size].reshape(stem_weight.shape)
-    project_red = small_red[stem_weight.size : stem_weight.size + project_weight.size].reshape(
-        project_weight.shape
-    )
-    size = stem_weight.size + project_weight.size
+    early_grads, pyramid_red = lax.optimization_barrier((early_grads, pyramid_red))
+    early_red = lax.psum_scatter(early_grads, "dp", scatter_dimension=0, tiled=True)
+    late_grads = jnp.concatenate(
+        [
+            reduce_grad.reshape(dp_size, row_share * 256),
+            stem_grad.reshape(dp_size, stem_share * PATCH),
+        ],
+        1,
+    ).reshape(dp_size, -1, 256)
+    late_grads, early_red = lax.optimization_barrier((late_grads, early_red))
+    late_red = lax.psum_scatter(late_grads, "dp", scatter_dimension=0, tiled=True)
+    early_red = early_red[0].astype(jnp.float32)
+    late_red = late_red[0].astype(jnp.float32)
+    bottle_red = jnp.stack([late_red[:row_share], early_red[:row_share]])
+    middle_red = early_red[row_share : row_share + 9 * mid_share].reshape(middle_weight.shape)
+    small_red = early_red[row_share + 9 * mid_share :].reshape(-1)
+    project_red = small_red[:size].reshape(project_weight.shape)
     head_red = small_red[size : size + head_weight.size].reshape(head_weight.shape)
+    stem_red = late_red[row_share:].reshape(stem_share, PATCH).T.reshape(stem_weight.shape)
     pyramid_red = pyramid_red.astype(jnp.float32)
     norm_grad = jnp.stack(
         [

time: 706 us -> 773 us (1.095)
  waiting for transfers between devices: 160 us -> 298 us
  Pallas kernels: 341 us -> 293 us
  local copies, waits for them, and re-layouts: 67.5 us -> 55.5 us
    ppermute x6 -> x7, waiting for transfers between devices: 89.4 us -> 161 us  [swap_chan(): return lax.ppermute(values, 'chan', [(0, 1), (1, 0)])]
    pallas_call x1, Pallas kernels: 118 us -> 65.7 us  [gather_trunk(): pl.pallas_call(functools.partial(gather_kernel, count // 4), out_shape=[j...]
    reduce_scatter x1 -> x2, waiting for transfers between devices: 71 us -> 109 us  [the longest x1 57.6 us: on_device(): lax.psum_scatter(early_grads, 'dp', scatter_dimension=0, tiled=True)]
    all_gather x1, waiting for transfers between devices: 0.01 us -> 27.4 us  [on_device(): pyramid_low = lax.all_gather(pyramid_shard, 'dp', axis=1, tiled=True)]
    reshape x13 -> x10, local copies, waits for them, and re-layouts: 23.6 us -> 13 us  [the longest x2 6.27 us: on_device(): small_grads = jnp.concatenate([project_grad.astype(low).reshape(5 * 128,...]
    pallas_call x2 -> x1, Pallas kernels: 37.2 us -> 33 us  [pyramid_field(): pl.pallas_call(field_kernel, out_shape=jax.ShapeDtypeStruct((POSITIONS, d...]
  transfers between devices with their start and end apart: 9 -> 12, of which waited for: 4 -> 7; matrix products, arithmetic and copies ran while one was open for 19% -> 14% of each run, Pallas kernels for 33% -> 17%
where the time goes in v4:
time: 773 us; the launch traced here: 769 us
  waiting for transfers between devices  298 us (39%)
  Pallas kernels  293 us (38%)
  other arithmetic  72.9 us (9%)
  local copies, waits for them, and re-layouts  55.5 us (7%)
  between operations  23.7 us (3%)
  matrix products  17 us (2%)
  starting transfers between devices  8.75 us (1%)
    ppermute x7, waiting for transfers between devices, swap_chan(): return lax.ppermute(values, 'chan', [(0, 1), (1, 0)])  161 us
    pallas_call x1, Pallas kernels, gather_trunk(): pl.pallas_call(functools.partial(gather_kernel, count // 4), out_shape=[j...  65.7 us
    reduce_scatter x1, waiting for transfers between devices, on_device(): lax.psum_scatter(early_grads, 'dp', scatter_dimension=0, tiled=True)  57.6 us
    pallas_call x5, Pallas kernels, all_sum(): pl.pallas_call(functools.partial(sum_kernel, sizes, axes, count), out_sha...  55 us
    reduce_scatter x1, waiting for transfers between devices, on_device(): lax.psum_scatter(late_grads, 'dp', scatter_dimension=0, tiled=True)  51.6 us
    pallas_call x1, Pallas kernels, pyramid_forward(): pl.pallas_call(pyramid_kernel, out_shape=[jax.ShapeDtypeStruct((POSITIONS...  40.5 us
    pallas_call x1, Pallas kernels, pyramid_weights(): pl.pallas_call(weight_kernel, out_shape=jax.ShapeDtypeStruct((29, depth,...  37.6 us
    pallas_call x1, Pallas kernels, pyramid_field(): pl.pallas_call(field_kernel, out_shape=jax.ShapeDtypeStruct((POSITIONS, d...  33 us
  transfers between devices with their start and end apart: 12, of which 7 were waited for; matrix products, arithmetic and copies ran while one was open for 14% of the time, Pallas kernels for 17%

profile of v4, /device:TPU:0, one launch (start us, length us, event | category | flops | bytes accessed | tf_op | source)
XLA Modules:
  0.0 768.5 jit_solution(5396486121829688577)
XLA Ops:
  9.7 1.6 convert_element_type.163.bottle
  11.8 1.6 convert_element_type.164.middle
  13.4 2.7 convert_element_type.162
  16.8 65.7 %gather_trunk.1 = (bf16[2,2048,512]{2,1,0:T(8,128)(2,1)}, bf16[9,512,512]{2,1,0:T(8,128)(2,1)}, bf16[2048,384]{1,0:T(8,128)(2,1)}) custom-call(bf16[2,128,256]{2,1,0:T(8,128)(2,1)} %convert_element_type.163.bottle, bf16[9,32,256]{2,1,0:T(8,128)(2,1)} %convert_element_type.164.middle, bf16[64,384]{1,0:T(8,128)(2,1)} %pad_maximum_fusion.3.small), custom_call_target="tpu_custom_call" | custom-call | tf_op jit(solution)/shard_map/gather_trunk/pallas_call | solution.py:390
  84.1 1.7 copy.113
  86.6 1.2 fusion.58
  87.8 2.0 select_maximum_fusion
  89.8 11.3 %stem_reduce.1 = (bf16[1600,2048]{1,0:T(8,128)(2,1)}, f32[1600,512]{1,0:T(8,128)}, f32[8,512]{1,0:T(8,128)S(1)}) custom-call(bf16[1600,192]{1,0:T(8,128)(2,1)S(1)} %bitcast.150, bf16[2048,384]{1,0:T(8,128)(2,1)S(1)} %copy-done.6, bf16[2,2048,512]{2,1,0:T(8,128)(2,1)} %get-tuple-element.58.reduce_ref.w_ref, f32[1600,1]{1,0:T(8,128)S(1)} %copy.114.crop_ref, ...), custom_call_target="tpu_custom_call" | custom-call | flops 5000000000 | bytes 14680064 | tf_op jit(solution)/shard_map/stem_reduce/pallas_call | solution.py:693
  101.2 13.1 %small_sum.5.stat_ref.count_ref = f32[8,512]{1,0:T(8,128)S(1)} custom-call(f32[8,512]{1,0:T(8,128)S(1)} %get-tuple-element.60.x_ref), custom_call_target="tpu_custom_call" | custom-call | tf_op jit(solution)/shard_map/small_sum/pallas_call | solution.py:109
  118.1 2.5 fusion.41
  123.5 2.9 reshape.427
  126.4 2.1 copy.117
  130.6 2.3 pad.36.target_ref
  134.9 17.5 %norm_middle.1 = (bf16[1600,512]{1,0:T(8,128)(2,1)}, bf16[512,1600]{1,0:T(8,128)(2,1)}, bf16[1600,512]{1,0:T(8,128)(2,1)}) custom-call(f32[1600,512]{1,0:T(8,128)} %get-tuple-element.59.a_ref, f32[8,512]{1,0:T(8,128)S(1)} %small_sum.5.stat_ref.count_ref, f32[2,512]{1,0:T(2,128)S(1)} %pad_maximum_fusion.8.gain_ref, f32[1600,1]{1,0:T(8,128)S(1)} %copy.114.crop_ref, ...), custom_call_target="tpu_custom_call" | custom-call | flops 8000000000 | bytes 14680064 | tf_op jit(solution)/shard_map/norm_middle/pallas_call | solution.py:757
  152.4 1.4 copy-done.13
  153.8 8.8 %expand_forward.1 = (bf16[1600,2048]{1,0:T(8,128)(2,1)}, f32[8,512]{1,0:T(8,128)S(1)}) custom-call(bf16[1600,512]{1,0:T(8,128)(2,1)S(1)} %copy-done.13, bf16[2,2048,512]{2,1,0:T(8,128)(2,1)} %get-tuple-element.58.reduce_ref.w_ref, f32[1600,1]{1,0:T(8,128)S(1)} %copy.114.crop_ref), custom_call_target="tpu_custom_call" | custom-call | flops 4000000000 | bytes 12582912 | tf_op jit(solution)/shard_map/expand_forward/pallas_call | solution.py:794
  162.6 17.2 %small_sum.6.stat_ref = f32[8,512]{1,0:T(8,128)S(1)} custom-call(f32[8,512]{1,0:T(8,128)S(1)} %get-tuple-element.64.x_ref), custom_call_target="tpu_custom_call" | custom-call | tf_op jit(solution)/shard_map/small_sum/pallas_call | solution.py:109
  181.1 27.4 %all-gather.2.cloned.1.call-done.w_hbm = bf16[29,2048,128]{2,1,0:T(8,128)(2,1)} async-done(((bf16[29,128,128]{2,1,0:T(8,128)(2,1)}), bf16[29,2048,128]{2,1,0:T(8,128)(2,1)}) %all-gather.2.cloned.1.call-update) | async-done | bytes 15204368 | tf_op jit(solution)/shard_map/all_gather | solution.py:1127
  208.6 40.5 %pyramid_fwd.1 = (bf16[1600,2048]{1,0:T(8,128)(2,1)}, bf16[2048,1600]{1,0:T(8,128)(2,1)}, f32[1,2048]{1,0:T(1,128)}, f32[4,1600,128]{2,1,0:T(8,128)}, f32[1,128]...) custom-call(bf16[1600,192]{1,0:T(8,128)(2,1)} %bitcast.151, ...), custom_call_target="tpu_custom_call" | custom-call | flops 15938355200 | bytes 41943040 | tf_op jit(solution)/shard_map/pyramid_fwd/pallas_call | solution.py:933
  249.1 1.6 collective-permute-start.3
  251.8 1.8 multiply_add_fusion.2.mask_ref
  253.6 2.0 copy.122.pool_ref
  255.7 14.1 %collective-permute-done.3.other_ref = bf16[1600,256]{1,0:T(8,128)(2,1)S(1)} collective-permute-done((bf16[1600,256]{1,0:T(8,128)(2,1)}, bf16[1600,256]{1,0:T(8,128)(2,1)S(1)}, u32[]{:S(2)}, u32[]{:S(2)}) %collective-permute-start.3) | collective-permute-done | bytes 819232 | tf_op jit(solution)/shard_map/ppermute | solution.py:141
  271.5 9.6 %head_step.1 = (bf16[1600,256]{1,0:T(8,128)(2,1)S(1)}, bf16[1600,128]{1,0:T(8,128)(2,1)S(1)}, bf16[1600,256]{1,0:T(8,128)(2,1)S(1)}, bf16[4,1600,128]{2,1,0:T(8,...) custom-call(bf16[1600,256]{1,0:T(8,128)(2,1)S(1)} %copy-done.1, ...), custom_call_target="tpu_custom_call" | custom-call | flops 2000000000 | bytes 16777216 | tf_op jit(solution)/shard_map/head_step/pallas_call | solution.py:1037
  281.6 37.6 %pyramid_weights.1 = bf16[29,2048,128]{2,1,0:T(8,128)(2,1)} custom-call(bf16[2048,1600]{1,0:T(8,128)(2,1)} %get-tuple-element.69.xt_ref, bf16[4,1600,128]{2,1,0:T(8,128)(2,1)} %get-tuple-element.72.g_ref, f32[1600,128]{1,0:T(8,128)} %copy-done.2, f32[2048,1]{1,0:T(8,128)} %copy.122.pool_ref, f32[1,128]{1,0:T(1,128)} %copy-done.10), custom_call_target="tpu_custom_call" | custom-call | flops 15099494400 | bytes 26214400 | tf_op jit(solution)/shard_map/pyramid_weights/pallas_call | solution.py:572
  319.3 2.3 constant_dynamic-slice_fusion.3
  321.6 1.6 collective-permute-start
  323.2 79.3 %collective-permute-done.near_hbm = bf16[14,1024,128]{2,1,0:T(8,128)(2,1)} collective-permute-done((bf16[14,1024,128]{2,1,0:T(8,128)(2,1)S(1)}, bf16[14,1024,128]{2,1,0:T(8,128)(2,1)}, u32[]{:S(2)}, u32[]{:S(2)}) %collective-permute-start) | collective-permute-done | bytes 3670048 | tf_op jit(solution)/shard_map/ppermute | solution.py:141
  404.3 1.4 add_rsqrt_fusion
  405.8 4.7 fusion.60
  410.4 1.5 collective-permute-start.4
  412.7 1.3 fusion.21
  417.4 1.2 copy.125
  418.7 5.0 reshape.441
  425.0 24.0 %collective-permute-done.5 = f32[1,1024]{1,0:T(1,128)S(1)} collective-permute-done((f32[1,1024]{1,0:T(1,128)S(1)}, f32[1,1024]{1,0:T(1,128)S(1)}, u32[]{:S(2)}, u32[]{:S(2)}) %collective-permute-start.5) | collective-permute-done | bytes 4128 | tf_op jit(solution)/shard_map/ppermute | solution.py:141
  449.0 33.0 %pyramid_field.1 = f32[1600,1024]{1,0:T(8,128)} custom-call(s32[2]{0:T(128)} %pad_add_fusion.place_ref, bf16[29,2048,128]{2,1,0:T(8,128)(2,1)} %all-gather.2.cloned.1.call-done.w_hbm, bf16[14,1024,128]{2,1,0:T(8,128)(2,1)} %collective-permute-done.near_hbm, bf16[14,1024,128]{2,1,0:T(8,128)(2,1)} %collective-permute-done.1.far_hbm, ...), custom_call_target="tpu_custom_call" | custom-call | flops 14260633600 | bytes 26214400 | tf_op jit(solution)/shard_map/pyramid_field/pallas_call | solution.py:643
  482.1 4.2 fusion.1
  486.3 1.4 concatenate.77
  487.7 7.2 small_sum.7
  495.0 6.9 multiply_convert_fusion.1
  501.9 1.9 convolution_convert_fusion
  503.8 1.6 collective-permute-start.6
  505.3 2.1 convolution_convert_fusion.2
  509.0 43.9 %collective-permute-done.7 = bf16[1024,256]{1,0:T(8,128)(2,1)S(1)} collective-permute-done((bf16[1024,256]{1,0:T(8,128)(2,1)S(1)}, bf16[1024,256]{1,0:T(8,128)(2,1)S(1)}, u32[]{:S(2)}, u32[]{:S(2)}) %collective-permute-start.7) | collective-permute-done | bytes 524320 | tf_op jit(solution)/shard_map/ppermute | solution.py:141
  552.9 1.3 maximum_select_fusion
  555.8 4.2 middle_weights.1
  560.3 9.4 %middle_back.1 = f32[1600,512]{1,0:T(8,128)S(1)} custom-call(bf16[1600,512]{1,0:T(8,128)(2,1)S(1)} %add_convert_fusion.x_ref, bf16[9,512,512]{2,1,0:T(8,128)(2,1)S(1)} %bitcast.157, f32[1600,128]{1,0:T(8,128)S(1)} %copy-done.3), custom_call_target="tpu_custom_call" | custom-call | flops 7549747200 | bytes 16777216 | tf_op jit(solution)/shard_map/middle_back/pallas_call | solution.py:478
  569.8 3.8 multiply_reduce_fusion.1
  573.5 8.5 %small_sum.8 = f32[8,128]{1,0:T(8,128)S(1)} custom-call(f32[8,128]{1,0:T(8,128)S(1)} %pad_maximum_fusion.9.x_ref), custom_call_target="tpu_custom_call" | custom-call | tf_op jit(solution)/shard_map/small_sum/pallas_call | solution.py:109
  582.1 2.4 multiply_convert_fusion.2
  585.6 3.1 convolution_convert_fusion.1
  588.7 1.6 reshape.435
  590.3 3.1 pad_maximum_fusion
  593.5 1.5 copy-done.19
  595.0 7.4 convolution_convert_fusion.3
  602.4 1.2 copy.123
  604.3 1.4 copy.139
  605.7 57.6 %reduce-scatter.6.cloned.1.call-done = bf16[1,464,256]{2,1,0:T(8,128)(2,1)} async-done(((bf16[16,464,256]{2,1,0:T(8,128)(2,1)}), bf16[1,464,256]{2,1,0:T(8,128)(2,1)}) %reduce-scatter.6.cloned.1.call-update) | async-done | bytes 237584 | tf_op jit(solution)/shard_map/reduce_scatter | solution.py:1359
  673.6 51.6 %reduce-scatter.8.cloned.1.call-done = bf16[1,176,256]{2,1,0:T(8,128)(2,1)} async-done(((bf16[16,176,256]{2,1,0:T(8,128)(2,1)}), bf16[1,176,256]{2,1,0:T(8,128)(2,1)}) %reduce-scatter.8.cloned.1.call-update) | async-done | bytes 90128 | tf_op jit(solution)/shard_map/reduce_scatter | solution.py:1368
  732.9 8.9 %small_sum.9 = f32[8,128]{1,0:T(8,128)S(1)} custom-call(f32[8,128]{1,0:T(8,128)S(1)} %pad_bitcast_fusion.1.x_ref), custom_call_target="tpu_custom_call" | custom-call | tf_op jit(solution)/shard_map/small_sum/pallas_call | solution.py:109
  746.3 1.4 multiply_subtract_fusion.7
  747.6 1.4 multiply_subtract_fusion.5
  749.0 2.2 multiply_subtract_fusion.2
  751.4 5.9 multiply_subtract_fusion
  (255 shorter events, 52.2 us)
Async XLA Ops:
  7.2 75.3 %copy-start.35 = (f32[2,1,1280]{2,1,0:T(1,128)S(1)}, f32[2,1,1280]{2,1,0:T(1,128)}, u32[]{:S(2)}) copy-start(f32[2,1,1280]{2,1,0:T(1,128)} %param.56) | copy-start | bytes 30724
  7.2 76.5 %copy-start.48 = (f32[25]{0:T(128)S(1)}, f32[25]{0:T(128)}, u32[]{:S(2)}) copy-start(f32[25]{0:T(128)} %param.59) | copy-start | bytes 304
  7.2 76.6 %copy-start.40 = (s32[1,1600]{1,0:T(1,128)S(1)}, s32[1,1600]{1,0:T(1,128)}, u32[]{:S(2)}) copy-start(s32[1,1600]{1,0:T(1,128)} %param.37) | copy-start | bytes 19204
  7.2 201.3 %all-gather.2.cloned.1.call-start = ((), (), s32[]{:S(2)}) async-start(), calls=%async_computation.3 | async-start | bytes 16154624 | tf_op jit(solution)/shard_map/all_gather | solution.py:1127
  13.4 73.1 %copy-start.46 = (s32[1,1600]{1,0:T(1,128)S(1)}, s32[1,1600]{1,0:T(1,128)}, u32[]{:S(2)}) copy-start(s32[1,1600]{1,0:T(1,128)} %param.36) | copy-start | bytes 19204
  13.4 73.1 %copy-start.47 = (s32[1,1600]{1,0:T(1,128)S(1)}, s32[1,1600]{1,0:T(1,128)}, u32[]{:S(2)}) copy-start(s32[1,1600]{1,0:T(1,128)} %param.34) | copy-start | bytes 19204
  82.4 7.4 copy-start.6
  82.5 511.0 %reduce-scatter.4.cloned.1.call-start = ((), (), s32[]{:S(2)}) async-start(), calls=%async_computation.4 | async-start | bytes 16154624 | tf_op jit(solution)/shard_map/reduce_scatter | solution.py:1265
  82.5 51.1 %collective-permute-start.2 = (f32[2,1,1280]{2,1,0:T(1,128)S(1)}, f32[2,1,1280]{2,1,0:T(1,128)}, u32[]{:S(2)}, u32[]{:S(2)}) collective-permute-start(f32[2,1,1280]{2,1,0:T(1,128)S(1)} %copy-done.35), channel_id=1, source_target_pairs={{0,1},{1,0},{2,3},{3,2},{4,5},{5,4},{6,7},{7,6},{8,9},{9,8},{10,11... | collective-permute-start | bytes 30728 | tf_op jit(solution)/shard_map/ppermute | solution.py:141
  84.1 68.3 %copy-start.4 = (f32[1600,1]{1,0:T(8,128)}, f32[1600,1]{1,0:T(8,128)S(1)}, u32[]{:S(2)}) copy-start(f32[1600,1]{1,0:T(8,128)S(1)} %copy.114.crop_ref) | copy-start | bytes 19204
  85.8 15.4 %copy-start.5 = (bf16[1,1600,192]{2,1,0:T(8,128)(2,1)}, bf16[1,1600,192]{2,1,0:T(8,128)(2,1)S(1)}, u32[]{:S(2)}) copy-start(bf16[1,1600,192]{2,1,0:T(8,128)(2,1)S(1)} %copy.113) | copy-start | bytes 1843204
  89.8 28.3 %copy-start.41 = (f32[1,2,1600]{2,1,0:T(2,128)S(1)}, f32[1,2,1600]{2,1,0:T(2,128)}, u32[]{:S(2)}) copy-start(f32[1,2,1600]{2,1,0:T(2,128)} %param.33) | copy-start | bytes 38404
  89.8 28.3 %copy-start.44 = (f32[1,1600]{1,0:T(1,128)S(1)}, f32[1,1600]{1,0:T(1,128)}, u32[]{:S(2)}) copy-start(f32[1,1600]{1,0:T(1,128)} %param.35) | copy-start | bytes 19204
  89.8 32.4 %copy-start.45 = (s32[1,1600]{1,0:T(1,128)S(1)}, s32[1,1600]{1,0:T(1,128)}, u32[]{:S(2)}) copy-start(s32[1,1600]{1,0:T(1,128)} %param.32) | copy-start | bytes 19204
  114.3 20.6 %copy-start.9 = (f32[8,512]{1,0:T(8,128)}, f32[8,512]{1,0:T(8,128)S(1)}, u32[]{:S(2)}) copy-start(f32[8,512]{1,0:T(8,128)S(1)} %small_sum.5.stat_ref.count_ref) | copy-start | bytes 49156
  128.5 6.1 copy-start.36
  134.9 17.5 %copy-start.2 = (f32[1600,128]{1,0:T(8,128)}, f32[1600,128]{1,0:T(8,128)S(1)}, u32[]{:S(2)}) copy-start(f32[1600,128]{1,0:T(8,128)S(1)} %broadcast_in_dim.14.col_ref) | copy-start | bytes 2457604
  152.4 1.4 copy-start.13
  208.6 43.2 %copy-start.37 = (f32[1600]{0:T(1024)S(1)}, f32[1600]{0:T(1024)}, u32[]{:S(2)}) copy-start(f32[1600]{0:T(1024)} %get-tuple-element.174) | copy-start | bytes 19204
  208.6 43.2 %copy-start.38 = (f32[1600]{0:T(1024)S(1)}, f32[1600]{0:T(1024)}, u32[]{:S(2)}) copy-start(f32[1600]{0:T(1024)} %get-tuple-element.195) | copy-start | bytes 19204
  208.6 43.2 %copy-start.51 = (f32[128]{0:T(128)S(1)}, f32[128]{0:T(128)}, u32[]{:S(2)}) copy-start(f32[128]{0:T(128)} %compare_convert_fusion.1) | copy-start | bytes 1540
  208.6 43.2 %copy-start.52 = (f32[128]{0:T(128)S(1)}, f32[128]{0:T(128)}, u32[]{:S(2)}) copy-start(f32[128]{0:T(128)} %get-tuple-element.209) | copy-start | bytes 1540
  208.6 43.2 %copy-start.53 = (f32[128]{0:T(128)S(1)}, f32[128]{0:T(128)}, u32[]{:S(2)}) copy-start(f32[128]{0:T(128)} %get-tuple-element.210) | copy-start | bytes 1540
  208.6 61.2 %copy-start = (bf16[640,256]{1,0:T(8,128)(2,1)S(1)}, bf16[640,256]{1,0:T(8,128)(2,1)}, u32[]{:S(2)}) copy-start(bf16[640,256]{1,0:T(8,128)(2,1)} %copy.119.project_ref) | copy-start | bytes 983044
  249.1 20.7 %collective-permute-start.3 = (bf16[1600,256]{1,0:T(8,128)(2,1)}, bf16[1600,256]{1,0:T(8,128)(2,1)S(1)}, u32[]{:S(2)}, u32[]{:S(2)}) collective-permute-start(bf16[1600,256]{1,0:T(8,128)(2,1)} %get-tuple-element.65.own_ref), channel_id=1, source_target_pairs={{0,1},{1,0},{2,3},{3,2},{4,5},{5,4},{6,7},{7,6},{8,9},{9,8},{10,11... | collective-permute-start | bytes 2457608 | tf_op jit(solution)/shard_map/ppermute | solution.py:141
  319.2 344.0 %reduce-scatter.6.cloned.1.call-start = ((), (), s32[]{:S(2)}) async-start(), calls=%async_computation.5 | async-start | bytes 4038656 | tf_op jit(solution)/shard_map/reduce_scatter | solution.py:1359
  321.6 80.9 %collective-permute-start = (bf16[14,1024,128]{2,1,0:T(8,128)(2,1)S(1)}, bf16[14,1024,128]{2,1,0:T(8,128)(2,1)}, u32[]{:S(2)}, u32[]{:S(2)}) collective-permute-start(bf16[14,1024,128]{2,1,0:T(8,128)(2,1)S(1)} %constant_dynamic-slice_fusion.3), channel_id=1, source_target_pairs={{0,1},{1,0},{2,3},{3,2},{4,5},{5,4},{6,7},{7,6},{8,9},{9,8},{10,11... | collective-permute-start | bytes 11010056 | tf_op jit(solution)/shard_map/ppermute | solution.py:141
  402.5 46.5 %collective-permute-start.1 = (bf16[14,1024,128]{2,1,0:T(8,128)(2,1)}, bf16[14,1024,128]{2,1,0:T(8,128)(2,1)}, u32[]{:S(2)}, u32[]{:S(2)}) collective-permute-start(bf16[14,1024,128]{2,1,0:T(8,128)(2,1)} %collective-permute-done.near_hbm), channel_id=1, source_target_pairs={{0,2},{2,0},{4,6},{6,4},{8,10},{10,8},{12,14},{14,12},{16,18},{18,... | collective-permute-start | bytes 11010056 | tf_op jit(solution)/shard_map/ppermute | solution.py:1146
  405.7 6.2 copy-start.8
  405.7 6.9 copy-start.11
  405.8 9.8 %copy-start.54 = (bf16[1600,640]{1,0:T(8,128)(2,1)S(1)}, bf16[1600,640]{1,0:T(8,128)(2,1)}, u32[]{:S(2)}) copy-start(bf16[1600,640]{1,0:T(8,128)(2,1)} %get-tuple-element.76) | copy-start | bytes 6144004
  410.4 38.6 %collective-permute-start.4 = (bf16[4,1600,128]{2,1,0:T(8,128)(2,1)}, bf16[4,1600,128]{2,1,0:T(8,128)(2,1)}, u32[]{:S(2)}, u32[]{:S(2)}) collective-permute-start(bf16[4,1600,128]{2,1,0:T(8,128)(2,1)} %get-tuple-element.72.g_ref), channel_id=1, source_target_pairs={{0,1},{1,0},{2,3},{3,2},{4,5},{5,4},{6,7},{7,6},{8,9},{9,8},{10,11... | collective-permute-start | bytes 4915208 | tf_op jit(solution)/shard_map/ppermute | solution.py:141
  414.7 34.3 %collective-permute-start.5 = (f32[1,1024]{1,0:T(1,128)S(1)}, f32[1,1024]{1,0:T(1,128)S(1)}, u32[]{:S(2)}, u32[]{:S(2)}) collective-permute-start(f32[1,1024]{1,0:T(1,128)S(1)} %bitcast.198), channel_id=1, source_target_pairs={{0,1},{1,0},{2,3},{3,2},{4,5},{5,4},{6,7},{7,6},{8,9},{9,8},{10,11... | collective-permute-start | bytes 12296 | tf_op jit(solution)/shard_map/ppermute | solution.py:141
  449.0 33.1 %slice-start.2 = ((s8[6553600]{0:T(1024)(128)(4,1)}), s8[4194304]{0:T(1024)(128)(4,1)S(1)}, s32[]{:S(2)}) async-start(s8[6553600]{0:T(1024)(128)(4,1)} %bitcast.161), calls=%async_computation.9 | async-start | bytes 8388608
  449.0 33.1 %slice-start.3 = ((s8[6553600]{0:T(1024)(128)(4,1)}), s8[2359296]{0:T(1024)(128)(4,1)S(1)}, s32[]{:S(2)}) async-start(s8[6553600]{0:T(1024)(128)(4,1)} %bitcast.161), calls=%async_computation.10 | async-start | bytes 4718592
  495.0 6.9 copy-start.20
  501.9 3.5 copy-start.14
  503.8 50.4 %collective-permute-start.6 = (bf16[1600,512]{1,0:T(8,128)(2,1)S(1)}, bf16[1600,512]{1,0:T(8,128)(2,1)S(1)}, u32[]{:S(2)}, u32[]{:S(2)}) collective-permute-start(bf16[1600,512]{1,0:T(8,128)(2,1)S(1)} %convolution_convert_fusion), channel_id=1, source_target_pairs={{0,1},{1,0},{2,3},{3,2},{4,5},{5,4},{6,7},{7,6},{8,9},{9,8},{10,11... | collective-permute-start | bytes 4915208 | tf_op jit(solution)/shard_map/ppermute | solution.py:141
  507.5 45.3 %collective-permute-start.7 = (bf16[1024,256]{1,0:T(8,128)(2,1)S(1)}, bf16[1024,256]{1,0:T(8,128)(2,1)S(1)}, u32[]{:S(2)}, u32[]{:S(2)}) collective-permute-start(bf16[1024,256]{1,0:T(8,128)(2,1)S(1)} %get-tuple-element.180), channel_id=1, source_target_pairs={{0,1},{1,0},{2,3},{3,2},{4,5},{5,4},{6,7},{7,6},{8,9},{9,8},{10,11... | collective-permute-start | bytes 1572872 | tf_op jit(solution)/shard_map/ppermute | solution.py:141
  554.1 1.7 copy-start.15
  554.1 6.2 slice-start
  555.8 4.5 slice-start.1
  560.1 25.6 %slice-start.4 = ((s8[6553600]{0:T(1024)(128)(4,1)}), s8[4194304]{0:T(1024)(128)(4,1)S(1)}, s32[]{:S(2)}) async-start(s8[6553600]{0:T(1024)(128)(4,1)} %bitcast.199), calls=%async_computation.11 | async-start | bytes 8388608
  560.3 9.4 %copy-start.16 = (f32[1600,512]{1,0:T(8,128)S(1)}, f32[1600,512]{1,0:T(8,128)}, u32[]{:S(2)}) copy-start(f32[1600,512]{1,0:T(8,128)} %get-tuple-element.59.a_ref) | copy-start | bytes 9830404
  560.3 25.3 %slice-start.5 = ((s8[6553600]{0:T(1024)(128)(4,1)}), s8[2359296]{0:T(1024)(128)(4,1)S(1)}, s32[]{:S(2)}) async-start(s8[6553600]{0:T(1024)(128)(4,1)} %bitcast.199), calls=%async_computation.12 | async-start | bytes 4718592
  593.4 1.6 copy-start.19
  593.4 131.8 %reduce-scatter.8.cloned.1.call-start = ((), (), s32[]{:S(2)}) async-start(), calls=%async_computation.6 | async-start | bytes 1531904 | tf_op jit(solution)/shard_map/reduce_scatter | solution.py:1368
  604.3 63.8 %copy-start.18 = (bf16[29,128,128]{2,1,0:T(8,128)(2,1)S(1)}, bf16[29,128,128]{2,1,0:T(8,128)(2,1)}, u32[]{:S(2)}) copy-start(bf16[29,128,128]{2,1,0:T(8,128)(2,1)} %reduce-scatter.4.cloned.1.call-done) | copy-start | bytes 2850820
  663.4 4.7 copy-start.50
  664.1 4.0 copy-start.49
  668.1 83.2 %copy-start.17 = (f32[29,128,128]{2,1,0:T(8,128)S(1)}, f32[29,128,128]{2,1,0:T(8,128)}, u32[]{:S(2)}) copy-start(f32[29,128,128]{2,1,0:T(8,128)} %param.47) | copy-start | bytes 5701636
  751.2 6.1 copy-start.39
  751.2 6.1 copy-start.42
  751.2 6.1 copy-start.43
  751.3 6.7 copy-start.28
  751.3 6.7 copy-start.30
  751.3 6.7 copy-start.31
  751.3 7.4 copy-start.29
  751.3 7.4 copy-start.33
  751.3 7.4 copy-start.34
  751.3 8.0 %copy-start.22 = (f32[9,32,256]{2,1,0:T(8,128)S(1)}, f32[9,32,256]{2,1,0:T(8,128)}, u32[]{:S(2)}) copy-start(f32[9,32,256]{2,1,0:T(8,128)} %param.44) | copy-start | bytes 884740
  751.3 8.0 %copy-start.23 = (f32[1,288,256]{2,1,0:T(8,128)S(1)}, f32[1,288,256]{2,1,0:T(8,128)}, u32[]{:S(2)}) copy-start(f32[1,288,256]{2,1,0:T(8,128)} %slice_multiply_fusion) | copy-start | bytes 884740
  751.3 8.0 %copy-start.26 = (f32[9,32,256]{2,1,0:T(8,128)S(1)}, f32[9,32,256]{2,1,0:T(8,128)}, u32[]{:S(2)}) copy-start(f32[9,32,256]{2,1,0:T(8,128)} %param.45) | copy-start | bytes 884740
  751.4 8.0 %copy-start.27 = (f32[9,32,256]{2,1,0:T(8,128)S(1)}, f32[9,32,256]{2,1,0:T(8,128)}, u32[]{:S(2)}) copy-start(f32[9,32,256]{2,1,0:T(8,128)} %param.46) | copy-start | bytes 884740
  (9 other events, 7.2 us)
Sparse Core Ops, SparseCore 0:
  82.6 125.9 all-gather.1
  319.4 152.2 reduce-scatter.3
  593.6 69.6 reduce-scatter.5
  667.3 57.8 reduce-scatter.7

commit v5 on v3

--- a/solution.py
+++ b/solution.py
@@ -224,9 +224,11 @@
     bottle,
     middle,
     small,
+    head,
     bottle_all,
     middle_all,
     small_all,
+    head_all,
     send_sems,
     recv_sems,
     local_sems,
@@ -234,7 +236,9 @@
     z, y, core, x = place_of()
     rows = bottle.shape[1]
     mid_rows = middle.shape[1]
-    own_refs = (bottle, middle, small)
+    small_rows = small.shape[0]
+    head_rows = head.shape[0]
+    own_refs = (bottle, middle, small, head)
 
     def region(kind, block):
         zz, yy, kk, xx = block
@@ -244,7 +248,10 @@
             return bottle_all.at[:, pl.ds(pl.multiple_of(index * rows, 16), rows), cols]
         if kind == 1:
             return middle_all.at[:, pl.ds(pl.multiple_of(index * mid_rows, 16), mid_rows), cols]
-        return small_all.at[index, xx]
+        if kind == 3:
+            return head_all.at[pl.ds(pl.multiple_of(index * head_rows, 16), head_rows)]
+        first = xx * (small_all.shape[0] // 2) + index * small_rows
+        return small_all.at[pl.ds(pl.multiple_of(first, 16), small_rows)]
 
     def semaphore(kind, block):
         zz, yy, kk, xx = block
@@ -280,7 +287,7 @@
 
     locals_ = [
         pltpu.make_async_copy(own_refs[kind], region(kind, own), local_sems.at[kind])
-        for kind in range(3)
+        for kind in range(4)
     ]
     for copy in locals_:
         copy.start()
@@ -310,9 +317,11 @@
     send(1, own, other_x)
     send(0, own, other_y)
     along_z(2, own)
+    along_z(3, own)
+    send(3, own, other_y)
     send(0, own, other_x)
     send(1, own, other_y)
-    for kind in range(3):
+    for kind in range(4):
         send(kind, own, sibling)
 
     block = (z, y, core, 1 - x)
@@ -336,6 +345,11 @@
                 send(kind, block, near)
                 send(kind, block, far)
                 send(kind, block, sibling)
+            block = (zz, y, core, x)
+            arrive(3, block)
+            along_z(3, block)
+            send(3, block, other_y)
+            send(3, block, sibling)
         block = (zz, 1 - y, core, x)
         arrive(0, block)
         send(0, block, other_x)
@@ -360,11 +374,14 @@
             block = (zz, 1 - y, core, xx)
             arrive(1, block)
             send(1, block, sibling)
-    for kind in range(3):
+        block = (zz, 1 - y, core, x)
+        arrive(3, block)
+        send(3, block, sibling)
+    for kind in range(4):
         for turn in range(layers):
             zz = z if turn == 0 else z_flip(z, turn)
             for yy in (y, 1 - y):
-                for xx in (x, 1 - x):
+                for xx in (x, 1 - x) if kind < 3 else (x,):
                     arrive(kind, (zz, yy, 1 - core, xx))
     for copy in locals_:
         copy.wait()
@@ -375,7 +392,7 @@
             pl.when(when)(copy.wait_send)
 
 
-def gather_trunk(sizes, bottle, middle, small):
+def gather_trunk(sizes, bottle, middle, small, head):
     count = sizes["dp"]
     if count != 16 or middle.shape[1] % 16:
         packed = [
@@ -384,24 +401,28 @@
             )
             for part in (bottle, middle)
         ]
-        return packed + [lax.all_gather(small, ("dp", "chan")).reshape((count, 2) + small.shape)]
+        return packed + [
+            lax.all_gather(small, ("chan", "dp")).reshape(D, small.shape[1]),
+            lax.all_gather(head, "dp", axis=0, tiled=True),
+        ]
     return pl.pallas_call(
         functools.partial(gather_kernel, count // 4),
         out_shape=[
             jax.ShapeDtypeStruct((2, D, MID), jnp.bfloat16),
             jax.ShapeDtypeStruct((9, MID, MID), jnp.bfloat16),
-            jax.ShapeDtypeStruct((count, 2) + small.shape, jnp.bfloat16),
-        ],
-        in_specs=[pl.BlockSpec(memory_space=pl.ANY)] * 3,
-        out_specs=[pl.BlockSpec(memory_space=pl.ANY)] * 3,
+            jax.ShapeDtypeStruct((D, small.shape[1]), jnp.bfloat16),
+            jax.ShapeDtypeStruct((BRANCH, head.shape[1]), jnp.bfloat16),
+        ],
+        in_specs=[pl.BlockSpec(memory_space=pl.ANY)] * 4,
+        out_specs=[pl.BlockSpec(memory_space=pl.ANY)] * 4,
         scratch_shapes=[
-            pltpu.SemaphoreType.DMA((160,)),
-            pltpu.SemaphoreType.DMA((3, 2 * count)),
-            pltpu.SemaphoreType.DMA((3,)),
+            pltpu.SemaphoreType.DMA((176,)),
+            pltpu.SemaphoreType.DMA((4, 2 * count)),
+            pltpu.SemaphoreType.DMA((4,)),
         ],
         compiler_params=pltpu.CompilerParams(collective_id=5, has_side_effects=True),
         name="gather_trunk",
-    )(bottle, middle, small)
+    )(bottle, middle, small, head)
 
 
 PAD = 128
@@ -430,6 +451,13 @@
 PLACE_ORDER = [place for group in ROW_GROUPS for tap, place in group]
 
 
+EARLY_TAPS = 10
+
+
+def tap_of(early, late, tap):
+    return early.at[tap] if tap < EARLY_TAPS else late.at[tap - EARLY_TAPS]
+
+
 def roll_cols(values, columns, step):
     if step == 0:
         return values
@@ -575,26 +603,35 @@
         scratch_shapes=[pltpu.VMEM((10, POSITIONS + 2 * PAD, width), jnp.bfloat16)],
         compiler_params=pltpu.CompilerParams(vmem_limit_bytes=56 << 20),
         cost_estimate=pl.CostEstimate(
-            flops=2 * POSITIONS * 18 * depth * width, bytes_accessed=25 << 20, transcendentals=0
+            flops=3 * 10**10, bytes_accessed=20 << 20, transcendentals=0
         ),
         name="pyramid_weights",
     )(field_t, grads, columns, pooled, pool_grad)
 
 
-def field_kernel(half_ref, w_hbm, g_ref, col_ref, o_ref, weights, fields, stack, sems):
+def field_kernel(
+    half_ref, a_hbm, b_hbm, g_ref, pool_ref, crop_ref, col_ref, o_ref, weights, pool_weights, fields, stack, sems
+):
     width = g_ref.shape[2]
     depth = o_ref.shape[1]
     half = pl.ds(pl.multiple_of(half_ref[0] * depth, 16), depth)
     copies = []
     for slot, tap in enumerate(TAP_ORDER):
         copy = pltpu.make_async_copy(
-            w_hbm.at[tap, half], weights.at[:, pl.ds(slot * width, width)], sems.at[slot]
+            tap_of(a_hbm, b_hbm, tap).at[half], weights.at[:, pl.ds(slot * width, width)], sems.at[slot]
         )
         copy.start()
         copies.append(copy)
+    copies.append(
+        pltpu.make_async_copy(tap_of(a_hbm, b_hbm, 28).at[half], pool_weights, sems.at[28])
+    )
+    copies[-1].start()
     fill_fields(g_ref, col_ref, fields)
     for copy in copies:
         copy.wait()
+    pooled = dot(
+        jnp.broadcast_to(pool_ref[...], (16, width)).astype(jnp.bfloat16), pool_weights[...], (1, 1)
+    )[0:1] / jnp.sum(crop_ref[...], keepdims=True)
     step_of = [step for step, group in zip(PYRAMID_ROWS, ROW_GROUPS) for entry in group]
     for r0, r1 in ((0, 4), (4, 12), (12, 16), (16, 24), (24, 28), (28, 36), (36, 40)):
         slots = [
@@ -606,37 +643,44 @@
             stack[:count, at * width : (at + 1) * width] = fields[
                 PLACE_ORDER[slot], base : base + count
             ]
-        o_ref[r0 * FW : r1 * FW] = dot(
+        part = dot(
             stack[:count, : len(slots) * width],
             weights[:, slots[0] * width : (slots[-1] + 1) * width],
             (1, 1),
-        ).astype(o_ref.dtype)
-
-
-def pyramid_field(half, weights, grads, columns):
-    depth, width = weights.shape[1] // 2, weights.shape[2]
+        )
+        o_ref[r0 * FW : r1 * FW] = (part + crop_ref[r0 * FW : r1 * FW] * pooled).astype(
+            o_ref.dtype
+        )
+
+
+def pyramid_field(half, weights, grads, pool_grad, crop, columns):
+    depth, width = weights[0].shape[1] // 2, weights[0].shape[2]
     return pl.pallas_call(
         field_kernel,
         out_shape=jax.ShapeDtypeStruct((POSITIONS, depth), jnp.bfloat16),
         in_specs=[
             pl.BlockSpec(memory_space=pltpu.SMEM),
             pl.BlockSpec(memory_space=pl.ANY),
+            pl.BlockSpec(memory_space=pl.ANY),
+            pl.BlockSpec(memory_space=pltpu.VMEM),
+            pl.BlockSpec(memory_space=pltpu.VMEM),
             pl.BlockSpec(memory_space=pltpu.VMEM),
             pl.BlockSpec(memory_space=pltpu.VMEM),
         ],
         out_specs=vmem(1)[0],
         scratch_shapes=[
             pltpu.VMEM((depth, 28 * width), jnp.bfloat16),
+            pltpu.VMEM((depth, width), jnp.bfloat16),
             pltpu.VMEM((10, POSITIONS + 2 * PAD, width), jnp.bfloat16),
             pltpu.VMEM((8 * FW, 19 * width), jnp.bfloat16),
-            pltpu.SemaphoreType.DMA((28,)),
+            pltpu.SemaphoreType.DMA((29,)),
         ],
         compiler_params=pltpu.CompilerParams(vmem_limit_bytes=56 << 20),
         cost_estimate=pl.CostEstimate(
-            flops=2 * POSITIONS * 17 * depth * width, bytes_accessed=15 << 20, transcendentals=0
+            flops=3 * 10**10, bytes_accessed=20 << 20, transcendentals=0
         ),
         name="pyramid_field",
-    )(half, weights, grads, columns)
+    )(half, weights[0], weights[1], grads, pool_grad, crop, columns)
 
 
 BLOCK = 320
@@ -653,7 +697,7 @@
 def stem_kernel(p_ref, stem_ref, reduce_ref, crop_ref, count_ref, x_ref, a_ref, stat_ref):
     def step(index, carry):
         rows = block_rows(index)
-        low = (crop_ref[rows] * dot(p_ref[rows], stem_ref[...])).astype(x_ref.dtype)
+        low = (crop_ref[rows] * dot(p_ref[rows], stem_ref[...], (1, 1))).astype(x_ref.dtype)
         x_ref[rows] = low
         value = dot(low, reduce_ref[0])
         a_ref[rows] = value
@@ -680,7 +724,7 @@
         ],
         in_specs=[
             pl.BlockSpec((POSITIONS, PATCH), lambda i: (0, 0)),
-            pl.BlockSpec((PATCH, D), lambda i: (0, 0)),
+            pl.BlockSpec(stem.shape, lambda i: (0, 0)),
             pl.BlockSpec((1, D, MID), lambda i: (0, 0, 0)),
             pl.BlockSpec((POSITIONS, 1), lambda i: (0, 0)),
             pl.BlockSpec((1, MID), lambda i: (0, 0)),
@@ -696,18 +740,26 @@
     )(patches, stem, bottle, crop, counts)
 
 
+def both_halves(gain_refs, first, last):
+    place_ref, own_ref, other_ref = gain_refs
+    own, other = own_ref[:, first:last], other_ref[:, first:last]
+    lower = place_ref[0] == 0
+    return jnp.concatenate([jnp.where(lower, own, other), jnp.where(lower, other, own)], 1)
+
+
 def norm_rows(stat, count):
     mean = stat[0:1] / count
     return mean, lax.rsqrt(stat[1:2] / count - mean * mean + norm_eps)
 
 
 def norm_middle_kernel(
-    a_ref, stat_ref, gain_ref, crop_ref, w_ref, col_ref, h_ref, ht_ref, o_ref, canvas
+    a_ref, stat_ref, place_ref, own_ref, other_ref, crop_ref, w_ref, col_ref, h_ref, ht_ref, o_ref, canvas
 ):
     edge = 4 * FW
     mean, scale = norm_rows(stat_ref[...], stat_ref[2:3, 0:1])
-    gain = gain_ref[0:1] * scale
-    shift = gain_ref[1:2] - mean * gain
+    pair = both_halves((place_ref, own_ref, other_ref), 0, MID // 2)
+    gain = pair[0:1] * scale
+    shift = pair[1:2] - mean * gain
     low = (crop_ref[...] * jax.nn.gelu(a_ref[...] * gain + shift)).astype(h_ref.dtype)
     h_ref[...] = low
     ht_ref[...] = low.T
@@ -741,13 +793,13 @@
             jax.ShapeDtypeStruct((MID, POSITIONS), jnp.bfloat16),
             jax.ShapeDtypeStruct((POSITIONS, MID), jnp.bfloat16),
         ],
-        in_specs=vmem(6),
+        in_specs=vmem(2) + [pl.BlockSpec(memory_space=pltpu.SMEM)] + vmem(5),
         out_specs=vmem(3),
         scratch_shapes=[pltpu.VMEM((3, POSITIONS + 8 * FW, MID), jnp.bfloat16)],
         compiler_params=pltpu.CompilerParams(vmem_limit_bytes=50 << 20),
         cost_estimate=pl.CostEstimate(flops=8 * 10**9, bytes_accessed=14 << 20, transcendentals=0),
         name="norm_middle",
-    )(first_pre, stat, gains, crop, weights, columns)
+    )(first_pre, stat, *gains, crop, weights, columns)
 
 
 def expand_kernel(a_ref, w_ref, crop_ref, y_ref, stat_ref):
@@ -793,20 +845,58 @@
     )(second, bottle, crop)
 
 
+def residual_kernel(
+    p_ref, stem_ref, y_ref, stat_ref, count_ref, place_ref, own_ref, other_ref, crop_ref, x_ref, xt_ref, pool_ref
+):
+    count = count_ref[2:3, 0:1]
+    stat = stat_ref[...]
+    total = jnp.concatenate([stat[part : part + 1] for part in range(4)], 1)
+    square = jnp.concatenate([stat[part : part + 1] for part in range(4, 8)], 1)
+    mean = total / count
+    pair = both_halves((place_ref, own_ref, other_ref), MID // 2, MID // 2 + D // 2)
+    gain = pair[0:1] * lax.rsqrt(square / count - mean * mean + norm_eps)
+    shift = pair[1:2] - mean * gain
+
+    def residual(index, carry):
+        rows = block_rows(index)
+        value = dot(p_ref[rows], stem_ref[...], (1, 1)) + (
+            y_ref[rows].astype(jnp.float32) * gain + shift
+        )
+        low = (crop_ref[rows] * value).astype(x_ref.dtype)
+        x_ref[rows] = low
+        return carry + jnp.sum(low.astype(jnp.float32), 0, keepdims=True)
+
+    pooled = lax.fori_loop(0, POSITIONS // BLOCK, residual, jnp.zeros((1, D), jnp.float32))
+    pooled = (pooled / jnp.sum(crop_ref[...], keepdims=True)).astype(jnp.bfloat16)
+    pool_ref[...] = pooled.astype(jnp.float32)
+    for at in range(0, D, 256):
+        xt_ref[at : at + 256] = x_ref[:, at : at + 256].T
+
+
+def residual_stream(patches, stem, expanded, stat, counts, gains, crop):
+    low = jnp.bfloat16
+    return pl.pallas_call(
+        residual_kernel,
+        out_shape=[
+            jax.ShapeDtypeStruct((POSITIONS, D), low),
+            jax.ShapeDtypeStruct((D, POSITIONS), low),
+            jax.ShapeDtypeStruct((1, D), jnp.float32),
+        ],
+        in_specs=vmem(5) + [pl.BlockSpec(memory_space=pltpu.SMEM)] + vmem(3),
+        out_specs=vmem(3),
+        compiler_params=pltpu.CompilerParams(vmem_limit_bytes=50 << 20),
+        cost_estimate=pl.CostEstimate(flops=2 * 10**9, bytes_accessed=22 << 20, transcendentals=0),
+        name="residual_stream",
+    )(patches, stem, expanded, stat, counts, *gains, crop)
+
+
 def pyramid_kernel(
-    p_ref,
-    stem_ref,
-    y_ref,
-    stat_ref,
-    count_ref,
-    gain_ref,
-    crop_ref,
-    w_hbm,
+    x_ref,
+    pool_ref,
+    a_hbm,
+    b_hbm,
     project_ref,
     col_ref,
-    x_ref,
-    xt_ref,
-    pool_ref,
     o_ref,
     pool_pre_ref,
     cat_ref,
@@ -829,34 +919,13 @@
         for offset, (tap, _) in enumerate(ROW_GROUPS[turn]):
             slot = starts[turn] + offset
             copy = pltpu.make_async_copy(
-                w_hbm.at[tap], weights.at[:, pl.ds(slot * width, width)], sems.at[slot]
+                tap_of(a_hbm, b_hbm, tap), weights.at[:, pl.ds(slot * width, width)], sems.at[slot]
             )
             copy.start()
             group_copies.append(copy)
         copies.append(group_copies)
-    pool_copy = pltpu.make_async_copy(w_hbm.at[28], pool_weights, sems.at[28])
+    pool_copy = pltpu.make_async_copy(tap_of(a_hbm, b_hbm, 28), pool_weights, sems.at[28])
     pool_copy.start()
-
-    count = count_ref[2:3, 0:1]
-    stat = stat_ref[...]
-    total = jnp.concatenate([stat[part : part + 1] for part in range(4)], 1)
-    square = jnp.concatenate([stat[part : part + 1] for part in range(4, 8)], 1)
-    mean = total / count
-    gain = gain_ref[0:1] * lax.rsqrt(square / count - mean * mean + norm_eps)
-    shift = gain_ref[1:2] - mean * gain
-
-    def residual(index, carry):
-        rows = block_rows(index)
-        value = dot(p_ref[rows], stem_ref[...]) + (y_ref[rows].astype(jnp.float32) * gain + shift)
-        low = (crop_ref[rows] * value).astype(x_ref.dtype)
-        x_ref[rows] = low
-        return carry + jnp.sum(low.astype(jnp.float32), 0, keepdims=True)
-
-    pooled = lax.fori_loop(0, POSITIONS // BLOCK, residual, jnp.zeros((1, D), jnp.float32))
-    pooled = (pooled / jnp.sum(crop_ref[...], keepdims=True)).astype(jnp.bfloat16)
-    pool_ref[...] = pooled.astype(jnp.float32)
-    for at in range(0, D, 256):
-        xt_ref[at : at + 256] = x_ref[:, at : at + 256].T
 
     for turn, group_copies in zip(order, copies):
         for copy in group_copies:
@@ -883,7 +952,7 @@
 
         lax.fori_loop(0, length // block, step, 0)
     pool_copy.wait()
-    pool_pre = dot(jnp.broadcast_to(pooled, (16, D)), pool_weights[...])[0:1]
+    pool_pre = dot(jnp.broadcast_to(pool_ref[...], (16, D)).astype(jnp.bfloat16), pool_weights[...])[0:1]
     pool_pre_ref[...] = pool_pre
     for branch in range(4):
         values = fields[0] if branch == 0 else fields[3 * branch - 1]
@@ -901,28 +970,25 @@
 
     def project(index, carry):
         rows = block_rows(index)
-        part_ref[rows] = dot(cat_ref[rows], project_ref[...]).astype(part_ref.dtype)
+        part_ref[rows] = dot(cat_ref[rows], project_ref[:, : 5 * width], (1, 1)).astype(part_ref.dtype)
         return carry
 
     lax.fori_loop(0, POSITIONS // BLOCK, project, 0)
 
 
-def pyramid_forward(patches, stem, expanded, stat, counts, gains, crop, weights, project, columns):
-    depth, width = weights.shape[1:]
+def pyramid_forward(field, pooled, weights, project, columns):
+    depth, width = weights[0].shape[1:]
     low = jnp.bfloat16
     return pl.pallas_call(
         pyramid_kernel,
         out_shape=[
-            jax.ShapeDtypeStruct((POSITIONS, depth), low),
-            jax.ShapeDtypeStruct((depth, POSITIONS), low),
-            jax.ShapeDtypeStruct((1, depth), jnp.float32),
             jax.ShapeDtypeStruct((4, POSITIONS, width), jnp.float32),
             jax.ShapeDtypeStruct((1, width), jnp.float32),
             jax.ShapeDtypeStruct((POSITIONS, 5 * width), low),
             jax.ShapeDtypeStruct((POSITIONS, BRANCH), low),
         ],
-        in_specs=vmem(7) + [pl.BlockSpec(memory_space=pl.ANY)] + vmem(2),
-        out_specs=vmem(7),
+        in_specs=vmem(2) + [pl.BlockSpec(memory_space=pl.ANY)] * 2 + vmem(2),
+        out_specs=vmem(4),
         scratch_shapes=[
             pltpu.VMEM((depth, 28 * width), low),
             pltpu.VMEM((depth, width), low),
@@ -934,13 +1000,12 @@
             flops=2 * POSITIONS * 19 * depth * width, bytes_accessed=40 << 20, transcendentals=0
         ),
         name="pyramid_fwd",
-    )(patches, stem, expanded, stat, counts, gains, crop, weights, project, columns)
+    )(field, pooled, weights[0], weights[1], project, columns)
 
 
 def head_kernel(
     own_ref,
     other_ref,
-    head_ref,
     row_ref,
     label_ref,
     target_ref,
@@ -964,7 +1029,7 @@
         mixed = own_ref[rows].astype(jnp.float32) + other_ref[rows].astype(jnp.float32)
         feature = jax.nn.gelu(mixed).astype(feature_ref.dtype)
         feature_ref[rows] = feature
-        logits = dot(feature, head_ref[...]) + bias
+        logits = dot(feature, project_ref[:, 5 * width :]) + bias
         is_class = class_lane > 0.0
         top = jnp.max(jnp.where(is_class, logits, -jnp.inf), 1, keepdims=True)
         powers = jnp.where(is_class, jnp.exp(jnp.where(is_class, logits - top, 0.0)), 0.0)
@@ -984,9 +1049,9 @@
         grad = scale * mask * jnp.where(is_class, powers / total - onehot, other)
         low = grad.astype(logit_ref.dtype)
         logit_ref[rows] = low
-        up = gelu_slope(mixed, dot(low, head_ref[...], (1, 1))).astype(mixed_ref.dtype)
+        up = gelu_slope(mixed, dot(low, project_ref[:, 5 * width :], (1, 1))).astype(mixed_ref.dtype)
         mixed_ref[rows] = up
-        cat = dot(up, project_ref[...], (1, 1))
+        cat = dot(up, project_ref[:, : 5 * width])
         for branch in range(4):
             grad_ref[branch, rows] = gelu_slope(
                 z_ref[branch, rows], cat[:, branch * width : (branch + 1) * width]
@@ -1011,7 +1076,7 @@
     )
 
 
-def head_step(own, other, head, rows, label, target, mask, project, branches, pool_pre):
+def head_step(own, other, rows, label, target, mask, project, branches, pool_pre):
     width = branches.shape[2]
     low = jnp.bfloat16
     return pl.pallas_call(
@@ -1024,12 +1089,168 @@
             jax.ShapeDtypeStruct((1, width), jnp.float32),
             jax.ShapeDtypeStruct((8, 128), jnp.float32),
         ],
-        in_specs=vmem(10),
+        in_specs=vmem(9),
         out_specs=vmem(6),
         compiler_params=pltpu.CompilerParams(vmem_limit_bytes=50 << 20),
         cost_estimate=pl.CostEstimate(flops=2 * 10**9, bytes_accessed=16 << 20, transcendentals=0),
         name="head_step",
-    )(own, other, head, rows, label, target, mask, project, branches, pool_pre)
+    )(own, other, rows, label, target, mask, project, branches, pool_pre)
+
+
+def own_rows(stat, place_ref, first):
+    lower = place_ref[0] == 0
+    return jnp.concatenate(
+        [
+            jnp.where(lower, stat[first + part : first + part + 1], stat[first + 2 + part : first + 3 + part])
+            for part in range(2)
+        ],
+        1,
+    )
+
+
+def own_norm(place_ref, stat_ref, count_ref):
+    stat = stat_ref[...]
+    count = count_ref[2:3, 0:1]
+    mean = own_rows(stat, place_ref, 0) / count
+    return mean, lax.rsqrt(own_rows(stat, place_ref, 4) / count - mean * mean + norm_eps), count
+
+
+def residual_sums_kernel(
+    place_ref,
+    own_ref,
+    other_hbm,
+    y_hbm,
+    stat_ref,
+    count_ref,
+    crop_ref,
+    head_ref,
+    o_ref,
+    y_ref,
+    other_ref,
+    sems,
+):
+    depth = own_ref.shape[1]
+    half = pl.ds(pl.multiple_of(place_ref[0] * depth, 128), depth)
+    copy = pltpu.make_async_copy(y_hbm.at[:, half], y_ref, sems.at[0])
+    copy.start()
+    other_copy = pltpu.make_async_copy(other_hbm.at[1 - place_ref[0]], other_ref, sems.at[1])
+    other_copy.start()
+    mean, scale, count = own_norm(place_ref, stat_ref, count_ref)
+    copy.wait()
+    other_copy.wait()
+
+    def step(index, carry):
+        rows = block_rows(index)
+        up = crop_ref[rows] * (
+            own_ref[rows].astype(jnp.float32) + other_ref[rows].astype(jnp.float32)
+        )
+        normed = (y_ref[rows].astype(jnp.float32) - mean) * scale
+        return (
+            carry[0] + jnp.sum(up * normed, 0, keepdims=True),
+            carry[1] + jnp.sum(up, 0, keepdims=True),
+        )
+
+    zero = jnp.zeros((1, depth), jnp.float32)
+    sums = lax.fori_loop(0, POSITIONS // BLOCK, step, (zero, zero))
+    for turn, values in enumerate(sums):
+        for part in range(2):
+            row = 2 * turn + part
+            o_ref[row : row + 1] = values[:, part * MID : (part + 1) * MID]
+    o_ref[4:5] = jnp.concatenate(
+        [head_ref[0:1], head_ref[1:2], head_ref[2:3], jnp.zeros((1, 128), jnp.float32)], 1
+    )
+    o_ref[5:8] = jnp.zeros((3, MID), jnp.float32)
+
+
+def residual_sums(place, own, other, expanded, stat, counts, crop, head_stat):
+    return pl.pallas_call(
+        residual_sums_kernel,
+        out_shape=jax.ShapeDtypeStruct((8, MID), jnp.float32),
+        in_specs=[pl.BlockSpec(memory_space=pltpu.SMEM)]
+        + vmem(1)
+        + [pl.BlockSpec(memory_space=pl.ANY)] * 2
+        + vmem(4),
+        out_specs=vmem(1)[0],
+        scratch_shapes=[
+            pltpu.VMEM(own.shape, jnp.bfloat16),
+            pltpu.VMEM(own.shape, jnp.bfloat16),
+            pltpu.SemaphoreType.DMA((2,)),
+        ],
+        compiler_params=pltpu.CompilerParams(vmem_limit_bytes=40 << 20),
+        cost_estimate=pl.CostEstimate(flops=10**8, bytes_accessed=12 << 20, transcendentals=0),
+        name="residual_sums",
+    )(place, own, other, expanded, stat, counts, crop, head_stat)
+
+
+def residual_back_kernel(
+    place_ref,
+    own_ref,
+    other_hbm,
+    y_hbm,
+    stat_ref,
+    count_ref,
+    sum_ref,
+    gain_ref,
+    crop_ref,
+    bottle_hbm,
+    o_ref,
+    part_ref,
+    y_ref,
+    other_ref,
+    weights,
+    sems,
+):
+    depth = own_ref.shape[1]
+    half = pl.ds(pl.multiple_of(place_ref[0] * depth, 128), depth)
+    copy = pltpu.make_async_copy(y_hbm.at[:, half], y_ref, sems.at[0])
+    copy.start()
+    weight_copy = pltpu.make_async_copy(bottle_hbm.at[1, half], weights, sems.at[1])
+    weight_copy.start()
+    other_copy = pltpu.make_async_copy(other_hbm.at[1 - place_ref[0]], other_ref, sems.at[2])
+    other_copy.start()
+    mean, scale, count = own_norm(place_ref, stat_ref, count_ref)
+    sums = sum_ref[...]
+    gain_grad = jnp.concatenate([sums[0:1], sums[1:2]], 1) / count
+    shift_grad = jnp.concatenate([sums[2:3], sums[3:4]], 1) / count
+    factor = gain_ref[0:1, MID // 2 :] * scale
+    copy.wait()
+    weight_copy.wait()
+    other_copy.wait()
+
+    def step(index, carry):
+        rows = block_rows(index)
+        crop = crop_ref[rows]
+        up = crop * (own_ref[rows].astype(jnp.float32) + other_ref[rows].astype(jnp.float32))
+        normed = (y_ref[rows].astype(jnp.float32) - mean) * scale
+        low = (crop * factor * (up - (shift_grad + normed * gain_grad))).astype(o_ref.dtype)
+        o_ref[rows] = low
+        part_ref[rows] = dot(low, weights[...]).astype(part_ref.dtype)
+        return carry
+
+    lax.fori_loop(0, POSITIONS // BLOCK, step, 0)
+
+
+def residual_back(place, own, other, expanded, stat, counts, sums, gains, crop, bottle):
+    hbm = pl.BlockSpec(memory_space=pl.ANY)
+    depth = own.shape[1]
+    return pl.pallas_call(
+        residual_back_kernel,
+        out_shape=[
+            jax.ShapeDtypeStruct((POSITIONS, depth), jnp.bfloat16),
+            jax.ShapeDtypeStruct((POSITIONS, MID), jnp.bfloat16),
+        ],
+        in_specs=[pl.BlockSpec(memory_space=pltpu.SMEM)] + vmem(1) + [hbm] * 2 + vmem(5) + [hbm],
+        out_specs=vmem(2),
+        scratch_shapes=[
+            pltpu.VMEM(own.shape, jnp.bfloat16),
+            pltpu.VMEM(own.shape, jnp.bfloat16),
+            pltpu.VMEM((depth, MID), jnp.bfloat16),
+            pltpu.SemaphoreType.DMA((3,)),
+        ],
+        compiler_params=pltpu.CompilerParams(vmem_limit_bytes=40 << 20),
+        cost_estimate=pl.CostEstimate(flops=2 * 10**9, bytes_accessed=16 << 20, transcendentals=0),
+        name="residual_back",
+    )(place, own, other, expanded, stat, counts, sums, gains, crop, bottle)
 
 
 def adam_step(weight, first, second, gradient, factor, rate, decay):
@@ -1091,43 +1312,32 @@
     stem_share = stem_weight.shape[2]
     project_share = project_weight.shape[2]
     head_share = head_weight.shape[0]
-    small_parts = [stem_weight, project_weight, head_weight]
-    small_flat = jnp.concatenate([part.astype(low).reshape(-1) for part in small_parts])
-    small_rows = -(-small_flat.shape[0] // (16 * 256)) * 16
-    small_flat = jnp.pad(small_flat, (0, small_rows * 256 - small_flat.shape[0]))
-    small_flat = small_flat.reshape(small_rows, 256)
-    pyramid_low = lax.all_gather(pyramid_weight.astype(low), "dp", axis=1, tiled=True)
-    bottle_low, middle_low, small = gather_trunk(
-        sizes, bottle_weight.astype(low), middle_weight.astype(low), small_flat
-    )
-    small = small.reshape(dp_size, 2, small_rows * 256)
-    size = PATCH * stem_share
-    stem_low = (
-        small[:, :, :size]
-        .reshape(dp_size, 2, PATCH, stem_share)
-        .transpose(2, 1, 0, 3)
-        .reshape(PATCH, D)
-    )
-    own_small = lax.dynamic_index_in_dim(small, chan_place, 1, keepdims=False)
-    project_low = (
-        own_small[:, size : size + 5 * 128 * project_share]
-        .reshape(dp_size, 5, 128, project_share)
-        .transpose(1, 2, 0, 3)
-        .reshape(5 * 128, BRANCH)
-    )
-    size += 5 * 128 * project_share
-    head_low = own_small[:, size : size + head_share * 22].reshape(BRANCH, 22)
-
-    gains_other = swap_chan(norm_gains)
-    gains_all = jnp.where(
-        chan_place == 0,
-        jnp.concatenate([norm_gains, gains_other], 1),
-        jnp.concatenate([gains_other, norm_gains], 1),
-    )
-    gain_one = gains_all[0, :, :mid_half].reshape(MID)
-    shift_one = gains_all[1, :, :mid_half].reshape(MID)
-    gain_two = gains_all[0, :, mid_half:].reshape(D)
-    shift_two = gains_all[1, :, mid_half:].reshape(D)
+    stem_shard = stem_weight.astype(low).reshape(PATCH, stem_share).T
+    head_shard = jnp.concatenate(
+        [
+            project_weight.astype(low).transpose(2, 0, 1).reshape(project_share, 5 * 128),
+            jnp.pad(head_weight.astype(low), ((0, 0), (0, 128 - 22))),
+        ],
+        1,
+    )
+    bottle_low, middle_low, stem_low, head_low = gather_trunk(
+        sizes, bottle_weight.astype(low), middle_weight.astype(low), stem_shard, head_shard
+    )
+    pyramid_shard = pyramid_weight.astype(low)
+    late_shard, bottle_low = lax.optimization_barrier((pyramid_shard[EARLY_TAPS:], bottle_low))
+    pyramid_low = (
+        lax.all_gather(pyramid_shard[:EARLY_TAPS], "dp", axis=1, tiled=True),
+        lax.all_gather(late_shard, "dp", axis=1, tiled=True),
+    )
+    own_place = chan_place.reshape(1)
+    own_gains = norm_gains.reshape(2, mid_half + half)
+    gains = (own_place, own_gains, swap_chan(own_gains))
+    gain_low = jnp.where(chan_place == 0, own_gains[:, :mid_half], gains[2][:, :mid_half])
+    gain_high = jnp.where(chan_place == 0, gains[2][:, :mid_half], own_gains[:, :mid_half])
+    gain_one, shift_one = jnp.concatenate([gain_low, gain_high], 1)
+
+    def own_bottle(which):
+        return lax.dynamic_slice(bottle_low, (which, chan_place * half, 0), (1, half, MID))[0]
 
     def own_half(values, axis):
         width = values.shape[axis] // 2
@@ -1141,6 +1351,39 @@
         lax.rem(lax.broadcasted_iota(jnp.int32, (POSITIONS, 1), 0), FW).astype(jnp.float32),
         (POSITIONS, 128),
     )
+    patch_rows = patches.reshape(POSITIONS, PATCH)
+    stream_low, first_pre, stat_one = stem_reduce(
+        patch_rows,
+        stem_low,
+        bottle_low,
+        crop_field,
+        jnp.pad(local_counts, (0, MID - 3)).reshape(1, MID),
+    )
+    stat_one = all_sum(sizes, stat_one, ("dp",), 0)
+    hidden_low, hidden_t, second_low = norm_middle(
+        first_pre, stat_one, gains, crop_field, middle_low, columns
+    )
+    expand_pre, stat_two = expand_forward(second_low, bottle_low, crop_field)
+    stat_two = all_sum(sizes, stat_two, ("dp",), 1)
+    output_low, output_t, pooled = residual_stream(
+        patch_rows,
+        stem_low,
+        expand_pre,
+        stat_two,
+        stat_one,
+        gains,
+        crop_field,
+    )
+    branch_pre, pool_pre, concat_low, project_part = pyramid_forward(
+        output_low, pooled, pyramid_low, head_low, columns
+    )
+    labels, offset_valid, lidar_valid, offset_target, depth_target, project_part = (
+        lax.optimization_barrier(
+            (labels, offset_valid, lidar_valid, offset_target, depth_target, project_part)
+        )
+    )
+    offset_field = crop_field[:, 0] * offset_valid.astype(jnp.float32).reshape(POSITIONS)
+    lidar_field = crop_field[:, 0] * lidar_valid.astype(jnp.float32).reshape(POSITIONS)
     lane = lax.broadcasted_iota(jnp.int32, (1, 128), 1)
     class_lane = (lane < CLASSES).astype(jnp.float32)
     offset_lane = ((lane >= CLASSES) & (lane < CLASSES + 2)).astype(jnp.float32)
@@ -1155,42 +1398,9 @@
         jnp.concatenate([offset_target[0], depth_target], 0).T,
         ((0, 0), (CLASSES, 128 - CLASSES - 3)),
     )
-    head_wide = jnp.pad(head_low, ((0, 0), (0, 128 - 22)))
     task_scale = task_params[:3]
-
-    patch_rows = patches.reshape(POSITIONS, PATCH)
-    stream_low, first_pre, stat_one = stem_reduce(
-        patch_rows,
-        stem_low,
-        bottle_low,
-        crop_field,
-        jnp.pad(local_counts, (0, MID - 3)).reshape(1, MID),
-    )
-    stat_one = all_sum(sizes, stat_one, ("dp",), 0)
-    hidden_low, hidden_t, second_low = norm_middle(
-        first_pre, stat_one, jnp.stack([gain_one, shift_one]), crop_field, middle_low, columns
-    )
-    expand_pre, stat_two = expand_forward(second_low, bottle_low, crop_field)
-    stat_two = all_sum(sizes, stat_two, ("dp",), 1)
-    output_low, output_t, pooled, branch_pre, pool_pre, concat_low, project_part = pyramid_forward(
-        patch_rows,
-        stem_low,
-        expand_pre,
-        stat_two,
-        stat_one,
-        jnp.stack([gain_two, shift_two]),
-        crop_field,
-        pyramid_low,
-        project_low,
-        columns,
-    )
     counts = stat_one[2, :3]
     crop_total = counts[0]
-    mean_one = stat_one[0] / crop_total
-    scale_one = lax.rsqrt(stat_one[1] / crop_total - mean_one * mean_one + norm_eps)
-    mean_two = stat_two[:4].reshape(D) / crop_total
-    scale_two = lax.rsqrt(stat_two[4:].reshape(D) / crop_total - mean_two * mean_two + norm_eps)
-    image_count = jnp.sum(crop_field)
     task_weights = jnp.exp(-task_scale) / counts
     lane_rows = jnp.concatenate(
         [
@@ -1208,67 +1418,67 @@
     feature_low, logit_low, project_grad_low, branch_grads, pool_grad, head_stat = head_step(
         project_part,
         swap_chan(project_part),
-        head_wide,
         lane_rows,
         onehot,
         target,
         mask,
-        project_low,
+        head_low,
         branch_pre,
         pool_pre,
     )
-    local_bias = head_stat[0, :22]
-    local_sums = jnp.stack(
+    other_part = pyramid_field(
+        1 - own_place, pyramid_low, branch_grads, pool_grad, crop_field, columns
+    )
+    other_sent = lax.all_gather(other_part, "chan")
+    later_grads, other_part = lax.optimization_barrier((branch_grads, other_part))
+    own_part = pyramid_field(own_place, pyramid_low, later_grads, pool_grad, crop_field, columns)
+    later_grads, own_part = lax.optimization_barrier((later_grads, own_part))
+    pyramid_grad = pyramid_weights(
+        output_t, later_grads, columns, pooled.reshape(D, 1), pool_grad
+    )
+    pyramid_red = lax.psum_scatter(pyramid_grad, "dp", scatter_dimension=1, tiled=True)
+
+    stat_three = residual_sums(
+        own_place, own_part, other_sent, expand_pre, stat_two, stat_one, crop_field, head_stat
+    )
+    stat_three = all_sum(sizes, stat_three, ("dp",), 2)
+    expand_grad_low, second_part = residual_back(
+        own_place,
+        own_part,
+        other_sent,
+        expand_pre,
+        stat_two,
+        stat_one,
+        stat_three,
+        own_gains,
+        crop_field,
+        bottle_low,
+    )
+    stat_one, stat_three, own_part, second_part = lax.optimization_barrier(
+        (stat_one, stat_three, own_part, second_part)
+    )
+    gain_two_grad = stat_three[:2].reshape(half)
+    shift_two_grad = stat_three[2:4].reshape(half)
+    bias_grad = stat_three[4, :22]
+    error_sums = stat_three[4, 128:256]
+    loss_sums = jnp.stack(
         [
-            head_stat[2, 0],
-            head_stat[1, CLASSES] + head_stat[1, CLASSES + 1],
-            head_stat[1, CLASSES + 2],
+            stat_three[4, 256],
+            error_sums[CLASSES] + error_sums[CLASSES + 1],
+            error_sums[CLASSES + 2],
         ]
     )
-    head_grad = dot(feature_low, logit_low, (0, 0))[:, :22]
-    project_grad = dot(concat_low, project_grad_low, (0, 0))
-    pool_grad_low = pool_grad.astype(low)
-
-    own_place = chan_place.reshape(1)
-    other_part = pyramid_field(1 - own_place, pyramid_low, branch_grads, columns)
-    other_sent = swap_chan(other_part)
-    later_grads, other_part = lax.optimization_barrier((branch_grads, other_part))
-    pyramid_grad = pyramid_weights(
-        output_t,
-        later_grads,
-        columns,
-        pooled.reshape(D, 1),
-        pool_grad,
-    )
-    pyramid_red = lax.psum_scatter(pyramid_grad, "dp", scatter_dimension=1, tiled=True)
-    later_grads, pyramid_grad = lax.optimization_barrier((later_grads, pyramid_grad))
-    own_part = pyramid_field(own_place, pyramid_low, later_grads, columns)
-    pool_part = dot(pool_grad_low, pyramid_low[28], (1, 1)) / image_count
-    pool_sum = own_half(pool_part, 1) + swap_chan(other_half(pool_part, 1))
-    stream_grad = (
-        own_part.astype(jnp.float32) + other_sent.astype(jnp.float32) + crop_field * pool_sum
-    )
-
-    own_gain_two = own_half(gain_two, 0)
-    own_scale_two = own_half(scale_two, 0)
-    normed_two = (own_half(expand_pre, 1).astype(jnp.float32) - own_half(mean_two, 0)) * own_scale_two
-    upstream_two = crop_field * stream_grad
-    gain_two_grad, shift_two_grad, loss_sums, bias_grad = small_sum(
-        sizes,
-        [jnp.sum(upstream_two * normed_two, 0), jnp.sum(upstream_two, 0), local_sums, local_bias],
-        ("dp",),
-        2,
-    )
+    mean_one = stat_one[0] / crop_total
+    scale_one = lax.rsqrt(stat_one[1] / crop_total - mean_one * mean_one + norm_eps)
+    stream_grad = own_part.astype(jnp.float32) + lax.dynamic_index_in_dim(
+        other_sent, 1 - chan_place, 0, keepdims=False
+    ).astype(jnp.float32)
     task_means = loss_sums / counts
     total_loss = jnp.sum(jnp.exp(-task_scale) * task_means + task_scale)
     scale_grad = 1.0 - jnp.exp(-task_scale) * task_means
-    expand_grad_low = (
-        crop_field
-        * own_gain_two
-        * own_scale_two
-        * (upstream_two - (shift_two_grad + normed_two * gain_two_grad) / crop_total)
-    ).astype(low)
-    second_part = dot(expand_grad_low, own_half(bottle_low[1], 0)).astype(low)
+    second_part, feature_low, logit_low, concat_low, project_grad_low = lax.optimization_barrier(
+        (second_part, feature_low, logit_low, concat_low, project_grad_low)
+    )
     second_other = swap_chan(second_part)
     expand_rows = dot(expand_grad_low, second_low, (0, 0)).astype(low)
     expand_sent = swap_chan(other_half(expand_rows, 1))
@@ -1295,9 +1505,9 @@
     ).astype(low)
     middle_grad = middle_weights(hidden_t, own_half(second_grad_low, 1), columns)
     reduce_grad = dot(stream_low, own_half(first_grad_low, 1), (0, 0)).astype(low)
-    start_grad = dot(first_grad_low, own_half(bottle_low[0], 0), (1, 1)) + stream_grad
+    start_grad = dot(first_grad_low, own_bottle(0), (1, 1)) + stream_grad
     start_grad_low = (crop_field * start_grad).astype(low)
-    stem_grad = dot(patch_rows, start_grad_low, (0, 0)).astype(low)
+    stem_grad = dot(start_grad_low, patch_rows, (0, 0)).astype(low)
     expand_own = own_half(expand_rows, 1)
     expand_grad = jnp.where(
         chan_place == 0,
@@ -1307,45 +1517,37 @@
 
     small_grads = jnp.concatenate(
         [
-            stem_grad.reshape(PATCH, dp_size, stem_share)
-            .transpose(1, 0, 2)
-            .reshape(dp_size, PATCH * stem_share),
-            project_grad.astype(low)
-            .reshape(5 * 128, dp_size, project_share)
-            .transpose(1, 0, 2)
-            .reshape(dp_size, 5 * 128 * project_share),
-            head_grad.astype(low).reshape(dp_size, head_share * 22),
+            dot(project_grad_low, concat_low, (0, 0)).astype(low),
+            dot(feature_low, logit_low, (0, 0)).astype(low),
         ],
         1,
     )
-    small_grads = jnp.pad(small_grads, ((0, 0), (0, small_rows * 256 - small_grads.shape[1])))
-    packed_grads = jnp.concatenate(
+    small_rows = project_share * 3
+    trunk_grads = jnp.concatenate(
         [
             reduce_grad.reshape(dp_size, row_share, 256),
             expand_grad.reshape(dp_size, row_share, 256),
             middle_grad.reshape(9, dp_size, mid_share, 256)
             .transpose(1, 0, 2, 3)
             .reshape(dp_size, 9 * mid_share, 256),
+            stem_grad.reshape(dp_size, stem_share * PATCH // 256, 256),
             small_grads.reshape(dp_size, small_rows, 256),
         ],
         1,
     )
-    packed_grads, pyramid_red = lax.optimization_barrier((packed_grads, pyramid_red))
-    trunk_red = (
-        lax.psum_scatter(packed_grads, "dp", scatter_dimension=0, tiled=True)
-        .reshape(packed_grads.shape[1:])
-        .astype(jnp.float32)
-    )
+    trunk_grads, pyramid_red = lax.optimization_barrier((trunk_grads, pyramid_red))
+    trunk_red = lax.psum_scatter(trunk_grads, "dp", scatter_dimension=0, tiled=True)[0]
+    trunk_red = trunk_red.astype(jnp.float32)
+    bottle_red = trunk_red[: 2 * row_share].reshape(bottle_weight.shape)
     start = 2 * row_share
-    bottle_red = trunk_red[: 2 * row_share].reshape(bottle_weight.shape)
     middle_red = trunk_red[start : start + 9 * mid_share].reshape(middle_weight.shape)
-    small_red = trunk_red[start + 9 * mid_share :].reshape(-1)
-    stem_red = small_red[: stem_weight.size].reshape(stem_weight.shape)
-    project_red = small_red[stem_weight.size : stem_weight.size + project_weight.size].reshape(
-        project_weight.shape
-    )
-    size = stem_weight.size + project_weight.size
-    head_red = small_red[size : size + head_weight.size].reshape(head_weight.shape)
+    start += 9 * mid_share
+    stem_rows = stem_share * PATCH // 256
+    stem_red = trunk_red[start : start + stem_rows]
+    stem_red = stem_red.reshape(stem_share, PATCH).T.reshape(stem_weight.shape)
+    small_red = trunk_red[start + stem_rows :].reshape(project_share, 768)
+    project_red = small_red[:, : 5 * 128].reshape(project_share, 5, 128).transpose(1, 2, 0)
+    head_red = small_red[:, 5 * 128 : 5 * 128 + 22]
     pyramid_red = pyramid_red.astype(jnp.float32)
     norm_grad = jnp.stack(
         [

time: 706 us -> 647 us (0.916)
  local copies, waits for them, and re-layouts: 67.5 us -> 31.6 us
  waiting for transfers between devices: 160 us -> 185 us
  other arithmetic: 73.8 us -> 51.4 us
  Pallas kernels: 341 us -> 331 us
    ppermute x6 -> x4, waiting for transfers between devices: 89.4 us -> 55.4 us  [swap_chan(): return lax.ppermute(values, 'chan', [(0, 1), (1, 0)])]
    pallas_call x1, Pallas kernels: 118 us -> 85 us  [gather_trunk(): pl.pallas_call(functools.partial(gather_kernel, count // 4), out_shape=[j...]
    all_gather x1 -> x3, waiting for transfers between devices: 0.01 us -> 31.4 us  [the longest x1 26.4 us: on_device(): other_sent = lax.all_gather(other_part, 'chan')]
    reduce_scatter x1, waiting for transfers between devices: 0.01 us -> 24.8 us  [on_device(): lax.psum_scatter(pyramid_grad, 'dp', scatter_dimension=1, tiled=True)]
    reshape x14 -> x3, local copies, waits for them, and re-layouts: 22.3 us -> 2.67 us  [the longest x1 1.92 us: on_device(): small_grads.reshape(dp_size, small_rows, 256)]
    pallas_call x1 -> x4, Pallas kernels: 40 us -> 57.4 us  [the longest x1 31.2 us: pyramid_forward(): pl.pallas_call(pyramid_kernel, out_shape=[jax.ShapeDtypeStruct((4, POSITI...]
    convert_element_type x6 -> x4, other arithmetic: 11.2 us -> 2.83 us  [the longest x1 1.79 us: on_device(): pyramid_shard = pyramid_weight.astype(low)]
    dot_general x7 -> x5, matrix products: 21.4 us -> 16.4 us  [dot(): lax.dot_general(left, right, (((contract[0],), (contract[1],)), ((), ()))...]
  transfers between devices with their start and end apart: 9 -> 9, of which waited for: 4 -> 6; matrix products, arithmetic and copies ran while one was open for 19% -> 10% of each run, Pallas kernels for 33% -> 41%
where the time goes in v5:
time: 647 us; the launch traced here: 644 us
  Pallas kernels  331 us (51%)
  waiting for transfers between devices  185 us (29%)
  other arithmetic  51.4 us (8%)
  local copies, waits for them, and re-layouts  31.6 us (5%)
  between operations  23.5 us (4%)
  matrix products  16.4 us (3%)
    pallas_call x1, Pallas kernels, gather_trunk(): pl.pallas_call(functools.partial(gather_kernel, count // 4), out_shape=[j...  85 us
    reduce_scatter x1, waiting for transfers between devices, on_device(): lax.psum_scatter(trunk_grads, 'dp', scatter_dimension=0, tiled=True)[0]  73.7 us
    ppermute x4, waiting for transfers between devices, swap_chan(): return lax.ppermute(values, 'chan', [(0, 1), (1, 0)])  55.4 us
    pallas_call x5, Pallas kernels, all_sum(): pl.pallas_call(functools.partial(sum_kernel, sizes, axes, count), out_sha...  54.1 us
    pallas_call x1, Pallas kernels, pyramid_weights(): pl.pallas_call(weight_kernel, out_shape=jax.ShapeDtypeStruct((29, depth,...  37.9 us
    pallas_call x2, Pallas kernels, pyramid_field(): pl.pallas_call(field_kernel, out_shape=jax.ShapeDtypeStruct((POSITIONS, d...  37.2 us
    pallas_call x1, Pallas kernels, pyramid_forward(): pl.pallas_call(pyramid_kernel, out_shape=[jax.ShapeDtypeStruct((4, POSITI...  31.2 us
    all_gather x1, waiting for transfers between devices, on_device(): other_sent = lax.all_gather(other_part, 'chan')  26.4 us
  transfers between devices with their start and end apart: 9, of which 6 were waited for; matrix products, arithmetic and copies ran while one was open for 10% of the time, Pallas kernels for 41%

profile of v5, /device:TPU:0, one launch (start us, length us, event | category | flops | bytes accessed | tf_op | source)
XLA Modules:
  0.0 643.5 jit_solution(2209750921945772156)
XLA Ops:
  7.4 1.8 convert_element_type.163
  13.5 85.0 %gather_trunk.1 = (bf16[2,2048,512]{2,1,0:T(8,128)(2,1)}, bf16[9,512,512]{2,1,0:T(8,128)(2,1)}, bf16[2048,192]{1,0:T(8,128)(2,1)}, bf16[256,768]{1,0:T(8,128)(2,1)}) custom-call(bf16[2,128,256]{2,1,0:T(8,128)(2,1)} %convert_element_type.158.bottle, bf16[9,32,256]{2,1,0:T(8,128)(2,1)} %convert_element_type.159.middle, ...), custom_call_target="tpu_custom_call" | custom-call | tf_op jit(solution)/shard_map/gather_trunk/pallas_call | solution.py:408
  100.9 2.0 select_maximum_fusion
  102.9 1.3 copy-done.5
  104.2 11.5 %stem_reduce.1 = (bf16[1600,2048]{1,0:T(8,128)(2,1)}, f32[1600,512]{1,0:T(8,128)}, f32[8,512]{1,0:T(8,128)S(1)}) custom-call(bf16[1600,192]{1,0:T(8,128)(2,1)S(1)} %bitcast.129, bf16[2048,192]{1,0:T(8,128)(2,1)S(1)} %copy-done.5, bf16[2,2048,512]{2,1,0:T(8,128)(2,1)} %get-tuple-element.76.reduce_ref.w_ref.bottle_hbm, f32[1600,1]{1,0:T(8,128)S(1)} %copy.110.crop_ref, ...), custom_call_target="tpu_custom_call" | custom-call | flops 5000000000 | bytes 14680064 | tf_op jit(solution)/shard_map/stem_reduce/pallas_call | solution.py:717
  115.7 11.6 %small_sum.5.stat_ref.count_ref = f32[8,512]{1,0:T(8,128)S(1)} custom-call(f32[8,512]{1,0:T(8,128)S(1)} %get-tuple-element.77.x_ref), custom_call_target="tpu_custom_call" | custom-call | tf_op jit(solution)/shard_map/small_sum/pallas_call | solution.py:109
  128.0 1.9 fusion.33
  130.3 15.6 %norm_middle.1 = (bf16[1600,512]{1,0:T(8,128)(2,1)}, bf16[512,1600]{1,0:T(8,128)(2,1)}, bf16[1600,512]{1,0:T(8,128)(2,1)}) custom-call(f32[1600,512]{1,0:T(8,128)} %get-tuple-element.78.a_ref, f32[8,512]{1,0:T(8,128)S(1)} %small_sum.5.stat_ref.count_ref, s32[1]{0:T(128)} %bitcast.9.place_ref.half_ref, f32[2,1280]{1,0:T(2,128)S(1)} %bitcast.133, ...), custom_call_target="tpu_custom_call" | custom-call | flops 8000000000 | bytes 14680064 | tf_op jit(solution)/shard_map/norm_middle/pallas_call | solution.py:789
  145.9 1.5 copy-done.21
  147.4 9.0 %expand_forward.1 = (bf16[1600,2048]{1,0:T(8,128)(2,1)}, f32[8,512]{1,0:T(8,128)S(1)}) custom-call(bf16[1600,512]{1,0:T(8,128)(2,1)S(1)} %copy-done.21, bf16[2,2048,512]{2,1,0:T(8,128)(2,1)} %get-tuple-element.76.reduce_ref.w_ref.bottle_hbm, f32[1600,1]{1,0:T(8,128)S(1)} %copy.110.crop_ref), custom_call_target="tpu_custom_call" | custom-call | flops 4000000000 | bytes 12582912 | tf_op jit(solution)/shard_map/expand_forward/pallas_call | solution.py:826
  156.3 15.3 %small_sum.6.stat_ref = f32[8,512]{1,0:T(8,128)S(1)} custom-call(f32[8,512]{1,0:T(8,128)S(1)} %get-tuple-element.82.x_ref), custom_call_target="tpu_custom_call" | custom-call | tf_op jit(solution)/shard_map/small_sum/pallas_call | solution.py:109
  171.7 12.8 %residual_stream.1 = (bf16[1600,2048]{1,0:T(8,128)(2,1)}, bf16[2048,1600]{1,0:T(8,128)(2,1)}, f32[1,2048]{1,0:T(1,128)S(1)}) custom-call(bf16[1600,192]{1,0:T(8,128)(2,1)S(1)} %bitcast.130, bf16[2048,192]{1,0:T(8,128)(2,1)S(1)} %copy-done.6, bf16[1600,2048]{1,0:T(8,128)(2,1)} %get-tuple-element.81.y_ref.y_hbm, f32[8,512]{1,0:T(8,128)S(1)} %small_sum.6.stat_ref, ...), custom_call_target="tpu_custom_call" | custom-call | flops 2000000000 | bytes 23068672 | tf_op jit(solution)/shard_map/residual_stream/pallas_call | solution.py:878
  185.0 5.0 all-gather.7.cloned.1.call-done.b_hbm
  190.1 31.2 %pyramid_fwd.1 = (f32[4,1600,128]{2,1,0:T(8,128)}, f32[1,128]{1,0:T(1,128)}, bf16[1600,640]{1,0:T(8,128)(2,1)}, bf16[1600,256]{1,0:T(8,128)(2,1)}) custom-call(bf16[1600,2048]{1,0:T(8,128)(2,1)} %get-tuple-element.83.x_ref, f32[1,2048]{1,0:T(1,128)} %copy-done.15, bf16[10,2048,128]{2,1,0:T(8,128)(2,1)} %all-gather.5.cloned.1.call-done.a_hbm, ...), custom_call_target="tpu_custom_call" | custom-call | flops 15938355200 | bytes 41943040 | tf_op jit(solution)/shard_map/pyramid_fwd/pallas_call | solution.py:982
  221.4 1.2 fusion.16.label_ref
  222.5 1.4 collective-permute-start.1
  224.3 1.2 pad.23.target_ref
  225.6 1.8 multiply_add_fusion.1.mask_ref
  227.4 15.8 %collective-permute-done.1.other_ref = bf16[1600,256]{1,0:T(8,128)(2,1)S(1)} collective-permute-done((bf16[1600,256]{1,0:T(8,128)(2,1)}, bf16[1600,256]{1,0:T(8,128)(2,1)S(1)}, u32[]{:S(2)}, u32[]{:S(2)}) %collective-permute-start.1) | collective-permute-done | bytes 819232 | tf_op jit(solution)/shard_map/ppermute | solution.py:141
  243.2 9.5 %head_step.1 = (bf16[1600,256]{1,0:T(8,128)(2,1)S(1)}, bf16[1600,128]{1,0:T(8,128)(2,1)S(1)}, bf16[1600,256]{1,0:T(8,128)(2,1)S(1)}, bf16[4,1600,128]{2,1,0:T(8,...) custom-call(bf16[1600,256]{1,0:T(8,128)(2,1)S(1)} %copy-done.7, ...), custom_call_target="tpu_custom_call" | custom-call | flops 2000000000 | bytes 16777216 | tf_op jit(solution)/shard_map/head_step/pallas_call | solution.py:1082
  252.7 0.9 copy-done.10
  254.9 18.7 %pyramid_field.2 = bf16[1600,1024]{1,0:T(8,128)(2,1)} custom-call(s32[1]{0:T(128)S(6)} %sub.54.half_ref, bf16[10,2048,128]{2,1,0:T(8,128)(2,1)} %all-gather.5.cloned.1.call-done.a_hbm, bf16[19,2048,128]{2,1,0:T(8,128)(2,1)} %all-gather.7.cloned.1.call-done.b_hbm, bf16[4,1600,128]{2,1,0:T(8,128)(2,1)} %get-tuple-element.119.g_ref, f32[1,128]{1,0:T(1,128)} %copy-done.20, ...), custom_call_target="tpu_custom_call" | custom-call | flops 30000001024 | bytes 20971520 | tf_op jit(solution)/shard_map/pyramid_field/pallas_call | solution.py:658
  274.3 1.4 copy.122.pool_ref
  275.7 18.5 %pyramid_field.3.own_ref = bf16[1600,1024]{1,0:T(8,128)(2,1)} custom-call(s32[1]{0:T(128)} %bitcast.9.place_ref.half_ref, bf16[10,2048,128]{2,1,0:T(8,128)(2,1)} %all-gather.5.cloned.1.call-done.a_hbm, bf16[19,2048,128]{2,1,0:T(8,128)(2,1)} %all-gather.7.cloned.1.call-done.b_hbm, bf16[4,1600,128]{2,1,0:T(8,128)(2,1)} %get-tuple-element.119.g_ref, ...), custom_call_target="tpu_custom_call" | custom-call | flops 30000001024 | bytes 20971520 | tf_op jit(solution)/shard_map/pyramid_field/pallas_call | solution.py:658
  294.2 37.9 %pyramid_weights.1 = bf16[29,2048,128]{2,1,0:T(8,128)(2,1)} custom-call(bf16[2048,1600]{1,0:T(8,128)(2,1)} %get-tuple-element.118.xt_ref, bf16[4,1600,128]{2,1,0:T(8,128)(2,1)} %get-tuple-element.119.g_ref, f32[1600,128]{1,0:T(8,128)} %copy-done.8, f32[2048,1]{1,0:T(8,128)} %copy.122.pool_ref, f32[1,128]{1,0:T(1,128)} %copy-done.20), custom_call_target="tpu_custom_call" | custom-call | flops 30000001024 | bytes 20971520 | tf_op jit(solution)/shard_map/pyramid_weights/pallas_call | solution.py:598
  332.6 26.4 %all-gather.9.cloned.1.call-done = bf16[3200,1024]{1,0:T(8,128)(2,1)} async-done(((bf16[1600,1024]{1,0:T(8,128)(2,1)}), bf16[3200,1024]{1,0:T(8,128)(2,1)}) %all-gather.9.cloned.1.call-update) | async-done | bytes 6553616 | tf_op jit(solution)/shard_map/all_gather | solution.py:1432
  359.0 2.9 copy-done
  361.9 1.1 copy-done.3
  363.0 4.4 residual_sums.1.x_ref
  367.4 9.8 %small_sum.7.sum_ref = f32[8,512]{1,0:T(8,128)S(1)} custom-call(f32[8,512]{1,0:T(8,128)S(1)} %residual_sums.1.x_ref), custom_call_target="tpu_custom_call" | custom-call | tf_op jit(solution)/shard_map/small_sum/pallas_call | solution.py:109
  377.2 9.0 %residual_back.1 = (bf16[1600,1024]{1,0:T(8,128)(2,1)S(1)}, bf16[1600,512]{1,0:T(8,128)(2,1)}) custom-call(s32[1]{0:T(128)} %bitcast.9.place_ref.half_ref, bf16[1600,1024]{1,0:T(8,128)(2,1)S(1)} %copy-done.1, bf16[2,1600,1024]{2,1,0:T(8,128)(2,1)} %bitcast.126, bf16[1600,2048]{1,0:T(8,128)(2,1)} %get-tuple-element.81.y_ref.y_hbm, ...), custom_call_target="tpu_custom_call" | custom-call | flops 2000000000 | bytes 16777216 | tf_op jit(solution)/shard_map/residual_back/pallas_call | solution.py:1236
  386.9 2.1 convolution_convert_fusion.1
  389.0 1.0 constant_dynamic-slice_fusion.2
  390.1 1.5 collective-permute-start.3
  391.5 0.9 convolution_convert_fusion.3
  393.7 1.9 reshape.390
  396.3 39.6 %collective-permute-done.3 = bf16[1024,256]{1,0:T(8,128)(2,1)} collective-permute-done((bf16[1024,256]{1,0:T(8,128)(2,1)}, bf16[1024,256]{1,0:T(8,128)(2,1)}, u32[]{:S(2)}, u32[]{:S(2)}) %collective-permute-start.3) | collective-permute-done | bytes 524320 | tf_op jit(solution)/shard_map/ppermute | solution.py:141
  435.8 2.7 maximum_select_fusion
  438.6 2.6 add_convert_fusion.x_ref
  441.4 4.2 middle_weights.1
  445.6 1.6 copy.119
  447.3 9.4 %middle_back.1 = f32[1600,512]{1,0:T(8,128)S(1)} custom-call(bf16[1600,512]{1,0:T(8,128)(2,1)S(1)} %add_convert_fusion.x_ref, bf16[9,512,512]{2,1,0:T(8,128)(2,1)S(1)} %bitcast.141, f32[1600,128]{1,0:T(8,128)S(1)} %copy-done.9), custom_call_target="tpu_custom_call" | custom-call | flops 7549747200 | bytes 16777216 | tf_op jit(solution)/shard_map/middle_back/pallas_call | solution.py:504
  456.7 4.0 multiply_reduce_fusion
  460.7 8.2 %small_sum.8 = f32[8,128]{1,0:T(8,128)S(1)} custom-call(f32[8,128]{1,0:T(8,128)S(1)} %pad_maximum_fusion.4.x_ref), custom_call_target="tpu_custom_call" | custom-call | tf_op jit(solution)/shard_map/small_sum/pallas_call | solution.py:109
  468.9 3.0 multiply_convert_fusion
  471.8 7.1 %convolution_convert_fusion.2 = bf16[1024,192]{0,1:T(8,128)(2,1)} fusion(bf16[1600,1024]{1,0:T(8,128)(2,1)S(1)} %copy-done.1, bf16[1600,512]{1,0:T(8,128)(2,1)} %multiply_convert_fusion, bf16[2,1600,1024]{2,1,0:T(8,128)(2,1)} %bitcast.127, s32[]{:T(128)S(6)} %select_n.50, f32[1600]{0:T(1024)S(1)} %get-tuple-element.179, ...), kind=kOutput, calls=%fused_computation.25 | convolution fusion | flops 2316894208 | bytes 10279176 | tf_op jit(solution)/shard_map/dot_general | solution.py:171
  478.9 1.2 copy.120
  480.9 5.9 convolution_convert_fusion
  486.8 1.1 constant_dynamic-update-slice_fusion.4
  487.9 1.1 constant_dynamic-update-slice_fusion.3
  489.0 1.6 constant_dynamic-update-slice_fusion.2
  492.2 24.8 %reduce-scatter.3.cloned.1.call-done = bf16[29,128,128]{2,1,0:T(8,128)(2,1)} async-done(((bf16[29,2048,128]{2,1,0:T(8,128)(2,1)}), bf16[29,128,128]{2,1,0:T(8,128)(2,1)}) %reduce-scatter.3.cloned.1.call-update) | async-done | bytes 950288 | tf_op jit(solution)/shard_map/reduce_scatter | solution.py:1439
  519.2 1.4 broadcast_subtract_fusion
  524.0 1.1 fusion.9
  525.1 73.7 %reduce-scatter.5.cloned.1.call-done = bf16[1,640,256]{2,1,0:T(8,128)(2,1)} async-done(((bf16[16,640,256]{2,1,0:T(8,128)(2,1)}), bf16[1,640,256]{2,1,0:T(8,128)(2,1)}) %reduce-scatter.5.cloned.1.call-update) | async-done | bytes 327696 | tf_op jit(solution)/shard_map/reduce_scatter | solution.py:1539
  600.8 1.0 convert_element_type.190
  607.6 9.2 %small_sum.9 = f32[8,128]{1,0:T(8,128)S(1)} custom-call(f32[8,128]{1,0:T(8,128)S(1)} %pad_bitcast_fusion.x_ref), custom_call_target="tpu_custom_call" | custom-call | tf_op jit(solution)/shard_map/small_sum/pallas_call | solution.py:109
  621.1 1.3 multiply_subtract_fusion.7
  622.4 1.4 multiply_subtract_fusion.5
  623.8 1.4 multiply_subtract_fusion.6
  625.1 1.5 multiply_subtract_fusion.4
  626.8 6.0 multiply_subtract_fusion
  633.5 1.0 multiply_subtract_fusion.2
  634.5 1.1 multiply_subtract_fusion.1
  (210 shorter events, 27.2 us)
Async XLA Ops:
  7.2 3.7 copy-start.49
  7.2 3.7 copy-start.35
  7.2 4.4 copy-start.31
  7.2 5.0 copy-start.45
  7.2 5.6 copy-start.43
  7.3 91.3 %copy-start.48 = (f32[2,1,1280]{2,1,0:T(1,128)S(1)}, f32[2,1,1280]{2,1,0:T(1,128)}, u32[]{:S(2)}) copy-start(f32[2,1,1280]{2,1,0:T(1,128)} %param.56) | copy-start | bytes 30724
  7.3 91.6 %copy-start.56 = (f32[25]{0:T(128)S(1)}, f32[25]{0:T(128)}, u32[]{:S(2)}) copy-start(f32[25]{0:T(128)} %param.59) | copy-start | bytes 304
  7.3 91.7 %copy-start.50 = (s32[1,1600]{1,0:T(1,128)S(1)}, s32[1,1600]{1,0:T(1,128)}, u32[]{:S(2)}) copy-start(s32[1,1600]{1,0:T(1,128)} %param.37) | copy-start | bytes 19204
  7.3 92.0 %copy-start.37 = (bf16[1,1600,192]{1,2,0:T(8,128)(2,1)S(1)}, bf16[1,1600,192]{1,2,0:T(8,128)(2,1)}, u32[]{:S(2)}) copy-start(bf16[1,1600,192]{1,2,0:T(8,128)(2,1)} %param.31) | copy-start | bytes 1843204
  7.3 177.7 %all-gather.5.cloned.1.call-start = ((), (), s32[]{:S(2)}) async-start(), calls=%async_computation.2 | async-start | bytes 5570560 | tf_op jit(solution)/shard_map/all_gather | solution.py:1329
  9.2 91.1 %copy-start.51 = (s32[1,1600]{1,0:T(1,128)S(1)}, s32[1,1600]{1,0:T(1,128)}, u32[]{:S(2)}) copy-start(s32[1,1600]{1,0:T(1,128)} %param.34) | copy-start | bytes 19204
  9.2 91.1 %copy-start.52 = (s32[1,1600]{1,0:T(1,128)S(1)}, s32[1,1600]{1,0:T(1,128)}, u32[]{:S(2)}) copy-start(s32[1,1600]{1,0:T(1,128)} %param.36) | copy-start | bytes 19204
  10.0 180.1 %all-gather.7.cloned.1.call-start = ((), (), s32[]{:S(2)}) async-start(), calls=%async_computation.3 | async-start | bytes 10584064 | tf_op jit(solution)/shard_map/all_gather | solution.py:1330
  98.5 260.5 %all-gather.9.cloned.1.call-start = ((), (), s32[]{:S(2)}) async-start(), calls=%async_computation.6 | async-start | bytes 9830400 | tf_op jit(solution)/shard_map/all_gather | solution.py:1432
  98.6 31.4 %collective-permute-start = (f32[2,1280]{1,0:T(2,128)S(1)}, f32[2,1280]{1,0:T(2,128)S(1)}, u32[]{:S(2)}, u32[]{:S(2)}) collective-permute-start(f32[2,1280]{1,0:T(2,128)S(1)} %bitcast.132), channel_id=1, source_target_pairs={{0,1},{1,0},{2,3},{3,2},{4,5},{5,4},{6,7},{7,6},{8,9},{9,8},{10,11... | collective-permute-start | bytes 30728 | tf_op jit(solution)/shard_map/ppermute | solution.py:141
  99.3 72.4 %copy-start.2 = (f32[1600,1]{1,0:T(8,128)}, f32[1600,1]{1,0:T(8,128)S(1)}, u32[]{:S(2)}) copy-start(f32[1600,1]{1,0:T(8,128)S(1)} %copy.110.crop_ref) | copy-start | bytes 19204
  130.3 15.6 %copy-start.8 = (f32[1600,128]{1,0:T(8,128)}, f32[1600,128]{1,0:T(8,128)S(1)}, u32[]{:S(2)}) copy-start(f32[1600,128]{1,0:T(8,128)S(1)} %broadcast_in_dim.28.col_ref) | copy-start | bytes 2457604
  145.9 1.5 copy-start.21
  147.4 24.3 %copy-start.6 = (bf16[2048,192]{1,0:T(8,128)(2,1)S(1)}, bf16[2048,192]{1,0:T(8,128)(2,1)}, u32[]{:S(2)}) copy-start(bf16[2048,192]{1,0:T(8,128)(2,1)} %get-tuple-element.74.stem_ref) | copy-start | bytes 2359300
  190.1 31.3 %copy-start.54 = (s32[1,1600]{1,0:T(1,128)S(1)}, s32[1,1600]{1,0:T(1,128)}, u32[]{:S(2)}) copy-start(s32[1,1600]{1,0:T(1,128)} %param.32) | copy-start | bytes 19204
  190.1 33.9 %copy-start.53 = (f32[1,2,1600]{2,1,0:T(2,128)S(1)}, f32[1,2,1600]{2,1,0:T(2,128)}, u32[]{:S(2)}) copy-start(f32[1,2,1600]{2,1,0:T(2,128)} %param.33) | copy-start | bytes 38404
  190.1 33.9 %copy-start.55 = (f32[1,1600]{1,0:T(1,128)S(1)}, f32[1,1600]{1,0:T(1,128)}, u32[]{:S(2)}) copy-start(f32[1,1600]{1,0:T(1,128)} %param.35) | copy-start | bytes 19204
  221.3 21.9 %copy-start.7 = (bf16[1600,256]{1,0:T(8,128)(2,1)S(1)}, bf16[1600,256]{1,0:T(8,128)(2,1)}, u32[]{:S(2)}) copy-start(bf16[1600,256]{1,0:T(8,128)(2,1)} %get-tuple-element.88.own_ref) | copy-start | bytes 2457604
  221.3 21.9 %copy-start.14 = (bf16[256,768]{1,0:T(8,128)(2,1)S(1)}, bf16[256,768]{1,0:T(8,128)(2,1)}, u32[]{:S(2)}) copy-start(bf16[256,768]{1,0:T(8,128)(2,1)} %get-tuple-element.86.project_ref) | copy-start | bytes 1179652
  221.3 21.9 %copy-start.17 = (f32[1,128]{1,0:T(1,128)S(1)}, f32[1,128]{1,0:T(1,128)}, u32[]{:S(2)}) copy-start(f32[1,128]{1,0:T(1,128)} %get-tuple-element.95.pool_pre_ref) | copy-start | bytes 1540
  222.5 20.6 %collective-permute-start.1 = (bf16[1600,256]{1,0:T(8,128)(2,1)}, bf16[1600,256]{1,0:T(8,128)(2,1)S(1)}, u32[]{:S(2)}, u32[]{:S(2)}) collective-permute-start(bf16[1600,256]{1,0:T(8,128)(2,1)} %get-tuple-element.88.own_ref), channel_id=1, source_target_pairs={{0,1},{1,0},{2,3},{3,2},{4,5},{5,4},{6,7},{7,6},{8,9},{9,8},{10,11... | collective-permute-start | bytes 2457608 | tf_op jit(solution)/shard_map/ppermute | solution.py:141
  254.9 18.7 %copy-start.18 = (bf16[1600,256]{1,0:T(8,128)(2,1)}, bf16[1600,256]{1,0:T(8,128)(2,1)S(1)}, u32[]{:S(2)}) copy-start(bf16[1600,256]{1,0:T(8,128)(2,1)S(1)} %get-tuple-element.114) | copy-start | bytes 2457604
  273.7 243.3 %reduce-scatter.3.cloned.1.call-start = ((), (), s32[]{:S(2)}) async-start(), calls=%async_computation.4 | async-start | bytes 16154624 | tf_op jit(solution)/shard_map/reduce_scatter | solution.py:1439
  332.0 27.0 %copy-start.1 = (bf16[1600,1024]{1,0:T(8,128)(2,1)S(1)}, bf16[1600,1024]{1,0:T(8,128)(2,1)}, u32[]{:S(2)}) copy-start(bf16[1600,1024]{1,0:T(8,128)(2,1)} %pyramid_field.3.own_ref) | copy-start | bytes 9830404
  332.1 266.7 %reduce-scatter.5.cloned.1.call-start = ((), (), s32[]{:S(2)}) async-start(), calls=%async_computation.5 | async-start | bytes 5570560 | tf_op jit(solution)/shard_map/reduce_scatter | solution.py:1539
  359.0 2.9 copy-start
  363.0 14.2 %copy-start.4 = (bf16[2,2048,512]{2,1,0:T(8,128)(2,1)S(1)}, bf16[2,2048,512]{2,1,0:T(8,128)(2,1)}, u32[]{:S(2)}) copy-start(bf16[2,2048,512]{2,1,0:T(8,128)(2,1)} %get-tuple-element.76.reduce_ref.w_ref.bottle_hbm) | copy-start | bytes 12582916
  377.2 9.7 %copy-start.22 = (bf16[1600,512]{1,0:T(8,128)(2,1)S(1)}, bf16[1600,512]{1,0:T(8,128)(2,1)}, u32[]{:S(2)}) copy-start(bf16[1600,512]{1,0:T(8,128)(2,1)} %get-tuple-element.80.a_ref) | copy-start | bytes 4915204
  386.3 52.3 %collective-permute-start.2 = (bf16[1600,512]{1,0:T(8,128)(2,1)}, bf16[1600,512]{1,0:T(8,128)(2,1)}, u32[]{:S(2)}, u32[]{:S(2)}) collective-permute-start(bf16[1600,512]{1,0:T(8,128)(2,1)} %get-tuple-element.110), channel_id=1, source_target_pairs={{0,1},{1,0},{2,3},{3,2},{4,5},{5,4},{6,7},{7,6},{8,9},{9,8},{10,11... | collective-permute-start | bytes 4915208 | tf_op jit(solution)/shard_map/ppermute | solution.py:141
  386.9 4.6 copy-start.19
  386.9 4.6 copy-start.60
  389.0 3.4 copy-start.11
  389.0 3.4 copy-start.13
  390.1 45.8 %collective-permute-start.3 = (bf16[1024,256]{1,0:T(8,128)(2,1)}, bf16[1024,256]{1,0:T(8,128)(2,1)}, u32[]{:S(2)}, u32[]{:S(2)}) collective-permute-start(bf16[1024,256]{1,0:T(8,128)(2,1)} %get-tuple-element.210), channel_id=1, source_target_pairs={{0,1},{1,0},{2,3},{3,2},{4,5},{5,4},{6,7},{7,6},{8,9},{9,8},{10,11... | collective-permute-start | bytes 1572872 | tf_op jit(solution)/shard_map/ppermute | solution.py:141
  438.6 2.7 copy-start.9
  438.6 2.8 copy-start.23
  438.6 8.7 %slice-start = ((s8[4718592]{0:T(1024)(128)(4,1)}), s8[4194304]{0:T(1024)(128)(4,1)S(1)}, s32[]{:S(2)}) async-start(s8[4718592]{0:T(1024)(128)(4,1)} %bitcast.140), calls=%async_computation.7 | async-start | bytes 8388608
  441.4 5.9 slice-start.1
  447.2 9.4 %copy-start.24 = (f32[1600,512]{1,0:T(8,128)S(1)}, f32[1600,512]{1,0:T(8,128)}, u32[]{:S(2)}) copy-start(f32[1600,512]{1,0:T(8,128)} %get-tuple-element.78.a_ref) | copy-start | bytes 9830404
  480.9 7.1 %copy-start.27 = (bf16[2048,256]{1,0:T(8,128)(2,1)S(1)}, bf16[2048,256]{1,0:T(8,128)(2,1)}, u32[]{:S(2)}) copy-start(bf16[2048,256]{1,0:T(8,128)(2,1)} %maximum_select_fusion) | copy-start | bytes 3145732
  486.8 2.2 copy-start.25
  489.0 2.4 copy-start.30
  490.6 28.6 %copy-start.57 = (f32[25]{0:T(128)S(1)}, f32[25]{0:T(128)}, u32[]{:S(2)}) copy-start(f32[25]{0:T(128)} %param.59) | copy-start | bytes 304
  517.0 7.0 %copy-start.28 = (bf16[29,128,128]{2,1,0:T(8,128)(2,1)S(1)}, bf16[29,128,128]{2,1,0:T(8,128)(2,1)}, u32[]{:S(2)}) copy-start(bf16[29,128,128]{2,1,0:T(8,128)(2,1)} %reduce-scatter.3.cloned.1.call-done) | copy-start | bytes 2850820
  517.0 109.6 %copy-start.26 = (f32[29,128,128]{2,1,0:T(8,128)S(1)}, f32[29,128,128]{2,1,0:T(8,128)}, u32[]{:S(2)}) copy-start(f32[29,128,128]{2,1,0:T(8,128)} %param.47) | copy-start | bytes 5701636
  519.2 2.7 copy-start.58
  522.5 98.6 %copy-start.59 = (f32[22]{0:T(128)S(1)}, f32[22]{0:T(128)}, u32[]{:S(2)}) copy-start(f32[22]{0:T(128)} %copy-done.58) | copy-start | bytes 268
  525.1 101.6 %copy-start.29 = (bf16[29,128,128]{2,1,0:T(8,128)(2,1)S(1)}, bf16[29,128,128]{2,1,0:T(8,128)(2,1)}, u32[]{:S(2)}) copy-start(bf16[29,128,128]{2,1,0:T(8,128)(2,1)} %reduce-scatter.3.cloned.1.call-done) | copy-start | bytes 2850820
  626.6 6.1 copy-start.44
  626.6 6.1 copy-start.46
  626.7 6.1 copy-start.47
  626.7 6.8 %copy-start.34 = (f32[1,256,256]{2,1,0:T(8,128)S(1)}, f32[1,256,256]{2,1,0:T(8,128)}, u32[]{:S(2)}) copy-start(f32[1,256,256]{2,1,0:T(8,128)} %slice_multiply_fusion.1) | copy-start | bytes 786436
  626.7 6.8 %copy-start.36 = (f32[2,128,256]{2,1,0:T(8,128)S(1)}, f32[2,128,256]{2,1,0:T(8,128)}, u32[]{:S(2)}) copy-start(f32[2,128,256]{2,1,0:T(8,128)} %param.41) | copy-start | bytes 786436
  626.7 6.8 %copy-start.41 = (f32[2,128,256]{2,1,0:T(8,128)S(1)}, f32[2,128,256]{2,1,0:T(8,128)}, u32[]{:S(2)}) copy-start(f32[2,128,256]{2,1,0:T(8,128)} %param.42) | copy-start | bytes 786436
  626.7 6.8 %copy-start.42 = (f32[2,128,256]{2,1,0:T(8,128)S(1)}, f32[2,128,256]{2,1,0:T(8,128)}, u32[]{:S(2)}) copy-start(f32[2,128,256]{2,1,0:T(8,128)} %param.43) | copy-start | bytes 786436
  626.7 7.8 %copy-start.32 = (f32[9,32,256]{2,1,0:T(8,128)S(1)}, f32[9,32,256]{2,1,0:T(8,128)}, u32[]{:S(2)}) copy-start(f32[9,32,256]{2,1,0:T(8,128)} %param.44) | copy-start | bytes 884740
  626.7 7.8 %copy-start.33 = (f32[1,288,256]{2,1,0:T(8,128)S(1)}, f32[1,288,256]{2,1,0:T(8,128)}, u32[]{:S(2)}) copy-start(f32[1,288,256]{2,1,0:T(8,128)} %slice_multiply_fusion) | copy-start | bytes 884740
  626.7 7.8 %copy-start.39 = (f32[9,32,256]{2,1,0:T(8,128)S(1)}, f32[9,32,256]{2,1,0:T(8,128)}, u32[]{:S(2)}) copy-start(f32[9,32,256]{2,1,0:T(8,128)} %param.45) | copy-start | bytes 884740
  626.8 7.8 %copy-start.40 = (f32[9,32,256]{2,1,0:T(8,128)S(1)}, f32[9,32,256]{2,1,0:T(8,128)}, u32[]{:S(2)}) copy-start(f32[9,32,256]{2,1,0:T(8,128)} %param.46) | copy-start | bytes 884740
  (8 other events, 6.6 us)
Sparse Core Ops, SparseCore 0:
  10.3 78.0 all-gather.4
  98.6 91.3 all-gather.6
  273.8 85.1 all-gather.8
  363.0 153.9 reduce-scatter.2
  521.2 77.5 reduce-scatter.4

commit v6 on v5

--- a/solution.py
+++ b/solution.py
@@ -563,72 +563,27 @@
         ).astype(fields.dtype)
 
 
-def weight_kernel(xt_ref, g_ref, col_ref, pool_ref, pool_grad_ref, o_ref, fields):
-    width = g_ref.shape[2]
-    depth = xt_ref.shape[0]
-    fill_fields(g_ref, col_ref, fields)
-    block = 512
-    for row_step, group in zip(PYRAMID_ROWS, ROW_GROUPS):
-        r0, r1 = valid(row_step, FH)
-        first = r0 * FW // 128 * 128
-        last = min(POSITIONS, -(-r1 * FW // 128) * 128)
-        base = PAD + first - row_step * FW
-        sets = [group[at : at + 2] for at in range(0, 10, 2)] if row_step == 0 else [group]
-        for chosen in sets:
-            right = jnp.concatenate(
-                [fields[place, base : base + last - first] for tap, place in chosen], 1
-            )
-
-            def step(index, carry):
-                rows = pl.ds(pl.multiple_of(index * block, 16), block)
-                part = dot(xt_ref[rows, first:last], right)
-                for offset, (tap, place) in enumerate(chosen):
-                    o_ref[tap, rows] = part[:, offset * width : (offset + 1) * width].astype(
-                        o_ref.dtype
-                    )
-                return carry
-
-            lax.fori_loop(0, depth // block, step, 0)
-    o_ref[28] = (pool_ref[...] * pool_grad_ref[...]).astype(o_ref.dtype)
-
-
-def pyramid_weights(field_t, grads, columns, pooled, pool_grad):
-    depth = field_t.shape[0]
-    width = grads.shape[2]
-    return pl.pallas_call(
-        weight_kernel,
-        out_shape=jax.ShapeDtypeStruct((29, depth, width), jnp.bfloat16),
-        in_specs=vmem(5),
-        out_specs=vmem(1)[0],
-        scratch_shapes=[pltpu.VMEM((10, POSITIONS + 2 * PAD, width), jnp.bfloat16)],
-        compiler_params=pltpu.CompilerParams(vmem_limit_bytes=56 << 20),
-        cost_estimate=pl.CostEstimate(
-            flops=3 * 10**10, bytes_accessed=20 << 20, transcendentals=0
-        ),
-        name="pyramid_weights",
-    )(field_t, grads, columns, pooled, pool_grad)
-
-
-def field_kernel(
-    half_ref, a_hbm, b_hbm, g_ref, pool_ref, crop_ref, col_ref, o_ref, weights, pool_weights, fields, stack, sems
-):
-    width = g_ref.shape[2]
-    depth = o_ref.shape[1]
-    half = pl.ds(pl.multiple_of(half_ref[0] * depth, 16), depth)
-    copies = []
-    for slot, tap in enumerate(TAP_ORDER):
-        copy = pltpu.make_async_copy(
-            tap_of(a_hbm, b_hbm, tap).at[half], weights.at[:, pl.ds(slot * width, width)], sems.at[slot]
-        )
+def start_field_copies(place_ref, a_hbm, b_hbm, depth, weights, pool_weights, sems):
+    width = pool_weights.shape[1]
+    rows = pl.ds(pl.multiple_of(place_ref[0] * depth, 16), depth)
+    copies = [
+        pltpu.make_async_copy(
+            tap_of(a_hbm, b_hbm, tap).at[rows],
+            weights.at[:, pl.ds(slot * width, width)],
+            sems.at[slot],
+        )
+        for slot, tap in enumerate(TAP_ORDER)
+    ]
+    copies.append(
+        pltpu.make_async_copy(tap_of(a_hbm, b_hbm, 28).at[rows], pool_weights, sems.at[28])
+    )
+    for copy in copies:
         copy.start()
-        copies.append(copy)
-    copies.append(
-        pltpu.make_async_copy(tap_of(a_hbm, b_hbm, 28).at[half], pool_weights, sems.at[28])
-    )
-    copies[-1].start()
-    fill_fields(g_ref, col_ref, fields)
-    for copy in copies:
-        copy.wait()
+    return copies
+
+
+def field_products(pool_ref, crop_ref, o_ref, weights, pool_weights, fields, stack):
+    width = pool_weights.shape[1]
     pooled = dot(
         jnp.broadcast_to(pool_ref[...], (16, width)).astype(jnp.bfloat16), pool_weights[...], (1, 1)
     )[0:1] / jnp.sum(crop_ref[...], keepdims=True)
@@ -653,15 +608,137 @@
         )
 
 
-def pyramid_field(half, weights, grads, pool_grad, crop, columns):
-    depth, width = weights[0].shape[1] // 2, weights[0].shape[2]
+def field_kernel(
+    place_ref, a_hbm, b_hbm, g_ref, pool_ref, crop_ref, col_ref, o_ref, weights, pool_weights, fields, stack, sems
+):
+    copies = start_field_copies(
+        place_ref, a_hbm, b_hbm, o_ref.shape[1], weights, pool_weights, sems
+    )
+    fill_fields(g_ref, col_ref, fields)
+    for copy in copies:
+        copy.wait()
+    field_products(pool_ref, crop_ref, o_ref, weights, pool_weights, fields, stack)
+
+
+def own_kernel(
+    place_ref,
+    a_hbm,
+    b_hbm,
+    xt_hbm,
+    g_ref,
+    pool_ref,
+    crop_ref,
+    col_ref,
+    pooled_ref,
+    o_ref,
+    w_out,
+    weights,
+    pool_weights,
+    fields,
+    stack,
+    xt_ref,
+    stage,
+    sems,
+    xt_sem,
+    out_sems,
+):
+    copies = start_field_copies(
+        place_ref, a_hbm, b_hbm, o_ref.shape[1], weights, pool_weights, sems
+    )
+    xt_copy = pltpu.make_async_copy(xt_hbm, xt_ref, xt_sem)
+    xt_copy.start()
+    fill_fields(g_ref, col_ref, fields)
+    for copy in copies:
+        copy.wait()
+    field_products(pool_ref, crop_ref, o_ref, weights, pool_weights, fields, stack)
+    xt_copy.wait()
+    width = g_ref.shape[2]
+    depth = xt_ref.shape[0]
+    block = 1024
+    waiting = [[], []]
+    turn = 0
+    for row_step, group in zip(PYRAMID_ROWS, ROW_GROUPS):
+        r0, r1 = valid(row_step, FH)
+        first = r0 * FW // 128 * 128
+        last = min(POSITIONS, -(-r1 * FW // 128) * 128)
+        base = PAD + first - row_step * FW
+        sets = [group[at : at + 2] for at in range(0, 10, 2)] if row_step == 0 else [group]
+        for chosen in sets:
+            slot = turn % 2
+            turn += 1
+            for copy in waiting[slot]:
+                copy.wait()
+            right = jnp.concatenate(
+                [fields[place, base : base + last - first] for tap, place in chosen], 1
+            )
+
+            def step(index, carry):
+                rows = pl.ds(pl.multiple_of(index * block, 16), block)
+                part = dot(xt_ref[rows, first:last], right)
+                for offset in range(len(chosen)):
+                    stage[slot, offset, rows] = part[
+                        :, offset * width : (offset + 1) * width
+                    ].astype(stage.dtype)
+                return carry
+
+            lax.fori_loop(0, depth // block, step, 0)
+            waiting[slot] = [
+                pltpu.make_async_copy(
+                    stage.at[slot, offset], w_out.at[tap], out_sems.at[slot, offset]
+                )
+                for offset, (tap, place) in enumerate(chosen)
+            ]
+            for copy in waiting[slot]:
+                copy.start()
+    slot = turn % 2
+    for copy in waiting[slot]:
+        copy.wait()
+    stage[slot, 0] = (pooled_ref[...] * pool_ref[...]).astype(stage.dtype)
+    last_copy = pltpu.make_async_copy(stage.at[slot, 0], w_out.at[28], out_sems.at[slot, 0])
+    last_copy.start()
+    for copy in waiting[1 - slot]:
+        copy.wait()
+    last_copy.wait()
+
+
+def own_gradients(place, weights, field_t, grads, pool_grad, crop, columns, pooled):
+    depth, width = weights[0].shape[1:]
+    hbm = pl.BlockSpec(memory_space=pltpu.HBM)
+    half = depth // 2
+    return pl.pallas_call(
+        own_kernel,
+        out_shape=[
+            jax.ShapeDtypeStruct((POSITIONS, half), jnp.bfloat16),
+            jax.ShapeDtypeStruct((29, depth, width), jnp.bfloat16),
+        ],
+        in_specs=[pl.BlockSpec(memory_space=pltpu.SMEM), hbm, hbm, hbm] + vmem(5),
+        out_specs=[pl.BlockSpec(memory_space=pltpu.VMEM), hbm],
+        scratch_shapes=[
+            pltpu.VMEM((half, 28 * width), jnp.bfloat16),
+            pltpu.VMEM((half, width), jnp.bfloat16),
+            pltpu.VMEM((10, POSITIONS + 2 * PAD, width), jnp.bfloat16),
+            pltpu.VMEM((8 * FW, 19 * width), jnp.bfloat16),
+            pltpu.VMEM((depth, POSITIONS), jnp.bfloat16),
+            pltpu.VMEM((2, 3, depth, width), jnp.bfloat16),
+            pltpu.SemaphoreType.DMA((29,)),
+            pltpu.SemaphoreType.DMA,
+            pltpu.SemaphoreType.DMA((2, 3)),
+        ],
+        compiler_params=pltpu.CompilerParams(vmem_limit_bytes=60 << 20),
+        cost_estimate=pl.CostEstimate(flops=1000, bytes_accessed=1024, transcendentals=0),
+        name="own_gradients",
+    )(place, weights[0], weights[1], field_t, grads, pool_grad, crop, columns, pooled)
+
+
+def pyramid_field(place, depth, weights, grads, pool_grad, crop, columns):
+    width = weights[0].shape[2]
     return pl.pallas_call(
         field_kernel,
         out_shape=jax.ShapeDtypeStruct((POSITIONS, depth), jnp.bfloat16),
         in_specs=[
             pl.BlockSpec(memory_space=pltpu.SMEM),
-            pl.BlockSpec(memory_space=pl.ANY),
-            pl.BlockSpec(memory_space=pl.ANY),
+            pl.BlockSpec(memory_space=pltpu.HBM),
+            pl.BlockSpec(memory_space=pltpu.HBM),
             pl.BlockSpec(memory_space=pltpu.VMEM),
             pl.BlockSpec(memory_space=pltpu.VMEM),
             pl.BlockSpec(memory_space=pltpu.VMEM),
@@ -675,12 +752,12 @@
             pltpu.VMEM((8 * FW, 19 * width), jnp.bfloat16),
             pltpu.SemaphoreType.DMA((29,)),
         ],
-        compiler_params=pltpu.CompilerParams(vmem_limit_bytes=56 << 20),
+        compiler_params=pltpu.CompilerParams(vmem_limit_bytes=60 << 20),
         cost_estimate=pl.CostEstimate(
-            flops=3 * 10**10, bytes_accessed=20 << 20, transcendentals=0
+            flops=1000, bytes_accessed=1024, transcendentals=0
         ),
         name="pyramid_field",
-    )(half, weights[0], weights[1], grads, pool_grad, crop, columns)
+    )(place, weights[0], weights[1], grads, pool_grad, crop, columns)
 
 
 BLOCK = 320
@@ -694,7 +771,7 @@
     return jax.vjp(jax.nn.gelu, values)[1](upstream)[0]
 
 
-def stem_kernel(p_ref, stem_ref, reduce_ref, crop_ref, count_ref, x_ref, a_ref, stat_ref):
+def stem_kernel(p_ref, stem_ref, reduce_ref, crop_ref, mask_ref, xt_ref, a_ref, stat_ref, x_ref):
     def step(index, carry):
         rows = block_rows(index)
         low = (crop_ref[rows] * dot(p_ref[rows], stem_ref[...], (1, 1))).astype(x_ref.dtype)
@@ -708,17 +785,23 @@
 
     zero = jnp.zeros((1, MID), jnp.float32)
     total, square = lax.fori_loop(0, POSITIONS // BLOCK, step, (zero, zero))
-    stat_ref[...] = jnp.concatenate(
-        [total, square, count_ref[...], jnp.zeros((5, MID), jnp.float32)], 0
-    )
-
-
-def stem_reduce(patches, stem, bottle, crop, counts):
+    for at in range(0, D, 256):
+        xt_ref[at : at + 256] = x_ref[:, at : at + 256].T
+    masks = mask_ref[...].astype(jnp.float32)
+    lane = lax.broadcasted_iota(jnp.int32, (1, MID), 1)
+    counts = jnp.zeros((1, MID), jnp.float32)
+    for place in range(3):
+        kept = masks[0:1] if place == 0 else masks[0:1] * masks[place : place + 1]
+        counts = jnp.where(lane == place, jnp.sum(kept, 1, keepdims=True), counts)
+    stat_ref[...] = jnp.concatenate([total, square, counts, jnp.zeros((5, MID), jnp.float32)], 0)
+
+
+def stem_reduce(patches, stem, bottle, crop, masks):
     return pl.pallas_call(
         stem_kernel,
         grid=(1,),
         out_shape=[
-            jax.ShapeDtypeStruct((POSITIONS, D), jnp.bfloat16),
+            jax.ShapeDtypeStruct((D, POSITIONS), jnp.bfloat16),
             jax.ShapeDtypeStruct((POSITIONS, MID), jnp.float32),
             jax.ShapeDtypeStruct((8, MID), jnp.float32),
         ],
@@ -727,17 +810,18 @@
             pl.BlockSpec(stem.shape, lambda i: (0, 0)),
             pl.BlockSpec((1, D, MID), lambda i: (0, 0, 0)),
             pl.BlockSpec((POSITIONS, 1), lambda i: (0, 0)),
-            pl.BlockSpec((1, MID), lambda i: (0, 0)),
+            pl.BlockSpec((3, POSITIONS), lambda i: (0, 0)),
         ],
         out_specs=[
-            pl.BlockSpec((POSITIONS, D), lambda i: (0, 0)),
+            pl.BlockSpec((D, POSITIONS), lambda i: (0, 0)),
             pl.BlockSpec((POSITIONS, MID), lambda i: (0, 0)),
             pl.BlockSpec((8, MID), lambda i: (0, 0)),
         ],
+        scratch_shapes=[pltpu.VMEM((POSITIONS, D), jnp.bfloat16)],
         compiler_params=pltpu.CompilerParams(vmem_limit_bytes=50 << 20),
         cost_estimate=pl.CostEstimate(flops=5 * 10**9, bytes_accessed=14 << 20, transcendentals=0),
         name="stem_reduce",
-    )(patches, stem, bottle, crop, counts)
+    )(patches, stem, bottle, crop, masks)
 
 
 def both_halves(gain_refs, first, last):
@@ -987,7 +1071,7 @@
             jax.ShapeDtypeStruct((POSITIONS, 5 * width), low),
             jax.ShapeDtypeStruct((POSITIONS, BRANCH), low),
         ],
-        in_specs=vmem(2) + [pl.BlockSpec(memory_space=pl.ANY)] * 2 + vmem(2),
+        in_specs=vmem(2) + [pl.BlockSpec(memory_space=pltpu.HBM)] * 2 + vmem(2),
         out_specs=vmem(4),
         scratch_shapes=[
             pltpu.VMEM((depth, 28 * width), low),
@@ -1115,43 +1199,62 @@
     return mean, lax.rsqrt(own_rows(stat, place_ref, 4) / count - mean * mean + norm_eps), count
 
 
+def start_rows(place_ref, sources, targets, sems):
+    depth = targets[0].shape[1]
+    half = pl.ds(pl.multiple_of(place_ref[0] * depth, 128), depth)
+    own_hbm, first_hbm, second_hbm, y_hbm = sources
+    own_ref, other_ref, y_ref = targets
+    blocks = []
+    for index in range(POSITIONS // BLOCK):
+        rows = pl.ds(index * BLOCK, BLOCK)
+        pairs = (
+            (own_hbm.at[rows], own_ref.at[rows]),
+            (first_hbm.at[rows], other_ref.at[rows, : depth // 2]),
+            (second_hbm.at[rows], other_ref.at[rows, depth // 2 :]),
+            (y_hbm.at[rows, half], y_ref.at[rows]),
+        )
+        copies = [
+            pltpu.make_async_copy(source, target, sems.at[index, at])
+            for at, (source, target) in enumerate(pairs)
+        ]
+        for copy in copies:
+            copy.start()
+        blocks.append(copies)
+    return blocks
+
+
 def residual_sums_kernel(
     place_ref,
-    own_ref,
-    other_hbm,
+    own_hbm,
+    first_hbm,
+    second_hbm,
     y_hbm,
     stat_ref,
     count_ref,
     crop_ref,
     head_ref,
     o_ref,
+    own_ref,
+    other_ref,
     y_ref,
-    other_ref,
     sems,
 ):
     depth = own_ref.shape[1]
-    half = pl.ds(pl.multiple_of(place_ref[0] * depth, 128), depth)
-    copy = pltpu.make_async_copy(y_hbm.at[:, half], y_ref, sems.at[0])
-    copy.start()
-    other_copy = pltpu.make_async_copy(other_hbm.at[1 - place_ref[0]], other_ref, sems.at[1])
-    other_copy.start()
+    blocks = start_rows(
+        place_ref, (own_hbm, first_hbm, second_hbm, y_hbm), (own_ref, other_ref, y_ref), sems
+    )
     mean, scale, count = own_norm(place_ref, stat_ref, count_ref)
-    copy.wait()
-    other_copy.wait()
-
-    def step(index, carry):
-        rows = block_rows(index)
+    sums = [jnp.zeros((1, depth), jnp.float32)] * 2
+    for index, copies in enumerate(blocks):
+        for copy in copies:
+            copy.wait()
+        rows = slice(index * BLOCK, (index + 1) * BLOCK)
         up = crop_ref[rows] * (
             own_ref[rows].astype(jnp.float32) + other_ref[rows].astype(jnp.float32)
         )
         normed = (y_ref[rows].astype(jnp.float32) - mean) * scale
-        return (
-            carry[0] + jnp.sum(up * normed, 0, keepdims=True),
-            carry[1] + jnp.sum(up, 0, keepdims=True),
-        )
-
-    zero = jnp.zeros((1, depth), jnp.float32)
-    sums = lax.fori_loop(0, POSITIONS // BLOCK, step, (zero, zero))
+        sums[0] = sums[0] + jnp.sum(up * normed, 0, keepdims=True)
+        sums[1] = sums[1] + jnp.sum(up, 0, keepdims=True)
     for turn, values in enumerate(sums):
         for part in range(2):
             row = 2 * turn + part
@@ -1163,29 +1266,25 @@
 
 
 def residual_sums(place, own, other, expanded, stat, counts, crop, head_stat):
+    hbm = pl.BlockSpec(memory_space=pltpu.HBM)
     return pl.pallas_call(
         residual_sums_kernel,
         out_shape=jax.ShapeDtypeStruct((8, MID), jnp.float32),
-        in_specs=[pl.BlockSpec(memory_space=pltpu.SMEM)]
-        + vmem(1)
-        + [pl.BlockSpec(memory_space=pl.ANY)] * 2
-        + vmem(4),
+        in_specs=[pl.BlockSpec(memory_space=pltpu.SMEM)] + [hbm] * 4 + vmem(4),
         out_specs=vmem(1)[0],
-        scratch_shapes=[
-            pltpu.VMEM(own.shape, jnp.bfloat16),
-            pltpu.VMEM(own.shape, jnp.bfloat16),
-            pltpu.SemaphoreType.DMA((2,)),
-        ],
-        compiler_params=pltpu.CompilerParams(vmem_limit_bytes=40 << 20),
+        scratch_shapes=[pltpu.VMEM(own.shape, jnp.bfloat16)] * 3
+        + [pltpu.SemaphoreType.DMA((POSITIONS // BLOCK, 4))],
+        compiler_params=pltpu.CompilerParams(vmem_limit_bytes=60 << 20),
         cost_estimate=pl.CostEstimate(flops=10**8, bytes_accessed=12 << 20, transcendentals=0),
         name="residual_sums",
-    )(place, own, other, expanded, stat, counts, crop, head_stat)
+    )(place, own, *other, expanded, stat, counts, crop, head_stat)
 
 
 def residual_back_kernel(
     place_ref,
-    own_ref,
-    other_hbm,
+    own_hbm,
+    first_hbm,
+    second_hbm,
     y_hbm,
     stat_ref,
     count_ref,
@@ -1195,43 +1294,40 @@
     bottle_hbm,
     o_ref,
     part_ref,
+    own_ref,
+    other_ref,
     y_ref,
-    other_ref,
     weights,
     sems,
+    weight_sem,
 ):
     depth = own_ref.shape[1]
-    half = pl.ds(pl.multiple_of(place_ref[0] * depth, 128), depth)
-    copy = pltpu.make_async_copy(y_hbm.at[:, half], y_ref, sems.at[0])
-    copy.start()
-    weight_copy = pltpu.make_async_copy(bottle_hbm.at[1, half], weights, sems.at[1])
+    half = pl.ds(pl.multiple_of(place_ref[0] * depth, 16), depth)
+    weight_copy = pltpu.make_async_copy(bottle_hbm.at[1, half], weights, weight_sem)
     weight_copy.start()
-    other_copy = pltpu.make_async_copy(other_hbm.at[1 - place_ref[0]], other_ref, sems.at[2])
-    other_copy.start()
+    blocks = start_rows(
+        place_ref, (own_hbm, first_hbm, second_hbm, y_hbm), (own_ref, other_ref, y_ref), sems
+    )
     mean, scale, count = own_norm(place_ref, stat_ref, count_ref)
     sums = sum_ref[...]
     gain_grad = jnp.concatenate([sums[0:1], sums[1:2]], 1) / count
     shift_grad = jnp.concatenate([sums[2:3], sums[3:4]], 1) / count
     factor = gain_ref[0:1, MID // 2 :] * scale
-    copy.wait()
     weight_copy.wait()
-    other_copy.wait()
-
-    def step(index, carry):
-        rows = block_rows(index)
+    for index, copies in enumerate(blocks):
+        for copy in copies:
+            copy.wait()
+        rows = slice(index * BLOCK, (index + 1) * BLOCK)
         crop = crop_ref[rows]
         up = crop * (own_ref[rows].astype(jnp.float32) + other_ref[rows].astype(jnp.float32))
         normed = (y_ref[rows].astype(jnp.float32) - mean) * scale
         low = (crop * factor * (up - (shift_grad + normed * gain_grad))).astype(o_ref.dtype)
         o_ref[rows] = low
         part_ref[rows] = dot(low, weights[...]).astype(part_ref.dtype)
-        return carry
-
-    lax.fori_loop(0, POSITIONS // BLOCK, step, 0)
 
 
 def residual_back(place, own, other, expanded, stat, counts, sums, gains, crop, bottle):
-    hbm = pl.BlockSpec(memory_space=pl.ANY)
+    hbm = pl.BlockSpec(memory_space=pltpu.HBM)
     depth = own.shape[1]
     return pl.pallas_call(
         residual_back_kernel,
@@ -1239,18 +1335,458 @@
             jax.ShapeDtypeStruct((POSITIONS, depth), jnp.bfloat16),
             jax.ShapeDtypeStruct((POSITIONS, MID), jnp.bfloat16),
         ],
-        in_specs=[pl.BlockSpec(memory_space=pltpu.SMEM)] + vmem(1) + [hbm] * 2 + vmem(5) + [hbm],
+        in_specs=[pl.BlockSpec(memory_space=pltpu.SMEM)] + [hbm] * 4 + vmem(5) + [hbm],
+        out_specs=vmem(2),
+        scratch_shapes=[pltpu.VMEM(own.shape, jnp.bfloat16)] * 3
+        + [
+            pltpu.VMEM((depth, MID), jnp.bfloat16),
+            pltpu.SemaphoreType.DMA((POSITIONS // BLOCK, 4)),
+            pltpu.SemaphoreType.DMA,
+        ],
+        compiler_params=pltpu.CompilerParams(vmem_limit_bytes=60 << 20),
+        cost_estimate=pl.CostEstimate(flops=2 * 10**9, bytes_accessed=16 << 20, transcendentals=0),
+        name="residual_back",
+    )(place, own, *other, expanded, stat, counts, sums, gains, crop, bottle)
+
+
+def late_kernel(
+    place_ref,
+    up_ref,
+    a_ref,
+    stat_ref,
+    sum_ref,
+    gain_ref,
+    other_gain_ref,
+    crop_ref,
+    patch_ref,
+    bottle_hbm,
+    own_hbm,
+    first_hbm,
+    second_hbm,
+    xt_hbm,
+    reduce_ref,
+    stem_ref,
+    weights,
+    own_ref,
+    other_ref,
+    xt_ref,
+    low_ref,
+    start_ref,
+    sems,
+):
+    depth = own_ref.shape[1]
+    half = pl.ds(pl.multiple_of(place_ref[0] * depth, 16), depth)
+    copies = [
+        pltpu.make_async_copy(source, target, sems.at[at])
+        for at, (source, target) in enumerate(
+            (
+                (bottle_hbm.at[0, half], weights),
+                (own_hbm, own_ref),
+                (first_hbm, other_ref.at[:, : depth // 2]),
+                (second_hbm, other_ref.at[:, depth // 2 :]),
+                (xt_hbm, xt_ref),
+            )
+        )
+    ]
+    for copy in copies:
+        copy.start()
+    count = stat_ref[2:3, 0:1]
+    mean, scale = norm_rows(stat_ref[...], count)
+    pair = both_halves((place_ref, gain_ref, other_gain_ref), 0, MID // 2)
+    factor = pair[0:1] * scale
+    gain_grad = sum_ref[0:1] / count
+    shift_grad = sum_ref[1:2] / count
+
+    def step(index, carry):
+        rows = block_rows(index)
+        normed = (a_ref[rows] - mean) * scale
+        low_ref[rows] = (
+            crop_ref[rows] * factor * (up_ref[rows] - (shift_grad + normed * gain_grad))
+        ).astype(low_ref.dtype)
+        return carry
+
+    lax.fori_loop(0, POSITIONS // BLOCK, step, 0)
+    for copy in copies[:4]:
+        copy.wait()
+
+    def start_step(index, carry):
+        rows = block_rows(index)
+        total = dot(low_ref[rows], weights[...], (1, 1)) + (
+            own_ref[rows].astype(jnp.float32) + other_ref[rows].astype(jnp.float32)
+        )
+        start_ref[rows] = (crop_ref[rows] * total).astype(start_ref.dtype)
+        return carry
+
+    lax.fori_loop(0, POSITIONS // BLOCK, start_step, 0)
+    for at in range(0, depth, 256):
+        part = dot(patch_ref[...], start_ref[:, at : at + 256]).astype(stem_ref.dtype)
+        stem_ref[at : at + 256] = part.T
+    copies[4].wait()
+    low = low_ref[...]
+    own_low = jnp.where(place_ref[0] == 0, low[:, : MID // 2], low[:, MID // 2 :])
+    block = 512
+
+    def reduce_step(index, carry):
+        rows = pl.ds(pl.multiple_of(index * block, 16), block)
+        reduce_ref[rows] = dot(xt_ref[rows], own_low).astype(reduce_ref.dtype)
+        return carry
+
+    lax.fori_loop(0, D // block, reduce_step, 0)
+
+
+def late_gradients(place, up, first_pre, stat, sums, gains, crop, patches_t, bottle, own, other, xt):
+    hbm = pl.BlockSpec(memory_space=pltpu.HBM)
+    depth = own.shape[1]
+    low = jnp.bfloat16
+    return pl.pallas_call(
+        late_kernel,
+        out_shape=[
+            jax.ShapeDtypeStruct((D, MID // 2), low),
+            jax.ShapeDtypeStruct((depth, PATCH), low),
+        ],
+        in_specs=[pl.BlockSpec(memory_space=pltpu.SMEM)] + vmem(8) + [hbm] * 5,
         out_specs=vmem(2),
         scratch_shapes=[
-            pltpu.VMEM(own.shape, jnp.bfloat16),
-            pltpu.VMEM(own.shape, jnp.bfloat16),
-            pltpu.VMEM((depth, MID), jnp.bfloat16),
-            pltpu.SemaphoreType.DMA((3,)),
-        ],
-        compiler_params=pltpu.CompilerParams(vmem_limit_bytes=40 << 20),
-        cost_estimate=pl.CostEstimate(flops=2 * 10**9, bytes_accessed=16 << 20, transcendentals=0),
-        name="residual_back",
-    )(place, own, other, expanded, stat, counts, sums, gains, crop, bottle)
+            pltpu.VMEM((depth, MID), low),
+            pltpu.VMEM(own.shape, low),
+            pltpu.VMEM(own.shape, low),
+            pltpu.VMEM(xt.shape, low),
+            pltpu.VMEM((POSITIONS, MID), low),
+            pltpu.VMEM(own.shape, low),
+            pltpu.SemaphoreType.DMA((5,)),
+        ],
+        compiler_params=pltpu.CompilerParams(vmem_limit_bytes=60 << 20),
+        cost_estimate=pl.CostEstimate(flops=4 * 10**9, bytes_accessed=24 << 20, transcendentals=0),
+        name="late_gradients",
+    )(place, up, first_pre, stat, sums, gains[1], gains[2], crop, patches_t, bottle, own, *other, xt)
+
+
+def scatter_kernel(
+    layers,
+    p_ref,
+    o_ref,
+    square_ref,
+    core_in,
+    y_out,
+    kept,
+    y_in,
+    z_out,
+    z_in,
+    core_send,
+    core_recv,
+    y_send,
+    y_recv,
+    z_send,
+    z_recv,
+):
+    z, y, core, x = place_of()
+    barrier = pltpu.get_barrier_semaphore()
+    sibling = device_at(z, y, 1 - core, x)
+    other_y = device_at(z, 1 - y, core, x)
+    layer_order = [z_flip(z, turn) for turn in range(1, layers)]
+    for target in [sibling, other_y] + [device_at(zz, y, core, x) for zz in layer_order]:
+        pl.semaphore_signal(barrier, inc=1, device_id=target, device_id_type=MESH_ID)
+    pl.semaphore_wait(barrier, layers + 1)
+    order = layer_order + [z]
+    pending = []
+
+    def send(source, target_ref, sems, place, device):
+        copy = pltpu.make_async_remote_copy(
+            src_ref=source,
+            dst_ref=target_ref,
+            send_sem=sems[0].at[place],
+            recv_sem=sems[1].at[place],
+            device_id=device,
+            device_id_type=MESH_ID,
+        )
+        copy.start()
+        pending.append(copy)
+
+    def arrive(target_ref, sems, place):
+        pltpu.make_async_remote_copy(
+            src_ref=target_ref,
+            dst_ref=target_ref,
+            send_sem=sems[0].at[place],
+            recv_sem=sems[1].at[place],
+            device_id=sibling,
+            device_id_type=MESH_ID,
+        ).wait_recv()
+
+    core_sems, y_sems, z_sems = (core_send, core_recv), (y_send, y_recv), (z_send, z_recv)
+    for zz in order:
+        for yy in (1 - y, y):
+            pair = zz * 2 + yy
+            send(p_ref.at[pair * 2 + 1 - core], core_in.at[pair], core_sems, pair, sibling)
+    for zz in order:
+        for yy in (1 - y, y):
+            pair = zz * 2 + yy
+            arrive(core_in.at[pair], core_sems, pair)
+            total = p_ref[pair * 2 + core].astype(jnp.float32) + core_in[pair].astype(jnp.float32)
+            if yy is y:
+                kept[zz] = total
+            else:
+                y_out[zz] = total.astype(y_out.dtype)
+                send(y_out.at[zz], y_in.at[zz], y_sems, zz, other_y)
+    for zz in order:
+        arrive(y_in.at[zz], y_sems, zz)
+        total = kept[zz] + y_in[zz].astype(jnp.float32)
+        if zz is z:
+            o_ref[...] = total
+        else:
+            z_out[zz] = total.astype(z_out.dtype)
+            copy = pltpu.make_async_remote_copy(
+                src_ref=z_out.at[zz],
+                dst_ref=z_in.at[z],
+                send_sem=z_send.at[zz],
+                recv_sem=z_recv.at[z],
+                device_id=device_at(zz, y, core, x),
+                device_id_type=MESH_ID,
+            )
+            copy.start()
+            pending.append(copy)
+    for zz in layer_order:
+        arrive(z_in.at[zz], z_sems, zz)
+        o_ref[...] += z_in[zz].astype(jnp.float32)
+    rows = o_ref.shape[0] - 48
+    values = o_ref[:rows]
+    small = o_ref[rows:]
+    row = lax.broadcasted_iota(jnp.int32, (48, 256), 0)
+    lane = lax.broadcasted_iota(jnp.int32, (48, 256), 1)
+    is_head = jnp.logical_and(row % 3 == 2, lane >= 128)
+    small = jnp.where(jnp.logical_and(is_head, x != 0), 0.0, small)
+    squares = jnp.sum(values * values, 0, keepdims=True) + jnp.sum(small * small, 0, keepdims=True)
+    square_ref[...] = jnp.concatenate(
+        [squares[:, :128] + squares[:, 128:], jnp.zeros((7, 128), jnp.float32)], 0
+    )
+    for copy in pending:
+        copy.wait_send()
+
+
+def scatter_trunk(sizes, grads):
+    count, rows = grads.shape[:2]
+    if count != 16:
+        summed = lax.psum_scatter(grads, "dp", scatter_dimension=0, tiled=True)[0]
+        summed = summed.astype(jnp.float32)
+        flat = jnp.square(summed).reshape(-1)
+        small = 3 * 256 * (BRANCH // count)
+        place = lax.rem(lax.broadcasted_iota(jnp.int32, (small,), 0), 768)
+        keep = jnp.logical_or(place < 640, lax.axis_index("chan") == 0)
+        total = jnp.sum(flat[:-small]) + jnp.sum(jnp.where(keep, flat[-small:], 0.0))
+        return summed, jnp.pad(total.reshape(1, 1), ((0, 7), (0, 127)))
+    layers = count // 4
+    low = jnp.bfloat16
+    return pl.pallas_call(
+        functools.partial(scatter_kernel, layers),
+        out_shape=[
+            jax.ShapeDtypeStruct((rows, 256), jnp.float32),
+            jax.ShapeDtypeStruct((8, 128), jnp.float32),
+        ],
+        in_specs=vmem(1),
+        out_specs=vmem(2),
+        scratch_shapes=[
+            pltpu.VMEM((count // 2, rows, 256), low),
+            pltpu.VMEM((layers, rows, 256), low),
+            pltpu.VMEM((layers, rows, 256), jnp.float32),
+            pltpu.VMEM((layers, rows, 256), low),
+            pltpu.VMEM((layers, rows, 256), low),
+            pltpu.VMEM((layers, rows, 256), low),
+            pltpu.SemaphoreType.DMA((count // 2,)),
+            pltpu.SemaphoreType.DMA((count // 2,)),
+            pltpu.SemaphoreType.DMA((layers,)),
+            pltpu.SemaphoreType.DMA((layers,)),
+            pltpu.SemaphoreType.DMA((layers,)),
+            pltpu.SemaphoreType.DMA((layers,)),
+        ],
+        compiler_params=pltpu.CompilerParams(
+            collective_id=6, has_side_effects=True, vmem_limit_bytes=48 << 20
+        ),
+        name="scatter_trunk",
+    )(grads)
+
+
+def first_back_kernel(
+    place_ref,
+    part_ref,
+    other_ref,
+    w_ref,
+    col_ref,
+    a_ref,
+    stat_ref,
+    own_ref,
+    gain_ref,
+    crop_ref,
+    up_ref,
+    g_ref,
+    o_ref,
+    canvas,
+):
+    edge = 4 * FW
+    values = part_ref[...].astype(jnp.float32) + other_ref[...].astype(jnp.float32)
+    low = values.astype(jnp.bfloat16)
+    g_ref[...] = jnp.where(place_ref[0] == 0, low[:, : MID // 2], low[:, MID // 2 :])
+    values = low.astype(jnp.float32)
+    for turn in range(3):
+        canvas[turn, :edge] = jnp.zeros((edge, MID), canvas.dtype)
+        canvas[turn, POSITIONS + edge :] = jnp.zeros((edge, MID), canvas.dtype)
+        canvas[turn, edge : POSITIONS + edge] = roll_cols(values, col_ref, -4 * (turn - 1)).astype(
+            canvas.dtype
+        )
+    mean, scale = norm_rows(stat_ref[...], stat_ref[2:3, 0:1])
+    pair = both_halves((place_ref, own_ref, gain_ref), 0, MID // 2)
+    block = 400
+
+    def step(index, carry):
+        total = None
+        for row in range(3):
+            first = pl.multiple_of(index * block + edge * (2 - row), 16)
+            for turn in range(3):
+                part = dot(canvas[turn, pl.ds(first, block)], w_ref[3 * row + turn], (1, 1))
+                total = part if total is None else total + part
+        rows = pl.ds(pl.multiple_of(index * block, 16), block)
+        normed = (a_ref[rows] - mean) * scale
+        up = gelu_slope(pair[0:1] * normed + pair[1:2], crop_ref[rows] * total)
+        up_ref[rows] = up
+        return (
+            carry[0] + jnp.sum(up * normed, 0, keepdims=True),
+            carry[1] + jnp.sum(up, 0, keepdims=True),
+        )
+
+    zero = jnp.zeros((1, MID), jnp.float32)
+    sums = lax.fori_loop(0, POSITIONS // block, step, (zero, zero))
+    o_ref[...] = jnp.concatenate([sums[0], sums[1], jnp.zeros((6, MID), jnp.float32)], 0)
+
+
+def first_back(place, part, other, weights, columns, first_pre, stat, gains, crop):
+    return pl.pallas_call(
+        first_back_kernel,
+        out_shape=[
+            jax.ShapeDtypeStruct((POSITIONS, MID), jnp.float32),
+            jax.ShapeDtypeStruct((POSITIONS, MID // 2), jnp.bfloat16),
+            jax.ShapeDtypeStruct((8, MID), jnp.float32),
+        ],
+        in_specs=[pl.BlockSpec(memory_space=pltpu.SMEM)] + vmem(9),
+        out_specs=vmem(3),
+        scratch_shapes=[pltpu.VMEM((3, POSITIONS + 8 * FW, MID), jnp.bfloat16)],
+        compiler_params=pltpu.CompilerParams(vmem_limit_bytes=50 << 20),
+        cost_estimate=pl.CostEstimate(flops=8 * 10**9, bytes_accessed=20 << 20, transcendentals=0),
+        name="first_back",
+    )(place, part, other, weights, columns, first_pre, stat, gains[1], gains[2], crop)
+
+
+ADAM_GROUPS = 8
+
+
+def adam_kernel(row_share, mid_share, *refs):
+    sum_ref, pyramid_ref, trunk_ref, stem_ref, small_ref, norm_ref, task_ref = refs[:7]
+    states = [refs[7 + 3 * group : 10 + 3 * group] for group in range(ADAM_GROUPS)]
+    base = 7 + 3 * ADAM_GROUPS
+    outs = [refs[base + 3 * group : base + 3 + 3 * group] for group in range(ADAM_GROUPS)]
+    norm = jnp.sqrt(jnp.sum(sum_ref[0:1], 1, keepdims=True))
+    factor = clip_level / jnp.maximum(norm, clip_level)
+
+    def update(group, at, gradient, rate, decay):
+        values = [ref[at] for ref in states[group]]
+        for ref, value in zip(outs[group], adam_step(*values, gradient, factor, rate, decay)):
+            ref[at] = value
+
+    def pyramid_step(tap, carry):
+        update(0, tap, pyramid_ref[tap].astype(jnp.float32), (3 * D) ** (-0.5), decay_rate)
+        return carry
+
+    lax.fori_loop(0, 29, pyramid_step, 0)
+    for which in range(2):
+        rows = trunk_ref[which * row_share : (which + 1) * row_share]
+        update(1, which, rows, D ** (-0.5), decay_rate)
+    for tap in range(9):
+        first = 2 * row_share + tap * mid_share
+        update(2, tap, trunk_ref[first : first + mid_share], (9 * MID) ** (-0.5), decay_rate)
+    every = slice(None)
+    update(3, every, stem_ref[...], PATCH ** (-0.5), decay_rate)
+    for branch in range(5):
+        update(
+            4,
+            branch,
+            small_ref[:, branch * 128 : (branch + 1) * 128],
+            (5 * BRANCH) ** (-0.5),
+            decay_rate,
+        )
+    update(5, every, small_ref[:, 640:662], BRANCH ** (-0.5), decay_rate)
+    update(6, every, norm_ref[...], 0.3, 0.0)
+    update(7, every, task_ref[:, :25], 0.3, 0.0)
+
+
+def adam_all(row_share, mid_share, gradients, states):
+    flat = [part for state in states for part in state]
+    return pl.pallas_call(
+        functools.partial(adam_kernel, row_share, mid_share),
+        out_shape=[jax.ShapeDtypeStruct(part.shape, jnp.float32) for part in flat],
+        in_specs=vmem(len(gradients) + len(flat)),
+        out_specs=vmem(len(flat)),
+        compiler_params=pltpu.CompilerParams(vmem_limit_bytes=50 << 20),
+        cost_estimate=pl.CostEstimate(flops=10**8, bytes_accessed=18 << 20, transcendentals=0),
+        name="adam",
+    )(*gradients, *flat)
+
+
+def square_kernel(
+    place_ref, three_ref, four_ref, one_ref, trunk_ref, pyramid_ref, task_ref, o_ref, norm_ref, task_grad_ref, loss_ref
+):
+    lower = place_ref[0] == 0
+    three = three_ref[...]
+    four = four_ref[...]
+    mid = MID // 2
+    for row in range(2):
+        own = jnp.where(lower, four[row : row + 1, :mid], four[row : row + 1, mid:])
+        norm_ref[row : row + 1] = jnp.concatenate(
+            [own, three[2 * row : 2 * row + 1], three[2 * row + 1 : 2 * row + 2]], 1
+        )
+    lane = lax.broadcasted_iota(jnp.int32, (1, 128), 1)
+    errors = three[4:5, 128:256]
+
+    def lane_sum(values, first, last):
+        kept = jnp.where((lane >= first) & (lane < last), values, 0.0)
+        return jnp.sum(kept, 1, keepdims=True)
+
+    seg = lane_sum(three[4:5, 256:384], 0, 1)
+    off = lane_sum(errors, CLASSES, CLASSES + 2)
+    dep = lane_sum(errors, CLASSES + 2, CLASSES + 3)
+    is_task = lane < 3
+    totals = jnp.where(lane == 0, seg, jnp.where(lane == 1, off, dep))
+    means = totals / jnp.where(is_task, one_ref[2:3, :128], 1.0)
+    scale = jnp.where(is_task, task_ref[...], 0.0)
+    weighted = jnp.exp(-scale) * means
+    loss_ref[...] = lane_sum(weighted + scale, 0, 3)
+    bias = pltpu.roll(jnp.broadcast_to(three[4:5, :128], (8, 128)), 3, 1)[0:1]
+    task_grad = jnp.where(is_task, 1.0 - weighted, jnp.where(lane < 25, bias, 0.0))
+    task_grad_ref[...] = task_grad
+
+    def tap_square(tap, total):
+        values = pyramid_ref[tap].astype(jnp.float32)
+        return total + jnp.sum(values * values, 0, keepdims=True)
+
+    squares = lax.fori_loop(0, 29, tap_square, jnp.zeros((1, 128), jnp.float32))
+    first = jnp.where(place_ref[1] == 0, 1.0, 0.0)
+    norms = norm_ref[...]
+    norm_square = jnp.sum(jnp.sum(norms * norms, 0, keepdims=True), 1, keepdims=True)
+    task_square = jnp.sum(task_grad * task_grad, 1, keepdims=True)
+    extra = first * (norm_square + jnp.where(lower, 1.0, 0.0) * task_square)
+    squares = squares + trunk_ref[0:1] + jnp.where(lane == 0, extra, 0.0)
+    o_ref[...] = jnp.concatenate([squares, jnp.zeros((7, 128), jnp.float32)], 0)
+
+
+def own_squares_of(place, stat_three, stat_four, stat_one, trunk_squares, pyramid, task):
+    return pl.pallas_call(
+        square_kernel,
+        out_shape=[
+            jax.ShapeDtypeStruct((8, 128), jnp.float32),
+            jax.ShapeDtypeStruct((2, MID // 2 + D // 2), jnp.float32),
+            jax.ShapeDtypeStruct((1, 128), jnp.float32),
+            jax.ShapeDtypeStruct((1, 1), jnp.float32),
+        ],
+        in_specs=[pl.BlockSpec(memory_space=pltpu.SMEM)] + vmem(6),
+        out_specs=vmem(4),
+        name="own_squares",
+    )(place, stat_three, stat_four, stat_one, trunk_squares, pyramid, task)
 
 
 def adam_step(weight, first, second, gradient, factor, rate, decay):
@@ -1301,9 +1837,7 @@
     dp_size = sizes["dp"]
     low = jnp.bfloat16
     crop_field = crop_mask.astype(jnp.float32).reshape(POSITIONS, 1)
-    offset_field = crop_field[:, 0] * offset_valid.astype(jnp.float32).reshape(POSITIONS)
-    lidar_field = crop_field[:, 0] * lidar_valid.astype(jnp.float32).reshape(POSITIONS)
-    local_counts = jnp.stack([jnp.sum(crop_field), jnp.sum(offset_field), jnp.sum(lidar_field)])
+    count_masks = jnp.concatenate([crop_mask, offset_valid, lidar_valid], 0)
     half = D // 2
     mid_half = MID // 2
 
@@ -1324,7 +1858,7 @@
         sizes, bottle_weight.astype(low), middle_weight.astype(low), stem_shard, head_shard
     )
     pyramid_shard = pyramid_weight.astype(low)
-    late_shard, bottle_low = lax.optimization_barrier((pyramid_shard[EARLY_TAPS:], bottle_low))
+    late_shard = pyramid_shard[EARLY_TAPS:]
     pyramid_low = (
         lax.all_gather(pyramid_shard[:EARLY_TAPS], "dp", axis=1, tiled=True),
         lax.all_gather(late_shard, "dp", axis=1, tiled=True),
@@ -1332,9 +1866,6 @@
     own_place = chan_place.reshape(1)
     own_gains = norm_gains.reshape(2, mid_half + half)
     gains = (own_place, own_gains, swap_chan(own_gains))
-    gain_low = jnp.where(chan_place == 0, own_gains[:, :mid_half], gains[2][:, :mid_half])
-    gain_high = jnp.where(chan_place == 0, gains[2][:, :mid_half], own_gains[:, :mid_half])
-    gain_one, shift_one = jnp.concatenate([gain_low, gain_high], 1)
 
     def own_bottle(which):
         return lax.dynamic_slice(bottle_low, (which, chan_place * half, 0), (1, half, MID))[0]
@@ -1352,12 +1883,12 @@
         (POSITIONS, 128),
     )
     patch_rows = patches.reshape(POSITIONS, PATCH)
-    stream_low, first_pre, stat_one = stem_reduce(
+    stream_t, first_pre, stat_one = stem_reduce(
         patch_rows,
         stem_low,
         bottle_low,
         crop_field,
-        jnp.pad(local_counts, (0, MID - 3)).reshape(1, MID),
+        count_masks,
     )
     stat_one = all_sum(sizes, stat_one, ("dp",), 0)
     hidden_low, hidden_t, second_low = norm_middle(
@@ -1377,9 +1908,9 @@
     branch_pre, pool_pre, concat_low, project_part = pyramid_forward(
         output_low, pooled, pyramid_low, head_low, columns
     )
-    labels, offset_valid, lidar_valid, offset_target, depth_target, project_part = (
+    labels, offset_valid, lidar_valid, offset_target, depth_target, stat_one, project_part = (
         lax.optimization_barrier(
-            (labels, offset_valid, lidar_valid, offset_target, depth_target, project_part)
+            (labels, offset_valid, lidar_valid, offset_target, depth_target, stat_one, project_part)
         )
     )
     offset_field = crop_field[:, 0] * offset_valid.astype(jnp.float32).reshape(POSITIONS)
@@ -1426,26 +1957,55 @@
         branch_pre,
         pool_pre,
     )
-    other_part = pyramid_field(
-        1 - own_place, pyramid_low, branch_grads, pool_grad, crop_field, columns
-    )
-    other_sent = lax.all_gather(other_part, "chan")
-    later_grads, other_part = lax.optimization_barrier((branch_grads, other_part))
-    own_part = pyramid_field(own_place, pyramid_low, later_grads, pool_grad, crop_field, columns)
-    later_grads, own_part = lax.optimization_barrier((later_grads, own_part))
-    pyramid_grad = pyramid_weights(
-        output_t, later_grads, columns, pooled.reshape(D, 1), pool_grad
+    other_parts = []
+    later_grads = branch_grads
+    for quarter in range(2):
+        part = pyramid_field(
+            2 - 2 * own_place + quarter,
+            half // 2,
+            pyramid_low,
+            later_grads,
+            pool_grad,
+            crop_field,
+            columns,
+        )
+        other_parts.append(swap_chan(part))
+        later_grads, part = lax.optimization_barrier((later_grads, part))
+    own_part, pyramid_grad = own_gradients(
+        own_place,
+        pyramid_low,
+        output_t,
+        later_grads,
+        pool_grad,
+        crop_field,
+        columns,
+        pooled.reshape(D, 1),
+    )
+    small_grads = jnp.concatenate(
+        [
+            dot(project_grad_low, concat_low, (0, 0)).astype(low),
+            dot(feature_low, logit_low, (0, 0)).astype(low),
+        ],
+        1,
+    )
+    small_rows = project_share * 3
+    small_grads = small_grads.reshape(dp_size, small_rows, 256)
+    first_other, own_part, pyramid_grad, small_grads = lax.optimization_barrier(
+        (other_parts[0], own_part, pyramid_grad, small_grads)
+    )
+    other_parts, own_part, pyramid_grad = lax.optimization_barrier(
+        ([first_other, other_parts[1]], own_part, pyramid_grad)
     )
     pyramid_red = lax.psum_scatter(pyramid_grad, "dp", scatter_dimension=1, tiled=True)
 
     stat_three = residual_sums(
-        own_place, own_part, other_sent, expand_pre, stat_two, stat_one, crop_field, head_stat
+        own_place, own_part, other_parts, expand_pre, stat_two, stat_one, crop_field, head_stat
     )
     stat_three = all_sum(sizes, stat_three, ("dp",), 2)
     expand_grad_low, second_part = residual_back(
         own_place,
         own_part,
-        other_sent,
+        other_parts,
         expand_pre,
         stat_two,
         stat_one,
@@ -1454,60 +2014,42 @@
         crop_field,
         bottle_low,
     )
-    stat_one, stat_three, own_part, second_part = lax.optimization_barrier(
-        (stat_one, stat_three, own_part, second_part)
-    )
-    gain_two_grad = stat_three[:2].reshape(half)
-    shift_two_grad = stat_three[2:4].reshape(half)
-    bias_grad = stat_three[4, :22]
-    error_sums = stat_three[4, 128:256]
-    loss_sums = jnp.stack(
-        [
-            stat_three[4, 256],
-            error_sums[CLASSES] + error_sums[CLASSES + 1],
-            error_sums[CLASSES + 2],
-        ]
-    )
-    mean_one = stat_one[0] / crop_total
-    scale_one = lax.rsqrt(stat_one[1] / crop_total - mean_one * mean_one + norm_eps)
-    stream_grad = own_part.astype(jnp.float32) + lax.dynamic_index_in_dim(
-        other_sent, 1 - chan_place, 0, keepdims=False
-    ).astype(jnp.float32)
-    task_means = loss_sums / counts
-    total_loss = jnp.sum(jnp.exp(-task_scale) * task_means + task_scale)
-    scale_grad = 1.0 - jnp.exp(-task_scale) * task_means
-    second_part, feature_low, logit_low, concat_low, project_grad_low = lax.optimization_barrier(
-        (second_part, feature_low, logit_low, concat_low, project_grad_low)
-    )
     second_other = swap_chan(second_part)
     expand_rows = dot(expand_grad_low, second_low, (0, 0)).astype(low)
+    second_other, expand_rows, stat_three, own_part = lax.optimization_barrier(
+        (second_other, expand_rows, stat_three, own_part)
+    )
     expand_sent = swap_chan(other_half(expand_rows, 1))
-    second_grad_low = (
-        second_part.astype(jnp.float32) + second_other.astype(jnp.float32)
-    ).astype(low)
-    hidden_grad = middle_conv(second_grad_low, middle_low, columns, True, jnp.float32)
-    normed_one = (first_pre - mean_one) * scale_one
-    act_input = gain_one * normed_one + shift_one
-    upstream_one = gelu_grad(act_input, crop_field * hidden_grad)
-    gain_one_all, shift_one_all = small_sum(
-        sizes,
-        [jnp.sum(upstream_one * normed_one, 0), jnp.sum(upstream_one, 0)],
-        ("dp",),
-        3,
-    )
-    gain_one_grad = own_half(gain_one_all, 0)
-    shift_one_grad = own_half(shift_one_all, 0)
-    first_grad_low = (
-        crop_field
-        * gain_one
-        * scale_one
-        * (upstream_one - (shift_one_all + normed_one * gain_one_all) / crop_total)
-    ).astype(low)
-    middle_grad = middle_weights(hidden_t, own_half(second_grad_low, 1), columns)
-    reduce_grad = dot(stream_low, own_half(first_grad_low, 1), (0, 0)).astype(low)
-    start_grad = dot(first_grad_low, own_bottle(0), (1, 1)) + stream_grad
-    start_grad_low = (crop_field * start_grad).astype(low)
-    stem_grad = dot(start_grad_low, patch_rows, (0, 0)).astype(low)
+    upstream_one, second_own, stat_four = first_back(
+        own_place,
+        second_part,
+        second_other,
+        middle_low,
+        columns,
+        first_pre,
+        stat_one,
+        gains,
+        crop_field,
+    )
+    stat_four = all_sum(sizes, stat_four, ("dp",), 3)
+    stat_one, stat_three, stat_four, own_part, expand_sent = lax.optimization_barrier(
+        (stat_one, stat_three, stat_four, own_part, expand_sent)
+    )
+    reduce_grad, stem_grad = late_gradients(
+        own_place,
+        upstream_one,
+        first_pre,
+        stat_one,
+        stat_four,
+        gains,
+        crop_field,
+        patch_rows.T,
+        bottle_low,
+        own_part,
+        other_parts,
+        stream_t,
+    )
+    middle_grad = middle_weights(hidden_t, second_own, columns)
     expand_own = own_half(expand_rows, 1)
     expand_grad = jnp.where(
         chan_place == 0,
@@ -1515,14 +2057,6 @@
         jnp.concatenate([expand_sent, expand_own], 0),
     )
 
-    small_grads = jnp.concatenate(
-        [
-            dot(project_grad_low, concat_low, (0, 0)).astype(low),
-            dot(feature_low, logit_low, (0, 0)).astype(low),
-        ],
-        1,
-    )
-    small_rows = project_share * 3
     trunk_grads = jnp.concatenate(
         [
             reduce_grad.reshape(dp_size, row_share, 256),
@@ -1531,83 +2065,66 @@
             .transpose(1, 0, 2, 3)
             .reshape(dp_size, 9 * mid_share, 256),
             stem_grad.reshape(dp_size, stem_share * PATCH // 256, 256),
-            small_grads.reshape(dp_size, small_rows, 256),
+            small_grads,
         ],
         1,
     )
-    trunk_grads, pyramid_red = lax.optimization_barrier((trunk_grads, pyramid_red))
-    trunk_red = lax.psum_scatter(trunk_grads, "dp", scatter_dimension=0, tiled=True)[0]
-    trunk_red = trunk_red.astype(jnp.float32)
-    bottle_red = trunk_red[: 2 * row_share].reshape(bottle_weight.shape)
-    start = 2 * row_share
-    middle_red = trunk_red[start : start + 9 * mid_share].reshape(middle_weight.shape)
-    start += 9 * mid_share
+    trunk_red, trunk_squares = scatter_trunk(sizes, trunk_grads)
+    start = 2 * row_share + 9 * mid_share
     stem_rows = stem_share * PATCH // 256
-    stem_red = trunk_red[start : start + stem_rows]
-    stem_red = stem_red.reshape(stem_share, PATCH).T.reshape(stem_weight.shape)
+    stem_red = trunk_red[start : start + stem_rows].reshape(stem_share, PATCH)
     small_red = trunk_red[start + stem_rows :].reshape(project_share, 768)
-    project_red = small_red[:, : 5 * 128].reshape(project_share, 5, 128).transpose(1, 2, 0)
-    head_red = small_red[:, 5 * 128 : 5 * 128 + 22]
-    pyramid_red = pyramid_red.astype(jnp.float32)
-    norm_grad = jnp.stack(
+    own_squares, norm_grad, task_grad, total_loss = own_squares_of(
+        jnp.stack([chan_place, lax.axis_index("dp")]),
+        stat_three,
+        stat_four,
+        stat_one,
+        trunk_squares,
+        pyramid_red,
+        jnp.pad(task_params[:3], (0, 125)).reshape(1, 128),
+    )
+    total_loss = total_loss.reshape(())
+    all_squares = all_sum(sizes, own_squares, ("dp", "chan"), 4)
+    grad_norm = jnp.sqrt(jnp.sum(all_squares[0]))
+
+    def turn_stem(part):
+        return part.reshape(PATCH, stem_share).T
+
+    def turn_project(part):
+        return part.transpose(0, 2, 1)
+
+    def flat_norm(part):
+        return part.reshape(2, mid_half + half)
+
+    updated = adam_all(
+        row_share,
+        mid_share,
         [
-            jnp.concatenate([gain_one_grad, gain_two_grad]),
-            jnp.concatenate([shift_one_grad, shift_two_grad]),
-        ]
-    )[:, None, :]
-    task_grad = jnp.concatenate([scale_grad, bias_grad])
-    dp_first = (lax.axis_index("dp") == 0).astype(jnp.float32)
-    chan_first = (chan_place == 0).astype(jnp.float32)
-    own_squares = (
-        jnp.sum(stem_red * stem_red)
-        + jnp.sum(bottle_red * bottle_red)
-        + jnp.sum(middle_red * middle_red)
-        + jnp.sum(pyramid_red * pyramid_red)
-        + jnp.sum(project_red * project_red)
-        + chan_first * jnp.sum(head_red * head_red)
-        + dp_first * jnp.sum(norm_grad * norm_grad)
-        + dp_first * chan_first * jnp.sum(task_grad * task_grad)
-    )
-    grad_norm = jnp.sqrt(small_sum(sizes, [own_squares], ("dp", "chan"), 4)[0])
-    factor = clip_level / jnp.maximum(grad_norm, clip_level)
-    new_stem = adam_step(
-        stem_weight, stem_first, stem_second, stem_red, factor, PATCH ** (-0.5), decay_rate
-    )
-    new_bottle = adam_step(
-        bottle_weight, bottle_first, bottle_second, bottle_red, factor, D ** (-0.5), decay_rate
-    )
-    new_middle = adam_step(
-        middle_weight,
-        middle_first,
-        middle_second,
-        middle_red,
-        factor,
-        (9 * MID) ** (-0.5),
-        decay_rate,
-    )
-    new_pyramid = adam_step(
-        pyramid_weight,
-        pyramid_first,
-        pyramid_second,
-        pyramid_red,
-        factor,
-        (3 * D) ** (-0.5),
-        decay_rate,
-    )
-    new_project = adam_step(
-        project_weight,
-        project_first,
-        project_second,
-        project_red,
-        factor,
-        (5 * BRANCH) ** (-0.5),
-        decay_rate,
-    )
-    new_head = adam_step(
-        head_weight, head_first, head_second, head_red, factor, BRANCH ** (-0.5), decay_rate
-    )
-    new_norm = adam_step(norm_gains, norm_first, norm_second, norm_grad, factor, 0.3, 0.0)
-    new_task = adam_step(task_params, task_first, task_second, task_grad, factor, 0.3, 0.0)
+            all_squares,
+            pyramid_red,
+            trunk_red,
+            stem_red,
+            small_red,
+            norm_grad,
+            task_grad,
+        ],
+        [
+            (pyramid_weight, pyramid_first, pyramid_second),
+            (bottle_weight, bottle_first, bottle_second),
+            (middle_weight, middle_first, middle_second),
+            tuple(turn_stem(part) for part in (stem_weight, stem_first, stem_second)),
+            tuple(turn_project(part) for part in (project_weight, project_first, project_second)),
+            (head_weight, head_first, head_second),
+            tuple(flat_norm(part) for part in (norm_gains, norm_first, norm_second)),
+            tuple(part.reshape(1, 25) for part in (task_params, task_first, task_second)),
+        ],
+    )
+    groups = [updated[3 * group : 3 * group + 3] for group in range(ADAM_GROUPS)]
+    new_pyramid, new_bottle, new_middle, new_stem, new_project, new_head, new_norm, new_task = groups
+    new_stem = [part.T.reshape(stem_weight.shape) for part in new_stem]
+    new_project = [part.transpose(0, 2, 1) for part in new_project]
+    new_norm = [part.reshape(norm_gains.shape) for part in new_norm]
+    new_task = [part.reshape(25) for part in new_task]
     return (
         total_loss,
         grad_norm,

time: 647 us -> 560 us (0.87)
  waiting for transfers between devices: 185 us -> 59.9 us
  Pallas kernels: 331 us -> 428 us
  other arithmetic: 51.4 us -> 12.1 us
  matrix products: 16.4 us -> 7.05 us
  between operations: 23.5 us -> 16.7 us
    pallas_call x3 -> x7, Pallas kernels: 58.7 us -> 151 us  [the longest x1 52.2 us: scatter_trunk(): pl.pallas_call(functools.partial(scatter_kernel, layers), out_shape=[jax....]
    reduce_scatter x1 -> x0, waiting for transfers between devices: 73.7 us -> none  [on_device(): lax.psum_scatter(trunk_grads, 'dp', scatter_dimension=0, tiled=True)[0]]
    all_gather x1 -> x0, waiting for transfers between devices: 26.4 us -> none  [on_device(): other_sent = lax.all_gather(other_part, 'chan')]
    reduce_scatter x1, waiting for transfers between devices: 24.8 us -> 0.02 us  [on_device(): lax.psum_scatter(pyramid_grad, 'dp', scatter_dimension=1, tiled=True)]
    sub x9 -> x0, other arithmetic: 15.7 us -> none  [the longest x8 14.3 us: adam_step(): return (weight - rate * (direction + decay * weight), first_new, second_new)]
    pallas_call x2, Pallas kernels: 37.2 us -> 23.3 us  [pyramid_field(): pl.pallas_call(field_kernel, out_shape=jax.ShapeDtypeStruct((POSITIONS, d...]
    reduce_sum x12 -> x1, other arithmetic: 11.3 us -> 0.6 us  [on_device(): grad_norm = jnp.sqrt(jnp.sum(all_squares[0]))]
    pallas_call x1, Pallas kernels: 31.2 us -> 41.3 us  [pyramid_forward(): pl.pallas_call(pyramid_kernel, out_shape=[jax.ShapeDtypeStruct((4, POSITI...]
  transfers between devices with their start and end apart: 9 -> 9, of which waited for: 6 -> 4; matrix products, arithmetic and copies ran while one was open for 10% -> 5% of each run, Pallas kernels for 41% -> 61%
where the time goes in v6:
time: 560 us; the launch traced here: 561 us
  Pallas kernels  428 us (76%)
  waiting for transfers between devices  59.9 us (11%)
  local copies, waits for them, and re-layouts  27.2 us (5%)
  between operations  16.7 us (3%)
  other arithmetic  12.1 us (2%)
  starting transfers between devices  9.82 us (2%)
  matrix products  7.05 us (1%)
    pallas_call x1, Pallas kernels, gather_trunk(): pl.pallas_call(functools.partial(gather_kernel, count // 4), out_shape=[j...  83 us
    pallas_call x5, Pallas kernels, all_sum(): pl.pallas_call(functools.partial(sum_kernel, sizes, axes, count), out_sha...  58.7 us
    ppermute x6, waiting for transfers between devices, swap_chan(): return lax.ppermute(values, 'chan', [(0, 1), (1, 0)])  54.4 us
    pallas_call x1, Pallas kernels, scatter_trunk(): pl.pallas_call(functools.partial(scatter_kernel, layers), out_shape=[jax....  52.2 us
    pallas_call x1, Pallas kernels, own_gradients(): pl.pallas_call(own_kernel, out_shape=[jax.ShapeDtypeStruct((POSITIONS, ha...  43.2 us
    pallas_call x1, Pallas kernels, pyramid_forward(): pl.pallas_call(pyramid_kernel, out_shape=[jax.ShapeDtypeStruct((4, POSITI...  41.3 us
    pallas_call x2, Pallas kernels, pyramid_field(): pl.pallas_call(field_kernel, out_shape=jax.ShapeDtypeStruct((POSITIONS, d...  23.3 us
    pallas_call x1, Pallas kernels, first_back(): pl.pallas_call(first_back_kernel, out_shape=[jax.ShapeDtypeStruct((POSITI...  18.3 us
  transfers between devices with their start and end apart: 9, of which 4 were waited for; matrix products, arithmetic and copies ran while one was open for 5% of the time, Pallas kernels for 61%

profile of v6, /device:TPU:0, one launch (start us, length us, event | category | flops | bytes accessed | tf_op | source)
XLA Modules:
  0.0 561.0 jit_solution(5378788220307233488)
XLA Ops:
  7.3 1.7 convert_element_type.116
  9.0 0.8 slice.45
  9.9 0.9 slice.46
  10.9 3.0 collective-permute-start
  14.3 0.7 convert_element_type.110.middle
  15.0 0.7 convert_element_type.109.bottle
  16.1 0.6 fusion.2.head
  16.7 0.6 convert_bitcast_fusion.small
  17.3 83.0 %gather_trunk.1 = (bf16[2,2048,512]{2,1,0:T(8,128)(2,1)}, bf16[9,512,512]{2,1,0:T(8,128)(2,1)}, bf16[2048,192]{1,0:T(8,128)(2,1)}, bf16[256,768]{1,0:T(8,128)(2,1)}) custom-call(bf16[2,128,256]{2,1,0:T(8,128)(2,1)} %convert_element_type.109.bottle, bf16[9,32,256]{2,1,0:T(8,128)(2,1)} %convert_element_type.110.middle, ...), custom_call_target="tpu_custom_call" | custom-call | tf_op jit(solution)/shard_map/gather_trunk/pallas_call | solution.py:408
  100.5 1.2 copy-done.6
  101.7 12.7 %stem_reduce.1 = (bf16[2048,1600]{1,0:T(8,128)(2,1)}, f32[1600,512]{1,0:T(8,128)}, f32[8,512]{1,0:T(8,128)S(1)}) custom-call(bf16[1600,192]{1,0:T(8,128)(2,1)S(1)} %copy.90.p_ref, bf16[2048,192]{1,0:T(8,128)(2,1)S(1)} %copy-done.6, bf16[2,2048,512]{2,1,0:T(8,128)(2,1)} %get-tuple-element.116.reduce_ref.w_ref.bottle_hbm, f32[1600,1]{1,0:T(8,128)S(1)} %copy.91.crop_ref, ...), custom_call_target="tpu_custom_call" | custom-call | flops 5000000000 | bytes 14680064 | tf_op jit(solution)/shard_map/stem_reduce/pallas_call | solution.py:800
  114.4 8.9 %small_sum.5.stat_ref.count_ref.one_ref = f32[8,512]{1,0:T(8,128)S(1)} custom-call(f32[8,512]{1,0:T(8,128)S(1)} %get-tuple-element.117.x_ref), custom_call_target="tpu_custom_call" | custom-call | tf_op jit(solution)/shard_map/small_sum/pallas_call | solution.py:109
  123.7 15.7 %norm_middle.1 = (bf16[1600,512]{1,0:T(8,128)(2,1)}, bf16[512,1600]{1,0:T(8,128)(2,1)}, bf16[1600,512]{1,0:T(8,128)(2,1)}) custom-call(f32[1600,512]{1,0:T(8,128)} %get-tuple-element.118.a_ref, f32[8,512]{1,0:T(8,128)S(1)} %small_sum.5.stat_ref.count_ref.one_ref, s32[1]{0:T(128)} %bitcast.place_ref, f32[2,1280]{1,0:T(2,128)S(1)} %bitcast.85, ...), custom_call_target="tpu_custom_call" | custom-call | flops 8000000000 | bytes 14680064 | tf_op jit(solution)/shard_map/norm_middle/pallas_call | solution.py:873
  139.3 1.4 copy-done.49
  140.7 9.0 %expand_forward.1 = (bf16[1600,2048]{1,0:T(8,128)(2,1)}, f32[8,512]{1,0:T(8,128)S(1)}) custom-call(bf16[1600,512]{1,0:T(8,128)(2,1)S(1)} %copy-done.49, bf16[2,2048,512]{2,1,0:T(8,128)(2,1)} %get-tuple-element.116.reduce_ref.w_ref.bottle_hbm, f32[1600,1]{1,0:T(8,128)S(1)} %copy.91.crop_ref), custom_call_target="tpu_custom_call" | custom-call | flops 4000000000 | bytes 12582912 | tf_op jit(solution)/shard_map/expand_forward/pallas_call | solution.py:910
  149.7 13.7 %small_sum.6.stat_ref = f32[8,512]{1,0:T(8,128)S(1)} custom-call(f32[8,512]{1,0:T(8,128)S(1)} %get-tuple-element.122.x_ref), custom_call_target="tpu_custom_call" | custom-call | tf_op jit(solution)/shard_map/small_sum/pallas_call | solution.py:109
  163.4 13.0 %residual_stream.1 = (bf16[1600,2048]{1,0:T(8,128)(2,1)}, bf16[2048,1600]{1,0:T(8,128)(2,1)}, f32[1,2048]{1,0:T(1,128)S(1)}) custom-call(bf16[1600,192]{1,0:T(8,128)(2,1)S(1)} %copy.90.p_ref, bf16[2048,192]{1,0:T(8,128)(2,1)S(1)} %copy-done.7, bf16[1600,2048]{1,0:T(8,128)(2,1)} %get-tuple-element.121.y_ref.y_hbm, f32[8,512]{1,0:T(8,128)S(1)} %small_sum.6.stat_ref, ...), custom_call_target="tpu_custom_call" | custom-call | flops 2000000000 | bytes 23068672 | tf_op jit(solution)/shard_map/residual_stream/pallas_call | solution.py:962
  177.1 5.4 all-gather.5.cloned.1.call-done.b_hbm
  182.5 41.3 %pyramid_fwd.1 = (f32[4,1600,128]{2,1,0:T(8,128)}, f32[1,128]{1,0:T(1,128)}, bf16[1600,640]{1,0:T(8,128)(2,1)}, bf16[1600,256]{1,0:T(8,128)(2,1)}) custom-call(bf16[1600,2048]{1,0:T(8,128)(2,1)} %get-tuple-element.123.x_ref, f32[1,2048]{1,0:T(1,128)} %copy-done.34, bf16[10,2048,128]{2,1,0:T(8,128)(2,1)} %all-gather.3.cloned.1.call-done.a_hbm, ...), custom_call_target="tpu_custom_call" | custom-call | flops 15938355200 | bytes 41943040 | tf_op jit(solution)/shard_map/pyramid_fwd/pallas_call | solution.py:1066
  224.4 1.5 collective-permute-start.1
  225.9 1.2 fusion.label_ref
  227.1 1.9 fusion.4
  229.4 1.2 pad.18.target_ref
  230.7 1.8 multiply_add_fusion.mask_ref
  232.4 12.6 %collective-permute-done.1.other_ref = bf16[1600,256]{1,0:T(8,128)(2,1)S(1)} collective-permute-done((bf16[1600,256]{1,0:T(8,128)(2,1)}, bf16[1600,256]{1,0:T(8,128)(2,1)S(1)}, u32[]{:S(2)}, u32[]{:S(2)}) %collective-permute-start.1) | collective-permute-done | bytes 819232 | tf_op jit(solution)/shard_map/ppermute | solution.py:141
  245.0 1.0 copy-done.12
  246.0 9.6 %head_step.1 = (bf16[1600,256]{1,0:T(8,128)(2,1)S(1)}, bf16[1600,128]{1,0:T(8,128)(2,1)S(1)}, bf16[1600,256]{1,0:T(8,128)(2,1)S(1)}, bf16[4,1600,128]{2,1,0:T(8,...) custom-call(bf16[1600,256]{1,0:T(8,128)(2,1)S(1)} %copy-done.9, ...), custom_call_target="tpu_custom_call" | custom-call | flops 2000000000 | bytes 16777216 | tf_op jit(solution)/shard_map/head_step/pallas_call | solution.py:1166
  256.7 0.9 copy-done.47
  257.6 11.5 %pyramid_field.2 = bf16[1600,512]{1,0:T(8,128)(2,1)} custom-call(s32[1]{0:T(128)S(6)} %sub.7.place_ref, bf16[10,2048,128]{2,1,0:T(8,128)(2,1)} %all-gather.3.cloned.1.call-done.a_hbm, bf16[19,2048,128]{2,1,0:T(8,128)(2,1)} %all-gather.5.cloned.1.call-done.b_hbm, bf16[4,1600,128]{2,1,0:T(8,128)(2,1)} %get-tuple-element.140.g_ref, f32[1,128]{1,0:T(1,128)} %copy-done.38, ...), custom_call_target="tpu_custom_call" | custom-call | flops 1000 | bytes 1024 | tf_op jit(solution)/shard_map/pyramid_field/pallas_call | solution.py:735
  269.2 1.5 collective-permute-start.2
  270.7 11.8 %pyramid_field.3 = bf16[1600,512]{1,0:T(8,128)(2,1)} custom-call(s32[1]{0:T(128)S(6)} %add.52.place_ref, bf16[10,2048,128]{2,1,0:T(8,128)(2,1)} %all-gather.3.cloned.1.call-done.a_hbm, bf16[19,2048,128]{2,1,0:T(8,128)(2,1)} %all-gather.5.cloned.1.call-done.b_hbm, bf16[4,1600,128]{2,1,0:T(8,128)(2,1)} %get-tuple-element.140.g_ref, f32[1,128]{1,0:T(1,128)} %copy-done.38, ...), custom_call_target="tpu_custom_call" | custom-call | flops 1000 | bytes 1024 | tf_op jit(solution)/shard_map/pyramid_field/pallas_call | solution.py:735
  282.5 0.6 collective-permute-start.3
  283.1 1.4 copy.100.pooled_ref
  284.5 43.2 %own_gradients.1 = (bf16[1600,1024]{1,0:T(8,128)(2,1)}, bf16[29,2048,128]{2,1,0:T(8,128)(2,1)}) custom-call(s32[1]{0:T(128)} %bitcast.place_ref, bf16[10,2048,128]{2,1,0:T(8,128)(2,1)} %all-gather.3.cloned.1.call-done.a_hbm, bf16[19,2048,128]{2,1,0:T(8,128)(2,1)} %all-gather.5.cloned.1.call-done.b_hbm, bf16[2048,1600]{1,0:T(8,128)(2,1)} %get-tuple-element.138.xt_hbm, ...), custom_call_target="tpu_custom_call" | custom-call | flops 1000 | bytes 1024 | tf_op jit(solution)/shard_map/own_gradients/pallas_call | solution.py:708
  328.1 2.5 convolution_convert_fusion.1
  330.6 0.9 reshape.272
  331.6 10.2 %collective-permute-done.3.second_hbm = bf16[1600,512]{1,0:T(8,128)(2,1)} collective-permute-done((bf16[1600,512]{1,0:T(8,128)(2,1)}, bf16[1600,512]{1,0:T(8,128)(2,1)}, u32[]{:S(2)}, u32[]{:S(2)}) %collective-permute-start.3) | collective-permute-done | bytes 1638432 | tf_op jit(solution)/shard_map/ppermute | solution.py:141
  341.9 6.2 %residual_sums.1.x_ref = f32[8,512]{1,0:T(8,128)} custom-call(s32[1]{0:T(128)} %bitcast.place_ref, bf16[1600,1024]{1,0:T(8,128)(2,1)} %get-tuple-element.165.own_hbm, bf16[1600,512]{1,0:T(8,128)(2,1)} %collective-permute-done.2.first_hbm, bf16[1600,512]{1,0:T(8,128)(2,1)} %collective-permute-done.3.second_hbm, ...), custom_call_target="tpu_custom_call" | custom-call | flops 100000000 | bytes 12582912 | tf_op jit(solution)/shard_map/residual_sums/pallas_call | solution.py:1270
  348.1 0.7 copy-done.28
  348.8 11.2 %small_sum.7.sum_ref.three_ref = f32[8,512]{1,0:T(8,128)S(1)} custom-call(f32[8,512]{1,0:T(8,128)S(1)} %copy-done.28), custom_call_target="tpu_custom_call" | custom-call | tf_op jit(solution)/shard_map/small_sum/pallas_call | solution.py:109
  360.6 13.2 %residual_back.1 = (bf16[1600,1024]{1,0:T(8,128)(2,1)}, bf16[1600,512]{1,0:T(8,128)(2,1)}) custom-call(s32[1]{0:T(128)} %bitcast.place_ref, bf16[1600,1024]{1,0:T(8,128)(2,1)} %get-tuple-element.165.own_hbm, bf16[1600,512]{1,0:T(8,128)(2,1)} %collective-permute-done.2.first_hbm, bf16[1600,512]{1,0:T(8,128)(2,1)} %collective-permute-done.3.second_hbm, ...), custom_call_target="tpu_custom_call" | custom-call | flops 2000000000 | bytes 16777216 | tf_op jit(solution)/shard_map/residual_back/pallas_call | solution.py:1332
  373.8 1.6 collective-permute-start.4
  376.5 4.1 convolution_convert_fusion
  380.6 31.6 %collective-permute-done.4.other_ref = bf16[1600,512]{1,0:T(8,128)(2,1)} collective-permute-done((bf16[1600,512]{1,0:T(8,128)(2,1)}, bf16[1600,512]{1,0:T(8,128)(2,1)}, u32[]{:S(2)}, u32[]{:S(2)}) %collective-permute-start.4) | collective-permute-done | bytes 1638432 | tf_op jit(solution)/shard_map/ppermute | solution.py:141
  412.3 1.5 collective-permute-start.5
  413.8 18.3 %first_back.1 = (f32[1600,512]{1,0:T(8,128)}, bf16[1600,256]{1,0:T(8,128)(2,1)S(1)}, f32[8,512]{1,0:T(8,128)S(1)}) custom-call(s32[1]{0:T(128)} %bitcast.place_ref, bf16[1600,512]{1,0:T(8,128)(2,1)} %get-tuple-element.154.part_ref, bf16[1600,512]{1,0:T(8,128)(2,1)} %collective-permute-done.4.other_ref, bf16[9,512,512]{2,1,0:T(8,128)(2,1)} %get-tuple-element.119.w_ref, ...), custom_call_target="tpu_custom_call" | custom-call | flops 8000000000 | bytes 20971520 | tf_op jit(solution)/shard_map/first_back/pallas_call | solution.py:1660
  432.1 4.4 middle_weights.1
  436.7 11.4 %small_sum.8.sum_ref.four_ref = f32[8,512]{1,0:T(8,128)S(1)} custom-call(f32[8,512]{1,0:T(8,128)S(1)} %get-tuple-element.158.x_ref), custom_call_target="tpu_custom_call" | custom-call | tf_op jit(solution)/shard_map/small_sum/pallas_call | solution.py:109
  448.7 14.0 %late_gradients.1 = (bf16[2048,256]{1,0:T(8,128)(2,1)}, bf16[1024,192]{1,0:T(8,128)(2,1)}) custom-call(s32[1]{0:T(128)} %bitcast.place_ref, f32[1600,512]{1,0:T(8,128)} %get-tuple-element.164.up_ref, f32[1600,512]{1,0:T(8,128)} %get-tuple-element.118.a_ref, f32[8,512]{1,0:T(8,128)} %copy-done.10, f32[8,512]{1,0:T(8,128)} %copy-done.24, f32[2,1280]{1,0:T(2,128)} %bitcast.88, ...), custom_call_target="tpu_custom_call" | custom-call | flops 4000000000 | bytes 25165824 | tf_op jit(solution)/shard_map/late_gradients/pallas_call | solution.py:1441
  462.7 2.5 reshape.276
  465.2 1.6 constant_dynamic-update-slice_fusion.4
  466.8 1.4 maximum_select_fusion
  468.6 0.8 copy-done.54
  469.7 52.2 %scatter_trunk.1 = (f32[640,256]{1,0:T(8,128)S(1)}, f32[8,128]{1,0:T(8,128)S(1)}) custom-call(bf16[16,640,256]{2,1,0:T(8,128)(2,1)S(1)} %constant_dynamic-update-slice_fusion.p_ref), custom_call_target="tpu_custom_call" | custom-call | tf_op jit(solution)/shard_map/scatter_trunk/pallas_call | solution.py:1578
  522.5 2.9 own_squares.1
  525.4 0.7 copy-done.41
  526.0 13.5 %small_sum.9.refs_0_ = f32[8,128]{1,0:T(8,128)S(1)} custom-call(f32[8,128]{1,0:T(8,128)S(1)} %copy-done.41), custom_call_target="tpu_custom_call" | custom-call | tf_op jit(solution)/shard_map/small_sum/pallas_call | solution.py:109
  540.3 1.2 copy-done.4
  541.5 0.7 copy-done.33
  542.2 0.7 copy-done.46
  542.8 7.8 %adam.1 = (f32[29,128,128]{2,1,0:T(8,128)}, f32[29,128,128]{2,1,0:T(8,128)}, f32[29,128,128]{2,1,0:T(8,128)}, f32[2,128,256]{2,1,0:T(8,128)}, f32[2,128,256]{2,1...) custom-call(f32[8,128]{1,0:T(8,128)S(1)} %small_sum.9.refs_0_, ...), custom_call_target="tpu_custom_call" | custom-call | flops 100000000 | bytes 18874368 | tf_op jit(solution)/shard_map/adam/pallas_call | solution.py:1720
  550.6 0.6 copy.107
  551.2 0.6 copy.108
  551.8 0.6 copy.109
  (169 shorter events, 8.8 us)
Async XLA Ops:
  7.2 3.7 copy-start.61
  7.2 6.7 %copy-start.55 = (s32[1,1600]{1,0:T(1,128)S(1)}, s32[1,1600]{1,0:T(1,128)}, u32[]{:S(2)}) copy-start(s32[1,1600]{1,0:T(1,128)} %param.37) | copy-start | bytes 19204
  7.2 169.8 %all-gather.3.cloned.1.call-start = ((), (), s32[]{:S(2)}) async-start(), calls=%async_computation.1 | async-start | bytes 5570560 | tf_op jit(solution)/shard_map/all_gather | solution.py:1863
  9.0 5.3 copy-start.5
  9.0 6.0 %copy-start.8 = (f32[2,128,256]{2,1,0:T(8,128)S(1)}, f32[2,128,256]{2,1,0:T(8,128)}, u32[]{:S(2)}) copy-start(f32[2,128,256]{2,1,0:T(8,128)} %refs_10_.1) | copy-start | bytes 786436
  9.0 6.7 %copy-start.32 = (f32[16,22]{1,0:T(8,128)S(1)}, f32[16,22]{1,0:T(8,128)}, u32[]{:S(2)}) copy-start(f32[16,22]{1,0:T(8,128)} %refs_22_.1) | copy-start | bytes 4228
  9.0 6.7 %copy-start.52 = (bf16[1,1600,192]{1,2,0:T(8,128)(2,1)S(1)}, bf16[1,1600,192]{1,2,0:T(8,128)(2,1)}, u32[]{:S(2)}) copy-start(bf16[1,1600,192]{1,2,0:T(8,128)(2,1)} %param.31) | copy-start | bytes 1843204
  9.8 6.2 %copy-start.42 = (f32[25]{0:T(128)S(1)}, f32[25]{0:T(128)}, u32[]{:S(2)}) copy-start(f32[25]{0:T(128)} %param.59) | copy-start | bytes 304
  9.8 6.3 %copy-start.22 = (f32[5,128,16]{1,2,0:T(8,128)S(1)}, f32[5,128,16]{1,2,0:T(8,128)}, u32[]{:S(2)}) copy-start(f32[5,128,16]{1,2,0:T(8,128)} %param.50) | copy-start | bytes 122884
  9.8 6.9 %copy-start.15 = (f32[192,1,64]{0,2,1:T(8,128)S(1)}, f32[192,1,64]{0,2,1:T(8,128)}, u32[]{:S(2)}) copy-start(f32[192,1,64]{0,2,1:T(8,128)} %param.38) | copy-start | bytes 147460
  9.8 172.7 %all-gather.5.cloned.1.call-start = ((), (), s32[]{:S(2)}) async-start(), calls=%async_computation.2 | async-start | bytes 10584064 | tf_op jit(solution)/shard_map/all_gather | solution.py:1864
  10.8 89.6 %copy-start.56 = (s32[1,1600]{1,0:T(1,128)S(1)}, s32[1,1600]{1,0:T(1,128)}, u32[]{:S(2)}) copy-start(s32[1,1600]{1,0:T(1,128)} %param.36) | copy-start | bytes 19204
  10.8 89.6 %copy-start.57 = (s32[1,1600]{1,0:T(1,128)S(1)}, s32[1,1600]{1,0:T(1,128)}, u32[]{:S(2)}) copy-start(s32[1,1600]{1,0:T(1,128)} %param.34) | copy-start | bytes 19204
  10.8 511.2 %reduce-scatter.2.cloned.1.call-start = ((), (), s32[]{:S(2)}) async-start(), calls=%async_computation.3 | async-start | bytes 16154624 | tf_op jit(solution)/shard_map/reduce_scatter | solution.py:1999
  10.9 152.5 %copy-start.19 = (f32[2,1,1280]{2,0,1:T(2,128)}, f32[2,1,1280]{2,0,1:T(2,128)S(1)}, u32[]{:S(2)}) copy-start(f32[2,1,1280]{2,0,1:T(2,128)S(1)} %copy.119) | copy-start | bytes 30724
  10.9 112.4 %collective-permute-start = (f32[2,1280]{1,0:T(2,128)S(1)}, f32[2,1280]{1,0:T(2,128)S(1)}, u32[]{:S(2)}, u32[]{:S(2)}) collective-permute-start(f32[2,1280]{1,0:T(2,128)S(1)} %bitcast.84), channel_id=1, source_target_pairs={{0,1},{1,0},{2,3},{3,2},{4,5},{5,4},{6,7},{7,6},{8,9},{9,8},{10,11... | collective-permute-start | bytes 30728 | tf_op jit(solution)/shard_map/ppermute | solution.py:141
  14.2 149.2 %copy-start = (f32[1600,1]{1,0:T(8,128)}, f32[1600,1]{1,0:T(8,128)S(1)}, u32[]{:S(2)}) copy-start(f32[1600,1]{1,0:T(8,128)S(1)} %copy.91.crop_ref) | copy-start | bytes 19204
  100.5 1.2 copy-start.6
  123.3 100.5 %copy-start.10 = (f32[8,512]{1,0:T(8,128)}, f32[8,512]{1,0:T(8,128)S(1)}, u32[]{:S(2)}) copy-start(f32[8,512]{1,0:T(8,128)S(1)} %small_sum.5.stat_ref.count_ref.one_ref) | copy-start | bytes 49156
  123.4 290.4 %copy-start.29 = (f32[2,1280]{1,0:T(2,128)}, f32[2,1280]{1,0:T(2,128)S(1)}, u32[]{:S(2)}) copy-start(f32[2,1280]{1,0:T(2,128)S(1)} %collective-permute-done.other_ref.gain_ref.other_gain_ref) | copy-start | bytes 30724
  123.6 15.7 %copy-start.2 = (f32[1600,128]{1,0:T(8,128)}, f32[1600,128]{1,0:T(8,128)S(1)}, u32[]{:S(2)}) copy-start(f32[1600,128]{1,0:T(8,128)S(1)} %broadcast_in_dim.22.col_ref) | copy-start | bytes 2457604
  139.3 1.4 copy-start.49
  140.7 22.7 %copy-start.7 = (bf16[2048,192]{1,0:T(8,128)(2,1)S(1)}, bf16[2048,192]{1,0:T(8,128)(2,1)}, u32[]{:S(2)}) copy-start(bf16[2048,192]{1,0:T(8,128)(2,1)} %get-tuple-element.115.stem_ref) | copy-start | bytes 2359300
  163.4 13.1 %copy-start.18 = (f32[8,512]{1,0:T(8,128)}, f32[8,512]{1,0:T(8,128)S(1)}, u32[]{:S(2)}) copy-start(f32[8,512]{1,0:T(8,128)S(1)} %small_sum.6.stat_ref) | copy-start | bytes 49156
  182.5 43.4 %copy-start.62 = (s32[1,1600]{1,0:T(1,128)S(1)}, s32[1,1600]{1,0:T(1,128)}, u32[]{:S(2)}) copy-start(s32[1,1600]{1,0:T(1,128)} %param.32) | copy-start | bytes 19204
  182.5 44.6 %copy-start.58 = (f32[1,2,1600]{2,1,0:T(2,128)S(1)}, f32[1,2,1600]{2,1,0:T(2,128)}, u32[]{:S(2)}) copy-start(f32[1,2,1600]{2,1,0:T(2,128)} %param.33) | copy-start | bytes 38404
  182.5 44.6 %copy-start.63 = (f32[1,1600]{1,0:T(1,128)S(1)}, f32[1,1600]{1,0:T(1,128)}, u32[]{:S(2)}) copy-start(f32[1,1600]{1,0:T(1,128)} %param.35) | copy-start | bytes 19204
  223.8 21.3 %copy-start.9 = (bf16[1600,256]{1,0:T(8,128)(2,1)S(1)}, bf16[1600,256]{1,0:T(8,128)(2,1)}, u32[]{:S(2)}) copy-start(bf16[1600,256]{1,0:T(8,128)(2,1)} %get-tuple-element.128.own_ref) | copy-start | bytes 2457604
  223.8 21.2 %copy-start.45 = (f32[1,128]{1,0:T(1,128)S(1)}, f32[1,128]{1,0:T(1,128)}, u32[]{:S(2)}) copy-start(f32[1,128]{1,0:T(1,128)} %get-tuple-element.135.pool_pre_ref) | copy-start | bytes 1540
  224.4 20.6 %collective-permute-start.1 = (bf16[1600,256]{1,0:T(8,128)(2,1)}, bf16[1600,256]{1,0:T(8,128)(2,1)S(1)}, u32[]{:S(2)}, u32[]{:S(2)}) collective-permute-start(bf16[1600,256]{1,0:T(8,128)(2,1)} %get-tuple-element.128.own_ref), channel_id=1, source_target_pairs={{0,1},{1,0},{2,3},{3,2},{4,5},{5,4},{6,7},{7,6},{8,9},{9,8},{10,11... | collective-permute-start | bytes 2457608 | tf_op jit(solution)/shard_map/ppermute | solution.py:141
  245.0 1.0 copy-start.12
  256.7 0.9 copy-start.47
  269.2 14.0 %copy-start.35 = (f32[1,2048]{1,0:T(1,128)S(1)}, f32[1,2048]{1,0:T(1,128)}, u32[]{:S(2)}) copy-start(f32[1,2048]{1,0:T(1,128)} %copy-done.34) | copy-start | bytes 24580
  269.2 62.4 %collective-permute-start.2 = (bf16[1600,512]{1,0:T(8,128)(2,1)}, bf16[1600,512]{1,0:T(8,128)(2,1)}, u32[]{:S(2)}, u32[]{:S(2)}) collective-permute-start(bf16[1600,512]{1,0:T(8,128)(2,1)} %pyramid_field.2), channel_id=1, source_target_pairs={{0,1},{1,0},{2,3},{3,2},{4,5},{5,4},{6,7},{7,6},{8,9},{9,8},{10,11... | collective-permute-start | bytes 4915208 | tf_op jit(solution)/shard_map/ppermute | solution.py:141
  282.5 59.3 %collective-permute-start.3 = (bf16[1600,512]{1,0:T(8,128)(2,1)}, bf16[1600,512]{1,0:T(8,128)(2,1)}, u32[]{:S(2)}, u32[]{:S(2)}) collective-permute-start(bf16[1600,512]{1,0:T(8,128)(2,1)} %pyramid_field.3), channel_id=1, source_target_pairs={{0,1},{1,0},{2,3},{3,2},{4,5},{5,4},{6,7},{7,6},{8,9},{9,8},{10,11... | collective-permute-start | bytes 4915208 | tf_op jit(solution)/shard_map/ppermute | solution.py:141
  284.5 43.6 %copy-start.48 = (bf16[1600,256]{1,0:T(8,128)(2,1)S(1)}, bf16[1600,256]{1,0:T(8,128)(2,1)}, u32[]{:S(2)}) copy-start(bf16[1600,256]{1,0:T(8,128)(2,1)} %copy-done.47) | copy-start | bytes 2457604
  348.1 0.7 copy-start.28
  360.6 15.3 %copy-start.59 = (f32[2,1,1280]{2,1,0:T(1,128)S(1)}, f32[2,1,1280]{2,1,0:T(1,128)}, u32[]{:S(2)}) copy-start(f32[2,1,1280]{2,1,0:T(1,128)} %param.58) | copy-start | bytes 30724
  360.6 15.3 %copy-start.60 = (f32[2,1,1280]{2,1,0:T(1,128)S(1)}, f32[2,1,1280]{2,1,0:T(1,128)}, u32[]{:S(2)}) copy-start(f32[2,1,1280]{2,1,0:T(1,128)} %param.57) | copy-start | bytes 30724
  360.6 15.8 %copy-start.50 = (bf16[1600,512]{1,0:T(8,128)(2,1)S(1)}, bf16[1600,512]{1,0:T(8,128)(2,1)}, u32[]{:S(2)}) copy-start(bf16[1600,512]{1,0:T(8,128)(2,1)} %get-tuple-element.120.a_ref) | copy-start | bytes 4915204
  373.8 38.4 %collective-permute-start.4 = (bf16[1600,512]{1,0:T(8,128)(2,1)}, bf16[1600,512]{1,0:T(8,128)(2,1)}, u32[]{:S(2)}, u32[]{:S(2)}) collective-permute-start(bf16[1600,512]{1,0:T(8,128)(2,1)} %get-tuple-element.154.part_ref), channel_id=1, source_target_pairs={{0,1},{1,0},{2,3},{3,2},{4,5},{5,4},{6,7},{7,6},{8,9},{9,8},{10,11... | collective-permute-start | bytes 4915208 | tf_op jit(solution)/shard_map/ppermute | solution.py:141
  376.4 37.3 %copy-start.1 = (f32[1600,1]{1,0:T(8,128)S(1)}, f32[1600,1]{1,0:T(8,128)}, u32[]{:S(2)}) copy-start(f32[1600,1]{1,0:T(8,128)} %copy-done) | copy-start | bytes 19204
  376.5 37.3 %copy-start.3 = (f32[1600,128]{1,0:T(8,128)S(1)}, f32[1600,128]{1,0:T(8,128)}, u32[]{:S(2)}) copy-start(f32[1600,128]{1,0:T(8,128)} %copy-done.2) | copy-start | bytes 2457604
  376.5 37.3 %copy-start.11 = (f32[8,512]{1,0:T(8,128)S(1)}, f32[8,512]{1,0:T(8,128)}, u32[]{:S(2)}) copy-start(f32[8,512]{1,0:T(8,128)} %copy-done.10) | copy-start | bytes 49156
  376.5 37.3 %copy-start.20 = (f32[2,1,1280]{2,0,1:T(2,128)S(1)}, f32[2,1,1280]{2,0,1:T(2,128)}, u32[]{:S(2)}) copy-start(f32[2,1,1280]{2,0,1:T(2,128)} %copy-done.19) | copy-start | bytes 30724
  412.3 19.8 %copy-start.51 = (bf16[512,1600]{1,0:T(8,128)(2,1)S(1)}, bf16[512,1600]{1,0:T(8,128)(2,1)}, u32[]{:S(2)}) copy-start(bf16[512,1600]{1,0:T(8,128)(2,1)} %get-tuple-element.169.xt_ref) | copy-start | bytes 4915204
  412.3 36.4 %collective-permute-start.5 = (bf16[1024,256]{1,0:T(8,128)(2,1)S(1)}, bf16[1024,256]{1,0:T(8,128)(2,1)}, u32[]{:S(2)}, u32[]{:S(2)}) collective-permute-start(bf16[1024,256]{1,0:T(8,128)(2,1)S(1)} %get-tuple-element.283), channel_id=1, source_target_pairs={{0,1},{1,0},{2,3},{3,2},{4,5},{5,4},{6,7},{7,6},{8,9},{9,8},{10,11... | collective-permute-start | bytes 1572872 | tf_op jit(solution)/shard_map/ppermute | solution.py:141
  468.4 1.0 copy-start.54
  468.4 1.1 copy-start.53
  469.5 70.6 %copy-start.13 = (f32[9,32,256]{2,1,0:T(8,128)S(1)}, f32[9,32,256]{2,1,0:T(8,128)}, u32[]{:S(2)}) copy-start(f32[9,32,256]{2,1,0:T(8,128)} %refs_14_.1) | copy-start | bytes 884740
  469.5 70.6 %copy-start.14 = (f32[9,32,256]{2,1,0:T(8,128)S(1)}, f32[9,32,256]{2,1,0:T(8,128)}, u32[]{:S(2)}) copy-start(f32[9,32,256]{2,1,0:T(8,128)} %refs_15_.1) | copy-start | bytes 884740
  469.6 70.6 %copy-start.16 = (f32[2,128,256]{2,1,0:T(8,128)S(1)}, f32[2,128,256]{2,1,0:T(8,128)}, u32[]{:S(2)}) copy-start(f32[2,128,256]{2,1,0:T(8,128)} %refs_11_.1) | copy-start | bytes 786436
  469.6 70.6 %copy-start.17 = (f32[2,128,256]{2,1,0:T(8,128)S(1)}, f32[2,128,256]{2,1,0:T(8,128)}, u32[]{:S(2)}) copy-start(f32[2,128,256]{2,1,0:T(8,128)} %refs_12_.1) | copy-start | bytes 786436
  469.6 70.6 %copy-start.21 = (f32[2,1,1280]{2,0,1:T(2,128)S(1)}, f32[2,1,1280]{2,0,1:T(2,128)}, u32[]{:S(2)}) copy-start(f32[2,1,1280]{2,0,1:T(2,128)} %copy-done.19) | copy-start | bytes 30724
  469.6 70.6 %copy-start.23 = (f32[5,128,16]{1,2,0:T(8,128)S(1)}, f32[5,128,16]{1,2,0:T(8,128)}, u32[]{:S(2)}) copy-start(f32[5,128,16]{1,2,0:T(8,128)} %param.50) | copy-start | bytes 122884
  469.6 70.6 %copy-start.26 = (f32[192,1,64]{0,2,1:T(8,128)S(1)}, f32[192,1,64]{0,2,1:T(8,128)}, u32[]{:S(2)}) copy-start(f32[192,1,64]{0,2,1:T(8,128)} %param.39) | copy-start | bytes 147460
  469.6 70.6 %copy-start.27 = (f32[192,1,64]{0,2,1:T(8,128)S(1)}, f32[192,1,64]{0,2,1:T(8,128)}, u32[]{:S(2)}) copy-start(f32[192,1,64]{0,2,1:T(8,128)} %param.40) | copy-start | bytes 147460
  469.6 70.6 %copy-start.30 = (f32[5,128,16]{1,2,0:T(8,128)S(1)}, f32[5,128,16]{1,2,0:T(8,128)}, u32[]{:S(2)}) copy-start(f32[5,128,16]{1,2,0:T(8,128)} %param.51) | copy-start | bytes 122884
  469.6 70.6 %copy-start.31 = (f32[5,128,16]{1,2,0:T(8,128)S(1)}, f32[5,128,16]{1,2,0:T(8,128)}, u32[]{:S(2)}) copy-start(f32[5,128,16]{1,2,0:T(8,128)} %param.52) | copy-start | bytes 122884
  469.7 70.6 %copy-start.36 = (f32[16,22]{1,0:T(8,128)S(1)}, f32[16,22]{1,0:T(8,128)}, u32[]{:S(2)}) copy-start(f32[16,22]{1,0:T(8,128)} %refs_23_.1) | copy-start | bytes 4228
  469.7 70.6 %copy-start.37 = (f32[16,22]{1,0:T(8,128)S(1)}, f32[16,22]{1,0:T(8,128)}, u32[]{:S(2)}) copy-start(f32[16,22]{1,0:T(8,128)} %refs_24_.1) | copy-start | bytes 4228
  469.7 70.6 %copy-start.43 = (f32[25]{0:T(128)S(1)}, f32[25]{0:T(128)}, u32[]{:S(2)}) copy-start(f32[25]{0:T(128)} %param.60) | copy-start | bytes 304
  469.7 70.6 %copy-start.44 = (f32[25]{0:T(128)S(1)}, f32[25]{0:T(128)}, u32[]{:S(2)}) copy-start(f32[25]{0:T(128)} %param.61) | copy-start | bytes 304
  540.3 1.2 copy-start.4
  (9 other events, 5.6 us)
Sparse Core Ops, SparseCore 0:
  10.2 78.3 all-gather.2
  90.8 91.6 all-gather.4
  342.0 169.8 reduce-scatter.1

commit v7 on v6

--- a/solution.py
+++ b/solution.py
@@ -28,113 +28,98 @@
 MESH_ID = pl.DeviceIdType.MESH
 
 
-def group_place(sizes, axes):
-    place = jnp.int32(0)
-    for axis in axes:
-        place = place * sizes[axis] + lax.axis_index(axis)
-    return place
-
-
-def group_device(sizes, axes, index):
-    coords = {}
-    for axis in reversed(axes):
-        coords[axis] = lax.rem(index, sizes[axis])
-        index = lax.div(index, sizes[axis])
-    return tuple(coords.get(axis, lax.axis_index(axis)) for axis in ("dp", "chan"))
-
-
-def sum_kernel(sizes, axes, count, x_ref, o_ref, slots, send_sem, recv_sem):
-    me = group_place(sizes, axes)
+NEAR = 4
+
+
+def sum_kernel(near, far, chans, x_ref, o_ref, inner, part, outer, sems_in, sems_out):
+    dp = lax.axis_index("dp")
+    chan = lax.axis_index("chan")
+    layer, spot = lax.div(dp, near), lax.rem(dp, near)
     barrier = pltpu.get_barrier_semaphore()
 
-    def greet(step, carry):
-        other = lax.rem(me + step, count)
-        pl.semaphore_signal(
-            barrier, inc=1, device_id=group_device(sizes, axes, other), device_id_type=MESH_ID
-        )
-        return carry
-
-    lax.fori_loop(1, count, greet, 0)
-    pl.semaphore_wait(barrier, count - 1)
-
-    def copy_to(step):
-        other = lax.rem(me + step, count)
-        return pltpu.make_async_remote_copy(
-            src_ref=x_ref,
-            dst_ref=slots.at[me],
-            send_sem=send_sem.at[step],
-            recv_sem=recv_sem.at[me],
-            device_id=group_device(sizes, axes, other),
-            device_id_type=MESH_ID,
-        )
-
-    def copy_from(step):
-        other = lax.rem(me + step, count)
-        return pltpu.make_async_remote_copy(
-            src_ref=x_ref,
-            dst_ref=slots.at[other],
-            send_sem=send_sem.at[step],
-            recv_sem=recv_sem.at[other],
-            device_id=group_device(sizes, axes, other),
-            device_id_type=MESH_ID,
-        )
-
-    def start(step, carry):
-        copy_to(step).start()
-        return carry
-
-    lax.fori_loop(1, count, start, 0)
-    slots[me] = x_ref[...]
-
-    def arrive(step, carry):
-        copy_from(step).wait_recv()
-        return carry
-
-    lax.fori_loop(1, count, arrive, 0)
-    o_ref[...] = lax.fori_loop(
-        1, count, lambda index, total: total + slots[index], slots[0]
-    )
-
-    def leave(step, carry):
-        copy_to(step).wait_send()
-        return carry
-
-    lax.fori_loop(1, count, leave, 0)
+    def inner_device(step):
+        index = lax.rem((spot * chans + (chan if chans > 1 else 0)) + step, near * chans)
+        spot_of = lax.div(index, chans)
+        other = lax.rem(index, chans) if chans > 1 else chan
+        return index, (layer * near + spot_of, other)
+
+    def outer_device(step):
+        index = lax.rem(layer + step, far)
+        return index, (index * near + spot, chan)
+
+    rounds = (
+        (near * chans, inner_device, x_ref, inner, sems_in),
+        (far, outer_device, part, outer, sems_out),
+    )
+    for count, device_of, source, slots, sems in rounds:
+
+        def greet(step, carry, device_of=device_of):
+            pl.semaphore_signal(
+                barrier, inc=1, device_id=device_of(step)[1], device_id_type=MESH_ID
+            )
+            return carry
+
+        lax.fori_loop(1, count, greet, 0)
+    pl.semaphore_wait(barrier, near * chans + far - 2)
+    for count, device_of, source, slots, sems in rounds:
+        me = device_of(0)[0]
+
+        def copy_of(step, slot, device_of=device_of, source=source, slots=slots, sems=sems):
+            return pltpu.make_async_remote_copy(
+                src_ref=source,
+                dst_ref=slots.at[slot],
+                send_sem=sems.at[0, step],
+                recv_sem=sems.at[1, slot],
+                device_id=device_of(step)[1],
+                device_id_type=MESH_ID,
+            )
+
+        def start(step, carry):
+            copy_of(step, me).start()
+            return carry
+
+        def arrive(step, carry):
+            copy_of(step, device_of(step)[0]).wait_recv()
+            return carry
+
+        def leave(step, carry):
+            copy_of(step, me).wait_send()
+            return carry
+
+        lax.fori_loop(1, count, start, 0)
+        slots[me] = source[...]
+        lax.fori_loop(1, count, arrive, 0)
+        total = slots[0]
+        for index in range(1, count):
+            total = total + slots[index]
+        if source is x_ref:
+            part[...] = total
+        else:
+            o_ref[...] = total
+        lax.fori_loop(1, count, leave, 0)
 
 
 def all_sum(sizes, values, axes, collective):
-    count = 1
-    for axis in axes:
-        count *= sizes[axis]
+    near, far = NEAR, sizes["dp"] // NEAR
+    chans = sizes["chan"] if "chan" in axes else 1
+    shape = values.shape
     return pl.pallas_call(
-        functools.partial(sum_kernel, sizes, axes, count),
-        out_shape=jax.ShapeDtypeStruct(values.shape, jnp.float32),
+        functools.partial(sum_kernel, near, far, chans),
+        out_shape=jax.ShapeDtypeStruct(shape, jnp.float32),
         in_specs=[pl.BlockSpec(memory_space=pltpu.VMEM)],
         out_specs=pl.BlockSpec(memory_space=pltpu.VMEM),
         scratch_shapes=[
-            pltpu.VMEM((count,) + values.shape, jnp.float32),
-            pltpu.SemaphoreType.DMA((count,)),
-            pltpu.SemaphoreType.DMA((count,)),
+            pltpu.VMEM((near * chans,) + shape, jnp.float32),
+            pltpu.VMEM(shape, jnp.float32),
+            pltpu.VMEM((far,) + shape, jnp.float32),
+            pltpu.SemaphoreType.DMA((2, near * chans)),
+            pltpu.SemaphoreType.DMA((2, far)),
         ],
         compiler_params=pltpu.CompilerParams(
-            collective_id=collective, has_side_effects=True, vmem_limit_bytes=32 << 20
+            collective_id=collective, has_side_effects=True, vmem_limit_bytes=16 << 20
         ),
         name="small_sum",
     )(values)
-
-
-def small_sum(sizes, parts, axes, collective):
-    flat = jnp.concatenate([part.reshape(-1) for part in parts])
-    rows = -(-flat.shape[0] // 1024) * 8
-    packed = jnp.pad(flat, (0, rows * 128 - flat.shape[0])).reshape(rows, 128)
-    summed = all_sum(sizes, packed, axes, collective).reshape(-1)
-    result = []
-    start = 0
-    for part in parts:
-        size = part.size
-        result.append(summed[start : start + size].reshape(part.shape))
-        start += size
-    return result
 
 
 def swap_chan(values):
@@ -1343,7 +1328,7 @@
             pltpu.SemaphoreType.DMA((POSITIONS // BLOCK, 4)),
             pltpu.SemaphoreType.DMA,
         ],
-        compiler_params=pltpu.CompilerParams(vmem_limit_bytes=60 << 20),
+        compiler_params=pltpu.CompilerParams(vmem_limit_bytes=40 << 20),
         cost_estimate=pl.CostEstimate(flops=2 * 10**9, bytes_accessed=16 << 20, transcendentals=0),
         name="residual_back",
     )(place, own, *other, expanded, stat, counts, sums, gains, crop, bottle)
@@ -1455,7 +1440,7 @@
             pltpu.VMEM(own.shape, low),
             pltpu.SemaphoreType.DMA((5,)),
         ],
-        compiler_params=pltpu.CompilerParams(vmem_limit_bytes=60 << 20),
+        compiler_params=pltpu.CompilerParams(vmem_limit_bytes=40 << 20),
         cost_estimate=pl.CostEstimate(flops=4 * 10**9, bytes_accessed=24 << 20, transcendentals=0),
         name="late_gradients",
     )(place, up, first_pre, stat, sums, gains[1], gains[2], crop, patches_t, bottle, own, *other, xt)

time: 560 us -> 556 us (level)
  local copies, waits for them, and re-layouts: 27.2 us -> 35 us
  Pallas kernels: 428 us -> 421 us
    pallas_call x1, Pallas kernels: 52.2 us -> 63.1 us  [scatter_trunk(): pl.pallas_call(functools.partial(scatter_kernel, layers), out_shape=[jax....]
    pallas_call x5, Pallas kernels: 58.7 us -> 51.3 us  [all_sum(): pl.pallas_call(functools.partial(sum_kernel, near, far, chans), out_shape...]
    pallas_call x1, Pallas kernels: 13.2 us -> 6.97 us  [residual_back(): pl.pallas_call(residual_back_kernel, out_shape=[jax.ShapeDtypeStruct((POS...]
    unnamed x137 -> x171, local copies, waits for them, and re-layouts: 16.7 us -> 22.8 us
  transfers between devices with their start and end apart: 9 -> 9, of which waited for: 4 -> 4; matrix products, arithmetic and copies ran while one was open for 5% -> 5% of each run, Pallas kernels for 61% -> 60%
where the time goes in v7:
time: 556 us; the launch traced here: 557 us
  Pallas kernels  421 us (76%)
  waiting for transfers between devices  56.3 us (10%)
  local copies, waits for them, and re-layouts  35 us (6%)
  between operations  16.9 us (3%)
  other arithmetic  11 us (2%)
  starting transfers between devices  9.72 us (2%)
  matrix products  7.76 us (1%)
    pallas_call x1, Pallas kernels, gather_trunk(): pl.pallas_call(functools.partial(gather_kernel, count // 4), out_shape=[j...  82.7 us
    pallas_call x1, Pallas kernels, scatter_trunk(): pl.pallas_call(functools.partial(scatter_kernel, layers), out_shape=[jax....  63.1 us
    ppermute x6, waiting for transfers between devices, swap_chan(): return lax.ppermute(values, 'chan', [(0, 1), (1, 0)])  52.7 us
    pallas_call x5, Pallas kernels, all_sum(): pl.pallas_call(functools.partial(sum_kernel, near, far, chans), out_shape...  51.3 us
    pallas_call x1, Pallas kernels, own_gradients(): pl.pallas_call(own_kernel, out_shape=[jax.ShapeDtypeStruct((POSITIONS, ha...  43.1 us
    pallas_call x1, Pallas kernels, pyramid_forward(): pl.pallas_call(pyramid_kernel, out_shape=[jax.ShapeDtypeStruct((4, POSITI...  41.2 us
    pallas_call x2, Pallas kernels, pyramid_field(): pl.pallas_call(field_kernel, out_shape=jax.ShapeDtypeStruct((POSITIONS, d...  23.2 us
    unnamed x171, local copies, waits for them, and re-layouts  22.8 us
  transfers between devices with their start and end apart: 9, of which 4 were waited for; matrix products, arithmetic and copies ran while one was open for 5% of the time, Pallas kernels for 60%

profile of v7, /device:TPU:0, one launch (start us, length us, event | category | flops | bytes accessed | tf_op | source)
XLA Modules:
  0.0 557.4 jit_solution(4040908645798419364)
XLA Ops:
  7.3 1.7 convert_element_type.116
  9.0 0.9 copy-done.67
  9.9 0.8 slice.45
  10.8 2.0 slice.46
  12.9 3.0 collective-permute-start
  16.3 0.7 convert_element_type.110.middle
  17.0 0.7 convert_element_type.109.bottle
  19.3 82.7 %gather_trunk.1 = (bf16[2,2048,512]{2,1,0:T(8,128)(2,1)}, bf16[9,512,512]{2,1,0:T(8,128)(2,1)}, bf16[2048,192]{1,0:T(8,128)(2,1)}, bf16[256,768]{1,0:T(8,128)(2,1)}) custom-call(bf16[2,128,256]{2,1,0:T(8,128)(2,1)} %convert_element_type.109.bottle, bf16[9,32,256]{2,1,0:T(8,128)(2,1)} %convert_element_type.110.middle, ...), custom_call_target="tpu_custom_call" | custom-call | tf_op jit(solution)/shard_map/gather_trunk/pallas_call | solution.py:393
  102.2 1.2 copy-done.14
  103.4 12.7 %stem_reduce.1 = (bf16[2048,1600]{1,0:T(8,128)(2,1)}, f32[1600,512]{1,0:T(8,128)}, f32[8,512]{1,0:T(8,128)S(1)}) custom-call(bf16[1600,192]{1,0:T(8,128)(2,1)S(1)} %copy.90.p_ref, bf16[2048,192]{1,0:T(8,128)(2,1)S(1)} %copy-done.14, bf16[2,2048,512]{2,1,0:T(8,128)(2,1)} %get-tuple-element.116.reduce_ref.w_ref.bottle_hbm, f32[1600,1]{1,0:T(8,128)S(1)} %copy.91.crop_ref, ...), custom_call_target="tpu_custom_call" | custom-call | flops 5000000000 | bytes 14680064 | tf_op jit(solution)/shard_map/stem_reduce/pallas_call | solution.py:785
  116.1 9.7 %small_sum.5.stat_ref.count_ref.one_ref = f32[8,512]{1,0:T(8,128)S(1)} custom-call(f32[8,512]{1,0:T(8,128)S(1)} %get-tuple-element.117.x_ref), custom_call_target="tpu_custom_call" | custom-call | tf_op jit(solution)/shard_map/small_sum/pallas_call | solution.py:106
  126.1 15.6 %norm_middle.1 = (bf16[1600,512]{1,0:T(8,128)(2,1)}, bf16[512,1600]{1,0:T(8,128)(2,1)}, bf16[1600,512]{1,0:T(8,128)(2,1)}) custom-call(f32[1600,512]{1,0:T(8,128)} %get-tuple-element.118.a_ref, f32[8,512]{1,0:T(8,128)S(1)} %small_sum.5.stat_ref.count_ref.one_ref, s32[1]{0:T(128)} %bitcast.place_ref, f32[2,1280]{1,0:T(2,128)S(1)} %bitcast.88, ...), custom_call_target="tpu_custom_call" | custom-call | flops 8000000000 | bytes 14680064 | tf_op jit(solution)/shard_map/norm_middle/pallas_call | solution.py:858
  141.7 1.4 copy-done.64
  143.1 9.0 %expand_forward.1 = (bf16[1600,2048]{1,0:T(8,128)(2,1)}, f32[8,512]{1,0:T(8,128)S(1)}) custom-call(bf16[1600,512]{1,0:T(8,128)(2,1)S(1)} %copy-done.64, bf16[2,2048,512]{2,1,0:T(8,128)(2,1)} %get-tuple-element.116.reduce_ref.w_ref.bottle_hbm, f32[1600,1]{1,0:T(8,128)S(1)} %copy.91.crop_ref), custom_call_target="tpu_custom_call" | custom-call | flops 4000000000 | bytes 12582912 | tf_op jit(solution)/shard_map/expand_forward/pallas_call | solution.py:895
  152.1 9.5 %small_sum.6.stat_ref = f32[8,512]{1,0:T(8,128)S(1)} custom-call(f32[8,512]{1,0:T(8,128)S(1)} %get-tuple-element.122.x_ref), custom_call_target="tpu_custom_call" | custom-call | tf_op jit(solution)/shard_map/small_sum/pallas_call | solution.py:106
  161.6 12.8 %residual_stream.1 = (bf16[1600,2048]{1,0:T(8,128)(2,1)}, bf16[2048,1600]{1,0:T(8,128)(2,1)}, f32[1,2048]{1,0:T(1,128)S(1)}) custom-call(bf16[1600,192]{1,0:T(8,128)(2,1)S(1)} %copy.90.p_ref, bf16[2048,192]{1,0:T(8,128)(2,1)S(1)} %copy-done.15, bf16[1600,2048]{1,0:T(8,128)(2,1)} %get-tuple-element.121.y_ref.y_hbm, f32[8,512]{1,0:T(8,128)S(1)} %small_sum.6.stat_ref, ...), custom_call_target="tpu_custom_call" | custom-call | flops 2000000000 | bytes 23068672 | tf_op jit(solution)/shard_map/residual_stream/pallas_call | solution.py:947
  175.6 3.5 all-gather.5.cloned.1.call-done.b_hbm
  179.2 41.2 %pyramid_fwd.1 = (f32[4,1600,128]{2,1,0:T(8,128)}, f32[1,128]{1,0:T(1,128)}, bf16[1600,640]{1,0:T(8,128)(2,1)}, bf16[1600,256]{1,0:T(8,128)(2,1)}) custom-call(bf16[1600,2048]{1,0:T(8,128)(2,1)} %get-tuple-element.123.x_ref, f32[1,2048]{1,0:T(1,128)} %copy-done.48, bf16[10,2048,128]{2,1,0:T(8,128)(2,1)} %all-gather.3.cloned.1.call-done.a_hbm, ...), custom_call_target="tpu_custom_call" | custom-call | flops 15938355200 | bytes 41943040 | tf_op jit(solution)/shard_map/pyramid_fwd/pallas_call | solution.py:1051
  221.1 1.5 collective-permute-start.1
  222.6 1.2 fusion.label_ref
  223.8 1.9 fusion.4
  226.0 1.2 pad.18.target_ref
  227.3 1.9 multiply_add_fusion.mask_ref
  229.2 12.5 %collective-permute-done.1.other_ref = bf16[1600,256]{1,0:T(8,128)(2,1)S(1)} collective-permute-done((bf16[1600,256]{1,0:T(8,128)(2,1)}, bf16[1600,256]{1,0:T(8,128)(2,1)S(1)}, u32[]{:S(2)}, u32[]{:S(2)}) %collective-permute-start.1) | collective-permute-done | bytes 819232 | tf_op jit(solution)/shard_map/ppermute | solution.py:126
  241.7 9.5 %head_step.1 = (bf16[1600,256]{1,0:T(8,128)(2,1)S(1)}, bf16[1600,128]{1,0:T(8,128)(2,1)S(1)}, bf16[1600,256]{1,0:T(8,128)(2,1)S(1)}, bf16[4,1600,128]{2,1,0:T(8,...) custom-call(bf16[1600,256]{1,0:T(8,128)(2,1)S(1)} %copy-done.18, ...), custom_call_target="tpu_custom_call" | custom-call | flops 2000000000 | bytes 16777216 | tf_op jit(solution)/shard_map/head_step/pallas_call | solution.py:1151
  251.2 0.8 copy-done.21
  253.1 0.9 copy-done.63
  254.0 11.5 %pyramid_field.2 = bf16[1600,512]{1,0:T(8,128)(2,1)} custom-call(s32[1]{0:T(128)S(6)} %sub.7.place_ref, bf16[10,2048,128]{2,1,0:T(8,128)(2,1)} %all-gather.3.cloned.1.call-done.a_hbm, bf16[19,2048,128]{2,1,0:T(8,128)(2,1)} %all-gather.5.cloned.1.call-done.b_hbm, bf16[4,1600,128]{2,1,0:T(8,128)(2,1)} %get-tuple-element.140.g_ref, f32[1,128]{1,0:T(1,128)} %copy-done.52, ...), custom_call_target="tpu_custom_call" | custom-call | flops 1000 | bytes 1024 | tf_op jit(solution)/shard_map/pyramid_field/pallas_call | solution.py:720
  265.5 1.5 collective-permute-start.2
  267.1 11.7 %pyramid_field.3 = bf16[1600,512]{1,0:T(8,128)(2,1)} custom-call(s32[1]{0:T(128)S(6)} %add.52.place_ref, bf16[10,2048,128]{2,1,0:T(8,128)(2,1)} %all-gather.3.cloned.1.call-done.a_hbm, bf16[19,2048,128]{2,1,0:T(8,128)(2,1)} %all-gather.5.cloned.1.call-done.b_hbm, bf16[4,1600,128]{2,1,0:T(8,128)(2,1)} %get-tuple-element.140.g_ref, f32[1,128]{1,0:T(1,128)} %copy-done.52, ...), custom_call_target="tpu_custom_call" | custom-call | flops 1000 | bytes 1024 | tf_op jit(solution)/shard_map/pyramid_field/pallas_call | solution.py:720
  279.4 1.4 copy.100.pooled_ref
  280.8 43.1 %own_gradients.1 = (bf16[1600,1024]{1,0:T(8,128)(2,1)}, bf16[29,2048,128]{2,1,0:T(8,128)(2,1)}) custom-call(s32[1]{0:T(128)} %bitcast.place_ref, bf16[10,2048,128]{2,1,0:T(8,128)(2,1)} %all-gather.3.cloned.1.call-done.a_hbm, bf16[19,2048,128]{2,1,0:T(8,128)(2,1)} %all-gather.5.cloned.1.call-done.b_hbm, bf16[2048,1600]{1,0:T(8,128)(2,1)} %get-tuple-element.138.xt_hbm, ...), custom_call_target="tpu_custom_call" | custom-call | flops 1000 | bytes 1024 | tf_op jit(solution)/shard_map/own_gradients/pallas_call | solution.py:693
  324.4 2.7 convolution_convert_fusion.1
  327.1 0.9 reshape.272
  328.1 10.1 %collective-permute-done.3.second_hbm = bf16[1600,512]{1,0:T(8,128)(2,1)} collective-permute-done((bf16[1600,512]{1,0:T(8,128)(2,1)}, bf16[1600,512]{1,0:T(8,128)(2,1)}, u32[]{:S(2)}, u32[]{:S(2)}) %collective-permute-start.3) | collective-permute-done | bytes 1638432 | tf_op jit(solution)/shard_map/ppermute | solution.py:126
  338.3 7.0 %residual_sums.1.x_ref = f32[8,512]{1,0:T(8,128)} custom-call(s32[1]{0:T(128)} %bitcast.place_ref, bf16[1600,1024]{1,0:T(8,128)(2,1)} %get-tuple-element.165.own_hbm, bf16[1600,512]{1,0:T(8,128)(2,1)} %copy-done.3, bf16[1600,512]{1,0:T(8,128)(2,1)} %collective-permute-done.3.second_hbm, bf16[1600,2048]{1,0:T(8,128)(2,1)} %get-tuple-element.121.y_ref.y_hbm, ...), custom_call_target="tpu_custom_call" | custom-call | flops 100000000 | bytes 12582912 | tf_op jit(solution)/shard_map/residual_sums/pallas_call | solution.py:1255
  345.3 0.7 copy-done.40
  346.0 7.6 %small_sum.7.sum_ref.three_ref = f32[8,512]{1,0:T(8,128)S(1)} custom-call(f32[8,512]{1,0:T(8,128)S(1)} %copy-done.40), custom_call_target="tpu_custom_call" | custom-call | tf_op jit(solution)/shard_map/small_sum/pallas_call | solution.py:106
  353.6 2.5 copy-done.2
  356.1 7.0 %residual_back.1 = (bf16[1600,1024]{1,0:T(8,128)(2,1)S(1)}, bf16[1600,512]{1,0:T(8,128)(2,1)}) custom-call(s32[1]{0:T(128)} %bitcast.place_ref, bf16[1600,1024]{1,0:T(8,128)(2,1)S(1)} %copy-done.2, bf16[1600,512]{1,0:T(8,128)(2,1)S(1)} %copy-done.4, bf16[1600,512]{1,0:T(8,128)(2,1)} %collective-permute-done.3.second_hbm, ...), custom_call_target="tpu_custom_call" | custom-call | flops 2000000000 | bytes 16777216 | tf_op jit(solution)/shard_map/residual_back/pallas_call | solution.py:1317
  363.1 1.7 copy-done.62
  364.8 1.6 collective-permute-start.4
  367.5 4.6 convolution_convert_fusion
  372.1 30.1 %collective-permute-done.4.other_ref = bf16[1600,512]{1,0:T(8,128)(2,1)} collective-permute-done((bf16[1600,512]{1,0:T(8,128)(2,1)}, bf16[1600,512]{1,0:T(8,128)(2,1)}, u32[]{:S(2)}, u32[]{:S(2)}) %collective-permute-start.4) | collective-permute-done | bytes 1638432 | tf_op jit(solution)/shard_map/ppermute | solution.py:126
  402.2 0.9 constant_dynamic-slice_fusion
  403.1 1.4 collective-permute-start.5
  404.5 18.1 %first_back.1 = (f32[1600,512]{1,0:T(8,128)}, bf16[1600,256]{1,0:T(8,128)(2,1)S(1)}, f32[8,512]{1,0:T(8,128)S(1)}) custom-call(s32[1]{0:T(128)} %bitcast.place_ref, bf16[1600,512]{1,0:T(8,128)(2,1)} %get-tuple-element.154.part_ref, bf16[1600,512]{1,0:T(8,128)(2,1)} %collective-permute-done.4.other_ref, bf16[9,512,512]{2,1,0:T(8,128)(2,1)} %get-tuple-element.119.w_ref, ...), custom_call_target="tpu_custom_call" | custom-call | flops 8000000000 | bytes 20971520 | tf_op jit(solution)/shard_map/first_back/pallas_call | solution.py:1645
  422.6 4.4 middle_weights.1
  427.0 1.7 copy.106
  428.7 9.8 %small_sum.8.sum_ref.four_ref = f32[8,512]{1,0:T(8,128)S(1)} custom-call(f32[8,512]{1,0:T(8,128)S(1)} %get-tuple-element.158.x_ref), custom_call_target="tpu_custom_call" | custom-call | tf_op jit(solution)/shard_map/small_sum/pallas_call | solution.py:106
  438.5 9.4 %late_gradients.1 = (bf16[2048,256]{1,0:T(8,128)(2,1)S(1)}, bf16[1024,192]{1,0:T(8,128)(2,1)S(1)}) custom-call(s32[1]{0:T(128)} %bitcast.place_ref, f32[1600,512]{1,0:T(8,128)S(1)} %copy-done.9, f32[1600,512]{1,0:T(8,128)S(1)} %copy-done.8, f32[8,512]{1,0:T(8,128)S(1)} %copy-done.20, f32[8,512]{1,0:T(8,128)S(1)} %small_sum.8.sum_ref.four_ref, ...), custom_call_target="tpu_custom_call" | custom-call | flops 4000000000 | bytes 25165824 | tf_op jit(solution)/shard_map/late_gradients/pallas_call | solution.py:1426
  448.0 1.0 copy-done.17
  448.9 0.7 reshape.276
  449.7 1.3 constant_dynamic-update-slice_fusion.4
  451.4 1.3 copy-done.66
  452.9 0.8 copy-done.69
  453.9 63.1 %scatter_trunk.1 = (f32[640,256]{1,0:T(8,128)S(1)}, f32[8,128]{1,0:T(8,128)S(1)}) custom-call(bf16[16,640,256]{2,1,0:T(8,128)(2,1)S(1)} %constant_dynamic-update-slice_fusion.p_ref), custom_call_target="tpu_custom_call" | custom-call | tf_op jit(solution)/shard_map/scatter_trunk/pallas_call | solution.py:1563
  517.6 2.9 own_squares.1
  520.5 0.7 copy-done.55
  521.2 14.8 %small_sum.9.refs_0_ = f32[8,128]{1,0:T(8,128)S(1)} custom-call(f32[8,128]{1,0:T(8,128)S(1)} %copy-done.55), custom_call_target="tpu_custom_call" | custom-call | tf_op jit(solution)/shard_map/small_sum/pallas_call | solution.py:106
  536.7 1.2 copy-done.7
  537.9 0.7 copy-done.47
  538.6 0.7 copy-done.61
  539.3 7.8 %adam.1 = (f32[29,128,128]{2,1,0:T(8,128)}, f32[29,128,128]{2,1,0:T(8,128)}, f32[29,128,128]{2,1,0:T(8,128)}, f32[2,128,256]{2,1,0:T(8,128)}, f32[2,128,256]{2,1...) custom-call(f32[8,128]{1,0:T(8,128)S(1)} %small_sum.9.refs_0_, ...), custom_call_target="tpu_custom_call" | custom-call | flops 100000000 | bytes 18874368 | tf_op jit(solution)/shard_map/adam/pallas_call | solution.py:1705
  (203 shorter events, 11.9 us)
Async XLA Ops:
  7.2 8.7 %copy-start.72 = (s32[1,1600]{1,0:T(1,128)S(1)}, s32[1,1600]{1,0:T(1,128)}, u32[]{:S(2)}) copy-start(s32[1,1600]{1,0:T(1,128)} %param.37) | copy-start | bytes 19204
  7.2 168.4 %all-gather.3.cloned.1.call-start = ((), (), s32[]{:S(2)}) async-start(), calls=%async_computation.1 | async-start | bytes 5570560 | tf_op jit(solution)/shard_map/all_gather | solution.py:1848
  9.9 7.8 %copy-start.45 = (f32[16,22]{1,0:T(8,128)S(1)}, f32[16,22]{1,0:T(8,128)}, u32[]{:S(2)}) copy-start(f32[16,22]{1,0:T(8,128)} %refs_22_.1) | copy-start | bytes 4228
  9.9 7.8 %copy-start.10 = (bf16[1,1600,192]{1,2,0:T(8,128)(2,1)S(1)}, bf16[1,1600,192]{1,2,0:T(8,128)(2,1)}, u32[]{:S(2)}) copy-start(bf16[1,1600,192]{1,2,0:T(8,128)(2,1)} %param.31) | copy-start | bytes 1843204
  10.7 7.3 %copy-start.56 = (f32[25]{0:T(128)S(1)}, f32[25]{0:T(128)}, u32[]{:S(2)}) copy-start(f32[25]{0:T(128)} %param.59) | copy-start | bytes 304
  10.7 7.4 %copy-start.34 = (f32[5,128,16]{1,2,0:T(8,128)S(1)}, f32[5,128,16]{1,2,0:T(8,128)}, u32[]{:S(2)}) copy-start(f32[5,128,16]{1,2,0:T(8,128)} %param.50) | copy-start | bytes 122884
  10.7 8.0 %copy-start.26 = (f32[192,1,64]{0,2,1:T(8,128)S(1)}, f32[192,1,64]{0,2,1:T(8,128)}, u32[]{:S(2)}) copy-start(f32[192,1,64]{0,2,1:T(8,128)} %param.38) | copy-start | bytes 147460
  10.7 168.4 %all-gather.5.cloned.1.call-start = ((), (), s32[]{:S(2)}) async-start(), calls=%async_computation.2 | async-start | bytes 10584064 | tf_op jit(solution)/shard_map/all_gather | solution.py:1849
  12.8 89.3 %copy-start.73 = (s32[1,1600]{1,0:T(1,128)S(1)}, s32[1,1600]{1,0:T(1,128)}, u32[]{:S(2)}) copy-start(s32[1,1600]{1,0:T(1,128)} %param.36) | copy-start | bytes 19204
  12.8 89.3 %copy-start.74 = (s32[1,1600]{1,0:T(1,128)S(1)}, s32[1,1600]{1,0:T(1,128)}, u32[]{:S(2)}) copy-start(s32[1,1600]{1,0:T(1,128)} %param.34) | copy-start | bytes 19204
  12.8 504.4 %reduce-scatter.2.cloned.1.call-start = ((), (), s32[]{:S(2)}) async-start(), calls=%async_computation.3 | async-start | bytes 16154624 | tf_op jit(solution)/shard_map/reduce_scatter | solution.py:1984
  12.9 148.7 %copy-start.32 = (f32[2,1,1280]{2,0,1:T(2,128)}, f32[2,1,1280]{2,0,1:T(2,128)S(1)}, u32[]{:S(2)}) copy-start(f32[2,1,1280]{2,0,1:T(2,128)S(1)} %copy.119) | copy-start | bytes 30724
  12.9 112.9 %collective-permute-start = (f32[2,1280]{1,0:T(2,128)S(1)}, f32[2,1280]{1,0:T(2,128)S(1)}, u32[]{:S(2)}, u32[]{:S(2)}) collective-permute-start(f32[2,1280]{1,0:T(2,128)S(1)} %bitcast.87), channel_id=1, source_target_pairs={{0,1},{1,0},{2,3},{3,2},{4,5},{5,4},{6,7},{7,6},{8,9},{9,8},{10,11... | collective-permute-start | bytes 30728 | tf_op jit(solution)/shard_map/ppermute | solution.py:126
  16.2 145.4 %copy-start = (f32[1600,1]{1,0:T(8,128)}, f32[1600,1]{1,0:T(8,128)S(1)}, u32[]{:S(2)}) copy-start(f32[1600,1]{1,0:T(8,128)S(1)} %copy.91.crop_ref) | copy-start | bytes 19204
  125.7 94.7 %copy-start.19 = (f32[8,512]{1,0:T(8,128)}, f32[8,512]{1,0:T(8,128)S(1)}, u32[]{:S(2)}) copy-start(f32[8,512]{1,0:T(8,128)S(1)} %small_sum.5.stat_ref.count_ref.one_ref) | copy-start | bytes 49156
  125.8 35.9 %copy-start.41 = (f32[2,1280]{1,0:T(2,128)}, f32[2,1280]{1,0:T(2,128)S(1)}, u32[]{:S(2)}) copy-start(f32[2,1280]{1,0:T(2,128)S(1)} %collective-permute-done.other_ref.gain_ref.other_gain_ref) | copy-start | bytes 30724
  126.1 15.6 %copy-start.5 = (f32[1600,128]{1,0:T(8,128)}, f32[1600,128]{1,0:T(8,128)S(1)}, u32[]{:S(2)}) copy-start(f32[1600,128]{1,0:T(8,128)S(1)} %broadcast_in_dim.22.col_ref) | copy-start | bytes 2457604
  143.1 18.5 %copy-start.15 = (bf16[2048,192]{1,0:T(8,128)(2,1)S(1)}, bf16[2048,192]{1,0:T(8,128)(2,1)}, u32[]{:S(2)}) copy-start(bf16[2048,192]{1,0:T(8,128)(2,1)} %get-tuple-element.115.stem_ref) | copy-start | bytes 2359300
  179.2 43.4 %copy-start.79 = (s32[1,1600]{1,0:T(1,128)S(1)}, s32[1,1600]{1,0:T(1,128)}, u32[]{:S(2)}) copy-start(s32[1,1600]{1,0:T(1,128)} %param.32) | copy-start | bytes 19204
  179.2 44.6 %copy-start.75 = (f32[1,2,1600]{2,1,0:T(2,128)S(1)}, f32[1,2,1600]{2,1,0:T(2,128)}, u32[]{:S(2)}) copy-start(f32[1,2,1600]{2,1,0:T(2,128)} %param.33) | copy-start | bytes 38404
  179.2 44.6 %copy-start.80 = (f32[1,1600]{1,0:T(1,128)S(1)}, f32[1,1600]{1,0:T(1,128)}, u32[]{:S(2)}) copy-start(f32[1,1600]{1,0:T(1,128)} %param.35) | copy-start | bytes 19204
  220.4 21.3 %copy-start.18 = (bf16[1600,256]{1,0:T(8,128)(2,1)S(1)}, bf16[1600,256]{1,0:T(8,128)(2,1)}, u32[]{:S(2)}) copy-start(bf16[1600,256]{1,0:T(8,128)(2,1)} %get-tuple-element.128.own_ref) | copy-start | bytes 2457604
  220.4 21.3 %copy-start.23 = (bf16[256,768]{1,0:T(8,128)(2,1)S(1)}, bf16[256,768]{1,0:T(8,128)(2,1)}, u32[]{:S(2)}) copy-start(bf16[256,768]{1,0:T(8,128)(2,1)} %get-tuple-element.125.project_ref) | copy-start | bytes 1179652
  220.4 21.2 %copy-start.60 = (f32[1,128]{1,0:T(1,128)S(1)}, f32[1,128]{1,0:T(1,128)}, u32[]{:S(2)}) copy-start(f32[1,128]{1,0:T(1,128)} %get-tuple-element.135.pool_pre_ref) | copy-start | bytes 1540
  221.1 20.6 %collective-permute-start.1 = (bf16[1600,256]{1,0:T(8,128)(2,1)}, bf16[1600,256]{1,0:T(8,128)(2,1)S(1)}, u32[]{:S(2)}, u32[]{:S(2)}) collective-permute-start(bf16[1600,256]{1,0:T(8,128)(2,1)} %get-tuple-element.128.own_ref), channel_id=1, source_target_pairs={{0,1},{1,0},{2,3},{3,2},{4,5},{5,4},{6,7},{7,6},{8,9},{9,8},{10,11... | collective-permute-start | bytes 2457608 | tf_op jit(solution)/shard_map/ppermute | solution.py:126
  265.5 13.9 %copy-start.49 = (f32[1,2048]{1,0:T(1,128)S(1)}, f32[1,2048]{1,0:T(1,128)}, u32[]{:S(2)}) copy-start(f32[1,2048]{1,0:T(1,128)} %copy-done.48) | copy-start | bytes 24580
  265.5 62.5 %collective-permute-start.2 = (bf16[1600,512]{1,0:T(8,128)(2,1)}, bf16[1600,512]{1,0:T(8,128)(2,1)S(1)}, u32[]{:S(2)}, u32[]{:S(2)}) collective-permute-start(bf16[1600,512]{1,0:T(8,128)(2,1)} %pyramid_field.2), channel_id=1, source_target_pairs={{0,1},{1,0},{2,3},{3,2},{4,5},{5,4},{6,7},{7,6},{8,9},{9,8},{10,11... | collective-permute-start | bytes 4915208 | tf_op jit(solution)/shard_map/ppermute | solution.py:126
  278.8 59.4 %collective-permute-start.3 = (bf16[1600,512]{1,0:T(8,128)(2,1)}, bf16[1600,512]{1,0:T(8,128)(2,1)}, u32[]{:S(2)}, u32[]{:S(2)}) collective-permute-start(bf16[1600,512]{1,0:T(8,128)(2,1)} %pyramid_field.3), channel_id=1, source_target_pairs={{0,1},{1,0},{2,3},{3,2},{4,5},{5,4},{6,7},{7,6},{8,9},{9,8},{10,11... | collective-permute-start | bytes 4915208 | tf_op jit(solution)/shard_map/ppermute | solution.py:126
  280.8 43.1 %copy-start.22 = (bf16[1600,128]{1,0:T(8,128)(2,1)S(1)}, bf16[1600,128]{1,0:T(8,128)(2,1)}, u32[]{:S(2)}) copy-start(bf16[1600,128]{1,0:T(8,128)(2,1)} %copy-done.21) | copy-start | bytes 1228804
  328.1 10.1 %copy-start.3 = (bf16[1600,512]{1,0:T(8,128)(2,1)}, bf16[1600,512]{1,0:T(8,128)(2,1)S(1)}, u32[]{:S(2)}) copy-start(bf16[1600,512]{1,0:T(8,128)(2,1)S(1)} %collective-permute-done.2.first_hbm) | copy-start | bytes 4915204
  338.2 15.4 %copy-start.1 = (f32[1600,1]{1,0:T(8,128)S(1)}, f32[1600,1]{1,0:T(8,128)}, u32[]{:S(2)}) copy-start(f32[1600,1]{1,0:T(8,128)} %copy-done) | copy-start | bytes 19204
  338.2 15.4 %copy-start.4 = (bf16[1600,512]{1,0:T(8,128)(2,1)S(1)}, bf16[1600,512]{1,0:T(8,128)(2,1)}, u32[]{:S(2)}) copy-start(bf16[1600,512]{1,0:T(8,128)(2,1)} %copy-done.3) | copy-start | bytes 4915204
  338.2 15.4 %copy-start.20 = (f32[8,512]{1,0:T(8,128)S(1)}, f32[8,512]{1,0:T(8,128)}, u32[]{:S(2)}) copy-start(f32[8,512]{1,0:T(8,128)} %copy-done.19) | copy-start | bytes 49156
  338.2 15.4 %copy-start.31 = (f32[8,512]{1,0:T(8,128)S(1)}, f32[8,512]{1,0:T(8,128)}, u32[]{:S(2)}) copy-start(f32[8,512]{1,0:T(8,128)} %copy-done.30) | copy-start | bytes 49156
  338.3 15.4 %copy-start.33 = (f32[2,1,1280]{2,0,1:T(2,128)S(1)}, f32[2,1,1280]{2,0,1:T(2,128)}, u32[]{:S(2)}) copy-start(f32[2,1,1280]{2,0,1:T(2,128)} %copy-done.32) | copy-start | bytes 30724
  356.1 10.9 %copy-start.76 = (f32[2,1,1280]{2,1,0:T(1,128)S(1)}, f32[2,1,1280]{2,1,0:T(1,128)}, u32[]{:S(2)}) copy-start(f32[2,1,1280]{2,1,0:T(1,128)} %param.58) | copy-start | bytes 30724
  356.1 10.9 %copy-start.77 = (f32[2,1,1280]{2,1,0:T(1,128)S(1)}, f32[2,1,1280]{2,1,0:T(1,128)}, u32[]{:S(2)}) copy-start(f32[2,1,1280]{2,1,0:T(1,128)} %param.57) | copy-start | bytes 30724
  364.8 37.5 %collective-permute-start.4 = (bf16[1600,512]{1,0:T(8,128)(2,1)}, bf16[1600,512]{1,0:T(8,128)(2,1)}, u32[]{:S(2)}, u32[]{:S(2)}) collective-permute-start(bf16[1600,512]{1,0:T(8,128)(2,1)} %get-tuple-element.154.part_ref), channel_id=1, source_target_pairs={{0,1},{1,0},{2,3},{3,2},{4,5},{5,4},{6,7},{7,6},{8,9},{9,8},{10,11... | collective-permute-start | bytes 4915208 | tf_op jit(solution)/shard_map/ppermute | solution.py:126
  367.5 37.0 %copy-start.6 = (f32[1600,128]{1,0:T(8,128)S(1)}, f32[1600,128]{1,0:T(8,128)}, u32[]{:S(2)}) copy-start(f32[1600,128]{1,0:T(8,128)} %copy-done.5) | copy-start | bytes 2457604
  367.5 37.0 %copy-start.42 = (f32[2,1280]{1,0:T(2,128)S(1)}, f32[2,1280]{1,0:T(2,128)}, u32[]{:S(2)}) copy-start(f32[2,1280]{1,0:T(2,128)} %copy-done.41) | copy-start | bytes 30724
  403.1 19.5 %copy-start.65 = (bf16[512,1600]{1,0:T(8,128)(2,1)S(1)}, bf16[512,1600]{1,0:T(8,128)(2,1)}, u32[]{:S(2)}) copy-start(bf16[512,1600]{1,0:T(8,128)(2,1)} %get-tuple-element.169.xt_ref) | copy-start | bytes 4915204
  403.1 35.4 %collective-permute-start.5 = (bf16[1024,256]{1,0:T(8,128)(2,1)S(1)}, bf16[1024,256]{1,0:T(8,128)(2,1)S(1)}, u32[]{:S(2)}, u32[]{:S(2)}) collective-permute-start(bf16[1024,256]{1,0:T(8,128)(2,1)S(1)} %get-tuple-element.283), channel_id=1, source_target_pairs={{0,1},{1,0},{2,3},{3,2},{4,5},{5,4},{6,7},{7,6},{8,9},{9,8},{10,11... | collective-permute-start | bytes 1572872 | tf_op jit(solution)/shard_map/ppermute | solution.py:126
  422.6 15.9 %copy-start.9 = (f32[1600,512]{1,0:T(8,128)S(1)}, f32[1600,512]{1,0:T(8,128)}, u32[]{:S(2)}) copy-start(f32[1600,512]{1,0:T(8,128)} %get-tuple-element.164.up_ref) | copy-start | bytes 9830404
  427.0 11.5 %copy-start.8 = (f32[1600,512]{1,0:T(8,128)S(1)}, f32[1600,512]{1,0:T(8,128)}, u32[]{:S(2)}) copy-start(f32[1600,512]{1,0:T(8,128)} %get-tuple-element.118.a_ref) | copy-start | bytes 9830404
  427.0 11.5 %copy-start.11 = (bf16[1,1600,192]{1,2,0:T(8,128)(2,1)S(1)}, bf16[1,1600,192]{1,2,0:T(8,128)(2,1)}, u32[]{:S(2)}) copy-start(bf16[1,1600,192]{1,2,0:T(8,128)(2,1)} %param.31) | copy-start | bytes 1843204
  438.5 9.5 %copy-start.36 = (f32[8,512]{1,0:T(8,128)}, f32[8,512]{1,0:T(8,128)S(1)}, u32[]{:S(2)}) copy-start(f32[8,512]{1,0:T(8,128)S(1)} %small_sum.8.sum_ref.four_ref) | copy-start | bytes 49156
  438.5 9.5 %copy-start.70 = (bf16[1024,256]{1,0:T(8,128)(2,1)}, bf16[1024,256]{1,0:T(8,128)(2,1)S(1)}, u32[]{:S(2)}) copy-start(bf16[1024,256]{1,0:T(8,128)(2,1)S(1)} %collective-permute-done.5) | copy-start | bytes 1572868
  453.7 82.9 %copy-start.13 = (f32[9,32,256]{2,1,0:T(8,128)S(1)}, f32[9,32,256]{2,1,0:T(8,128)}, u32[]{:S(2)}) copy-start(f32[9,32,256]{2,1,0:T(8,128)} %refs_13_.1) | copy-start | bytes 884740
  453.7 82.9 %copy-start.24 = (f32[9,32,256]{2,1,0:T(8,128)S(1)}, f32[9,32,256]{2,1,0:T(8,128)}, u32[]{:S(2)}) copy-start(f32[9,32,256]{2,1,0:T(8,128)} %refs_14_.1) | copy-start | bytes 884740
  453.7 82.9 %copy-start.25 = (f32[9,32,256]{2,1,0:T(8,128)S(1)}, f32[9,32,256]{2,1,0:T(8,128)}, u32[]{:S(2)}) copy-start(f32[9,32,256]{2,1,0:T(8,128)} %refs_15_.1) | copy-start | bytes 884740
  453.7 82.9 %copy-start.27 = (f32[192,1,64]{0,2,1:T(8,128)S(1)}, f32[192,1,64]{0,2,1:T(8,128)}, u32[]{:S(2)}) copy-start(f32[192,1,64]{0,2,1:T(8,128)} %param.38) | copy-start | bytes 147460
  453.7 82.9 %copy-start.28 = (f32[2,128,256]{2,1,0:T(8,128)S(1)}, f32[2,128,256]{2,1,0:T(8,128)}, u32[]{:S(2)}) copy-start(f32[2,128,256]{2,1,0:T(8,128)} %refs_11_.1) | copy-start | bytes 786436
  453.7 82.9 %copy-start.29 = (f32[2,128,256]{2,1,0:T(8,128)S(1)}, f32[2,128,256]{2,1,0:T(8,128)}, u32[]{:S(2)}) copy-start(f32[2,128,256]{2,1,0:T(8,128)} %refs_12_.1) | copy-start | bytes 786436
  453.8 82.9 %copy-start.35 = (f32[5,128,16]{1,2,0:T(8,128)S(1)}, f32[5,128,16]{1,2,0:T(8,128)}, u32[]{:S(2)}) copy-start(f32[5,128,16]{1,2,0:T(8,128)} %param.50) | copy-start | bytes 122884
  453.8 82.9 %copy-start.38 = (f32[192,1,64]{0,2,1:T(8,128)S(1)}, f32[192,1,64]{0,2,1:T(8,128)}, u32[]{:S(2)}) copy-start(f32[192,1,64]{0,2,1:T(8,128)} %param.39) | copy-start | bytes 147460
  453.8 82.9 %copy-start.39 = (f32[192,1,64]{0,2,1:T(8,128)S(1)}, f32[192,1,64]{0,2,1:T(8,128)}, u32[]{:S(2)}) copy-start(f32[192,1,64]{0,2,1:T(8,128)} %param.40) | copy-start | bytes 147460
  453.8 82.8 %copy-start.43 = (f32[5,128,16]{1,2,0:T(8,128)S(1)}, f32[5,128,16]{1,2,0:T(8,128)}, u32[]{:S(2)}) copy-start(f32[5,128,16]{1,2,0:T(8,128)} %param.51) | copy-start | bytes 122884
  453.8 82.8 %copy-start.44 = (f32[5,128,16]{1,2,0:T(8,128)S(1)}, f32[5,128,16]{1,2,0:T(8,128)}, u32[]{:S(2)}) copy-start(f32[5,128,16]{1,2,0:T(8,128)} %param.52) | copy-start | bytes 122884
  453.8 82.8 %copy-start.46 = (f32[16,22]{1,0:T(8,128)S(1)}, f32[16,22]{1,0:T(8,128)}, u32[]{:S(2)}) copy-start(f32[16,22]{1,0:T(8,128)} %refs_22_.1) | copy-start | bytes 4228
  453.8 82.8 %copy-start.50 = (f32[16,22]{1,0:T(8,128)S(1)}, f32[16,22]{1,0:T(8,128)}, u32[]{:S(2)}) copy-start(f32[16,22]{1,0:T(8,128)} %refs_23_.1) | copy-start | bytes 4228
  453.8 82.8 %copy-start.51 = (f32[16,22]{1,0:T(8,128)S(1)}, f32[16,22]{1,0:T(8,128)}, u32[]{:S(2)}) copy-start(f32[16,22]{1,0:T(8,128)} %refs_24_.1) | copy-start | bytes 4228
  453.9 82.8 %copy-start.57 = (f32[25]{0:T(128)S(1)}, f32[25]{0:T(128)}, u32[]{:S(2)}) copy-start(f32[25]{0:T(128)} %param.59) | copy-start | bytes 304
  453.9 82.8 %copy-start.58 = (f32[25]{0:T(128)S(1)}, f32[25]{0:T(128)}, u32[]{:S(2)}) copy-start(f32[25]{0:T(128)} %param.60) | copy-start | bytes 304
  453.9 82.8 %copy-start.59 = (f32[25]{0:T(128)S(1)}, f32[25]{0:T(128)}, u32[]{:S(2)}) copy-start(f32[25]{0:T(128)} %param.61) | copy-start | bytes 304
  (26 other events, 50.1 us)
Sparse Core Ops, SparseCore 0:
  10.8 79.2 all-gather.2
  92.3 86.8 all-gather.4
  338.3 176.6 reduce-scatter.1

commit v8 on v7

--- a/solution.py
+++ b/solution.py
@@ -1208,130 +1208,118 @@
     return blocks
 
 
-def residual_sums_kernel(
-    place_ref,
+def residual_kernel_back(
+    near,
+    far,
     own_hbm,
     first_hbm,
     second_hbm,
     y_hbm,
     stat_ref,
     count_ref,
+    gain_ref,
     crop_ref,
     head_ref,
+    bottle_hbm,
     o_ref,
+    part_ref,
+    sum_ref,
     own_ref,
     other_ref,
     y_ref,
+    weights,
+    local_ref,
+    inner,
+    layer_ref,
+    outer,
     sems,
+    weight_sem,
+    sems_in,
+    sems_out,
 ):
+    place = [lax.axis_index("chan")]
     depth = own_ref.shape[1]
+    half = pl.ds(pl.multiple_of(place[0] * depth, 128), depth)
+    weight_copy = pltpu.make_async_copy(bottle_hbm.at[1, half], weights, weight_sem)
     blocks = start_rows(
-        place_ref, (own_hbm, first_hbm, second_hbm, y_hbm), (own_ref, other_ref, y_ref), sems
-    )
-    mean, scale, count = own_norm(place_ref, stat_ref, count_ref)
+        place, (own_hbm, first_hbm, second_hbm, y_hbm), (own_ref, other_ref, y_ref), sems
+    )
+    weight_copy.start()
+    mean, scale, count = own_norm(place, stat_ref, count_ref)
+
+    def upstream(rows):
+        up = crop_ref[rows] * (
+            own_ref[rows].astype(jnp.float32) + other_ref[rows].astype(jnp.float32)
+        )
+        return up, (y_ref[rows].astype(jnp.float32) - mean) * scale
+
     sums = [jnp.zeros((1, depth), jnp.float32)] * 2
     for index, copies in enumerate(blocks):
         for copy in copies:
             copy.wait()
-        rows = slice(index * BLOCK, (index + 1) * BLOCK)
-        up = crop_ref[rows] * (
-            own_ref[rows].astype(jnp.float32) + other_ref[rows].astype(jnp.float32)
-        )
-        normed = (y_ref[rows].astype(jnp.float32) - mean) * scale
+        up, normed = upstream(slice(index * BLOCK, (index + 1) * BLOCK))
         sums[0] = sums[0] + jnp.sum(up * normed, 0, keepdims=True)
         sums[1] = sums[1] + jnp.sum(up, 0, keepdims=True)
+    weight_copy.wait()
     for turn, values in enumerate(sums):
         for part in range(2):
             row = 2 * turn + part
-            o_ref[row : row + 1] = values[:, part * MID : (part + 1) * MID]
-    o_ref[4:5] = jnp.concatenate(
+            local_ref[row : row + 1] = values[:, part * MID : (part + 1) * MID]
+    local_ref[4:5] = jnp.concatenate(
         [head_ref[0:1], head_ref[1:2], head_ref[2:3], jnp.zeros((1, 128), jnp.float32)], 1
     )
-    o_ref[5:8] = jnp.zeros((3, MID), jnp.float32)
-
-
-def residual_sums(place, own, other, expanded, stat, counts, crop, head_stat):
-    hbm = pl.BlockSpec(memory_space=pltpu.HBM)
-    return pl.pallas_call(
-        residual_sums_kernel,
-        out_shape=jax.ShapeDtypeStruct((8, MID), jnp.float32),
-        in_specs=[pl.BlockSpec(memory_space=pltpu.SMEM)] + [hbm] * 4 + vmem(4),
-        out_specs=vmem(1)[0],
-        scratch_shapes=[pltpu.VMEM(own.shape, jnp.bfloat16)] * 3
-        + [pltpu.SemaphoreType.DMA((POSITIONS // BLOCK, 4))],
-        compiler_params=pltpu.CompilerParams(vmem_limit_bytes=60 << 20),
-        cost_estimate=pl.CostEstimate(flops=10**8, bytes_accessed=12 << 20, transcendentals=0),
-        name="residual_sums",
-    )(place, own, *other, expanded, stat, counts, crop, head_stat)
-
-
-def residual_back_kernel(
-    place_ref,
-    own_hbm,
-    first_hbm,
-    second_hbm,
-    y_hbm,
-    stat_ref,
-    count_ref,
-    sum_ref,
-    gain_ref,
-    crop_ref,
-    bottle_hbm,
-    o_ref,
-    part_ref,
-    own_ref,
-    other_ref,
-    y_ref,
-    weights,
-    sems,
-    weight_sem,
-):
-    depth = own_ref.shape[1]
-    half = pl.ds(pl.multiple_of(place_ref[0] * depth, 16), depth)
-    weight_copy = pltpu.make_async_copy(bottle_hbm.at[1, half], weights, weight_sem)
-    weight_copy.start()
-    blocks = start_rows(
-        place_ref, (own_hbm, first_hbm, second_hbm, y_hbm), (own_ref, other_ref, y_ref), sems
-    )
-    mean, scale, count = own_norm(place_ref, stat_ref, count_ref)
-    sums = sum_ref[...]
-    gain_grad = jnp.concatenate([sums[0:1], sums[1:2]], 1) / count
-    shift_grad = jnp.concatenate([sums[2:3], sums[3:4]], 1) / count
+    local_ref[5:8] = jnp.zeros((3, MID), jnp.float32)
+    sum_kernel(near, far, 1, local_ref, sum_ref, inner, layer_ref, outer, sems_in, sems_out)
+    total = sum_ref[...]
+    gain_grad = jnp.concatenate([total[0:1], total[1:2]], 1) / count
+    shift_grad = jnp.concatenate([total[2:3], total[3:4]], 1) / count
     factor = gain_ref[0:1, MID // 2 :] * scale
-    weight_copy.wait()
-    for index, copies in enumerate(blocks):
-        for copy in copies:
-            copy.wait()
-        rows = slice(index * BLOCK, (index + 1) * BLOCK)
-        crop = crop_ref[rows]
-        up = crop * (own_ref[rows].astype(jnp.float32) + other_ref[rows].astype(jnp.float32))
-        normed = (y_ref[rows].astype(jnp.float32) - mean) * scale
-        low = (crop * factor * (up - (shift_grad + normed * gain_grad))).astype(o_ref.dtype)
+
+    def step(index, carry):
+        rows = block_rows(index)
+        up, normed = upstream(rows)
+        low = (crop_ref[rows] * factor * (up - (shift_grad + normed * gain_grad))).astype(
+            o_ref.dtype
+        )
         o_ref[rows] = low
         part_ref[rows] = dot(low, weights[...]).astype(part_ref.dtype)
-
-
-def residual_back(place, own, other, expanded, stat, counts, sums, gains, crop, bottle):
+        return carry
+
+    lax.fori_loop(0, POSITIONS // BLOCK, step, 0)
+
+
+def residual_back(sizes, own, other, expanded, stat, counts, gains, crop, head_stat, bottle):
     hbm = pl.BlockSpec(memory_space=pltpu.HBM)
     depth = own.shape[1]
+    near, far = NEAR, sizes["dp"] // NEAR
+    shape = (8, MID)
     return pl.pallas_call(
-        residual_back_kernel,
+        functools.partial(residual_kernel_back, near, far),
         out_shape=[
             jax.ShapeDtypeStruct((POSITIONS, depth), jnp.bfloat16),
             jax.ShapeDtypeStruct((POSITIONS, MID), jnp.bfloat16),
-        ],
-        in_specs=[pl.BlockSpec(memory_space=pltpu.SMEM)] + [hbm] * 4 + vmem(5) + [hbm],
-        out_specs=vmem(2),
+            jax.ShapeDtypeStruct(shape, jnp.float32),
+        ],
+        in_specs=[hbm] * 4 + vmem(5) + [hbm],
+        out_specs=vmem(3),
         scratch_shapes=[pltpu.VMEM(own.shape, jnp.bfloat16)] * 3
         + [
             pltpu.VMEM((depth, MID), jnp.bfloat16),
+            pltpu.VMEM(shape, jnp.float32),
+            pltpu.VMEM((near,) + shape, jnp.float32),
+            pltpu.VMEM(shape, jnp.float32),
+            pltpu.VMEM((far,) + shape, jnp.float32),
             pltpu.SemaphoreType.DMA((POSITIONS // BLOCK, 4)),
             pltpu.SemaphoreType.DMA,
-        ],
-        compiler_params=pltpu.CompilerParams(vmem_limit_bytes=40 << 20),
+            pltpu.SemaphoreType.DMA((2, near)),
+            pltpu.SemaphoreType.DMA((2, far)),
+        ],
+        compiler_params=pltpu.CompilerParams(
+            collective_id=2, has_side_effects=True, vmem_limit_bytes=60 << 20
+        ),
         cost_estimate=pl.CostEstimate(flops=2 * 10**9, bytes_accessed=16 << 20, transcendentals=0),
         name="residual_back",
-    )(place, own, *other, expanded, stat, counts, sums, gains, crop, bottle)
+    )(own, *other, expanded, stat, counts, gains, crop, head_stat, bottle)
 
 
 def late_kernel(
@@ -1983,20 +1971,16 @@
     )
     pyramid_red = lax.psum_scatter(pyramid_grad, "dp", scatter_dimension=1, tiled=True)
 
-    stat_three = residual_sums(
-        own_place, own_part, other_parts, expand_pre, stat_two, stat_one, crop_field, head_stat
-    )
-    stat_three = all_sum(sizes, stat_three, ("dp",), 2)
-    expand_grad_low, second_part = residual_back(
-        own_place,
+    expand_grad_low, second_part, stat_three = residual_back(
+        sizes,
         own_part,
         other_parts,
         expand_pre,
         stat_two,
         stat_one,
-        stat_three,
         own_gains,
         crop_field,
+        head_stat,
         bottle_low,
     )
     second_other = swap_chan(second_part)

time: 556 us -> 553 us (level)
    pallas_call x1, Pallas kernels: 41.2 us -> 31.6 us  [pyramid_forward(): pl.pallas_call(pyramid_kernel, out_shape=[jax.ShapeDtypeStruct((4, POSITI...]
    pallas_call x5 -> x4, Pallas kernels: 51.3 us -> 43.2 us  [all_sum(): pl.pallas_call(functools.partial(sum_kernel, near, far, chans), out_shape...]
    pallas_call x1, Pallas kernels: 63.1 us -> 69.9 us  [scatter_trunk(): pl.pallas_call(functools.partial(scatter_kernel, layers), out_shape=[jax....]
    pallas_call x2 -> x1, Pallas kernels: 14 us -> 20.6 us  [residual_back(): pl.pallas_call(functools.partial(residual_kernel_back, near, far), out_sh...]
    unnamed x171 -> x161, local copies, waits for them, and re-layouts: 22.8 us -> 17.9 us
  transfers between devices with their start and end apart: 9 -> 9, of which waited for: 4 -> 5; matrix products, arithmetic and copies ran while one was open for 5% -> 5% of each run, Pallas kernels for 60% -> 62%
where the time goes in v8:
time: 553 us; the launch traced here: 549 us
  Pallas kernels  416 us (75%)
  waiting for transfers between devices  55.6 us (10%)
  local copies, waits for them, and re-layouts  30.2 us (5%)
  between operations  16.8 us (3%)
  other arithmetic  11.7 us (2%)
  starting transfers between devices  9.83 us (2%)
  matrix products  8.61 us (2%)
    pallas_call x1, Pallas kernels, gather_trunk(): pl.pallas_call(functools.partial(gather_kernel, count // 4), out_shape=[j...  82.7 us
    pallas_call x1, Pallas kernels, scatter_trunk(): pl.pallas_call(functools.partial(scatter_kernel, layers), out_shape=[jax....  69.9 us
    ppermute x6, waiting for transfers between devices, swap_chan(): return lax.ppermute(values, 'chan', [(0, 1), (1, 0)])  49.8 us
    pallas_call x1, Pallas kernels, own_gradients(): pl.pallas_call(own_kernel, out_shape=[jax.ShapeDtypeStruct((POSITIONS, ha...  43.3 us
    pallas_call x4, Pallas kernels, all_sum(): pl.pallas_call(functools.partial(sum_kernel, near, far, chans), out_shape...  43.2 us
    pallas_call x1, Pallas kernels, pyramid_forward(): pl.pallas_call(pyramid_kernel, out_shape=[jax.ShapeDtypeStruct((4, POSITI...  31.6 us
    pallas_call x2, Pallas kernels, pyramid_field(): pl.pallas_call(field_kernel, out_shape=jax.ShapeDtypeStruct((POSITIONS, d...  23.3 us
    pallas_call x1, Pallas kernels, residual_back(): pl.pallas_call(functools.partial(residual_kernel_back, near, far), out_sh...  20.6 us
  transfers between devices with their start and end apart: 9, of which 5 were waited for; matrix products, arithmetic and copies ran while one was open for 5% of the time, Pallas kernels for 62%

profile of v8, /device:TPU:0, one launch (start us, length us, event | category | flops | bytes accessed | tf_op | source)
XLA Modules:
  0.0 548.9 jit_solution(18130062603758456101)
XLA Ops:
  7.3 1.7 convert_element_type.116
  9.0 0.9 copy-done.65
  9.9 0.8 slice.45
  10.8 2.0 slice.46
  12.9 3.0 collective-permute-start
  16.2 0.7 convert_element_type.110.middle
  17.0 0.7 convert_element_type.109.bottle
  18.1 0.6 fusion.2.head
  18.7 0.6 convert_bitcast_fusion.small
  19.3 82.7 %gather_trunk.1 = (bf16[2,2048,512]{2,1,0:T(8,128)(2,1)}, bf16[9,512,512]{2,1,0:T(8,128)(2,1)}, bf16[2048,192]{1,0:T(8,128)(2,1)}, bf16[256,768]{1,0:T(8,128)(2,1)}) custom-call(bf16[2,128,256]{2,1,0:T(8,128)(2,1)} %convert_element_type.109.bottle, bf16[9,32,256]{2,1,0:T(8,128)(2,1)} %convert_element_type.110.middle, ...), custom_call_target="tpu_custom_call" | custom-call | tf_op jit(solution)/shard_map/gather_trunk/pallas_call | solution.py:393
  102.2 1.2 copy-done.15
  103.4 12.6 %stem_reduce.1 = (bf16[2048,1600]{1,0:T(8,128)(2,1)}, f32[1600,512]{1,0:T(8,128)}, f32[8,512]{1,0:T(8,128)S(1)}) custom-call(bf16[1600,192]{1,0:T(8,128)(2,1)S(1)} %copy.89.p_ref, bf16[2048,192]{1,0:T(8,128)(2,1)S(1)} %copy-done.15, bf16[2,2048,512]{2,1,0:T(8,128)(2,1)} %get-tuple-element.117.reduce_ref.w_ref.bottle_hbm, f32[1600,1]{1,0:T(8,128)S(1)} %copy.90.crop_ref, ...), custom_call_target="tpu_custom_call" | custom-call | flops 5000000000 | bytes 14680064 | tf_op jit(solution)/shard_map/stem_reduce/pallas_call | solution.py:785
  116.0 9.7 %small_sum.4.stat_ref.count_ref.one_ref = f32[8,512]{1,0:T(8,128)S(1)} custom-call(f32[8,512]{1,0:T(8,128)S(1)} %get-tuple-element.118.x_ref), custom_call_target="tpu_custom_call" | custom-call | tf_op jit(solution)/shard_map/small_sum/pallas_call | solution.py:106
  126.0 15.6 %norm_middle.1 = (bf16[1600,512]{1,0:T(8,128)(2,1)}, bf16[512,1600]{1,0:T(8,128)(2,1)}, bf16[1600,512]{1,0:T(8,128)(2,1)}) custom-call(f32[1600,512]{1,0:T(8,128)} %get-tuple-element.119.a_ref, f32[8,512]{1,0:T(8,128)S(1)} %small_sum.4.stat_ref.count_ref.one_ref, s32[1]{0:T(128)} %bitcast.place_ref, f32[2,1280]{1,0:T(2,128)S(1)} %bitcast.88, ...), custom_call_target="tpu_custom_call" | custom-call | flops 8000000000 | bytes 14680064 | tf_op jit(solution)/shard_map/norm_middle/pallas_call | solution.py:858
  141.6 1.4 copy-done.61
  143.1 8.9 %expand_forward.1 = (bf16[1600,2048]{1,0:T(8,128)(2,1)}, f32[8,512]{1,0:T(8,128)S(1)}) custom-call(bf16[1600,512]{1,0:T(8,128)(2,1)S(1)} %copy-done.61, bf16[2,2048,512]{2,1,0:T(8,128)(2,1)} %get-tuple-element.117.reduce_ref.w_ref.bottle_hbm, f32[1600,1]{1,0:T(8,128)S(1)} %copy.90.crop_ref), custom_call_target="tpu_custom_call" | custom-call | flops 4000000000 | bytes 12582912 | tf_op jit(solution)/shard_map/expand_forward/pallas_call | solution.py:895
  152.0 9.4 %small_sum.5.stat_ref = f32[8,512]{1,0:T(8,128)S(1)} custom-call(f32[8,512]{1,0:T(8,128)S(1)} %get-tuple-element.123.x_ref), custom_call_target="tpu_custom_call" | custom-call | tf_op jit(solution)/shard_map/small_sum/pallas_call | solution.py:106
  161.4 12.8 %residual_stream.1 = (bf16[1600,2048]{1,0:T(8,128)(2,1)}, bf16[2048,1600]{1,0:T(8,128)(2,1)}, f32[1,2048]{1,0:T(1,128)S(1)}) custom-call(bf16[1600,192]{1,0:T(8,128)(2,1)S(1)} %copy.89.p_ref, bf16[2048,192]{1,0:T(8,128)(2,1)S(1)} %copy-done.16, bf16[1600,2048]{1,0:T(8,128)(2,1)} %get-tuple-element.122.y_ref.y_hbm, f32[8,512]{1,0:T(8,128)S(1)} %small_sum.5.stat_ref, ...), custom_call_target="tpu_custom_call" | custom-call | flops 2000000000 | bytes 23068672 | tf_op jit(solution)/shard_map/residual_stream/pallas_call | solution.py:947
  175.5 3.6 all-gather.5.cloned.1.call-done.b_hbm
  179.1 31.6 %pyramid_fwd.1 = (f32[4,1600,128]{2,1,0:T(8,128)}, f32[1,128]{1,0:T(1,128)}, bf16[1600,640]{1,0:T(8,128)(2,1)}, bf16[1600,256]{1,0:T(8,128)(2,1)}) custom-call(bf16[1600,2048]{1,0:T(8,128)(2,1)} %get-tuple-element.124.x_ref, f32[1,2048]{1,0:T(1,128)} %copy-done.46, bf16[10,2048,128]{2,1,0:T(8,128)(2,1)} %all-gather.3.cloned.1.call-done.a_hbm, ...), custom_call_target="tpu_custom_call" | custom-call | flops 15938355200 | bytes 41943040 | tf_op jit(solution)/shard_map/pyramid_fwd/pallas_call | solution.py:1051
  211.4 1.5 collective-permute-start.1
  212.9 1.2 fusion.label_ref
  214.1 1.9 fusion.4
  216.3 1.2 pad.18.target_ref
  217.6 1.9 multiply_add_fusion.mask_ref
  219.5 12.5 %collective-permute-done.1.other_ref = bf16[1600,256]{1,0:T(8,128)(2,1)S(1)} collective-permute-done((bf16[1600,256]{1,0:T(8,128)(2,1)}, bf16[1600,256]{1,0:T(8,128)(2,1)S(1)}, u32[]{:S(2)}, u32[]{:S(2)}) %collective-permute-start.1) | collective-permute-done | bytes 819232 | tf_op jit(solution)/shard_map/ppermute | solution.py:126
  232.0 9.5 %head_step.1 = (bf16[1600,256]{1,0:T(8,128)(2,1)S(1)}, bf16[1600,128]{1,0:T(8,128)(2,1)S(1)}, bf16[1600,256]{1,0:T(8,128)(2,1)S(1)}, bf16[4,1600,128]{2,1,0:T(8,...) custom-call(bf16[1600,256]{1,0:T(8,128)(2,1)S(1)} %copy-done.18, ...), custom_call_target="tpu_custom_call" | custom-call | flops 2000000000 | bytes 16777216 | tf_op jit(solution)/shard_map/head_step/pallas_call | solution.py:1151
  241.5 0.9 copy-done.19
  242.5 0.7 copy-done.22
  244.3 0.9 copy-done.60
  245.2 11.5 %pyramid_field.2 = bf16[1600,512]{1,0:T(8,128)(2,1)} custom-call(s32[1]{0:T(128)S(6)} %sub.7.place_ref, bf16[10,2048,128]{2,1,0:T(8,128)(2,1)} %all-gather.3.cloned.1.call-done.a_hbm, bf16[19,2048,128]{2,1,0:T(8,128)(2,1)} %all-gather.5.cloned.1.call-done.b_hbm, bf16[4,1600,128]{2,1,0:T(8,128)(2,1)} %get-tuple-element.141.g_ref, f32[1,128]{1,0:T(1,128)} %copy-done.50, ...), custom_call_target="tpu_custom_call" | custom-call | flops 1000 | bytes 1024 | tf_op jit(solution)/shard_map/pyramid_field/pallas_call | solution.py:720
  256.8 1.5 collective-permute-start.2
  258.3 11.8 %pyramid_field.3 = bf16[1600,512]{1,0:T(8,128)(2,1)} custom-call(s32[1]{0:T(128)S(6)} %add.52.place_ref, bf16[10,2048,128]{2,1,0:T(8,128)(2,1)} %all-gather.3.cloned.1.call-done.a_hbm, bf16[19,2048,128]{2,1,0:T(8,128)(2,1)} %all-gather.5.cloned.1.call-done.b_hbm, bf16[4,1600,128]{2,1,0:T(8,128)(2,1)} %get-tuple-element.141.g_ref, f32[1,128]{1,0:T(1,128)} %copy-done.50, ...), custom_call_target="tpu_custom_call" | custom-call | flops 1000 | bytes 1024 | tf_op jit(solution)/shard_map/pyramid_field/pallas_call | solution.py:720
  270.1 0.6 collective-permute-start.3
  270.7 1.3 copy.99.pooled_ref
  272.0 43.3 %own_gradients.1 = (bf16[1600,1024]{1,0:T(8,128)(2,1)}, bf16[29,2048,128]{2,1,0:T(8,128)(2,1)}) custom-call(s32[1]{0:T(128)} %bitcast.place_ref, bf16[10,2048,128]{2,1,0:T(8,128)(2,1)} %all-gather.3.cloned.1.call-done.a_hbm, bf16[19,2048,128]{2,1,0:T(8,128)(2,1)} %all-gather.5.cloned.1.call-done.b_hbm, bf16[2048,1600]{1,0:T(8,128)(2,1)} %get-tuple-element.139.xt_hbm, ...), custom_call_target="tpu_custom_call" | custom-call | flops 1000 | bytes 1024 | tf_op jit(solution)/shard_map/own_gradients/pallas_call | solution.py:693
  315.3 1.6 convolution_convert_fusion.2
  316.9 2.7 convolution_convert_fusion.1
  319.6 0.8 pad_maximum_fusion
  320.4 1.9 reshape.272
  322.4 6.9 %collective-permute-done.3.second_hbm = bf16[1600,512]{1,0:T(8,128)(2,1)S(1)} collective-permute-done((bf16[1600,512]{1,0:T(8,128)(2,1)}, bf16[1600,512]{1,0:T(8,128)(2,1)S(1)}, u32[]{:S(2)}, u32[]{:S(2)}) %collective-permute-start.3) | collective-permute-done | bytes 1638432 | tf_op jit(solution)/shard_map/ppermute | solution.py:126
  329.3 1.1 copy-done.6
  330.5 20.6 %residual_back.1 = (bf16[1600,1024]{1,0:T(8,128)(2,1)}, bf16[1600,512]{1,0:T(8,128)(2,1)}, f32[8,512]{1,0:T(8,128)}) custom-call(bf16[1600,1024]{1,0:T(8,128)(2,1)} %get-tuple-element.167.own_hbm, bf16[1600,512]{1,0:T(8,128)(2,1)} %copy-done.4, bf16[1600,512]{1,0:T(8,128)(2,1)} %copy-done.6, bf16[1600,2048]{1,0:T(8,128)(2,1)} %get-tuple-element.122.y_ref.y_hbm, ...), custom_call_target="tpu_custom_call" | custom-call | flops 2000000000 | bytes 16777216 | tf_op jit(solution)/shard_map/residual_back/pallas_call | solution.py:1296
  351.1 1.5 collective-permute-start.4
  353.7 4.3 convolution_convert_fusion
  358.0 30.4 %collective-permute-done.4.other_ref = bf16[1600,512]{1,0:T(8,128)(2,1)} collective-permute-done((bf16[1600,512]{1,0:T(8,128)(2,1)}, bf16[1600,512]{1,0:T(8,128)(2,1)}, u32[]{:S(2)}, u32[]{:S(2)}) %collective-permute-start.4) | collective-permute-done | bytes 1638432 | tf_op jit(solution)/shard_map/ppermute | solution.py:126
  388.5 1.6 collective-permute-start.5
  390.1 18.1 %first_back.1 = (f32[1600,512]{1,0:T(8,128)}, bf16[1600,256]{1,0:T(8,128)(2,1)S(1)}, f32[8,512]{1,0:T(8,128)S(1)}) custom-call(s32[1]{0:T(128)} %bitcast.place_ref, bf16[1600,512]{1,0:T(8,128)(2,1)} %get-tuple-element.155.part_ref, bf16[1600,512]{1,0:T(8,128)(2,1)} %collective-permute-done.4.other_ref, bf16[9,512,512]{2,1,0:T(8,128)(2,1)} %get-tuple-element.120.w_ref, ...), custom_call_target="tpu_custom_call" | custom-call | flops 8000000000 | bytes 20971520 | tf_op jit(solution)/shard_map/first_back/pallas_call | solution.py:1633
  408.2 4.4 middle_weights.1
  412.7 1.7 copy.104
  414.4 10.9 %small_sum.6.sum_ref.four_ref = f32[8,512]{1,0:T(8,128)S(1)} custom-call(f32[8,512]{1,0:T(8,128)S(1)} %get-tuple-element.160.x_ref), custom_call_target="tpu_custom_call" | custom-call | tf_op jit(solution)/shard_map/small_sum/pallas_call | solution.py:106
  425.3 8.9 %late_gradients.1 = (bf16[2048,256]{1,0:T(8,128)(2,1)S(1)}, bf16[1024,192]{1,0:T(8,128)(2,1)S(1)}) custom-call(s32[1]{0:T(128)} %bitcast.place_ref, f32[1600,512]{1,0:T(8,128)S(1)} %copy-done.10, f32[1600,512]{1,0:T(8,128)S(1)} %copy-done.9, f32[8,512]{1,0:T(8,128)S(1)} %copy-done.21, f32[8,512]{1,0:T(8,128)S(1)} %small_sum.6.sum_ref.four_ref, ...), custom_call_target="tpu_custom_call" | custom-call | flops 4000000000 | bytes 25165824 | tf_op jit(solution)/shard_map/late_gradients/pallas_call | solution.py:1414
  434.3 0.7 reshape.276
  435.5 1.3 copy-done.64
  437.0 0.8 copy-done.66
  438.0 69.9 %scatter_trunk.1 = (f32[640,256]{1,0:T(8,128)S(1)}, f32[8,128]{1,0:T(8,128)S(1)}) custom-call(bf16[16,640,256]{2,1,0:T(8,128)(2,1)S(1)} %constant_dynamic-update-slice_fusion.p_ref), custom_call_target="tpu_custom_call" | custom-call | tf_op jit(solution)/shard_map/scatter_trunk/pallas_call | solution.py:1551
  508.5 2.2 reduce-scatter.2.cloned.1.call-done.pyramid_ref.refs_1_
  510.7 2.9 own_squares.1
  513.6 0.7 copy-done.53
  514.3 13.2 %small_sum.7.refs_0_ = f32[8,128]{1,0:T(8,128)S(1)} custom-call(f32[8,128]{1,0:T(8,128)S(1)} %copy-done.53), custom_call_target="tpu_custom_call" | custom-call | tf_op jit(solution)/shard_map/small_sum/pallas_call | solution.py:106
  528.2 1.2 copy-done.8
  529.4 0.7 copy-done.45
  530.1 0.7 copy-done.59
  530.8 7.8 %adam.1 = (f32[29,128,128]{2,1,0:T(8,128)}, f32[29,128,128]{2,1,0:T(8,128)}, f32[29,128,128]{2,1,0:T(8,128)}, f32[2,128,256]{2,1,0:T(8,128)}, f32[2,128,256]{2,1...) custom-call(f32[8,128]{1,0:T(8,128)S(1)} %small_sum.7.refs_0_, ...), custom_call_target="tpu_custom_call" | custom-call | flops 100000000 | bytes 18874368 | tf_op jit(solution)/shard_map/adam/pallas_call | solution.py:1693
  (191 shorter events, 9.7 us)
Async XLA Ops:
  7.2 8.7 %copy-start.67 = (s32[1,1600]{1,0:T(1,128)S(1)}, s32[1,1600]{1,0:T(1,128)}, u32[]{:S(2)}) copy-start(s32[1,1600]{1,0:T(1,128)} %param.37) | copy-start | bytes 19204
  7.2 168.3 %all-gather.3.cloned.1.call-start = ((), (), s32[]{:S(2)}) async-start(), calls=%async_computation.1 | async-start | bytes 5570560 | tf_op jit(solution)/shard_map/all_gather | solution.py:1836
  9.9 7.1 %copy-start.17 = (f32[2,128,256]{2,1,0:T(8,128)S(1)}, f32[2,128,256]{2,1,0:T(8,128)}, u32[]{:S(2)}) copy-start(f32[2,128,256]{2,1,0:T(8,128)} %refs_10_.1) | copy-start | bytes 786436
  9.9 7.8 %copy-start.43 = (f32[16,22]{1,0:T(8,128)S(1)}, f32[16,22]{1,0:T(8,128)}, u32[]{:S(2)}) copy-start(f32[16,22]{1,0:T(8,128)} %refs_22_.1) | copy-start | bytes 4228
  9.9 7.8 %copy-start.11 = (bf16[1,1600,192]{1,2,0:T(8,128)(2,1)S(1)}, bf16[1,1600,192]{1,2,0:T(8,128)(2,1)}, u32[]{:S(2)}) copy-start(bf16[1,1600,192]{1,2,0:T(8,128)(2,1)} %param.31) | copy-start | bytes 1843204
  10.7 7.3 %copy-start.54 = (f32[25]{0:T(128)S(1)}, f32[25]{0:T(128)}, u32[]{:S(2)}) copy-start(f32[25]{0:T(128)} %param.59) | copy-start | bytes 304
  10.7 7.4 %copy-start.33 = (f32[5,128,16]{1,2,0:T(8,128)S(1)}, f32[5,128,16]{1,2,0:T(8,128)}, u32[]{:S(2)}) copy-start(f32[5,128,16]{1,2,0:T(8,128)} %param.50) | copy-start | bytes 122884
  10.7 8.0 %copy-start.27 = (f32[192,1,64]{0,2,1:T(8,128)S(1)}, f32[192,1,64]{0,2,1:T(8,128)}, u32[]{:S(2)}) copy-start(f32[192,1,64]{0,2,1:T(8,128)} %param.38) | copy-start | bytes 147460
  10.7 168.4 %all-gather.5.cloned.1.call-start = ((), (), s32[]{:S(2)}) async-start(), calls=%async_computation.2 | async-start | bytes 10584064 | tf_op jit(solution)/shard_map/all_gather | solution.py:1837
  12.8 89.3 %copy-start.68 = (s32[1,1600]{1,0:T(1,128)S(1)}, s32[1,1600]{1,0:T(1,128)}, u32[]{:S(2)}) copy-start(s32[1,1600]{1,0:T(1,128)} %param.36) | copy-start | bytes 19204
  12.8 89.3 %copy-start.69 = (s32[1,1600]{1,0:T(1,128)S(1)}, s32[1,1600]{1,0:T(1,128)}, u32[]{:S(2)}) copy-start(s32[1,1600]{1,0:T(1,128)} %param.34) | copy-start | bytes 19204
  12.8 497.9 %reduce-scatter.2.cloned.1.call-start = ((), (), s32[]{:S(2)}) async-start(), calls=%async_computation.3 | async-start | bytes 16154624 | tf_op jit(solution)/shard_map/reduce_scatter | solution.py:1972
  12.9 148.5 %copy-start.31 = (f32[2,1,1280]{2,0,1:T(2,128)}, f32[2,1,1280]{2,0,1:T(2,128)S(1)}, u32[]{:S(2)}) copy-start(f32[2,1,1280]{2,0,1:T(2,128)S(1)} %copy.117) | copy-start | bytes 30724
  12.9 112.8 %collective-permute-start = (f32[2,1280]{1,0:T(2,128)S(1)}, f32[2,1280]{1,0:T(2,128)S(1)}, u32[]{:S(2)}, u32[]{:S(2)}) collective-permute-start(f32[2,1280]{1,0:T(2,128)S(1)} %bitcast.87), channel_id=1, source_target_pairs={{0,1},{1,0},{2,3},{3,2},{4,5},{5,4},{6,7},{7,6},{8,9},{9,8},{10,11... | collective-permute-start | bytes 30728 | tf_op jit(solution)/shard_map/ppermute | solution.py:126
  16.2 145.2 %copy-start = (f32[1600,1]{1,0:T(8,128)}, f32[1600,1]{1,0:T(8,128)S(1)}, u32[]{:S(2)}) copy-start(f32[1600,1]{1,0:T(8,128)S(1)} %copy.90.crop_ref) | copy-start | bytes 19204
  125.7 85.1 %copy-start.20 = (f32[8,512]{1,0:T(8,128)}, f32[8,512]{1,0:T(8,128)S(1)}, u32[]{:S(2)}) copy-start(f32[8,512]{1,0:T(8,128)S(1)} %small_sum.4.stat_ref.count_ref.one_ref) | copy-start | bytes 49156
  125.7 35.7 %copy-start.39 = (f32[2,1280]{1,0:T(2,128)}, f32[2,1280]{1,0:T(2,128)S(1)}, u32[]{:S(2)}) copy-start(f32[2,1280]{1,0:T(2,128)S(1)} %collective-permute-done.other_ref.gain_ref.other_gain_ref) | copy-start | bytes 30724
  126.0 15.6 %copy-start.2 = (f32[1600,128]{1,0:T(8,128)}, f32[1600,128]{1,0:T(8,128)S(1)}, u32[]{:S(2)}) copy-start(f32[1600,128]{1,0:T(8,128)S(1)} %broadcast_in_dim.22.col_ref) | copy-start | bytes 2457604
  143.1 18.4 %copy-start.16 = (bf16[2048,192]{1,0:T(8,128)(2,1)S(1)}, bf16[2048,192]{1,0:T(8,128)(2,1)}, u32[]{:S(2)}) copy-start(bf16[2048,192]{1,0:T(8,128)(2,1)} %get-tuple-element.116.stem_ref) | copy-start | bytes 2359300
  179.1 33.7 %copy-start.74 = (s32[1,1600]{1,0:T(1,128)S(1)}, s32[1,1600]{1,0:T(1,128)}, u32[]{:S(2)}) copy-start(s32[1,1600]{1,0:T(1,128)} %param.32) | copy-start | bytes 19204
  179.1 35.0 %copy-start.70 = (f32[1,2,1600]{2,1,0:T(2,128)S(1)}, f32[1,2,1600]{2,1,0:T(2,128)}, u32[]{:S(2)}) copy-start(f32[1,2,1600]{2,1,0:T(2,128)} %param.33) | copy-start | bytes 38404
  179.1 35.0 %copy-start.75 = (f32[1,1600]{1,0:T(1,128)S(1)}, f32[1,1600]{1,0:T(1,128)}, u32[]{:S(2)}) copy-start(f32[1,1600]{1,0:T(1,128)} %param.35) | copy-start | bytes 19204
  210.7 21.3 %copy-start.18 = (bf16[1600,256]{1,0:T(8,128)(2,1)S(1)}, bf16[1600,256]{1,0:T(8,128)(2,1)}, u32[]{:S(2)}) copy-start(bf16[1600,256]{1,0:T(8,128)(2,1)} %get-tuple-element.129.own_ref) | copy-start | bytes 2457604
  210.7 21.3 %copy-start.24 = (bf16[256,768]{1,0:T(8,128)(2,1)S(1)}, bf16[256,768]{1,0:T(8,128)(2,1)}, u32[]{:S(2)}) copy-start(bf16[256,768]{1,0:T(8,128)(2,1)} %get-tuple-element.126.project_ref) | copy-start | bytes 1179652
  210.7 21.3 %copy-start.58 = (f32[1,128]{1,0:T(1,128)S(1)}, f32[1,128]{1,0:T(1,128)}, u32[]{:S(2)}) copy-start(f32[1,128]{1,0:T(1,128)} %get-tuple-element.136.pool_pre_ref) | copy-start | bytes 1540
  211.4 20.6 %collective-permute-start.1 = (bf16[1600,256]{1,0:T(8,128)(2,1)}, bf16[1600,256]{1,0:T(8,128)(2,1)S(1)}, u32[]{:S(2)}, u32[]{:S(2)}) collective-permute-start(bf16[1600,256]{1,0:T(8,128)(2,1)} %get-tuple-element.129.own_ref), channel_id=1, source_target_pairs={{0,1},{1,0},{2,3},{3,2},{4,5},{5,4},{6,7},{7,6},{8,9},{9,8},{10,11... | collective-permute-start | bytes 2457608 | tf_op jit(solution)/shard_map/ppermute | solution.py:126
  256.7 13.9 %copy-start.47 = (f32[1,2048]{1,0:T(1,128)S(1)}, f32[1,2048]{1,0:T(1,128)}, u32[]{:S(2)}) copy-start(f32[1,2048]{1,0:T(1,128)} %copy-done.46) | copy-start | bytes 24580
  256.8 65.6 %collective-permute-start.2 = (bf16[1600,512]{1,0:T(8,128)(2,1)}, bf16[1600,512]{1,0:T(8,128)(2,1)S(1)}, u32[]{:S(2)}, u32[]{:S(2)}) collective-permute-start(bf16[1600,512]{1,0:T(8,128)(2,1)} %pyramid_field.2), channel_id=1, source_target_pairs={{0,1},{1,0},{2,3},{3,2},{4,5},{5,4},{6,7},{7,6},{8,9},{9,8},{10,11... | collective-permute-start | bytes 4915208 | tf_op jit(solution)/shard_map/ppermute | solution.py:126
  270.1 59.2 %collective-permute-start.3 = (bf16[1600,512]{1,0:T(8,128)(2,1)}, bf16[1600,512]{1,0:T(8,128)(2,1)S(1)}, u32[]{:S(2)}, u32[]{:S(2)}) collective-permute-start(bf16[1600,512]{1,0:T(8,128)(2,1)} %pyramid_field.3), channel_id=1, source_target_pairs={{0,1},{1,0},{2,3},{3,2},{4,5},{5,4},{6,7},{7,6},{8,9},{9,8},{10,11... | collective-permute-start | bytes 4915208 | tf_op jit(solution)/shard_map/ppermute | solution.py:126
  272.0 43.3 %copy-start.23 = (bf16[1600,128]{1,0:T(8,128)(2,1)S(1)}, bf16[1600,128]{1,0:T(8,128)(2,1)}, u32[]{:S(2)}) copy-start(bf16[1600,128]{1,0:T(8,128)(2,1)} %copy-done.22) | copy-start | bytes 1228804
  330.5 22.7 %copy-start.71 = (f32[2,1,1280]{2,1,0:T(1,128)S(1)}, f32[2,1,1280]{2,1,0:T(1,128)}, u32[]{:S(2)}) copy-start(f32[2,1,1280]{2,1,0:T(1,128)} %param.58) | copy-start | bytes 30724
  330.5 22.7 %copy-start.72 = (f32[2,1,1280]{2,1,0:T(1,128)S(1)}, f32[2,1,1280]{2,1,0:T(1,128)}, u32[]{:S(2)}) copy-start(f32[2,1,1280]{2,1,0:T(1,128)} %param.57) | copy-start | bytes 30724
  330.5 23.2 %copy-start.62 = (bf16[1600,512]{1,0:T(8,128)(2,1)S(1)}, bf16[1600,512]{1,0:T(8,128)(2,1)}, u32[]{:S(2)}) copy-start(bf16[1600,512]{1,0:T(8,128)(2,1)} %get-tuple-element.121.a_ref) | copy-start | bytes 4915204
  351.1 37.3 %collective-permute-start.4 = (bf16[1600,512]{1,0:T(8,128)(2,1)}, bf16[1600,512]{1,0:T(8,128)(2,1)}, u32[]{:S(2)}, u32[]{:S(2)}) collective-permute-start(bf16[1600,512]{1,0:T(8,128)(2,1)} %get-tuple-element.155.part_ref), channel_id=1, source_target_pairs={{0,1},{1,0},{2,3},{3,2},{4,5},{5,4},{6,7},{7,6},{8,9},{9,8},{10,11... | collective-permute-start | bytes 4915208 | tf_op jit(solution)/shard_map/ppermute | solution.py:126
  353.7 36.4 %copy-start.1 = (f32[1600,1]{1,0:T(8,128)S(1)}, f32[1600,1]{1,0:T(8,128)}, u32[]{:S(2)}) copy-start(f32[1600,1]{1,0:T(8,128)} %copy-done) | copy-start | bytes 19204
  353.7 36.4 %copy-start.3 = (f32[1600,128]{1,0:T(8,128)S(1)}, f32[1600,128]{1,0:T(8,128)}, u32[]{:S(2)}) copy-start(f32[1600,128]{1,0:T(8,128)} %copy-done.2) | copy-start | bytes 2457604
  353.7 36.4 %copy-start.21 = (f32[8,512]{1,0:T(8,128)S(1)}, f32[8,512]{1,0:T(8,128)}, u32[]{:S(2)}) copy-start(f32[8,512]{1,0:T(8,128)} %copy-done.20) | copy-start | bytes 49156
  353.7 36.4 %copy-start.32 = (f32[2,1,1280]{2,0,1:T(2,128)S(1)}, f32[2,1,1280]{2,0,1:T(2,128)}, u32[]{:S(2)}) copy-start(f32[2,1,1280]{2,0,1:T(2,128)} %copy-done.31) | copy-start | bytes 30724
  353.7 36.4 %copy-start.40 = (f32[2,1280]{1,0:T(2,128)S(1)}, f32[2,1280]{1,0:T(2,128)}, u32[]{:S(2)}) copy-start(f32[2,1280]{1,0:T(2,128)} %copy-done.39) | copy-start | bytes 30724
  388.4 19.8 %copy-start.63 = (bf16[512,1600]{1,0:T(8,128)(2,1)S(1)}, bf16[512,1600]{1,0:T(8,128)(2,1)}, u32[]{:S(2)}) copy-start(bf16[512,1600]{1,0:T(8,128)(2,1)} %get-tuple-element.171.xt_ref) | copy-start | bytes 4915204
  388.5 36.8 %collective-permute-start.5 = (bf16[1024,256]{1,0:T(8,128)(2,1)S(1)}, bf16[1024,256]{1,0:T(8,128)(2,1)S(1)}, u32[]{:S(2)}, u32[]{:S(2)}) collective-permute-start(bf16[1024,256]{1,0:T(8,128)(2,1)S(1)} %get-tuple-element.285), channel_id=1, source_target_pairs={{0,1},{1,0},{2,3},{3,2},{4,5},{5,4},{6,7},{7,6},{8,9},{9,8},{10,11... | collective-permute-start | bytes 1572872 | tf_op jit(solution)/shard_map/ppermute | solution.py:126
  408.2 17.1 %copy-start.9 = (f32[1600,512]{1,0:T(8,128)S(1)}, f32[1600,512]{1,0:T(8,128)}, u32[]{:S(2)}) copy-start(f32[1600,512]{1,0:T(8,128)} %get-tuple-element.119.a_ref) | copy-start | bytes 9830404
  408.2 17.1 %copy-start.10 = (f32[1600,512]{1,0:T(8,128)S(1)}, f32[1600,512]{1,0:T(8,128)}, u32[]{:S(2)}) copy-start(f32[1600,512]{1,0:T(8,128)} %get-tuple-element.166.up_ref) | copy-start | bytes 9830404
  412.6 12.7 %copy-start.5 = (bf16[1600,512]{1,0:T(8,128)(2,1)S(1)}, bf16[1600,512]{1,0:T(8,128)(2,1)}, u32[]{:S(2)}) copy-start(bf16[1600,512]{1,0:T(8,128)(2,1)} %copy-done.4) | copy-start | bytes 4915204
  412.6 12.7 %copy-start.7 = (bf16[1600,512]{1,0:T(8,128)(2,1)S(1)}, bf16[1600,512]{1,0:T(8,128)(2,1)}, u32[]{:S(2)}) copy-start(bf16[1600,512]{1,0:T(8,128)(2,1)} %copy-done.6) | copy-start | bytes 4915204
  412.6 12.7 %copy-start.12 = (bf16[1,1600,192]{1,2,0:T(8,128)(2,1)S(1)}, bf16[1,1600,192]{1,2,0:T(8,128)(2,1)}, u32[]{:S(2)}) copy-start(bf16[1,1600,192]{1,2,0:T(8,128)(2,1)} %param.31) | copy-start | bytes 1843204
  425.3 9.0 %copy-start.36 = (f32[8,512]{1,0:T(8,128)}, f32[8,512]{1,0:T(8,128)S(1)}, u32[]{:S(2)}) copy-start(f32[8,512]{1,0:T(8,128)S(1)} %small_sum.6.sum_ref.four_ref) | copy-start | bytes 49156
  437.8 90.3 %copy-start.14 = (f32[9,32,256]{2,1,0:T(8,128)S(1)}, f32[9,32,256]{2,1,0:T(8,128)}, u32[]{:S(2)}) copy-start(f32[9,32,256]{2,1,0:T(8,128)} %refs_13_.1) | copy-start | bytes 884740
  437.8 90.3 %copy-start.25 = (f32[9,32,256]{2,1,0:T(8,128)S(1)}, f32[9,32,256]{2,1,0:T(8,128)}, u32[]{:S(2)}) copy-start(f32[9,32,256]{2,1,0:T(8,128)} %refs_14_.1) | copy-start | bytes 884740
  437.8 90.3 %copy-start.26 = (f32[9,32,256]{2,1,0:T(8,128)S(1)}, f32[9,32,256]{2,1,0:T(8,128)}, u32[]{:S(2)}) copy-start(f32[9,32,256]{2,1,0:T(8,128)} %refs_15_.1) | copy-start | bytes 884740
  437.8 90.2 %copy-start.28 = (f32[192,1,64]{0,2,1:T(8,128)S(1)}, f32[192,1,64]{0,2,1:T(8,128)}, u32[]{:S(2)}) copy-start(f32[192,1,64]{0,2,1:T(8,128)} %param.38) | copy-start | bytes 147460
  437.8 90.2 %copy-start.29 = (f32[2,128,256]{2,1,0:T(8,128)S(1)}, f32[2,128,256]{2,1,0:T(8,128)}, u32[]{:S(2)}) copy-start(f32[2,128,256]{2,1,0:T(8,128)} %refs_11_.1) | copy-start | bytes 786436
  437.9 90.2 %copy-start.30 = (f32[2,128,256]{2,1,0:T(8,128)S(1)}, f32[2,128,256]{2,1,0:T(8,128)}, u32[]{:S(2)}) copy-start(f32[2,128,256]{2,1,0:T(8,128)} %refs_12_.1) | copy-start | bytes 786436
  437.9 90.2 %copy-start.34 = (f32[5,128,16]{1,2,0:T(8,128)S(1)}, f32[5,128,16]{1,2,0:T(8,128)}, u32[]{:S(2)}) copy-start(f32[5,128,16]{1,2,0:T(8,128)} %param.50) | copy-start | bytes 122884
  437.9 90.2 %copy-start.37 = (f32[192,1,64]{0,2,1:T(8,128)S(1)}, f32[192,1,64]{0,2,1:T(8,128)}, u32[]{:S(2)}) copy-start(f32[192,1,64]{0,2,1:T(8,128)} %param.39) | copy-start | bytes 147460
  437.9 90.2 %copy-start.38 = (f32[192,1,64]{0,2,1:T(8,128)S(1)}, f32[192,1,64]{0,2,1:T(8,128)}, u32[]{:S(2)}) copy-start(f32[192,1,64]{0,2,1:T(8,128)} %param.40) | copy-start | bytes 147460
  437.9 90.2 %copy-start.41 = (f32[5,128,16]{1,2,0:T(8,128)S(1)}, f32[5,128,16]{1,2,0:T(8,128)}, u32[]{:S(2)}) copy-start(f32[5,128,16]{1,2,0:T(8,128)} %param.51) | copy-start | bytes 122884
  437.9 90.2 %copy-start.42 = (f32[5,128,16]{1,2,0:T(8,128)S(1)}, f32[5,128,16]{1,2,0:T(8,128)}, u32[]{:S(2)}) copy-start(f32[5,128,16]{1,2,0:T(8,128)} %param.52) | copy-start | bytes 122884
  437.9 90.2 %copy-start.44 = (f32[16,22]{1,0:T(8,128)S(1)}, f32[16,22]{1,0:T(8,128)}, u32[]{:S(2)}) copy-start(f32[16,22]{1,0:T(8,128)} %refs_22_.1) | copy-start | bytes 4228
  437.9 90.2 %copy-start.48 = (f32[16,22]{1,0:T(8,128)S(1)}, f32[16,22]{1,0:T(8,128)}, u32[]{:S(2)}) copy-start(f32[16,22]{1,0:T(8,128)} %refs_23_.1) | copy-start | bytes 4228
  438.0 90.2 %copy-start.49 = (f32[16,22]{1,0:T(8,128)S(1)}, f32[16,22]{1,0:T(8,128)}, u32[]{:S(2)}) copy-start(f32[16,22]{1,0:T(8,128)} %refs_24_.1) | copy-start | bytes 4228
  438.0 90.2 %copy-start.55 = (f32[25]{0:T(128)S(1)}, f32[25]{0:T(128)}, u32[]{:S(2)}) copy-start(f32[25]{0:T(128)} %param.59) | copy-start | bytes 304
  438.0 90.2 %copy-start.56 = (f32[25]{0:T(128)S(1)}, f32[25]{0:T(128)}, u32[]{:S(2)}) copy-start(f32[25]{0:T(128)} %param.60) | copy-start | bytes 304
  438.0 90.2 %copy-start.57 = (f32[25]{0:T(128)S(1)}, f32[25]{0:T(128)}, u32[]{:S(2)}) copy-start(f32[25]{0:T(128)} %param.61) | copy-start | bytes 304
  (21 other events, 35.1 us)
Sparse Core Ops, SparseCore 0:
  10.8 79.2 all-gather.2
  92.3 86.7 all-gather.4
  329.4 181.1 reduce-scatter.1
